TPU v7x, 32 devices: a whole 2x2x4 slice. The times are simulated.
32 devices in a mesh: grp: 4 (over y, core), cache: 8 (over z, x).
Axes of the slice: x: 2, y: 2, z: 4, core: 2. Of those that a mesh axis runs over, the one named last changes fastest.
Arguments:
- queries: bfloat16 [128, 4, 8192], P(('grp', 'cache')), may hold values from -6 to 6
- new_kv: bfloat16 [128, 4, 2048], P(('grp', 'cache')), may hold values from -6 to 6
- kv_cache: bfloat16 [512, 128, 2048], P(('grp', 'cache')), may hold values from -6 to 6
- page_owner: int32 [128, 4], P(('grp', 'cache')), may hold values from 0 to 7, all different within a row; in each aligned block of 4 rows (0 to 3, 4 to 7, ...) at most 4 rows name the same one
- page_index: int32 [128, 4, 1], P(('grp', 'cache')), may hold values from 0 to 15
- lengths: int32 [128], P(('grp', 'cache')), may hold values from 1 to 512, as said below
Outputs:
- attention_out: bfloat16 [128, 4, 8192], P(('grp', 'cache'))
Inputs may be any that keep to these rules, and one draw needn't show every extreme that they name: `page_owner`: each row names 4 different owners; among the 4 rows held by one device no owner is named by more than 4 rows, and in every draw some owner is named by exactly 4 rows of some device. `lengths`: some request has exactly 512 valid tokens in every draw.
All inputs are finite; a program needn't handle non-finite values.
Results may differ from a plain program's by a relative error of at most 0.0051.
Values may be sent and summed in bfloat16 or wider, within the bound.
No kernel may reach another device: no remote copies, remote signals or barrier semaphores. Data moves between devices by JAX's collectives and lax.ppermute only.
A program may use at most 192 MiB of HBM per device.

v0:
```python
from functools import partial
import math

import jax
import jax.numpy as jnp
from jax import lax
from jax.sharding import PartitionSpec as P

KVH = 8
HD = 128
GQ = 8
STEPS = 4
PAGE = 128
SEL = 4
PPO = 1


neg_fill = -1e30
block_rows = 16


def item_partial(query_row, panel_rows, valid_count):
    token_count = panel_rows.shape[0]
    query_heads = query_row.reshape(STEPS, KVH, GQ, HD)
    key_rows = panel_rows[:, : KVH * HD].reshape(token_count, KVH, HD)
    value_rows = panel_rows[:, KVH * HD :].reshape(token_count, KVH, HD)
    scores = jnp.einsum(
        "tkgd,ukd->tkgu", query_heads, key_rows, preferred_element_type=jnp.float32
    ) * (1.0 / math.sqrt(HD))
    usable = jnp.arange(token_count, dtype=jnp.int32) < valid_count
    scores = jnp.where(usable, scores, neg_fill)
    highest = jnp.max(scores, axis=-1)
    weights = jnp.where(usable, jnp.exp(scores - highest[..., None]), 0.0)
    weight_sum = jnp.sum(weights, axis=-1)
    mixture = jnp.einsum(
        "tkgu,ukd->tkgd",
        weights.astype(jnp.bfloat16),
        value_rows,
        preferred_element_type=jnp.float32,
    )
    normed = (mixture / jnp.maximum(weight_sum, 1.0)[..., None]).astype(jnp.bfloat16)
    return (
        normed.reshape(STEPS, KVH * GQ * HD),
        highest.reshape(STEPS, KVH * GQ),
        weight_sum.reshape(STEPS, KVH * GQ),
    )


def new_partial(query_row, new_row):
    query_heads = query_row.reshape(STEPS, KVH, GQ, HD)
    key_rows = new_row[:, : KVH * HD].reshape(STEPS, KVH, HD)
    value_rows = new_row[:, KVH * HD :].reshape(STEPS, KVH, HD)
    scores = jnp.einsum(
        "tkgd,ukd->tkgu", query_heads, key_rows, preferred_element_type=jnp.float32
    ) * (1.0 / math.sqrt(HD))
    causal = (jnp.arange(STEPS)[:, None] >= jnp.arange(STEPS)[None, :])[:, None, None, :]
    scores = jnp.where(causal, scores, neg_fill)
    highest = jnp.max(scores, axis=-1)
    weights = jnp.where(causal, jnp.exp(scores - highest[..., None]), 0.0)
    weight_sum = jnp.sum(weights, axis=-1)
    mixture = jnp.einsum(
        "tkgu,ukd->tkgd",
        weights.astype(jnp.bfloat16),
        value_rows,
        preferred_element_type=jnp.float32,
    )
    return (
        mixture.reshape(STEPS, KVH * GQ, HD),
        highest.reshape(STEPS, KVH * GQ),
        weight_sum.reshape(STEPS, KVH * GQ),
    )


def plan_slots(owner_table, page_table, length_rows, owner_ids, capacity):
    visitor_count = owner_table.shape[0]
    matches = (owner_table[:, :, None] == owner_ids[None, None, :]).astype(jnp.int32)
    hit_table = jnp.sum(matches, axis=1)
    slot_rank = jnp.cumsum(hit_table, axis=0) - hit_table
    slot_ids = jnp.arange(capacity, dtype=jnp.int32)
    select = hit_table.T[:, None, :] * (slot_rank.T[:, None, :] == slot_ids[None, :, None]).astype(
        jnp.int32
    )
    item_span = PPO * PAGE
    starts = jnp.arange(SEL, dtype=jnp.int32) * item_span
    counts = jnp.clip(length_rows[:, None] - starts[None, :], 0, item_span)
    item_count = jnp.sum(matches * counts[:, :, None], axis=1)
    item_pages = jnp.sum(matches[:, :, :, None] * page_table[:, :, None, :], axis=1)
    item_meta = jnp.concatenate([item_count[:, :, None], item_pages], axis=2)
    slot_meta = jnp.sum(
        select[:, :, :, None] * jnp.transpose(item_meta, (1, 0, 2))[:, None, :, :], axis=2
    )
    slot_visitor = jnp.sum(
        select * jnp.arange(visitor_count, dtype=jnp.int32)[None, None, :], axis=2
    )
    return (select, slot_meta, hit_table, slot_rank, slot_visitor)


def owner_work(item_queries, item_meta, kv_cache):
    first_dim = item_queries.shape[0]
    second_dim = item_queries.shape[1]
    row_count = first_dim * second_dim
    flat_queries = item_queries.reshape(row_count, STEPS, -1)
    flat_meta = item_meta.reshape(row_count, -1)
    pieces_out = []
    pieces_top = []
    pieces_sum = []
    for offset in range(0, row_count, block_rows):
        finish = min(offset + block_rows, row_count)
        meta_part = flat_meta[offset:finish]
        panel_rows = kv_cache[meta_part[:, 1:]].reshape(finish - offset, -1, kv_cache.shape[2])
        part_out, part_top, part_sum = jax.vmap(item_partial)(
            flat_queries[offset:finish], panel_rows, meta_part[:, 0]
        )
        pieces_out.append(part_out)
        pieces_top.append(part_top)
        pieces_sum.append(part_sum)
    whole_out = jnp.concatenate(pieces_out, axis=0).reshape(first_dim, second_dim, -1)
    whole_top = jnp.concatenate(pieces_top, axis=0).reshape(first_dim, second_dim, -1)
    whole_sum = jnp.concatenate(pieces_sum, axis=0).reshape(first_dim, second_dim, -1)
    return (whole_out, whole_top, whole_sum)


def per_device(queries, new_kv, kv_cache, page_owner, page_index, lengths):
    group_count = lax.axis_size("grp")
    owner_count = lax.axis_size("cache")
    visitor_count = queries.shape[0]
    per_group = visitor_count // group_count
    capacity = max(2, (2 * visitor_count * SEL + owner_count - 1) // owner_count)
    sent_queries = queries.reshape(group_count, per_group, STEPS, -1)
    sent_new = new_kv.reshape(group_count, per_group, STEPS, -1)
    got_queries, got_new = (
        lax.all_to_all(sent_queries, "grp", split_axis=0, concat_axis=0, tiled=True),
        lax.all_to_all(sent_new, "grp", split_axis=0, concat_axis=0, tiled=True),
    )
    visit_queries = got_queries.reshape(visitor_count, STEPS, -1)
    visit_new = got_new.reshape(visitor_count, STEPS, -1)
    owner_ids = jnp.arange(owner_count, dtype=jnp.int32)
    select, slot_meta, hit_table, slot_rank, slot_visitor = plan_slots(
        page_owner, page_index, lengths, owner_ids, capacity
    )
    flat_queries = visit_queries.reshape(visitor_count, -1)
    all_queries, all_owner, all_pages, all_len = (
        lax.all_gather(flat_queries, "cache", axis=0, tiled=True),
        lax.all_gather(page_owner, "cache", axis=0, tiled=True),
        lax.all_gather(page_index, "cache", axis=0, tiled=True),
        lax.all_gather(lengths, "cache", axis=0, tiled=True),
    )
    owner_here = lax.axis_index("cache")
    owner_list = jnp.reshape(owner_here, (1,))
    plan_each = jax.vmap(partial(plan_slots, capacity=capacity), in_axes=(0, 0, 0, None))
    select_all, meta_all, unused_hits, unused_rank, unused_visitor = plan_each(
        all_owner.reshape(owner_count, visitor_count, SEL),
        all_pages.reshape(owner_count, visitor_count, SEL, PPO),
        all_len.reshape(owner_count, visitor_count),
        owner_list,
    )
    select_here = select_all[:, 0]
    meta_here = meta_all[:, 0]
    slot_queries = jnp.einsum(
        "scr,srx->scx",
        select_here.astype(jnp.bfloat16),
        all_queries.reshape(owner_count, visitor_count, -1),
        preferred_element_type=jnp.float32,
    ).astype(jnp.bfloat16)
    part_out, part_top, part_sum = owner_work(slot_queries, meta_here, kv_cache)
    back_out = lax.all_to_all(part_out, "cache", split_axis=0, concat_axis=0, tiled=True)
    back_top, back_sum = (
        lax.all_to_all(part_top, "cache", split_axis=0, concat_axis=0, tiled=True),
        lax.all_to_all(part_sum, "cache", split_axis=0, concat_axis=0, tiled=True),
    )
    new_mix, new_top, new_sum = jax.vmap(new_partial)(visit_queries, visit_new)
    head_rows = STEPS * KVH * GQ
    new_top_flat = new_top.reshape(visitor_count, head_rows)
    new_sum_flat = new_sum.reshape(visitor_count, head_rows)
    slot_index = jnp.clip(slot_rank, 0, capacity - 1).T
    item_top = jnp.take_along_axis(back_top, slot_index[:, :, None], axis=1)
    item_sum = jnp.take_along_axis(back_sum, slot_index[:, :, None], axis=1)
    present = hit_table.T[:, :, None] > 0
    item_top = jnp.where(present, item_top, neg_fill)
    item_sum = jnp.where(present, item_sum, 0.0)
    peak_score = jnp.maximum(new_top_flat, jnp.max(item_top, axis=0))
    item_weight = jnp.exp(item_top - peak_score[None]) * item_sum
    new_weight = jnp.exp(new_top_flat - peak_score)
    denominator = jnp.sum(item_weight, axis=0) + new_weight * new_sum_flat
    slot_peak = peak_score[slot_visitor]
    slot_weight = jnp.exp(back_top - slot_peak) * back_sum
    back_values = back_out.astype(jnp.float32).reshape(owner_count, capacity, head_rows, HD)
    weighted = (slot_weight[..., None] * back_values).reshape(owner_count, capacity, -1)
    numerator = jnp.einsum(
        "ocr,ocx->rx", select.astype(jnp.float32), weighted, precision=lax.Precision.HIGHEST
    )
    numerator = (
        numerator.reshape(visitor_count, STEPS, KVH * GQ, HD)
        + new_weight.reshape(visitor_count, STEPS, KVH * GQ, 1) * new_mix
    )
    result_rows = (numerator / denominator.reshape(visitor_count, STEPS, KVH * GQ, 1)).astype(
        jnp.bfloat16
    )
    result_rows = result_rows.reshape(group_count, per_group, STEPS, -1)
    at_home = lax.all_to_all(result_rows, "grp", split_axis=0, concat_axis=0, tiled=True)
    return at_home.reshape(visitor_count, STEPS, -1)


def solution(mesh):
    in_specs = (
        P(("grp", "cache"), None, None),
        P(("grp", "cache"), None, None),
        P(("grp", "cache"), None, None),
        P(("grp", "cache"), None),
        P(("grp", "cache"), None, None),
        P(("grp", "cache")),
    )
    out_specs = P(("grp", "cache"), None, None)
    return jax.shard_map(
        per_device, mesh=mesh, in_specs=in_specs, out_specs=out_specs, check_vma=False
    )
```

profile of v0, /device:TPU:0, one launch (start us, length us, event | category | flops | bytes accessed | tf_op | source)
XLA Modules:
  0.0 274.5 jit_solution(14885198344768787861)
XLA Ops:
  6.5 10.3 %all_to_all.30 = bf16[4,1,4,8192]{3,2,1,0:T(4,128)(2,1)S(1)} all-to-all(bf16[4,1,4,8192]{3,2,1,0:T(4,128)(2,1)} %bitcast.192), channel_id=1, replica_groups=mesh['grp'=4,'cache'=8] {'grp'}, dimensions={0} | all-to-all | bytes 524288 | tf_op jit(solution)/shard_map/all_to_all | solution.py:132
  21.1 27.2 %all-gather = s32[8,4,4]{2,1,0:T(4,128)S(1)} all-gather(s32[1,4,4]{2,1,0:T(4,128)} %bitcast.208), channel_id=1, replica_groups=mesh['grp'=4,'cache'=8] {'cache'}, dimensions={0}, use_global_device_ids=true | all-gather | bytes 576 | tf_op jit(solution)/shard_map/all_gather | solution.py:144
  51.5 9.6 %all-reduce = s32[32]{0:T(128)S(1)} all-reduce(s32[32]{0:T(128)S(1)} %dynamic-update-slice), channel_id=1, replica_groups=mesh['grp'=4,'cache'=8] {'cache'}, use_global_device_ids=true, to_apply=%add | all-reduce | flops 32 | bytes 256
  61.6 26.1 %all_gather.14 = s32[32,4,1]{1,2,0:T(1,128)S(1)} all-gather(s32[4,4,1]{1,2,0:T(1,128)} %param.12), channel_id=1, replica_groups=mesh['grp'=4,'cache'=8] {'cache'}, dimensions={0}, use_global_device_ids=true | all-gather | bytes 576 | tf_op jit(solution)/shard_map/all_gather | solution.py:145
  88.8 8.0 %gather_fusion.1 = bf16[16,128,2048]{2,1,0:T(8,128)(2,1)} fusion(bf16[16,128,2048]{2,1,0:T(8,128)(2,1)} %param.10, s32[1024]{0:T(1024)S(1)} %pad_clamp_fusion.1), kind=kCustom, calls=%fused_computation.3 | custom fusion | bytes 16777280 | tf_op jit(solution)/shard_map/gather | solution.py:110
  96.8 6.1 %fusion.75 = (bf16[16,128,1024]{2,1,0:T(8,128)(2,1)}, bf16[16,128,1024]{2,1,0:T(8,128)(2,1)}) fusion(bf16[16,128,2048]{2,1,0:T(8,128)(2,1)} %gather_fusion.1), kind=kLoop, calls=%fused_computation.121 | loop fusion | bytes 16777216 | tf_op jit(solution)/shard_map/vmap()/slice | solution.py:26
  102.9 6.4 %copy.271 = bf16[16,128,1024]{1,2,0:T(8,128)(2,1)} copy(bf16[16,128,1024]{2,1,0:T(8,128)(2,1)} %get-tuple-element.14) | data formatting | bytes 8388608 | tf_op jit(solution)/shard_map/vmap()/slice | solution.py:26
  109.3 6.4 %copy.254 = bf16[16,128,1024]{1,2,0:T(8,128)(2,1)} copy(bf16[16,128,1024]{2,1,0:T(8,128)(2,1)} %get-tuple-element.15) | data formatting | bytes 8388608 | tf_op jit(solution)/shard_map/vmap()/slice | solution.py:25
  115.7 8.0 %gather_fusion = bf16[16,128,2048]{2,1,0:T(8,128)(2,1)} fusion(bf16[16,128,2048]{2,1,0:T(8,128)(2,1)} %param.10, s32[1024]{0:T(1024)S(1)} %pad_clamp_fusion.2), kind=kCustom, calls=%fused_computation.2 | custom fusion | bytes 16777280 | tf_op jit(solution)/shard_map/gather | solution.py:110
  123.7 6.0 %fusion.74 = (bf16[16,128,1024]{2,1,0:T(8,128)(2,1)}, bf16[16,128,1024]{2,1,0:T(8,128)(2,1)}) fusion(bf16[16,128,2048]{2,1,0:T(8,128)(2,1)} %gather_fusion), kind=kLoop, calls=%fused_computation.120 | loop fusion | bytes 16777216 | tf_op jit(solution)/shard_map/vmap()/slice | solution.py:26
  129.7 6.4 %copy.268 = bf16[16,128,1024]{1,2,0:T(8,128)(2,1)} copy(bf16[16,128,1024]{2,1,0:T(8,128)(2,1)} %get-tuple-element.12) | data formatting | bytes 8388608 | tf_op jit(solution)/shard_map/vmap()/slice | solution.py:26
  136.1 6.4 %copy.248 = bf16[16,128,1024]{1,2,0:T(8,128)(2,1)} copy(bf16[16,128,1024]{2,1,0:T(8,128)(2,1)} %get-tuple-element.13) | data formatting | bytes 8388608 | tf_op jit(solution)/shard_map/vmap()/slice | solution.py:25
  150.0 3.8 %bitcast_reduce_fusion = (f32[16,4,8,8]{3,1,2,0:T(4,128)S(1)}, f32[16,8,128,4,8]{2,4,3,1,0:T(8,128)S(1)}) fusion(pred[16,128]{1,0:T(8,128)(4,1)S(1)} %iota_compare_fusion, bf16[16,128,8,128,1]{1,3,4,2,0:T(8,128)(2,1)} %bitcast.181, bf16[16,4,8,8,128]{4,3,2,1,0:T(8,128)(2,1)} %reshape.249), kind=kOutput, calls=%fused_computation.15 | convolution fusion | flops 135786496 | bytes 7358464 | tf_op jit(solution)/shard_map/vmap(tkgd,ukd->tkgu)/dot_general | solution.py:27
  156.8 4.8 %bitcast_reduce_fusion.1 = (f32[16,4,8,8]{3,1,2,0:T(4,128)S(1)}, f32[16,8,128,4,8]{2,4,3,1,0:T(8,128)}) fusion(pred[16,128]{1,0:T(8,128)(4,1)S(1)} %iota_compare_fusion.2, bf16[16,128,8,128,1]{1,3,4,2,0:T(8,128)(2,1)} %bitcast.182, bf16[16,4,8,8,128]{4,3,2,1,0:T(8,128)(2,1)S(1)} %copy-done.4), kind=kOutput, calls=%fused_computation.19 | convolution fusion | flops 135786496 | bytes 7358464 | tf_op jit(solution)/shard_map/vmap(tkgd,ukd->tkgu)/dot_general | solution.py:27
  165.2 5.3 %fusion.2 = bf16[16,4,8,8,128]{4,3,1,2,0:T(8,128)(2,1)} fusion(bf16[16,128,8,128,1]{1,3,4,2,0:T(8,128)(2,1)} %bitcast.179, f32[16,8,128,4,8]{2,4,3,1,0:T(8,128)S(1)} %get-tuple-element.27, f32[16,4,8,8]{3,1,2,0:T(4,128)} %broadcast_maximum_fusion, f32[16,4,8,8]{3,1,2,0:T(4,128)S(1)} %get-tuple-element.26, pred[16,128]{1,0:T(8,128)(4,1)S(1)} %iota_compare_fusion), kind=kOutput, calls=%fused_computation.11 | convolution fusion | flops 137887744 | bytes 7374848 | tf_op jit(solution)/shard_map/vmap(tkgu,ukd->tkgd)/dot_general | solution.py:35
  175.2 3.3 %all-to-all-start.1 = ((f32[8,4,256]{2,1,0:T(4,128)}), f32[8,4,256]{2,1,0:T(4,128)S(1)}, u32[]{:S(2)}, u32[]{:S(2)}) async-start(f32[8,4,256]{2,1,0:T(4,128)} %reshape.251), calls=%async_computation.1 | async-start | bytes 65536 | tf_op jit(solution)/shard_map/all_to_all | solution.py:168
  185.2 3.7 %all-to-all-start.3 = ((f32[8,4,256]{2,1,0:T(4,128)}), f32[8,4,256]{2,1,0:T(4,128)S(1)}, u32[]{:S(2)}, u32[]{:S(2)}) async-start(f32[8,4,256]{2,1,0:T(4,128)} %reshape.258), calls=%async_computation.3 | async-start | bytes 65536 | tf_op jit(solution)/shard_map/all_to_all | solution.py:169
  195.9 7.4 %all-to-all-start.4 = ((bf16[8,4,32768]{2,1,0:T(4,128)(2,1)}), bf16[8,4,32768]{2,1,0:T(4,128)(2,1)S(1)}, u32[]{:S(2)}, u32[]{:S(2)}) async-start(bf16[8,4,32768]{2,1,0:T(4,128)(2,1)} %reshape.263), calls=%async_computation.4 | async-start | bytes 4194304 | tf_op jit(solution)/shard_map/all_to_all | solution.py:166
  213.0 5.6 %mul.132 = f32[8,4,32768]{2,1,0:T(4,128)} reshape(f32[8,4,256,128]{3,2,1,0:T(8,128)} %mul.131) | data formatting | bytes 8388608 | tf_op jit(solution)/shard_map/mul | solution.py:188
  218.6 20.6 %all-to-all-done.4 = bf16[8,4,32768]{2,1,0:T(4,128)(2,1)S(1)} async-done(((bf16[8,4,32768]{2,1,0:T(4,128)(2,1)}), bf16[8,4,32768]{2,1,0:T(4,128)(2,1)S(1)}, u32[]{:S(2)}, u32[]{:S(2)}) %all-to-all-start.4) | async-done | bytes 2097184 | tf_op jit(solution)/shard_map/all_to_all | solution.py:166
  239.2 5.3 %multiply_bitcast_fusion = f32[32768,4,8]{0,1,2:T(4,128)} fusion(f32[8,4,32768]{2,1,0:T(4,128)} %mul.132, bf16[8,4,32768]{2,1,0:T(4,128)(2,1)S(1)} %all-to-all-done.4), kind=kLoop, calls=%fused_computation.8 | loop fusion | flops 2097152 | bytes 10485760 | tf_op jit(solution)/shard_map/ocr,ocx->rx/dot_general | solution.py:189
  244.5 6.1 %reshape.341 = f32[4,64,128,4,8]{2,1,0,3,4:T(8,128)} reshape(f32[32768,4,8]{0,1,2:T(4,128)} %multiply_bitcast_fusion) | data formatting | bytes 8388608 | tf_op jit(solution)/shard_map/ocr,ocx->rx/dot_general | solution.py:189
  250.6 7.6 %fusion.21 = bf16[4,4,64,128]{3,0,2,1:T(4,128)(2,1)S(1)} fusion(f32[4,64,128,4,8]{2,1,0,3,4:T(8,128)} %reshape.341, f32[4,4,64,128]{3,0,2,1:T(4,128)S(1)} %bitcast.191, f32[4,4,64]{0,2,1:T(8,128)S(1)} %copy.283, f32[4,4,64]{0,2,1:T(8,128)S(1)} %copy.278, s32[8,4]{0,1:T(4,128)S(1)} %bitcast.199, s32[8,4]{0,1:T(4,128)S(1)} %get-tuple-element.11), kind=kOutput, calls=%fused_computation.32 | convolution fusion | flops 50856320 | bytes 4989184 | tf_op jit(solution)/shard_map/ocr,ocx->rx/dot_general | solution.py:189
  258.4 8.5 %all_to_all.31 = bf16[4,1,4,8192]{3,2,1,0:T(4,128)(2,1)S(1)} all-to-all(bf16[4,1,4,8192]{3,2,1,0:T(4,128)(2,1)S(1)} %bitcast.185), channel_id=1, replica_groups=mesh['grp'=4,'cache'=8] {'grp'}, dimensions={0} | all-to-all | bytes 524288 | tf_op jit(solution)/shard_map/all_to_all | solution.py:200
  (131 shorter events, 50.9 us)
Async XLA Ops:
  6.5 136.1 %all-gather.4.cloned.1.call-start = ((), (), s32[]{:S(2)}) async-start(), calls=%async_computation.6 | async-start | bytes 2359296 | tf_op jit(solution)/shard_map/all_gather | solution.py:143
  17.8 157.4 %all-to-all-start.2 = ((bf16[4,1,4,2048]{3,2,1,0:T(4,128)(2,1)}), bf16[4,1,4,2048]{3,2,1,0:T(4,128)(2,1)S(1)}, u32[]{:S(2)}, u32[]{:S(2)}) async-start(bf16[4,1,4,2048]{3,2,1,0:T(4,128)(2,1)} %bitcast.197), calls=%async_computation.2 | async-start | bytes 131072 | tf_op jit(solution)/shard_map/all_to_all | solution.py:133
  154.7 2.2 copy-start.4
  165.2 5.3 %copy-start = (bf16[16,128,1024]{1,2,0:T(8,128)(2,1)S(1)}, bf16[16,128,1024]{1,2,0:T(8,128)(2,1)}, u32[]{:S(2)}) copy-start(bf16[16,128,1024]{1,2,0:T(8,128)(2,1)} %copy.268) | copy-start | bytes 12582916
  165.2 5.3 %copy-start.1 = (f32[16,8,128,4,8]{2,4,3,1,0:T(8,128)S(1)}, f32[16,8,128,4,8]{2,4,3,1,0:T(8,128)}, u32[]{:S(2)}) copy-start(f32[16,8,128,4,8]{2,4,3,1,0:T(8,128)} %get-tuple-element.29) | copy-start | bytes 6291460
  170.5 3.3 %copy-start.5 = (f32[16,4,8,8]{0,3,2,1:T(8,128)S(1)}, f32[16,4,8,8]{0,3,2,1:T(8,128)}, u32[]{:S(2)}) copy-start(f32[16,4,8,8]{0,3,2,1:T(8,128)} %copy.257) | copy-start | bytes 49156
  170.5 3.3 %copy-start.6 = (f32[16,4,8,8]{0,3,2,1:T(8,128)S(1)}, f32[16,4,8,8]{0,3,2,1:T(8,128)}, u32[]{:S(2)}) copy-start(f32[16,4,8,8]{0,3,2,1:T(8,128)} %copy.252) | copy-start | bytes 49156
  173.8 5.4 %copy-start.2 = (bf16[16,4,8,8,128]{4,3,1,2,0:T(8,128)(2,1)S(1)}, bf16[16,4,8,8,128]{4,3,1,2,0:T(8,128)(2,1)}, u32[]{:S(2)}) copy-start(bf16[16,4,8,8,128]{4,3,1,2,0:T(8,128)(2,1)} %fusion.2) | copy-start | bytes 3145732
  175.2 10.1 %all-to-all-start.1 = ((f32[8,4,256]{2,1,0:T(4,128)}), f32[8,4,256]{2,1,0:T(4,128)S(1)}, u32[]{:S(2)}, u32[]{:S(2)}) async-start(f32[8,4,256]{2,1,0:T(4,128)} %reshape.251), calls=%async_computation.1 | async-start | bytes 65536 | tf_op jit(solution)/shard_map/all_to_all | solution.py:168
  179.3 1.2 copy-start.3
  185.2 10.7 %all-to-all-start.3 = ((f32[8,4,256]{2,1,0:T(4,128)}), f32[8,4,256]{2,1,0:T(4,128)S(1)}, u32[]{:S(2)}, u32[]{:S(2)}) async-start(f32[8,4,256]{2,1,0:T(4,128)} %reshape.258), calls=%async_computation.3 | async-start | bytes 65536 | tf_op jit(solution)/shard_map/all_to_all | solution.py:169
  193.6 9.7 %copy-start.8 = (s32[4,4]{1,0:T(4,128)S(1)}, s32[4,4]{1,0:T(4,128)}, u32[]{:S(2)}) copy-start(s32[4,4]{1,0:T(4,128)} %param.11) | copy-start | bytes 196
  195.9 43.3 %all-to-all-start.4 = ((bf16[8,4,32768]{2,1,0:T(4,128)(2,1)}), bf16[8,4,32768]{2,1,0:T(4,128)(2,1)S(1)}, u32[]{:S(2)}, u32[]{:S(2)}) async-start(bf16[8,4,32768]{2,1,0:T(4,128)(2,1)} %reshape.263), calls=%async_computation.4 | async-start | bytes 4194304 | tf_op jit(solution)/shard_map/all_to_all | solution.py:166
  244.5 6.1 %copy-start.7 = (f32[4,4,8,8,128]{4,0,3,2,1:T(4,128)S(1)}, f32[4,4,8,8,128]{4,0,3,2,1:T(4,128)}, u32[]{:S(2)}) copy-start(f32[4,4,8,8,128]{4,0,3,2,1:T(4,128)} %copy.279) | copy-start | bytes 1572868
Sparse Core Ops, SparseCore 0:
  17.9 50.5 all-gather.3
where the time goes:
time: 276 us; the launch traced here: 274 us
  local copies, waits for them, and re-layouts  93.7 us (34%)
  blocking collectives  81.8 us (30%)
  matrix products  29.3 us (11%)
  waiting for transfers between devices  25.1 us (9%)
  starting transfers between devices  17.8 us (6%)
  between operations  14.4 us (5%)
  other arithmetic  12.4 us (4%)
    all_gather x1, blocking collectives, per_device(): lax.all_gather(page_owner, 'cache', axis=0, tiled=True)  27.2 us
    all_gather x1, blocking collectives, per_device(): lax.all_gather(page_index, 'cache', axis=0, tiled=True)  26.1 us
    slice x4, local copies, waits for them, and re-layouts, item_partial(): value_rows = panel_rows[:, KVH * HD:].reshape(token_count, KVH, HD)  24.9 us
    all_to_all x1, waiting for transfers between devices, per_device(): lax.all_to_all(part_out, 'cache', split_axis=0, concat_axis=0, tiled=True)  20.6 us
    gather x2, local copies, waits for them, and re-layouts, owner_work(): kv_cache[meta_part[:, 1:]].reshape(finish - offset, -1, kv_cache.shape[2])  16 us
    slice x2, local copies, waits for them, and re-layouts, item_partial(): key_rows = panel_rows[:, :KVH * HD].reshape(token_count, KVH, HD)  12.8 us
    all_to_all x1, blocking collectives, per_device(): lax.all_to_all(sent_queries, 'grp', split_axis=0, concat_axis=0, tiled=True)  10.3 us
    unnamed x1, blocking collectives  9.62 us
  transfers between devices with their start and end apart: 5, of which 3 were waited for; matrix products, arithmetic and copies ran while one was open for 42% of the time, Pallas kernels for 0%

commit v1 on v0

v1 whole, which is shorter than its diff:
```python
import functools
import math

import jax
import jax.numpy as jnp
from jax import lax
from jax.experimental import pallas as pl
from jax.experimental.pallas import tpu as pltpu
from jax.sharding import PartitionSpec as P

KVH = 8
HD = 128
GQ = 8
STEPS = 4
PAGE = 128
SEL = 4

LANES = 128
ROWS = GQ * STEPS
HALF = 16
BODY = KVH * ROWS
FULL = BODY + HALF
PIECE = 32
COLS = KVH * ROWS // HALF
EMPTY = -1e30
SCALE = math.log2(math.e) / math.sqrt(HD)
VMEM_BYTES = 24 * 1024 * 1024


def params():
    return pltpu.CompilerParams(vmem_limit_bytes=VMEM_BYTES)


def cost(flops, moved):
    return pl.CostEstimate(flops=flops, bytes_accessed=moved, transcendentals=0)


def lane_ids():
    return lax.broadcasted_iota(jnp.int32, (HALF, LANES), 1)


def pack_stats(stats):
    stats = jnp.where(lane_ids() < COLS, stats, 0.0)
    high = stats.astype(jnp.bfloat16).astype(jnp.float32)
    rest = stats - high
    middle = rest.astype(jnp.bfloat16).astype(jnp.float32)
    low = rest - middle
    tile = high + pltpu.roll(middle, PIECE, 1) + pltpu.roll(low, 2 * PIECE, 1)
    return tile.astype(jnp.bfloat16)


def unpack_stats(tile):
    tile = tile.astype(jnp.float32)
    return tile + pltpu.roll(tile, LANES - PIECE, 1) + pltpu.roll(tile, LANES - 2 * PIECE, 1)


def column(stats, index):
    return stats[:, index : index + 1]


def tile_rows(index):
    half, head = divmod(index, KVH)
    start = head * ROWS + half * HALF
    return slice(start, start + HALF)


def relayout_kernel(place_ref, queries_ref, *refs):
    outs, scratch = refs[:-1], refs[-1]
    per = outs[0].shape[0]
    for d, out in enumerate(outs):
        for k in range(per):
            row = (place_ref[0] ^ d) * per + k
            values = queries_ref[row].astype(jnp.float32)
            for head in range(KVH * GQ):
                scratch[head * STEPS : (head + 1) * STEPS, :] = values[:, head * HD : (head + 1) * HD]
            out[k] = scratch[...].astype(jnp.bfloat16)


def relayout(place, queries, groups):
    per = queries.shape[0] // groups
    whole = pl.BlockSpec(memory_space=pltpu.VMEM)
    return pl.pallas_call(
        relayout_kernel,
        out_shape=[jax.ShapeDtypeStruct((per, BODY, HD), jnp.bfloat16)] * groups,
        in_specs=[pl.BlockSpec(memory_space=pltpu.SMEM), whole],
        out_specs=[whole] * groups,
        scratch_shapes=[pltpu.VMEM((BODY, HD), jnp.float32)],
        compiler_params=params(),
        cost_estimate=cost(0, 2 * queries.size * 2),
    )(place, queries)


def new_kernel(groups, place_ref, *refs):
    queries, (new_ref, out_ref, stats_ref) = refs[:groups], refs[groups:]
    per = queries[0].shape[0]
    for d in range(groups):
        for k in range(per):
            row = (place_ref[0] ^ d) * per + k
            new = new_ref[row].astype(jnp.float32)
            step = lax.broadcasted_iota(jnp.int32, (ROWS, STEPS), 0) % STEPS
            usable = lax.broadcasted_iota(jnp.int32, (ROWS, STEPS), 1) <= step
            stats = jnp.full((HALF, LANES), EMPTY, jnp.float32)
            lanes = lane_ids()
            for head in range(KVH):
                rows = slice(head * ROWS, (head + 1) * ROWS)
                keys = new[:, head * HD : (head + 1) * HD].astype(jnp.bfloat16)
                values = new[:, (KVH + head) * HD : (KVH + head + 1) * HD].astype(jnp.bfloat16)
                scores = lax.dot_general(
                    queries[d][k, rows, :], keys, (((1,), (1,)), ((), ())), preferred_element_type=jnp.float32
                )
                scores = jnp.where(usable, scores * SCALE, EMPTY)
                top = jnp.max(scores, axis=1, keepdims=True)
                weights = jnp.exp2(scores - top)
                total = jnp.sum(weights, axis=1, keepdims=True)
                mixed = lax.dot_general(
                    weights.astype(jnp.bfloat16), values, (((1,), (0,)), ((), ())), preferred_element_type=jnp.float32
                )
                out_ref[d * per + k, rows, :] = mixed / total
                level = jnp.broadcast_to(top + jnp.log2(total), (ROWS, LANES))
                for half in range(ROWS // HALF):
                    part = level[half * HALF : (half + 1) * HALF, :]
                    stats = jnp.where(lanes == half * KVH + head, part, stats)
            stats_ref[d * per + k] = stats


def new_tokens(place, queries, new_kv):
    groups = len(queries)
    requests = new_kv.shape[0]
    whole = pl.BlockSpec(memory_space=pltpu.VMEM)
    return pl.pallas_call(
        functools.partial(new_kernel, groups),
        out_shape=[
            jax.ShapeDtypeStruct((requests, BODY, HD), jnp.float32),
            jax.ShapeDtypeStruct((requests, HALF, LANES), jnp.float32),
        ],
        in_specs=[pl.BlockSpec(memory_space=pltpu.SMEM)] + [whole] * (groups + 1),
        out_specs=[whole, whole],
        compiler_params=params(),
        cost_estimate=cost(requests * KVH * 4 * ROWS * HD * HD, requests * BODY * HD * 6),
    )(place, *queries, new_kv)


def item_kernel(sides, slots, entries, meta_ref, *refs):
    queries = refs[:sides]
    pages = refs[sides : sides + len(entries)]
    outs = refs[sides + len(entries) :]
    lanes = lane_ids()
    tokens = lax.broadcasted_iota(jnp.int32, (ROWS, PAGE), 1)
    for number, (side, slot, entry) in enumerate(entries):
        count = meta_ref[2 * entry]
        query, page, out = queries[side], pages[number], outs[side]

        @pl.when(count > 0)
        def _():
            stats = jnp.full((HALF, LANES), EMPTY, jnp.float32)
            for head in range(KVH):
                rows = slice(head * ROWS, (head + 1) * ROWS)
                scores = lax.dot_general(
                    query[slot, rows, :],
                    page[0, :, head * HD : (head + 1) * HD],
                    (((1,), (1,)), ((), ())),
                    preferred_element_type=jnp.float32,
                )
                scores = jnp.where(tokens < count, scores * SCALE, EMPTY)
                top = jnp.max(scores, axis=1, keepdims=True)
                weights = jnp.exp2(scores - top)
                total = jnp.sum(weights, axis=1, keepdims=True)
                mixed = lax.dot_general(
                    weights.astype(jnp.bfloat16),
                    page[0, :, (KVH + head) * HD : (KVH + head + 1) * HD],
                    (((1,), (0,)), ((), ())),
                    preferred_element_type=jnp.float32,
                )
                out[slot, rows, :] = (mixed / total).astype(jnp.bfloat16)
                level = jnp.broadcast_to(top + jnp.log2(total), (ROWS, LANES))
                for half in range(ROWS // HALF):
                    part = level[half * HALF : (half + 1) * HALF, :]
                    stats = jnp.where(lanes == half * KVH + head, part, stats)
            out[slot, BODY:FULL, :] = pack_stats(stats)

        @pl.when(count <= 0)
        def _():
            out[slot, :BODY, :] = jnp.zeros((BODY, HD), jnp.bfloat16)
            out[slot, BODY:FULL, :] = pack_stats(jnp.full((HALF, LANES), EMPTY, jnp.float32))


def page_map(entry):
    return lambda i, meta: (meta[2 * entry + 1], 0, 0)


def items(meta, queries, entries_of, kv_cache):
    entries = [(side, slot, e) for side, row in enumerate(entries_of) for slot, e in enumerate(row)]
    slots = [q.shape[0] for q in queries]

    def whole(count, rows):
        return pl.BlockSpec((count, rows, HD), lambda i, meta: (0, 0, 0))

    page_spec = [pl.BlockSpec((1, PAGE, kv_cache.shape[2]), page_map(e)) for _, _, e in entries]
    return pl.pallas_call(
        functools.partial(item_kernel, len(queries), slots, entries),
        out_shape=[jax.ShapeDtypeStruct((n, FULL, HD), jnp.bfloat16) for n in slots],
        grid_spec=pltpu.PrefetchScalarGridSpec(
            num_scalar_prefetch=1,
            grid=(1,),
            in_specs=[whole(n, BODY) for n in slots] + page_spec,
            out_specs=[whole(n, FULL) for n in slots],
        ),
        compiler_params=params(),
        cost_estimate=cost(len(entries) * KVH * 4 * ROWS * HD * PAGE, len(entries) * PAGE * kv_cache.shape[2] * 2),
    )(meta, *queries, *([kv_cache] * len(entries)))


def blend(sources, out, slot_out):
    levels = [unpack_stats(ref[slot, BODY:FULL, :]) for ref, slot in sources]
    peak = functools.reduce(jnp.maximum, levels)
    shares = [jnp.exp2(level - peak) for level in levels]
    total = functools.reduce(jnp.add, shares)
    shares = [share / total for share in shares]
    out[slot_out, BODY:FULL, :] = pack_stats(peak + jnp.log2(total))
    for index in range(COLS):
        rows = tile_rows(index)
        parts = [
            column(share, index) * ref[slot, rows, :].astype(jnp.float32)
            for share, (ref, slot) in zip(shares, sources)
        ]
        out[slot_out, rows, :] = functools.reduce(jnp.add, parts).astype(jnp.bfloat16)


def merge_kernel(plans, inputs, *refs):
    ins, outs = refs[:inputs], refs[inputs:]
    for out, plan in zip(outs, plans):
        for slot_out, sources in enumerate(plan):
            if len(sources) == 1:
                number, slot = sources[0]
                out[slot_out] = ins[number][slot]
            else:
                blend([(ins[number], slot) for number, slot in sources], out, slot_out)


def merge(arrays, plans):
    whole = pl.BlockSpec(memory_space=pltpu.VMEM)
    count = sum(len(plan) for plan in plans)
    return pl.pallas_call(
        functools.partial(merge_kernel, plans, len(arrays)),
        out_shape=[jax.ShapeDtypeStruct((len(plan), FULL, HD), jnp.bfloat16) for plan in plans],
        in_specs=[whole] * len(arrays),
        out_specs=[whole] * len(plans),
        compiler_params=params(),
        cost_estimate=cost(0, count * FULL * HD * 6),
    )(*arrays)


def final_kernel(groups, place_ref, *refs):
    parts, (new_ref, level_ref, out_ref, scratch) = refs[:groups], refs[groups:]
    per = parts[0].shape[0]
    for d in range(groups):
        for k in range(per):
            row = (place_ref[0] ^ d) * per + k
            cached = unpack_stats(parts[d][k, BODY:FULL, :])
            fresh = level_ref[d * per + k]
            peak = jnp.maximum(cached, fresh)
            share, share_new = jnp.exp2(cached - peak), jnp.exp2(fresh - peak)
            total = share + share_new
            share, share_new = share / total, share_new / total
            for index in range(COLS):
                rows = tile_rows(index)
                scratch[rows, :] = (
                    column(share, index) * parts[d][k, rows, :].astype(jnp.float32)
                    + column(share_new, index) * new_ref[d * per + k, rows, :]
                )
            for head in range(KVH * GQ):
                out_ref[row, :, head * HD : (head + 1) * HD] = scratch[
                    head * STEPS : (head + 1) * STEPS, :
                ].astype(jnp.bfloat16)


def final(place, parts, new_out, new_level):
    groups = len(parts)
    requests = new_out.shape[0]
    whole = pl.BlockSpec(memory_space=pltpu.VMEM)
    return pl.pallas_call(
        functools.partial(final_kernel, groups),
        out_shape=jax.ShapeDtypeStruct((requests, STEPS, KVH * GQ * HD), jnp.bfloat16),
        in_specs=[pl.BlockSpec(memory_space=pltpu.SMEM)] + [whole] * (groups + 2),
        out_specs=whole,
        scratch_shapes=[pltpu.VMEM((BODY, HD), jnp.float32)],
        compiler_params=params(),
        cost_estimate=cost(0, requests * BODY * HD * 8),
    )(place, *parts, new_out, new_level)


def ring_order(owners):
    return list(range(0, owners, 2)) + list(range(owners - 1, 0, -2))


def per_device(queries, new_kv, kv_cache, page_owner, page_index, lengths):
    groups = lax.axis_size("grp")
    owners = lax.axis_size("cache")
    requests = queries.shape[0]
    per = requests // groups
    reach = owners // 2
    order = ring_order(owners)
    here = [0] * owners
    for position, owner in enumerate(order):
        here[owner] = position
    forward = [(order[i], order[(i + 1) % owners]) for i in range(owners)]
    backward = [(b, a) for a, b in forward]

    group = lax.axis_index("grp")
    position = jnp.asarray(here, jnp.int32)[lax.axis_index("cache")]
    place = jnp.reshape(group, (1,)).astype(jnp.int32)

    visitor = (group ^ jnp.arange(groups, dtype=jnp.int32))[:, None] * per + jnp.arange(per, dtype=jnp.int32)
    visitor = visitor.reshape(-1)
    counts = jnp.clip(lengths[:, None] - jnp.arange(SEL, dtype=jnp.int32) * PAGE, 0, PAGE)
    named = (page_owner[None] == jnp.arange(owners, dtype=jnp.int32)[:, None, None]).astype(jnp.int32)
    sent = jnp.stack([jnp.sum(named * counts[None], -1), jnp.sum(named * page_index[None, :, :, 0], -1)], -1)
    sent = sent[:, visitor]
    got = lax.all_to_all(sent, "cache", split_axis=0, concat_axis=0, tiled=True)
    ring = jnp.asarray(order, jnp.int32)[(position + jnp.arange(owners, dtype=jnp.int32)) % owners]
    meta = got[ring].reshape(-1)

    rows = relayout(place, queries, groups)
    visits = [rows[0]]
    for d in range(1, groups):
        swap = [(g, g ^ d) for g in range(groups)]
        visits.append(lax.ppermute(rows[d], "grp", swap))
    new_out, new_level = new_tokens(place, rows, new_kv)

    chunks = [list(range(0, groups // 2)), list(range(groups // 2, groups))]
    returned = [None] * groups
    states = []
    for chunk in chunks:
        block = jnp.concatenate([visits[d] for d in chunk], axis=0)
        slots = [d * per + k for d in chunk for k in range(per)]
        cut = (len(slots) + 1) // 2
        ahead = behind = block
        parts = {}
        parts[0] = items(meta, [block], [[s for s in slots]], kv_cache)[0]
        for step in range(1, reach + 1):
            if step == reach:
                ahead, behind = ahead[:cut], behind[cut:]
            ahead = lax.ppermute(ahead, "cache", forward)
            behind = lax.ppermute(behind, "cache", backward)
            below = (owners - step) * requests
            above = step * requests
            if step < reach:
                entries = [[below + s for s in slots], [above + s for s in slots]]
            else:
                entries = [[below + s for s in slots[:cut]], [above + s for s in slots[cut:]]]
            from_below, from_above = items(meta, [ahead, behind], entries, kv_cache)
            parts[-step], parts[step] = from_below, from_above
        states.append((chunk, slots, cut, parts))

    for chunk, slots, cut, parts in reversed(states):
        count = len(slots)
        ahead, behind = parts[-reach], parts[reach]
        for step in range(reach - 1, -1, -1):
            ahead = lax.ppermute(ahead, "cache", forward)
            behind = lax.ppermute(behind, "cache", backward)
            first = step == reach - 1
            if step > 0:
                up, down = [], []
                for s in range(count):
                    low, high = first and s >= cut, first and s < cut
                    up.append([(1, s)] if low else [(0, s), (1, s)])
                    down.append([(3, s)] if high else [(2, s - cut if first else s), (3, s)])
                ahead, behind = merge([ahead, parts[step], behind, parts[-step]], [up, down])
            else:
                plans = []
                for number in range(len(chunk)):
                    plan = []
                    for k in range(per):
                        s = number * per + k
                        sources = [(2, s)]
                        if not (first and s >= cut):
                            sources.append((0, s))
                        if not (first and s < cut):
                            sources.append((1, s - cut if first else s))
                        plan.append(sources)
                    plans.append(plan)
                merged = merge([ahead, behind, parts[0]], plans)
                for d, part in zip(chunk, merged):
                    returned[d] = part

    home = [returned[0]]
    for d in range(1, groups):
        swap = [(g, g ^ d) for g in range(groups)]
        home.append(lax.ppermute(returned[d], "grp", swap))
    return final(place, home, new_out, new_level)


def solution(mesh):
    in_specs = (
        P(("grp", "cache"), None, None),
        P(("grp", "cache"), None, None),
        P(("grp", "cache"), None, None),
        P(("grp", "cache"), None),
        P(("grp", "cache"), None, None),
        P(("grp", "cache")),
    )
    out_specs = P(("grp", "cache"), None, None)
    return jax.shard_map(
        per_device, mesh=mesh, in_specs=in_specs, out_specs=out_specs, check_vma=False
    )
```

time: 276 us -> 120 us (0.43)
  the two profiles are of different devices: /device:TPU:0 before, /device:TPU:16 now
where the time goes in v1:
time: 120 us; the launch traced here: 122 us
  starting transfers between devices  52.3 us (44%)
  Pallas kernels  51.6 us (43%)
  local copies, waits for them, and re-layouts  9.04 us (8%)
  waiting for transfers between devices  6.22 us (5%)
  other arithmetic  2.2 us (2%)
    pallas_call x10, Pallas kernels, items(): pl.pallas_call(functools.partial(item_kernel, len(queries), slots, entrie...  43.4 us
    ppermute x16, starting transfers between devices, per_device(): ahead = lax.ppermute(ahead, 'cache', forward)  17 us
    ppermute x16, starting transfers between devices, per_device(): behind = lax.ppermute(behind, 'cache', backward)  16 us
    ppermute x3, starting transfers between devices, per_device(): home.append(lax.ppermute(returned[d], 'grp', swap))  11 us
    all_to_all x1, starting transfers between devices, per_device(): got = lax.all_to_all(sent, 'cache', split_axis=0, concat_axis=0, tiled=True)  6.14 us
    pallas_call x8, Pallas kernels, merge(): pl.pallas_call(functools.partial(merge_kernel, plans, len(arrays)), out_s...  5.79 us
    unnamed x10, local copies, waits for them, and re-layouts  4.35 us
  transfers between devices with their start and end apart: 39, of which 10 were waited for; matrix products, arithmetic and copies ran while one was open for 6% of the time, Pallas kernels for 41%

profile of v1, /device:TPU:16, one launch (start us, length us, event | category | flops | bytes accessed | tf_op | source)
XLA Modules:
  0.0 121.5 jit_solution(17032769743689171588)
XLA Ops:
  1.1 1.6 %collective-permute-start.18 = (bf16[1,256,128]{2,1,0:T(8,128)(2,1)S(1)}, bf16[1,256,128]{2,1,0:T(8,128)(2,1)S(1)}, u32[]{:S(2)}, u32[]{:S(2)}) collective-permute-start(bf16[1,256,128]{2,1,0:T(8,128)(2,1)S(1)} %get-tuple-element.61.refs_2_), channel_id=1, source_target_pairs={{0,16},{8,24},{16,0},{24,8},{1,17},{9,25},{17,1},{25,9},{2,18},{10... | collective-permute-start | bytes 196616 | tf_op jit(solution)/shard_map/ppermute | solution.py:327
  6.8 1.6 %collective-permute-start.20 = (bf16[2,256,128]{2,1,0:T(8,128)(2,1)S(1)}, bf16[2,256,128]{2,1,0:T(8,128)(2,1)S(1)}, u32[]{:S(2)}, u32[]{:S(2)}) collective-permute-start(bf16[2,256,128]{2,1,0:T(8,128)(2,1)S(1)} %constant_dynamic-update-slice_fusion.2.refs_0_), channel_id=1, source_target_pairs={{0,2},{2,4},{4,6},{6,7},{7,5},{5,3},{3,1},{1,0},{8,10},{10,12},{12... | collective-permute-start | bytes 393224 | tf_op jit(solution)/shard_map/ppermute | solution.py:343
  8.9 1.6 %collective-permute-start.1 = (bf16[2,256,128]{2,1,0:T(8,128)(2,1)S(1)}, bf16[2,256,128]{2,1,0:T(8,128)(2,1)S(1)}, u32[]{:S(2)}, u32[]{:S(2)}) collective-permute-start(bf16[2,256,128]{2,1,0:T(8,128)(2,1)S(1)} %constant_dynamic-update-slice_fusion.refs_0_), channel_id=1, source_target_pairs={{0,2},{2,4},{4,6},{6,7},{7,5},{5,3},{3,1},{1,0},{8,10},{10,12},{12... | collective-permute-start | bytes 393224 | tf_op jit(solution)/shard_map/ppermute | solution.py:343
  12.3 6.1 %all-to-all-start = ((s32[8,4,2]{1,2,0:T(2,128)}), s32[8,4,2]{1,2,0:T(2,128)S(1)}, u32[]{:S(2)}, u32[]{:S(2)}) async-start(s32[8,4,2]{1,2,0:T(2,128)} %copy.25), calls=%async_computation | async-start | bytes 16384 | tf_op jit(solution)/shard_map/all_to_all | solution.py:319
  25.7 1.5 %collective-permute-start.22 = (bf16[2,256,128]{2,1,0:T(8,128)(2,1)S(1)}, bf16[2,256,128]{2,1,0:T(8,128)(2,1)S(1)}, u32[]{:S(2)}, u32[]{:S(2)}) collective-permute-start(bf16[2,256,128]{2,1,0:T(8,128)(2,1)S(1)} %collective-permute-done.21.refs_0_), channel_id=1, source_target_pairs={{0,2},{2,4},{4,6},{6,7},{7,5},{5,3},{3,1},{1,0},{8,10},{10,12},{12... | collective-permute-start | bytes 393224 | tf_op jit(solution)/shard_map/ppermute | solution.py:343
  36.7 3.4 %copy-done = bf16[16,128,2048]{2,1,0:T(8,128)(2,1)S(1)} copy-done((bf16[16,128,2048]{2,1,0:T(8,128)(2,1)S(1)}, bf16[16,128,2048]{2,1,0:T(8,128)(2,1)}, u32[]{:S(2)}) %copy-start) | copy-done | bytes 8388632
  40.1 2.7 %shard_map.92 = (bf16[1,272,128]{2,1,0:T(8,128)(2,1)S(1)}, bf16[1,272,128]{2,1,0:T(8,128)(2,1)S(1)}) custom-call(s32[64]{0:T(128)S(1)} %reshape.118.meta_ref, bf16[1,256,128]{2,1,0:T(8,128)(2,1)S(1)} %collective-permute-done.23.refs_0_, bf16[1,256,128]{2,1,0:T(8,128)(2,1)S(1)} %collective-permute-done.27.refs_1_, bf16[16,128,2048]{2,1,0:T(8,128)(2,1)S(1)} %copy-done, ...), custom_call_target="tpu_custom_call" | custom-call | flops 33554432 | bytes 1048576 | tf_op jit(solution)/shard_map/pallas_call | solution.py:199
  44.8 2.7 %shard_map.83 = (bf16[1,272,128]{2,1,0:T(8,128)(2,1)S(1)}, bf16[1,272,128]{2,1,0:T(8,128)(2,1)S(1)}) custom-call(s32[64]{0:T(128)S(1)} %reshape.118.meta_ref, bf16[1,256,128]{2,1,0:T(8,128)(2,1)S(1)} %collective-permute-done.4.refs_0_, bf16[1,256,128]{2,1,0:T(8,128)(2,1)S(1)} %collective-permute-done.8.refs_1_, bf16[16,128,2048]{2,1,0:T(8,128)(2,1)S(1)} %copy-done.1, ...), custom_call_target="tpu_custom_call" | custom-call | flops 33554432 | bytes 1048576 | tf_op jit(solution)/shard_map/pallas_call | solution.py:199
  47.5 2.0 %collective-permute-start.9 = (bf16[1,272,128]{2,1,0:T(8,128)(2,1)S(1)}, bf16[1,272,128]{2,1,0:T(8,128)(2,1)S(1)}, u32[]{:S(2)}, u32[]{:S(2)}) collective-permute-start(bf16[1,272,128]{2,1,0:T(8,128)(2,1)S(1)} %get-tuple-element.45), channel_id=1, source_target_pairs={{0,2},{2,4},{4,6},{6,7},{7,5},{5,3},{3,1},{1,0},{8,10},{10,12},{12... | collective-permute-start | bytes 208904 | tf_op jit(solution)/shard_map/ppermute | solution.py:359
  49.5 4.8 %shard_map.93 = (bf16[2,272,128]{2,1,0:T(8,128)(2,1)S(1)}, bf16[2,272,128]{2,1,0:T(8,128)(2,1)S(1)}) custom-call(s32[64]{0:T(128)S(1)} %reshape.118.meta_ref, bf16[2,256,128]{2,1,0:T(8,128)(2,1)S(1)} %collective-permute-done.22.refs_0_, bf16[2,256,128]{2,1,0:T(8,128)(2,1)S(1)} %collective-permute-done.26.refs_1_, bf16[16,128,2048]{2,1,0:T(8,128)(2,1)S(1)} %copy-done.1, ...), custom_call_target="tpu_custom_call" | custom-call | flops 67108864 | bytes 2097152 | tf_op jit(solution)/shard_map/pallas_call | solution.py:199
  54.3 2.8 %shard_map.84 = (bf16[2,272,128]{2,1,0:T(8,128)(2,1)S(1)}, bf16[2,272,128]{2,1,0:T(8,128)(2,1)S(1)}) custom-call(s32[64]{0:T(128)S(1)} %reshape.118.meta_ref, bf16[2,256,128]{2,1,0:T(8,128)(2,1)S(1)} %collective-permute-done.3.refs_0_, bf16[2,256,128]{2,1,0:T(8,128)(2,1)S(1)} %collective-permute-done.7.refs_1_, bf16[16,128,2048]{2,1,0:T(8,128)(2,1)S(1)} %copy-done.1, ...), custom_call_target="tpu_custom_call" | custom-call | flops 67108864 | bytes 2097152 | tf_op jit(solution)/shard_map/pallas_call | solution.py:199
  57.6 2.0 %collective-permute-start.31 = (bf16[2,272,128]{2,1,0:T(8,128)(2,1)S(1)}, bf16[2,272,128]{2,1,0:T(8,128)(2,1)S(1)}, u32[]{:S(2)}, u32[]{:S(2)}) collective-permute-start(bf16[2,272,128]{2,1,0:T(8,128)(2,1)S(1)} %get-tuple-element.69), channel_id=1, source_target_pairs={{2,0},{4,2},{6,4},{7,6},{5,7},{3,5},{1,3},{0,1},{10,8},{12,10},{14... | collective-permute-start | bytes 417800 | tf_op jit(solution)/shard_map/ppermute | solution.py:360
  62.2 4.8 %shard_map.95 = (bf16[2,272,128]{2,1,0:T(8,128)(2,1)S(1)}, bf16[2,272,128]{2,1,0:T(8,128)(2,1)S(1)}) custom-call(s32[64]{0:T(128)S(1)} %reshape.118.meta_ref, bf16[2,256,128]{2,1,0:T(8,128)(2,1)S(1)} %collective-permute-done.21.refs_0_, bf16[2,256,128]{2,1,0:T(8,128)(2,1)S(1)} %collective-permute-done.25.refs_1_, bf16[16,128,2048]{2,1,0:T(8,128)(2,1)S(1)} %copy-done.1, ...), custom_call_target="tpu_custom_call" | custom-call | flops 67108864 | bytes 2097152 | tf_op jit(solution)/shard_map/pallas_call | solution.py:199
  67.0 6.9 %shard_map.86 = (bf16[2,272,128]{2,1,0:T(8,128)(2,1)S(1)}, bf16[2,272,128]{2,1,0:T(8,128)(2,1)S(1)}) custom-call(s32[64]{0:T(128)S(1)} %reshape.118.meta_ref, bf16[2,256,128]{2,1,0:T(8,128)(2,1)S(1)} %collective-permute-done.2.refs_0_, bf16[2,256,128]{2,1,0:T(8,128)(2,1)S(1)} %collective-permute-done.6.refs_1_, bf16[16,128,2048]{2,1,0:T(8,128)(2,1)S(1)} %copy-done.1, ...), custom_call_target="tpu_custom_call" | custom-call | flops 67108864 | bytes 2097152 | tf_op jit(solution)/shard_map/pallas_call | solution.py:199
  74.9 2.0 %collective-permute-start.33 = (bf16[2,272,128]{2,1,0:T(8,128)(2,1)S(1)}, bf16[2,272,128]{2,1,0:T(8,128)(2,1)S(1)}, u32[]{:S(2)}, u32[]{:S(2)}) collective-permute-start(bf16[2,272,128]{2,1,0:T(8,128)(2,1)S(1)} %get-tuple-element.73), channel_id=1, source_target_pairs={{2,0},{4,2},{6,4},{7,6},{5,7},{3,5},{1,3},{0,1},{10,8},{12,10},{14... | collective-permute-start | bytes 417800 | tf_op jit(solution)/shard_map/ppermute | solution.py:360
  78.0 2.0 %collective-permute-start.14 = (bf16[2,272,128]{2,1,0:T(8,128)(2,1)S(1)}, bf16[2,272,128]{2,1,0:T(8,128)(2,1)S(1)}, u32[]{:S(2)}, u32[]{:S(2)}) collective-permute-start(bf16[2,272,128]{2,1,0:T(8,128)(2,1)S(1)} %get-tuple-element.55), channel_id=1, source_target_pairs={{2,0},{4,2},{6,4},{7,6},{5,7},{3,5},{1,3},{0,1},{10,8},{12,10},{14... | collective-permute-start | bytes 417800 | tf_op jit(solution)/shard_map/ppermute | solution.py:360
  79.9 4.8 %shard_map.97 = (bf16[2,272,128]{2,1,0:T(8,128)(2,1)S(1)}, bf16[2,272,128]{2,1,0:T(8,128)(2,1)S(1)}) custom-call(s32[64]{0:T(128)S(1)} %reshape.118.meta_ref, bf16[2,256,128]{2,1,0:T(8,128)(2,1)S(1)} %collective-permute-done.20.refs_0_, bf16[2,256,128]{2,1,0:T(8,128)(2,1)S(1)} %collective-permute-done.24.refs_1_, bf16[16,128,2048]{2,1,0:T(8,128)(2,1)S(1)} %copy-done.1, ...), custom_call_target="tpu_custom_call" | custom-call | flops 67108864 | bytes 2097152 | tf_op jit(solution)/shard_map/pallas_call | solution.py:199
  84.7 6.8 %shard_map.88 = (bf16[2,272,128]{2,1,0:T(8,128)(2,1)S(1)}, bf16[2,272,128]{2,1,0:T(8,128)(2,1)S(1)}) custom-call(s32[64]{0:T(128)S(1)} %reshape.118.meta_ref, bf16[2,256,128]{2,1,0:T(8,128)(2,1)S(1)} %collective-permute-done.1.refs_0_, bf16[2,256,128]{2,1,0:T(8,128)(2,1)S(1)} %collective-permute-done.5.refs_1_, bf16[16,128,2048]{2,1,0:T(8,128)(2,1)S(1)} %copy-done.1, ...), custom_call_target="tpu_custom_call" | custom-call | flops 67108864 | bytes 2097152 | tf_op jit(solution)/shard_map/pallas_call | solution.py:199
  92.5 2.0 %collective-permute-start.35 = (bf16[2,272,128]{2,1,0:T(8,128)(2,1)S(1)}, bf16[2,272,128]{2,1,0:T(8,128)(2,1)S(1)}, u32[]{:S(2)}, u32[]{:S(2)}) collective-permute-start(bf16[2,272,128]{2,1,0:T(8,128)(2,1)S(1)} %get-tuple-element.76), channel_id=1, source_target_pairs={{2,0},{4,2},{6,4},{7,6},{5,7},{3,5},{1,3},{0,1},{10,8},{12,10},{14... | collective-permute-start | bytes 417800 | tf_op jit(solution)/shard_map/ppermute | solution.py:360
  95.6 2.0 %collective-permute-start.16 = (bf16[2,272,128]{2,1,0:T(8,128)(2,1)S(1)}, bf16[2,272,128]{2,1,0:T(8,128)(2,1)S(1)}, u32[]{:S(2)}, u32[]{:S(2)}) collective-permute-start(bf16[2,272,128]{2,1,0:T(8,128)(2,1)S(1)} %get-tuple-element.58), channel_id=1, source_target_pairs={{2,0},{4,2},{6,4},{7,6},{5,7},{3,5},{1,3},{0,1},{10,8},{12,10},{14... | collective-permute-start | bytes 417800 | tf_op jit(solution)/shard_map/ppermute | solution.py:360
  97.5 4.6 %shard_map.99.refs_2_ = bf16[2,272,128]{2,1,0:T(8,128)(2,1)S(1)} custom-call(s32[64]{0:T(128)S(1)} %reshape.118.meta_ref, bf16[2,256,128]{2,1,0:T(8,128)(2,1)S(1)} %constant_dynamic-update-slice_fusion.2.refs_0_, bf16[16,128,2048]{2,1,0:T(8,128)(2,1)S(1)} %copy-done.1, bf16[16,128,2048]{2,1,0:T(8,128)(2,1)S(1)} %copy-done.1), custom_call_target="tpu_custom_call" | custom-call | flops 33554432 | bytes 1048576 | tf_op jit(solution)/shard_map/pallas_call | solution.py:199
  102.2 2.7 %shard_map.90.refs_2_ = bf16[2,272,128]{2,1,0:T(8,128)(2,1)S(1)} custom-call(s32[64]{0:T(128)S(1)} %reshape.118.meta_ref, bf16[2,256,128]{2,1,0:T(8,128)(2,1)S(1)} %constant_dynamic-update-slice_fusion.refs_0_, bf16[16,128,2048]{2,1,0:T(8,128)(2,1)S(1)} %copy-done.1, bf16[16,128,2048]{2,1,0:T(8,128)(2,1)S(1)} %copy-done.1), custom_call_target="tpu_custom_call" | custom-call | flops 33554432 | bytes 1048576 | tf_op jit(solution)/shard_map/pallas_call | solution.py:199
  105.4 10.7 %collective-permute-start.36 = (bf16[1,272,128]{2,1,0:T(8,128)(2,1)S(1)}, bf16[1,272,128]{2,1,0:T(8,128)(2,1)S(1)}, u32[]{:S(2)}, u32[]{:S(2)}) collective-permute-start(bf16[1,272,128]{2,1,0:T(8,128)(2,1)S(1)} %get-tuple-element.77), channel_id=1, source_target_pairs={{0,16},{8,24},{16,0},{24,8},{1,17},{9,25},{17,1},{25,9},{2,18},{10... | collective-permute-start | bytes 208904 | tf_op jit(solution)/shard_map/ppermute | solution.py:389
  119.9 1.6 %shard_map.102 = bf16[4,4,8192]{2,1,0:T(4,128)(2,1)} custom-call(s32[1]{0:T(128)} %bitcast.place_ref, bf16[1,272,128]{2,1,0:T(8,128)(2,1)S(1)} %get-tuple-element.59.refs_0_, bf16[1,272,128]{2,1,0:T(8,128)(2,1)S(1)} %collective-permute-done.17.refs_1_, bf16[1,272,128]{2,1,0:T(8,128)(2,1)S(1)} %collective-permute-done.36.refs_2_, ...), custom_call_target="tpu_custom_call" | custom-call | bytes 1048576 | tf_op jit(solution)/shard_map/pallas_call | solution.py:281
  (108 shorter events, 37.7 us)
Async XLA Ops:
  6.8 12.9 %collective-permute-start.20 = (bf16[2,256,128]{2,1,0:T(8,128)(2,1)S(1)}, bf16[2,256,128]{2,1,0:T(8,128)(2,1)S(1)}, u32[]{:S(2)}, u32[]{:S(2)}) collective-permute-start(bf16[2,256,128]{2,1,0:T(8,128)(2,1)S(1)} %constant_dynamic-update-slice_fusion.2.refs_0_), channel_id=1, source_target_pairs={{0,2},{2,4},{4,6},{6,7},{7,5},{5,3},{3,1},{1,0},{8,10},{10,12},{12... | collective-permute-start | bytes 393224 | tf_op jit(solution)/shard_map/ppermute | solution.py:343
  8.4 12.7 %collective-permute-start.24 = (bf16[2,256,128]{2,1,0:T(8,128)(2,1)S(1)}, bf16[2,256,128]{2,1,0:T(8,128)(2,1)S(1)}, u32[]{:S(2)}, u32[]{:S(2)}) collective-permute-start(bf16[2,256,128]{2,1,0:T(8,128)(2,1)S(1)} %constant_dynamic-update-slice_fusion.2.refs_0_), channel_id=1, source_target_pairs={{2,0},{4,2},{6,4},{7,6},{5,7},{3,5},{1,3},{0,1},{10,8},{12,10},{14... | collective-permute-start | bytes 393224 | tf_op jit(solution)/shard_map/ppermute | solution.py:344
  8.9 12.8 %collective-permute-start.1 = (bf16[2,256,128]{2,1,0:T(8,128)(2,1)S(1)}, bf16[2,256,128]{2,1,0:T(8,128)(2,1)S(1)}, u32[]{:S(2)}, u32[]{:S(2)}) collective-permute-start(bf16[2,256,128]{2,1,0:T(8,128)(2,1)S(1)} %constant_dynamic-update-slice_fusion.refs_0_), channel_id=1, source_target_pairs={{0,2},{2,4},{4,6},{6,7},{7,5},{5,3},{3,1},{1,0},{8,10},{10,12},{12... | collective-permute-start | bytes 393224 | tf_op jit(solution)/shard_map/ppermute | solution.py:343
  10.5 12.6 %collective-permute-start.5 = (bf16[2,256,128]{2,1,0:T(8,128)(2,1)S(1)}, bf16[2,256,128]{2,1,0:T(8,128)(2,1)S(1)}, u32[]{:S(2)}, u32[]{:S(2)}) collective-permute-start(bf16[2,256,128]{2,1,0:T(8,128)(2,1)S(1)} %constant_dynamic-update-slice_fusion.refs_0_), channel_id=1, source_target_pairs={{2,0},{4,2},{6,4},{7,6},{5,7},{3,5},{1,3},{0,1},{10,8},{12,10},{14... | collective-permute-start | bytes 393224 | tf_op jit(solution)/shard_map/ppermute | solution.py:344
  12.3 23.5 %all-to-all-start = ((s32[8,4,2]{1,2,0:T(2,128)}), s32[8,4,2]{1,2,0:T(2,128)S(1)}, u32[]{:S(2)}, u32[]{:S(2)}) async-start(s32[8,4,2]{1,2,0:T(2,128)} %copy.25), calls=%async_computation | async-start | bytes 16384 | tf_op jit(solution)/shard_map/all_to_all | solution.py:319
  33.6 11.2 %collective-permute-start.4 = (bf16[1,256,128]{2,1,0:T(8,128)(2,1)S(1)}, bf16[1,256,128]{2,1,0:T(8,128)(2,1)S(1)}, u32[]{:S(2)}, u32[]{:S(2)}) collective-permute-start(bf16[1,256,128]{2,1,0:T(8,128)(2,1)S(1)} %slice.22), channel_id=1, source_target_pairs={{0,2},{2,4},{4,6},{6,7},{7,5},{5,3},{3,1},{1,0},{8,10},{10,12},{12... | collective-permute-start | bytes 196616 | tf_op jit(solution)/shard_map/ppermute | solution.py:343
  35.2 9.6 %collective-permute-start.8 = (bf16[1,256,128]{2,1,0:T(8,128)(2,1)S(1)}, bf16[1,256,128]{2,1,0:T(8,128)(2,1)S(1)}, u32[]{:S(2)}, u32[]{:S(2)}) collective-permute-start(bf16[1,256,128]{2,1,0:T(8,128)(2,1)S(1)} %slice.23), channel_id=1, source_target_pairs={{2,0},{4,2},{6,4},{7,6},{5,7},{3,5},{1,3},{0,1},{10,8},{12,10},{14... | collective-permute-start | bytes 196616 | tf_op jit(solution)/shard_map/ppermute | solution.py:344
  42.8 14.4 %collective-permute-start.28 = (bf16[1,272,128]{2,1,0:T(8,128)(2,1)S(1)}, bf16[1,272,128]{2,1,0:T(8,128)(2,1)S(1)}, u32[]{:S(2)}, u32[]{:S(2)}) collective-permute-start(bf16[1,272,128]{2,1,0:T(8,128)(2,1)S(1)} %get-tuple-element.63), channel_id=1, source_target_pairs={{0,2},{2,4},{4,6},{6,7},{7,5},{5,3},{3,1},{1,0},{8,10},{10,12},{12... | collective-permute-start | bytes 208904 | tf_op jit(solution)/shard_map/ppermute | solution.py:359
  44.2 12.9 %collective-permute-start.29 = (bf16[1,272,128]{2,1,0:T(8,128)(2,1)S(1)}, bf16[1,272,128]{2,1,0:T(8,128)(2,1)S(1)}, u32[]{:S(2)}, u32[]{:S(2)}) collective-permute-start(bf16[1,272,128]{2,1,0:T(8,128)(2,1)S(1)} %get-tuple-element.65), channel_id=1, source_target_pairs={{2,0},{4,2},{6,4},{7,6},{5,7},{3,5},{1,3},{0,1},{10,8},{12,10},{14... | collective-permute-start | bytes 208904 | tf_op jit(solution)/shard_map/ppermute | solution.py:360
  47.5 12.2 %collective-permute-start.10 = (bf16[1,272,128]{2,1,0:T(8,128)(2,1)S(1)}, bf16[1,272,128]{2,1,0:T(8,128)(2,1)S(1)}, u32[]{:S(2)}, u32[]{:S(2)}) collective-permute-start(bf16[1,272,128]{2,1,0:T(8,128)(2,1)S(1)} %get-tuple-element.47), channel_id=1, source_target_pairs={{2,0},{4,2},{6,4},{7,6},{5,7},{3,5},{1,3},{0,1},{10,8},{12,10},{14... | collective-permute-start | bytes 208904 | tf_op jit(solution)/shard_map/ppermute | solution.py:360
  47.5 12.2 %collective-permute-start.9 = (bf16[1,272,128]{2,1,0:T(8,128)(2,1)S(1)}, bf16[1,272,128]{2,1,0:T(8,128)(2,1)S(1)}, u32[]{:S(2)}, u32[]{:S(2)}) collective-permute-start(bf16[1,272,128]{2,1,0:T(8,128)(2,1)S(1)} %get-tuple-element.45), channel_id=1, source_target_pairs={{0,2},{2,4},{4,6},{6,7},{7,5},{5,3},{3,1},{1,0},{8,10},{10,12},{12... | collective-permute-start | bytes 208904 | tf_op jit(solution)/shard_map/ppermute | solution.py:359
  57.6 16.3 %collective-permute-start.30 = (bf16[2,272,128]{2,1,0:T(8,128)(2,1)S(1)}, bf16[2,272,128]{2,1,0:T(8,128)(2,1)S(1)}, u32[]{:S(2)}, u32[]{:S(2)}) collective-permute-start(bf16[2,272,128]{2,1,0:T(8,128)(2,1)S(1)} %get-tuple-element.67), channel_id=1, source_target_pairs={{0,2},{2,4},{4,6},{6,7},{7,5},{5,3},{3,1},{1,0},{8,10},{10,12},{12... | collective-permute-start | bytes 417800 | tf_op jit(solution)/shard_map/ppermute | solution.py:359
  57.6 16.2 %collective-permute-start.31 = (bf16[2,272,128]{2,1,0:T(8,128)(2,1)S(1)}, bf16[2,272,128]{2,1,0:T(8,128)(2,1)S(1)}, u32[]{:S(2)}, u32[]{:S(2)}) collective-permute-start(bf16[2,272,128]{2,1,0:T(8,128)(2,1)S(1)} %get-tuple-element.69), channel_id=1, source_target_pairs={{2,0},{4,2},{6,4},{7,6},{5,7},{3,5},{1,3},{0,1},{10,8},{12,10},{14... | collective-permute-start | bytes 417800 | tf_op jit(solution)/shard_map/ppermute | solution.py:360
  60.1 16.8 %collective-permute-start.11 = (bf16[2,272,128]{2,1,0:T(8,128)(2,1)S(1)}, bf16[2,272,128]{2,1,0:T(8,128)(2,1)S(1)}, u32[]{:S(2)}, u32[]{:S(2)}) collective-permute-start(bf16[2,272,128]{2,1,0:T(8,128)(2,1)S(1)} %get-tuple-element.49), channel_id=1, source_target_pairs={{0,2},{2,4},{4,6},{6,7},{7,5},{5,3},{3,1},{1,0},{8,10},{10,12},{12... | collective-permute-start | bytes 417800 | tf_op jit(solution)/shard_map/ppermute | solution.py:359
  61.1 15.8 %collective-permute-start.12 = (bf16[2,272,128]{2,1,0:T(8,128)(2,1)S(1)}, bf16[2,272,128]{2,1,0:T(8,128)(2,1)S(1)}, u32[]{:S(2)}, u32[]{:S(2)}) collective-permute-start(bf16[2,272,128]{2,1,0:T(8,128)(2,1)S(1)} %get-tuple-element.51), channel_id=1, source_target_pairs={{2,0},{4,2},{6,4},{7,6},{5,7},{3,5},{1,3},{0,1},{10,8},{12,10},{14... | collective-permute-start | bytes 417800 | tf_op jit(solution)/shard_map/ppermute | solution.py:360
  74.8 16.6 %collective-permute-start.32 = (bf16[2,272,128]{2,1,0:T(8,128)(2,1)S(1)}, bf16[2,272,128]{2,1,0:T(8,128)(2,1)S(1)}, u32[]{:S(2)}, u32[]{:S(2)}) collective-permute-start(bf16[2,272,128]{2,1,0:T(8,128)(2,1)S(1)} %get-tuple-element.71), channel_id=1, source_target_pairs={{0,2},{2,4},{4,6},{6,7},{7,5},{5,3},{3,1},{1,0},{8,10},{10,12},{12... | collective-permute-start | bytes 417800 | tf_op jit(solution)/shard_map/ppermute | solution.py:359
  74.9 16.6 %collective-permute-start.33 = (bf16[2,272,128]{2,1,0:T(8,128)(2,1)S(1)}, bf16[2,272,128]{2,1,0:T(8,128)(2,1)S(1)}, u32[]{:S(2)}, u32[]{:S(2)}) collective-permute-start(bf16[2,272,128]{2,1,0:T(8,128)(2,1)S(1)} %get-tuple-element.73), channel_id=1, source_target_pairs={{2,0},{4,2},{6,4},{7,6},{5,7},{3,5},{1,3},{0,1},{10,8},{12,10},{14... | collective-permute-start | bytes 417800 | tf_op jit(solution)/shard_map/ppermute | solution.py:360
  77.9 16.6 %collective-permute-start.13 = (bf16[2,272,128]{2,1,0:T(8,128)(2,1)S(1)}, bf16[2,272,128]{2,1,0:T(8,128)(2,1)S(1)}, u32[]{:S(2)}, u32[]{:S(2)}) collective-permute-start(bf16[2,272,128]{2,1,0:T(8,128)(2,1)S(1)} %get-tuple-element.53), channel_id=1, source_target_pairs={{0,2},{2,4},{4,6},{6,7},{7,5},{5,3},{3,1},{1,0},{8,10},{10,12},{12... | collective-permute-start | bytes 417800 | tf_op jit(solution)/shard_map/ppermute | solution.py:359
  78.0 16.5 %collective-permute-start.14 = (bf16[2,272,128]{2,1,0:T(8,128)(2,1)S(1)}, bf16[2,272,128]{2,1,0:T(8,128)(2,1)S(1)}, u32[]{:S(2)}, u32[]{:S(2)}) collective-permute-start(bf16[2,272,128]{2,1,0:T(8,128)(2,1)S(1)} %get-tuple-element.55), channel_id=1, source_target_pairs={{2,0},{4,2},{6,4},{7,6},{5,7},{3,5},{1,3},{0,1},{10,8},{12,10},{14... | collective-permute-start | bytes 417800 | tf_op jit(solution)/shard_map/ppermute | solution.py:360
  92.4 12.4 %collective-permute-start.34 = (bf16[2,272,128]{2,1,0:T(8,128)(2,1)S(1)}, bf16[2,272,128]{2,1,0:T(8,128)(2,1)S(1)}, u32[]{:S(2)}, u32[]{:S(2)}) collective-permute-start(bf16[2,272,128]{2,1,0:T(8,128)(2,1)S(1)} %get-tuple-element.75), channel_id=1, source_target_pairs={{0,2},{2,4},{4,6},{6,7},{7,5},{5,3},{3,1},{1,0},{8,10},{10,12},{12... | collective-permute-start | bytes 417800 | tf_op jit(solution)/shard_map/ppermute | solution.py:359
  92.5 12.3 %collective-permute-start.35 = (bf16[2,272,128]{2,1,0:T(8,128)(2,1)S(1)}, bf16[2,272,128]{2,1,0:T(8,128)(2,1)S(1)}, u32[]{:S(2)}, u32[]{:S(2)}) collective-permute-start(bf16[2,272,128]{2,1,0:T(8,128)(2,1)S(1)} %get-tuple-element.76), channel_id=1, source_target_pairs={{2,0},{4,2},{6,4},{7,6},{5,7},{3,5},{1,3},{0,1},{10,8},{12,10},{14... | collective-permute-start | bytes 417800 | tf_op jit(solution)/shard_map/ppermute | solution.py:360
  95.5 20.7 %collective-permute-start.15 = (bf16[2,272,128]{2,1,0:T(8,128)(2,1)S(1)}, bf16[2,272,128]{2,1,0:T(8,128)(2,1)S(1)}, u32[]{:S(2)}, u32[]{:S(2)}) collective-permute-start(bf16[2,272,128]{2,1,0:T(8,128)(2,1)S(1)} %get-tuple-element.57), channel_id=1, source_target_pairs={{0,2},{2,4},{4,6},{6,7},{7,5},{5,3},{3,1},{1,0},{8,10},{10,12},{12... | collective-permute-start | bytes 417800 | tf_op jit(solution)/shard_map/ppermute | solution.py:359
  95.6 20.6 %collective-permute-start.16 = (bf16[2,272,128]{2,1,0:T(8,128)(2,1)S(1)}, bf16[2,272,128]{2,1,0:T(8,128)(2,1)S(1)}, u32[]{:S(2)}, u32[]{:S(2)}) collective-permute-start(bf16[2,272,128]{2,1,0:T(8,128)(2,1)S(1)} %get-tuple-element.58), channel_id=1, source_target_pairs={{2,0},{4,2},{6,4},{7,6},{5,7},{3,5},{1,3},{0,1},{10,8},{12,10},{14... | collective-permute-start | bytes 417800 | tf_op jit(solution)/shard_map/ppermute | solution.py:360
  105.4 13.0 %collective-permute-start.36 = (bf16[1,272,128]{2,1,0:T(8,128)(2,1)S(1)}, bf16[1,272,128]{2,1,0:T(8,128)(2,1)S(1)}, u32[]{:S(2)}, u32[]{:S(2)}) collective-permute-start(bf16[1,272,128]{2,1,0:T(8,128)(2,1)S(1)} %get-tuple-element.77), channel_id=1, source_target_pairs={{0,16},{8,24},{16,0},{24,8},{1,17},{9,25},{17,1},{25,9},{2,18},{10... | collective-permute-start | bytes 208904 | tf_op jit(solution)/shard_map/ppermute | solution.py:389
  (19 other events, 102.0 us)

commit v2 on v0

v2 whole, which is shorter than its diff:
```python
import functools
import math

import jax
import jax.numpy as jnp
from jax import lax
from jax.experimental import pallas as pl
from jax.experimental.pallas import tpu as pltpu
from jax.sharding import PartitionSpec as P

KVH = 8
HD = 128
GQ = 8
STEPS = 4
PAGE = 128
SEL = 4

LANES = 128
ROWS = GQ * STEPS
HALF = 16
BODY = KVH * ROWS
COLS = BODY // HALF
SECOND = 3 * COLS
PAIR = 2 * BODY + HALF
LONE = BODY + HALF
EMPTY = -1e30
SCALE = math.log2(math.e) / math.sqrt(HD)
VMEM_BYTES = 24 * 1024 * 1024
BF16 = jnp.bfloat16
F32 = jnp.float32
IN_VMEM = pl.BlockSpec(memory_space=pltpu.VMEM)
IN_SMEM = pl.BlockSpec(memory_space=pltpu.SMEM)


def params():
    return pltpu.CompilerParams(vmem_limit_bytes=VMEM_BYTES)


def cost(flops, moved):
    return pl.CostEstimate(flops=flops, bytes_accessed=moved, transcendentals=0)


def list_rows(requests):
    return -(-2 * requests // HALF) * HALF


def lane_ids(rows=HALF):
    return lax.broadcasted_iota(jnp.int32, (rows, LANES), 1)


def pack_stats(stats):
    lanes = lane_ids()
    used = (lanes < COLS) | ((lanes >= SECOND) & (lanes < SECOND + COLS))
    stats = jnp.where(used, stats, 0.0)
    high = stats.astype(BF16).astype(F32)
    rest = stats - high
    middle = rest.astype(BF16).astype(F32)
    low = rest - middle
    return (high + pltpu.roll(middle, COLS, 1) + pltpu.roll(low, 2 * COLS, 1)).astype(BF16)


def unpack_stats(tile):
    tile = tile.astype(F32)
    return tile + pltpu.roll(tile, LANES - COLS, 1) + pltpu.roll(tile, LANES - 2 * COLS, 1)


def tile_start(index):
    half, head = divmod(index, KVH)
    return head * ROWS + half * HALF


def by_lane(columns):
    lanes = lane_ids()
    tile = jnp.zeros((HALF, LANES), F32)
    for head, values in enumerate(columns):
        for half in range(ROWS // HALF):
            part = values[half * HALF : (half + 1) * HALF, :]
            tile = jnp.where(lanes == half * KVH + head, part, tile)
    return tile


def attend(queries, keys, values, usable):
    across = (((1,), (1,)), ((), ()))
    along = (((1,), (0,)), ((), ()))
    scores = [lax.dot_general(q, k, across, preferred_element_type=F32) for q, k in zip(queries, keys)]
    scores = [jnp.where(usable, s * SCALE, EMPTY) for s in scores]
    tops = [jnp.max(s, axis=1, keepdims=True) for s in scores]
    weights = [jnp.exp2(s - t) for s, t in zip(scores, tops)]
    totals = [jnp.sum(w, axis=1, keepdims=True) for w in weights]
    mixed = [lax.dot_general(w.astype(BF16), v, along, preferred_element_type=F32) for w, v in zip(weights, values)]
    level = by_lane(tops) + jnp.log2(jnp.maximum(by_lane(totals), 1.0))
    return [m / t for m, t in zip(mixed, totals)], level


def relayout_kernel(place_ref, queries_ref, *outs):
    for d, out in enumerate(outs):
        values = queries_ref[place_ref[0] ^ d].astype(F32)
        for head in range(KVH):
            first = head * GQ
            parts = [values[:, (first + g) * HD : (first + g + 1) * HD] for g in range(GQ)]
            out[head * ROWS : (head + 1) * ROWS, :] = jnp.concatenate(parts, axis=0).astype(BF16)


def relayout(place, queries):
    groups = queries.shape[0]
    return pl.pallas_call(
        relayout_kernel,
        out_shape=[jax.ShapeDtypeStruct((BODY, HD), BF16)] * groups,
        in_specs=[IN_SMEM, IN_VMEM],
        out_specs=[IN_VMEM] * groups,
        compiler_params=params(),
        cost_estimate=cost(0, 4 * queries.size),
    )(place, queries)


def new_kernel(place_ref, *refs):
    queries, (new_ref, out_ref, level_ref) = refs[:-3], refs[-3:]
    step = lax.broadcasted_iota(jnp.int32, (ROWS, STEPS), 0) % STEPS
    usable = lax.broadcasted_iota(jnp.int32, (ROWS, STEPS), 1) <= step
    for d, query in enumerate(queries):
        new = new_ref[place_ref[0] ^ d]
        heads = [new[:, head * HD : (head + 1) * HD] for head in range(2 * KVH)]
        rows = [query[head * ROWS : (head + 1) * ROWS, :] for head in range(KVH)]
        mixed, level = attend(rows, heads[:KVH], heads[KVH:], usable)
        for head, values in enumerate(mixed):
            out_ref[d, head * ROWS : (head + 1) * ROWS, :] = values
        level_ref[d] = level


def new_tokens(place, queries, new_kv):
    groups = len(queries)
    return pl.pallas_call(
        new_kernel,
        out_shape=[
            jax.ShapeDtypeStruct((groups, BODY, HD), F32),
            jax.ShapeDtypeStruct((groups, HALF, LANES), F32),
        ],
        in_specs=[IN_SMEM] + [IN_VMEM] * (groups + 1),
        out_specs=[IN_VMEM, IN_VMEM],
        compiler_params=params(),
        cost_estimate=cost(groups * KVH * 4 * ROWS * HD * HD, groups * BODY * HD * 6),
    )(place, *queries, new_kv)


def payload_kernel(place_ref, owner_ref, index_ref, length_ref, *refs):
    visits, out = refs[:-1], refs[-1]
    cut = len(visits) // 2
    lists = list_rows(len(visits))
    rows = lax.broadcasted_iota(jnp.int32, (lists, LANES), 0)
    lanes = lane_ids(lists)
    tile = jnp.zeros((lists, LANES), F32)
    for d, visit in enumerate(visits):
        start = d * BODY + (lists if d >= cut else 0)
        out[start : start + BODY, :] = visit[...]
        row = place_ref[0] ^ d
        for s in range(SEL):
            count = jnp.clip(length_ref[row] - s * PAGE, 0, PAGE).astype(F32)
            mine = lanes == owner_ref[row, s]
            tile = jnp.where(mine & (rows == 2 * d), count, tile)
            tile = jnp.where(mine & (rows == 2 * d + 1), index_ref[row, s].astype(F32), tile)
    out[cut * BODY : cut * BODY + lists, :] = tile.astype(BF16)


def payload(place, page_owner, page_index, lengths, visits):
    groups = len(visits)
    rows = groups * BODY + list_rows(groups)
    return pl.pallas_call(
        payload_kernel,
        out_shape=jax.ShapeDtypeStruct((rows, HD), BF16),
        in_specs=[IN_SMEM] * 4 + [IN_VMEM] * groups,
        out_specs=IN_VMEM,
        compiler_params=params(),
        cost_estimate=cost(0, 4 * rows * HD),
    )(place, page_owner, page_index, lengths, *visits)


def item_kernel(slots, list_start, first, gap_at, lists, place_ref, query_ref, cache_ref, out_ref, level_ref, code_ref):
    owner = place_ref[1]
    table = query_ref[list_start : list_start + lists, :].astype(F32)
    rows = lax.broadcasted_iota(jnp.int32, (lists, LANES), 0)
    table = jnp.where(lane_ids(lists) == owner, table, 0.0)
    for entry, slot in enumerate(slots):
        code = jnp.where(rows == 2 * slot, table, jnp.where(rows == 2 * slot + 1, table * 256.0, 0.0))
        code_ref[entry] = jnp.sum(code).astype(jnp.int32)
    tokens = lax.broadcasted_iota(jnp.int32, (ROWS, PAGE), 1)

    @pl.loop(0, len(slots))
    def _(entry):
        code = code_ref[entry]
        count, page = code & 255, code >> 8
        start = first + entry * BODY + jnp.where(entry >= gap_at, lists, 0)
        out = (entry // 2) * PAIR + (entry % 2) * BODY

        @pl.when(count > 0)
        def _():
            queries = [query_ref[pl.ds(pl.multiple_of(start + h * ROWS, HALF), ROWS), :] for h in range(KVH)]
            keys = [cache_ref[page, :, h * HD : (h + 1) * HD] for h in range(KVH)]
            values = [cache_ref[page, :, (KVH + h) * HD : (KVH + h + 1) * HD] for h in range(KVH)]
            mixed, level = attend(queries, keys, values, tokens < count)
            for head, part in enumerate(mixed):
                out_ref[pl.ds(pl.multiple_of(out + head * ROWS, HALF), ROWS), :] = part.astype(BF16)
            level_ref[entry] = level

        @pl.when(count <= 0)
        def _():
            out_ref[pl.ds(pl.multiple_of(out, HALF), BODY), :] = jnp.zeros((BODY, HD), BF16)
            level_ref[entry] = jnp.full((HALF, LANES), EMPTY, F32)

    lanes = lane_ids()
    for pair in range(len(slots) // 2):
        level = jnp.where(lanes < COLS, level_ref[2 * pair], pltpu.roll(level_ref[2 * pair + 1], SECOND, 1))
        start = pair * PAIR + 2 * BODY
        out_ref[start : start + HALF, :] = pack_stats(level)


def items(place, queries, kv_cache, requests, slots):
    lists = list_rows(requests)
    cut = requests // 2
    if len(slots) == requests:
        list_start, first, gap_at = cut * BODY, 0, cut
    elif slots[0] == 0:
        list_start, first, gap_at = cut * BODY, 0, requests
    else:
        list_start, first, gap_at = 0, lists, requests
    count = len(slots)
    out_rows = count // 2 * PAIR
    return pl.pallas_call(
        functools.partial(item_kernel, slots, list_start, first, gap_at, lists),
        out_shape=jax.ShapeDtypeStruct((out_rows, HD), BF16),
        in_specs=[IN_SMEM, IN_VMEM, IN_VMEM],
        out_specs=IN_VMEM,
        scratch_shapes=[pltpu.VMEM((count, HALF, LANES), F32), pltpu.SMEM((count,), jnp.int32)],
        compiler_params=params(),
        cost_estimate=cost(count * KVH * 4 * ROWS * HD * PAGE, count * PAGE * kv_cache.shape[2] * 2),
    )(place, queries, kv_cache)


def blend(levels):
    peak = functools.reduce(jnp.maximum, levels)
    shares = [jnp.exp2(level - peak) for level in levels]
    total = functools.reduce(jnp.add, shares)
    return [share / total for share in shares], peak + jnp.log2(total)


def mix(shares, refs, start, first_lane):
    values = []
    for index in range(COLS):
        row, lane = start + tile_start(index), first_lane + index
        parts = [share[:, lane : lane + 1] * ref[row : row + HALF, :].astype(F32) for share, ref in zip(shares, refs)]
        values.append(functools.reduce(jnp.add, parts))
    return values


def merge_kernel(base, arrived_ref, own_ref, out_ref):
    pairs = out_ref.shape[0] // PAIR
    arrived_pairs = arrived_ref.shape[0] // PAIR
    for pair in range(pairs):
        start = pair * PAIR
        if not base <= pair < base + arrived_pairs:
            out_ref[start : start + PAIR, :] = own_ref[start : start + PAIR, :]
            continue
        arrived = arrived_ref.at[(pair - base) * PAIR : (pair - base + 1) * PAIR]
        own = own_ref.at[start : start + PAIR]
        out = out_ref.at[start : start + PAIR]
        levels = [unpack_stats(ref[2 * BODY : PAIR, :]) for ref in (arrived, own)]
        shares, level = blend(levels)
        values = [mix(shares, (arrived, own), second * BODY, second * SECOND) for second in range(2)]
        for second in range(2):
            for index in range(COLS):
                row = second * BODY + tile_start(index)
                out[row : row + HALF, :] = values[second][index].astype(BF16)
        out[2 * BODY : PAIR, :] = pack_stats(level)


def merge(arrived, own, base):
    return pl.pallas_call(
        functools.partial(merge_kernel, base),
        out_shape=jax.ShapeDtypeStruct(own.shape, BF16),
        in_specs=[IN_VMEM, IN_VMEM],
        out_specs=IN_VMEM,
        compiler_params=params(),
        cost_estimate=cost(0, 6 * own.size),
    )(arrived, own)


def gather_kernel(ahead_base, behind_base, ahead_ref, behind_ref, own_ref, *outs):
    for pair in range(len(outs) // 2):
        sources = [own_ref.at[pair * PAIR : (pair + 1) * PAIR]]
        for ref, base in ((ahead_ref, ahead_base), (behind_ref, behind_base)):
            if base <= pair < base + ref.shape[0] // PAIR:
                sources.append(ref.at[(pair - base) * PAIR : (pair - base + 1) * PAIR])
        shares, level = blend([unpack_stats(ref[2 * BODY : PAIR, :]) for ref in sources])
        for second in range(2):
            out = outs[2 * pair + second]
            for index, values in enumerate(mix(shares, sources, second * BODY, second * SECOND)):
                row = tile_start(index)
                out[row : row + HALF, :] = values.astype(BF16)
            here = pltpu.roll(level, LANES - SECOND, 1) if second else level
            out[BODY:LONE, :] = pack_stats(here)


def gather(ahead, behind, own, requests, ahead_base, behind_base):
    return pl.pallas_call(
        functools.partial(gather_kernel, ahead_base, behind_base),
        out_shape=[jax.ShapeDtypeStruct((LONE, HD), BF16)] * requests,
        in_specs=[IN_VMEM] * 3,
        out_specs=[IN_VMEM] * requests,
        compiler_params=params(),
        cost_estimate=cost(0, 8 * own.size),
    )(ahead, behind, own)


def final_kernel(place_ref, *refs):
    parts, (new_ref, level_ref, out_ref) = refs[:-3], refs[-3:]
    for d, part in enumerate(parts):
        row = place_ref[0] ^ d
        shares, _ = blend([unpack_stats(part[BODY:LONE, :]), level_ref[d]])
        values = mix(shares, (part, new_ref.at[d]), 0, 0)
        for index, tile in enumerate(values):
            first = tile_start(index) // STEPS
            for g in range(HALF // STEPS):
                head = first + g
                out_ref[row, :, head * HD : (head + 1) * HD] = tile[g * STEPS : (g + 1) * STEPS, :].astype(BF16)


def final(place, parts, new_out, new_level):
    groups = len(parts)
    return pl.pallas_call(
        final_kernel,
        out_shape=jax.ShapeDtypeStruct((groups, STEPS, KVH * GQ * HD), BF16),
        in_specs=[IN_SMEM] + [IN_VMEM] * (groups + 2),
        out_specs=IN_VMEM,
        compiler_params=params(),
        cost_estimate=cost(0, groups * BODY * HD * 8),
    )(place, *parts, new_out, new_level)


def ring_order(owners):
    return list(range(0, owners, 2)) + list(range(owners - 1, 0, -2))


def per_device(queries, new_kv, kv_cache, page_owner, page_index, lengths):
    groups = lax.axis_size("grp")
    owners = lax.axis_size("cache")
    requests = queries.shape[0]
    assert requests == groups and requests % 4 == 0 and owners <= LANES
    reach = owners // 2
    order = ring_order(owners)
    forward = [(order[i], order[(i + 1) % owners]) for i in range(owners)]
    backward = [(b, a) for a, b in forward]
    place = jnp.stack([lax.axis_index("grp"), lax.axis_index("cache")]).astype(jnp.int32)

    def swap(array, d):
        return lax.ppermute(array, "grp", [(g, g ^ d) for g in range(groups)]) if d else array

    rows = relayout(place, queries)
    visits = [swap(rows[d], d) for d in range(groups)]
    new_out, new_level = new_tokens(place, rows, new_kv)
    block = payload(place, page_owner, page_index[:, :, 0], lengths, visits)

    slots = list(range(requests))
    cut = requests // 2
    lists = list_rows(requests)
    ahead = behind = block
    parts = {0: items(place, block, kv_cache, requests, slots)}
    for step in range(1, reach + 1):
        if step == reach:
            ahead, behind = ahead[: cut * BODY + lists], behind[cut * BODY :]
        ahead = lax.ppermute(ahead, "cache", forward)
        behind = lax.ppermute(behind, "cache", backward)
        parts[-step] = items(place, ahead, kv_cache, requests, slots if step < reach else slots[:cut])
        parts[step] = items(place, behind, kv_cache, requests, slots if step < reach else slots[cut:])

    ahead, behind = parts[-reach], parts[reach]
    for step in range(reach - 1, -1, -1):
        ahead = lax.ppermute(ahead, "cache", forward)
        behind = lax.ppermute(behind, "cache", backward)
        base = cut // 2 if step == reach - 1 else 0
        if step > 0:
            ahead, behind = merge(ahead, parts[step], 0), merge(behind, parts[-step], base)
        else:
            returned = gather(ahead, behind, parts[0], requests, 0, base)
    home = [swap(returned[d], d) for d in range(groups)]
    return final(place, home, new_out, new_level)


def solution(mesh):
    in_specs = (
        P(("grp", "cache"), None, None),
        P(("grp", "cache"), None, None),
        P(("grp", "cache"), None, None),
        P(("grp", "cache"), None),
        P(("grp", "cache"), None, None),
        P(("grp", "cache")),
    )
    out_specs = P(("grp", "cache"), None, None)
    return jax.shard_map(
        per_device, mesh=mesh, in_specs=in_specs, out_specs=out_specs, check_vma=False
    )
```

time: 276 us -> 88.4 us (0.32)
  local copies, waits for them, and re-layouts: 93.7 us -> 7.31 us
  blocking collectives: 81.8 us -> 0 us
  matrix products: 29.3 us -> 0 us
  Pallas kernels: 0 us -> 20.9 us
  between operations: 14.4 us -> 0.13 us
  other arithmetic: 12.4 us -> 0.07 us
  waiting for transfers between devices: 25.1 us -> 34.4 us
  starting transfers between devices: 17.8 us -> 25.1 us
    all_gather x2 -> x0, blocking collectives: 53.3 us -> none  [the longest x1 27.2 us: per_device(): lax.all_gather(page_owner, 'cache', axis=0, tiled=True)]
    slice x12 -> x2, local copies, waits for them, and re-layouts: 38.8 us -> 0.02 us  [per_device(): ahead, behind = (ahead[:cut * BODY + lists], behind[cut * BODY:])]
    ppermute x0 -> x22, waiting for transfers between devices: none -> 34.4 us  [the longest x8 26 us: per_device(): ahead = lax.ppermute(ahead, 'cache', forward)]
    dot_general x8 -> x0, matrix products: 29.3 us -> none  [the longest x2 8.67 us: item_partial(): jnp.einsum('tkgd,ukd->tkgu', query_heads, key_rows, preferred_element_typ...]
    ppermute x0 -> x22, starting transfers between devices: none -> 25.1 us  [the longest x8 11.8 us: per_device(): behind = lax.ppermute(behind, 'cache', backward)]
    all_to_all x4 -> x0, waiting for transfers between devices: 25 us -> none  [the longest x1 20.6 us: per_device(): lax.all_to_all(part_out, 'cache', split_axis=0, concat_axis=0, tiled=True)]
    pallas_call x0 -> x20, Pallas kernels: none -> 20.9 us  [the longest x9 11.6 us: items(): pl.pallas_call(functools.partial(item_kernel, slots, list_start, first, g...]
    all_to_all x2 -> x0, blocking collectives: 18.8 us -> none  [the longest x1 10.3 us: per_device(): lax.all_to_all(sent_queries, 'grp', split_axis=0, concat_axis=0, tiled=True)]
  transfers between devices with their start and end apart: 5 -> 22, of which waited for: 3 -> 15; matrix products, arithmetic and copies ran while one was open for 42% -> 0% of each run, Pallas kernels for 0% -> 19%
where the time goes in v2:
time: 88.4 us; the launch traced here: 87.8 us
  waiting for transfers between devices  34.4 us (39%)
  starting transfers between devices  25.1 us (28%)
  Pallas kernels  20.9 us (24%)
  local copies, waits for them, and re-layouts  7.31 us (8%)
    ppermute x8, waiting for transfers between devices, per_device(): ahead = lax.ppermute(ahead, 'cache', forward)  26 us
    ppermute x8, starting transfers between devices, per_device(): behind = lax.ppermute(behind, 'cache', backward)  11.8 us
    pallas_call x9, Pallas kernels, items(): pl.pallas_call(functools.partial(item_kernel, slots, list_start, first, g...  11.6 us
    ppermute x8, starting transfers between devices, per_device(): ahead = lax.ppermute(ahead, 'cache', forward)  8.16 us
    unnamed x14, local copies, waits for them, and re-layouts  7.29 us
    ppermute x6, waiting for transfers between devices, swap(): lax.ppermute(array, 'grp', [(g, g ^ d) for g in range(groups)])  6.11 us
    ppermute x6, starting transfers between devices, swap(): lax.ppermute(array, 'grp', [(g, g ^ d) for g in range(groups)])  5.1 us
    pallas_call x6, Pallas kernels, merge(): pl.pallas_call(functools.partial(merge_kernel, base), out_shape=jax.Shape...  3.3 us
  transfers between devices with their start and end apart: 22, of which 15 were waited for; matrix products, arithmetic and copies ran while one was open for 0% of the time, Pallas kernels for 19%

profile of v2, /device:TPU:0, one launch (start us, length us, event | category | flops | bytes accessed | tf_op | source)
XLA Modules:
  0.0 87.8 jit_solution(4354684829560968240)
XLA Ops:
  2.1 2.6 %collective-permute-start.1 = (bf16[256,128]{1,0:T(8,128)(2,1)S(1)}, bf16[256,128]{1,0:T(8,128)(2,1)S(1)}, u32[]{:S(2)}, u32[]{:S(2)}) collective-permute-start(bf16[256,128]{1,0:T(8,128)(2,1)S(1)} %get-tuple-element.17.refs_2_), channel_id=1, source_target_pairs={{0,16},{8,24},{16,0},{24,8},{1,17},{9,25},{17,1},{25,9},{2,18},{10... | collective-permute-start | bytes 196616 | tf_op jit(solution)/shard_map/ppermute | solution.py:354
  4.8 2.6 %collective-permute-done.1.refs_2_ = bf16[256,128]{1,0:T(8,128)(2,1)S(1)} collective-permute-done((bf16[256,128]{1,0:T(8,128)(2,1)S(1)}, bf16[256,128]{1,0:T(8,128)(2,1)S(1)}, u32[]{:S(2)}, u32[]{:S(2)}) %collective-permute-start.1) | collective-permute-done | bytes 65568 | tf_op jit(solution)/shard_map/ppermute | solution.py:354
  7.4 1.4 %collective-permute-done.2.refs_3_ = bf16[256,128]{1,0:T(8,128)(2,1)S(1)} collective-permute-done((bf16[256,128]{1,0:T(8,128)(2,1)S(1)}, bf16[256,128]{1,0:T(8,128)(2,1)S(1)}, u32[]{:S(2)}, u32[]{:S(2)}) %collective-permute-start.2) | collective-permute-done | bytes 65568 | tf_op jit(solution)/shard_map/ppermute | solution.py:354
  11.5 1.6 %collective-permute-start.3 = (bf16[1040,128]{1,0:T(8,128)(2,1)S(1)}, bf16[1040,128]{1,0:T(8,128)(2,1)S(1)}, u32[]{:S(2)}, u32[]{:S(2)}) collective-permute-start(bf16[1040,128]{1,0:T(8,128)(2,1)S(1)} %shard_map.65.query_ref), channel_id=1, source_target_pairs={{0,2},{2,4},{4,6},{6,7},{7,5},{5,3},{3,1},{1,0},{8,10},{10,12},{12... | collective-permute-start | bytes 798728 | tf_op jit(solution)/shard_map/ppermute | solution.py:369
  13.5 6.4 %collective-permute-done.3.query_ref = bf16[1040,128]{1,0:T(8,128)(2,1)S(1)} collective-permute-done((bf16[1040,128]{1,0:T(8,128)(2,1)S(1)}, bf16[1040,128]{1,0:T(8,128)(2,1)S(1)}, u32[]{:S(2)}, u32[]{:S(2)}) %collective-permute-start.3) | collective-permute-done | bytes 266272 | tf_op jit(solution)/shard_map/ppermute | solution.py:369
  20.0 1.6 %collective-permute-start.4 = (bf16[1040,128]{1,0:T(8,128)(2,1)S(1)}, bf16[1040,128]{1,0:T(8,128)(2,1)S(1)}, u32[]{:S(2)}, u32[]{:S(2)}) collective-permute-start(bf16[1040,128]{1,0:T(8,128)(2,1)S(1)} %collective-permute-done.3.query_ref), channel_id=1, source_target_pairs={{0,2},{2,4},{4,6},{6,7},{7,5},{5,3},{3,1},{1,0},{8,10},{10,12},{12... | collective-permute-start | bytes 798728 | tf_op jit(solution)/shard_map/ppermute | solution.py:369
  22.0 5.6 %collective-permute-done.4.query_ref = bf16[1040,128]{1,0:T(8,128)(2,1)S(1)} collective-permute-done((bf16[1040,128]{1,0:T(8,128)(2,1)S(1)}, bf16[1040,128]{1,0:T(8,128)(2,1)S(1)}, u32[]{:S(2)}, u32[]{:S(2)}) %collective-permute-start.4) | collective-permute-done | bytes 266272 | tf_op jit(solution)/shard_map/ppermute | solution.py:369
  27.6 1.6 %collective-permute-start.5 = (bf16[1040,128]{1,0:T(8,128)(2,1)S(1)}, bf16[1040,128]{1,0:T(8,128)(2,1)S(1)}, u32[]{:S(2)}, u32[]{:S(2)}) collective-permute-start(bf16[1040,128]{1,0:T(8,128)(2,1)S(1)} %collective-permute-done.4.query_ref), channel_id=1, source_target_pairs={{0,2},{2,4},{4,6},{6,7},{7,5},{5,3},{3,1},{1,0},{8,10},{10,12},{12... | collective-permute-start | bytes 798728 | tf_op jit(solution)/shard_map/ppermute | solution.py:369
  29.7 4.7 %collective-permute-done.5.query_ref = bf16[1040,128]{1,0:T(8,128)(2,1)S(1)} collective-permute-done((bf16[1040,128]{1,0:T(8,128)(2,1)S(1)}, bf16[1040,128]{1,0:T(8,128)(2,1)S(1)}, u32[]{:S(2)}, u32[]{:S(2)}) %collective-permute-start.5) | collective-permute-done | bytes 266272 | tf_op jit(solution)/shard_map/ppermute | solution.py:369
  34.4 1.6 %collective-permute-start.6 = (bf16[528,128]{1,0:T(8,128)(2,1)S(1)}, bf16[528,128]{1,0:T(8,128)(2,1)S(1)}, u32[]{:S(2)}, u32[]{:S(2)}) collective-permute-start(bf16[528,128]{1,0:T(8,128)(2,1)S(1)} %slice.8), channel_id=1, source_target_pairs={{0,2},{2,4},{4,6},{6,7},{7,5},{5,3},{3,1},{1,0},{8,10},{10,12},{12... | collective-permute-start | bytes 405512 | tf_op jit(solution)/shard_map/ppermute | solution.py:369
  36.5 2.9 %collective-permute-done.6.query_ref = bf16[528,128]{1,0:T(8,128)(2,1)S(1)} collective-permute-done((bf16[528,128]{1,0:T(8,128)(2,1)S(1)}, bf16[528,128]{1,0:T(8,128)(2,1)S(1)}, u32[]{:S(2)}, u32[]{:S(2)}) %collective-permute-start.6) | collective-permute-done | bytes 135200 | tf_op jit(solution)/shard_map/ppermute | solution.py:369
  39.4 3.4 %copy-done = bf16[16,128,2048]{2,1,0:T(8,128)(2,1)S(1)} copy-done((bf16[16,128,2048]{2,1,0:T(8,128)(2,1)S(1)}, bf16[16,128,2048]{2,1,0:T(8,128)(2,1)}, u32[]{:S(2)}) %copy-start) | copy-done | bytes 8388632
  43.7 1.6 %collective-permute-start.7 = (bf16[528,128]{1,0:T(8,128)(2,1)S(1)}, bf16[528,128]{1,0:T(8,128)(2,1)S(1)}, u32[]{:S(2)}, u32[]{:S(2)}) collective-permute-start(bf16[528,128]{1,0:T(8,128)(2,1)S(1)} %shard_map.66), channel_id=1, source_target_pairs={{0,2},{2,4},{4,6},{6,7},{7,5},{5,3},{3,1},{1,0},{8,10},{10,12},{12... | collective-permute-start | bytes 405512 | tf_op jit(solution)/shard_map/ppermute | solution.py:376
  47.0 2.4 %collective-permute-start.15 = (bf16[528,128]{1,0:T(8,128)(2,1)S(1)}, bf16[528,128]{1,0:T(8,128)(2,1)S(1)}, u32[]{:S(2)}, u32[]{:S(2)}) collective-permute-start(bf16[528,128]{1,0:T(8,128)(2,1)S(1)} %shard_map.73), channel_id=1, source_target_pairs={{2,0},{4,2},{6,4},{7,6},{5,7},{3,5},{1,3},{0,1},{10,8},{12,10},{14... | collective-permute-start | bytes 405512 | tf_op jit(solution)/shard_map/ppermute | solution.py:377
  53.5 2.5 %collective-permute-start.16 = (bf16[1056,128]{1,0:T(8,128)(2,1)S(1)}, bf16[1056,128]{1,0:T(8,128)(2,1)S(1)}, u32[]{:S(2)}, u32[]{:S(2)}) collective-permute-start(bf16[1056,128]{1,0:T(8,128)(2,1)S(1)} %shard_map.75), channel_id=1, source_target_pairs={{2,0},{4,2},{6,4},{7,6},{5,7},{3,5},{1,3},{0,1},{10,8},{12,10},{14... | collective-permute-start | bytes 811016 | tf_op jit(solution)/shard_map/ppermute | solution.py:377
  57.4 1.8 %shard_map.76.own_ref = bf16[1056,128]{1,0:T(8,128)(2,1)S(1)} custom-call(s32[2]{0:T(128)S(1)} %pad_add_fusion.place_ref, bf16[1040,128]{1,0:T(8,128)(2,1)S(1)} %collective-permute-done.4.query_ref, bf16[16,128,2048]{2,1,0:T(8,128)(2,1)S(1)} %copy-done.1), custom_call_target="tpu_custom_call" | custom-call | flops 67108864 | bytes 2097152 | tf_op jit(solution)/shard_map/pallas_call | solution.py:227
  59.2 1.6 %collective-permute-done.11.arrived_ref = bf16[1056,128]{1,0:T(8,128)(2,1)S(1)} collective-permute-done((bf16[1056,128]{1,0:T(8,128)(2,1)S(1)}, bf16[1056,128]{1,0:T(8,128)(2,1)S(1)}, u32[]{:S(2)}, u32[]{:S(2)}) %collective-permute-start.11) | collective-permute-done | bytes 270368 | tf_op jit(solution)/shard_map/ppermute | solution.py:376
  62.4 2.5 %collective-permute-start.17 = (bf16[1056,128]{1,0:T(8,128)(2,1)S(1)}, bf16[1056,128]{1,0:T(8,128)(2,1)S(1)}, u32[]{:S(2)}, u32[]{:S(2)}) collective-permute-start(bf16[1056,128]{1,0:T(8,128)(2,1)S(1)} %shard_map.77), channel_id=1, source_target_pairs={{2,0},{4,2},{6,4},{7,6},{5,7},{3,5},{1,3},{0,1},{10,8},{12,10},{14... | collective-permute-start | bytes 811016 | tf_op jit(solution)/shard_map/ppermute | solution.py:377
  67.2 3.6 %collective-permute-done.12.arrived_ref = bf16[1056,128]{1,0:T(8,128)(2,1)S(1)} collective-permute-done((bf16[1056,128]{1,0:T(8,128)(2,1)S(1)}, bf16[1056,128]{1,0:T(8,128)(2,1)S(1)}, u32[]{:S(2)}, u32[]{:S(2)}) %collective-permute-start.12) | collective-permute-done | bytes 270368 | tf_op jit(solution)/shard_map/ppermute | solution.py:376
  72.4 2.5 %collective-permute-start.18 = (bf16[1056,128]{1,0:T(8,128)(2,1)S(1)}, bf16[1056,128]{1,0:T(8,128)(2,1)S(1)}, u32[]{:S(2)}, u32[]{:S(2)}) collective-permute-start(bf16[1056,128]{1,0:T(8,128)(2,1)S(1)} %shard_map.79), channel_id=1, source_target_pairs={{2,0},{4,2},{6,4},{7,6},{5,7},{3,5},{1,3},{0,1},{10,8},{12,10},{14... | collective-permute-start | bytes 811016 | tf_op jit(solution)/shard_map/ppermute | solution.py:377
  74.9 1.8 %shard_map.80.own_ref = bf16[1056,128]{1,0:T(8,128)(2,1)S(1)} custom-call(s32[2]{0:T(128)S(1)} %pad_add_fusion.place_ref, bf16[1040,128]{1,0:T(8,128)(2,1)S(1)} %shard_map.65.query_ref, bf16[16,128,2048]{2,1,0:T(8,128)(2,1)S(1)} %copy-done.1), custom_call_target="tpu_custom_call" | custom-call | flops 67108864 | bytes 2097152 | tf_op jit(solution)/shard_map/pallas_call | solution.py:227
  81.9 1.6 %shard_map.82 = (f32[4,256,128]{2,1,0:T(8,128)S(1)}, f32[4,16,128]{2,1,0:T(8,128)S(1)}) custom-call(s32[2]{0:T(128)S(1)} %pad_add_fusion.place_ref, bf16[256,128]{1,0:T(8,128)(2,1)S(1)} %get-tuple-element.15.refs_0_, bf16[256,128]{1,0:T(8,128)(2,1)S(1)} %get-tuple-element.16.refs_1_, bf16[256,128]{1,0:T(8,128)(2,1)S(1)} %get-tuple-element.17.refs_2_, ...), custom_call_target="tpu_custom_call" | custom-call | flops 67108864 | bytes 786432 | tf_op jit(solution)/shard_map/pallas_call | solution.py:132
  83.6 1.5 %collective-permute-done.20.refs_2_ = bf16[272,128]{1,0:T(8,128)(2,1)S(1)} collective-permute-done((bf16[272,128]{1,0:T(8,128)(2,1)S(1)}, bf16[272,128]{1,0:T(8,128)(2,1)S(1)}, u32[]{:S(2)}, u32[]{:S(2)}) %collective-permute-start.20) | collective-permute-done | bytes 69664 | tf_op jit(solution)/shard_map/ppermute | solution.py:354
  85.7 2.1 %shard_map.83 = bf16[4,4,8192]{2,1,0:T(4,128)(2,1)} custom-call(s32[2]{0:T(128)S(1)} %pad_add_fusion.place_ref, bf16[272,128]{1,0:T(8,128)(2,1)S(1)} %get-tuple-element.19.refs_0_, bf16[272,128]{1,0:T(8,128)(2,1)S(1)} %collective-permute-done.19.refs_1_, bf16[272,128]{1,0:T(8,128)(2,1)S(1)} %collective-permute-done.20.refs_2_, ...), custom_call_target="tpu_custom_call" | custom-call | bytes 1048576 | tf_op jit(solution)/shard_map/pallas_call | solution.py:328
  (57 shorter events, 26.1 us)
Async XLA Ops:
  1.6 3.2 %collective-permute-start = (bf16[256,128]{1,0:T(8,128)(2,1)S(1)}, bf16[256,128]{1,0:T(8,128)(2,1)S(1)}, u32[]{:S(2)}, u32[]{:S(2)}) collective-permute-start(bf16[256,128]{1,0:T(8,128)(2,1)S(1)} %get-tuple-element.16.refs_1_), channel_id=1, source_target_pairs={{0,8},{8,0},{16,24},{24,16},{1,9},{9,1},{17,25},{25,17},{2,10},{10... | collective-permute-start | bytes 196616 | tf_op jit(solution)/shard_map/ppermute | solution.py:354
  2.1 5.3 %collective-permute-start.1 = (bf16[256,128]{1,0:T(8,128)(2,1)S(1)}, bf16[256,128]{1,0:T(8,128)(2,1)S(1)}, u32[]{:S(2)}, u32[]{:S(2)}) collective-permute-start(bf16[256,128]{1,0:T(8,128)(2,1)S(1)} %get-tuple-element.17.refs_2_), channel_id=1, source_target_pairs={{0,16},{8,24},{16,0},{24,8},{1,17},{9,25},{17,1},{25,9},{2,18},{10... | collective-permute-start | bytes 196616 | tf_op jit(solution)/shard_map/ppermute | solution.py:354
  4.7 4.0 %collective-permute-start.2 = (bf16[256,128]{1,0:T(8,128)(2,1)S(1)}, bf16[256,128]{1,0:T(8,128)(2,1)S(1)}, u32[]{:S(2)}, u32[]{:S(2)}) collective-permute-start(bf16[256,128]{1,0:T(8,128)(2,1)S(1)} %get-tuple-element.18.refs_3_), channel_id=1, source_target_pairs={{0,24},{8,16},{16,8},{24,0},{1,25},{9,17},{17,9},{25,1},{2,26},{10... | collective-permute-start | bytes 196616 | tf_op jit(solution)/shard_map/ppermute | solution.py:354
  11.5 8.5 %collective-permute-start.3 = (bf16[1040,128]{1,0:T(8,128)(2,1)S(1)}, bf16[1040,128]{1,0:T(8,128)(2,1)S(1)}, u32[]{:S(2)}, u32[]{:S(2)}) collective-permute-start(bf16[1040,128]{1,0:T(8,128)(2,1)S(1)} %shard_map.65.query_ref), channel_id=1, source_target_pairs={{0,2},{2,4},{4,6},{6,7},{7,5},{5,3},{3,1},{1,0},{8,10},{10,12},{12... | collective-permute-start | bytes 798728 | tf_op jit(solution)/shard_map/ppermute | solution.py:369
  13.1 8.5 %collective-permute-start.8 = (bf16[1040,128]{1,0:T(8,128)(2,1)S(1)}, bf16[1040,128]{1,0:T(8,128)(2,1)S(1)}, u32[]{:S(2)}, u32[]{:S(2)}) collective-permute-start(bf16[1040,128]{1,0:T(8,128)(2,1)S(1)} %shard_map.65.query_ref), channel_id=1, source_target_pairs={{2,0},{4,2},{6,4},{7,6},{5,7},{3,5},{1,3},{0,1},{10,8},{12,10},{14... | collective-permute-start | bytes 798728 | tf_op jit(solution)/shard_map/ppermute | solution.py:370
  20.0 7.6 %collective-permute-start.4 = (bf16[1040,128]{1,0:T(8,128)(2,1)S(1)}, bf16[1040,128]{1,0:T(8,128)(2,1)S(1)}, u32[]{:S(2)}, u32[]{:S(2)}) collective-permute-start(bf16[1040,128]{1,0:T(8,128)(2,1)S(1)} %collective-permute-done.3.query_ref), channel_id=1, source_target_pairs={{0,2},{2,4},{4,6},{6,7},{7,5},{5,3},{3,1},{1,0},{8,10},{10,12},{12... | collective-permute-start | bytes 798728 | tf_op jit(solution)/shard_map/ppermute | solution.py:369
  21.6 7.6 %collective-permute-start.9 = (bf16[1040,128]{1,0:T(8,128)(2,1)S(1)}, bf16[1040,128]{1,0:T(8,128)(2,1)S(1)}, u32[]{:S(2)}, u32[]{:S(2)}) collective-permute-start(bf16[1040,128]{1,0:T(8,128)(2,1)S(1)} %collective-permute-done.8.query_ref), channel_id=1, source_target_pairs={{2,0},{4,2},{6,4},{7,6},{5,7},{3,5},{1,3},{0,1},{10,8},{12,10},{14... | collective-permute-start | bytes 798728 | tf_op jit(solution)/shard_map/ppermute | solution.py:370
  27.6 6.7 %collective-permute-start.5 = (bf16[1040,128]{1,0:T(8,128)(2,1)S(1)}, bf16[1040,128]{1,0:T(8,128)(2,1)S(1)}, u32[]{:S(2)}, u32[]{:S(2)}) collective-permute-start(bf16[1040,128]{1,0:T(8,128)(2,1)S(1)} %collective-permute-done.4.query_ref), channel_id=1, source_target_pairs={{0,2},{2,4},{4,6},{6,7},{7,5},{5,3},{3,1},{1,0},{8,10},{10,12},{12... | collective-permute-start | bytes 798728 | tf_op jit(solution)/shard_map/ppermute | solution.py:369
  29.2 6.8 %collective-permute-start.10 = (bf16[1040,128]{1,0:T(8,128)(2,1)S(1)}, bf16[1040,128]{1,0:T(8,128)(2,1)S(1)}, u32[]{:S(2)}, u32[]{:S(2)}) collective-permute-start(bf16[1040,128]{1,0:T(8,128)(2,1)S(1)} %collective-permute-done.9.query_ref), channel_id=1, source_target_pairs={{2,0},{4,2},{6,4},{7,6},{5,7},{3,5},{1,3},{0,1},{10,8},{12,10},{14... | collective-permute-start | bytes 798728 | tf_op jit(solution)/shard_map/ppermute | solution.py:370
  34.4 5.1 %collective-permute-start.6 = (bf16[528,128]{1,0:T(8,128)(2,1)S(1)}, bf16[528,128]{1,0:T(8,128)(2,1)S(1)}, u32[]{:S(2)}, u32[]{:S(2)}) collective-permute-start(bf16[528,128]{1,0:T(8,128)(2,1)S(1)} %slice.8), channel_id=1, source_target_pairs={{0,2},{2,4},{4,6},{6,7},{7,5},{5,3},{3,1},{1,0},{8,10},{10,12},{12... | collective-permute-start | bytes 405512 | tf_op jit(solution)/shard_map/ppermute | solution.py:369
  36.0 9.2 %collective-permute-start.14 = (bf16[528,128]{1,0:T(8,128)(2,1)S(1)}, bf16[528,128]{1,0:T(8,128)(2,1)S(1)}, u32[]{:S(2)}, u32[]{:S(2)}) collective-permute-start(bf16[528,128]{1,0:T(8,128)(2,1)S(1)} %slice.9), channel_id=1, source_target_pairs={{2,0},{4,2},{6,4},{7,6},{5,7},{3,5},{1,3},{0,1},{10,8},{12,10},{14... | collective-permute-start | bytes 405512 | tf_op jit(solution)/shard_map/ppermute | solution.py:370
  39.4 3.4 %copy-start = (bf16[16,128,2048]{2,1,0:T(8,128)(2,1)S(1)}, bf16[16,128,2048]{2,1,0:T(8,128)(2,1)}, u32[]{:S(2)}) copy-start(bf16[16,128,2048]{2,1,0:T(8,128)(2,1)} %cache_ref.17) | copy-start | bytes 25165828
  43.7 8.5 %collective-permute-start.7 = (bf16[528,128]{1,0:T(8,128)(2,1)S(1)}, bf16[528,128]{1,0:T(8,128)(2,1)S(1)}, u32[]{:S(2)}, u32[]{:S(2)}) collective-permute-start(bf16[528,128]{1,0:T(8,128)(2,1)S(1)} %shard_map.66), channel_id=1, source_target_pairs={{0,2},{2,4},{4,6},{6,7},{7,5},{5,3},{3,1},{1,0},{8,10},{10,12},{12... | collective-permute-start | bytes 405512 | tf_op jit(solution)/shard_map/ppermute | solution.py:376
  47.0 6.1 %collective-permute-start.15 = (bf16[528,128]{1,0:T(8,128)(2,1)S(1)}, bf16[528,128]{1,0:T(8,128)(2,1)S(1)}, u32[]{:S(2)}, u32[]{:S(2)}) collective-permute-start(bf16[528,128]{1,0:T(8,128)(2,1)S(1)} %shard_map.73), channel_id=1, source_target_pairs={{2,0},{4,2},{6,4},{7,6},{5,7},{3,5},{1,3},{0,1},{10,8},{12,10},{14... | collective-permute-start | bytes 405512 | tf_op jit(solution)/shard_map/ppermute | solution.py:377
  52.5 8.3 %collective-permute-start.11 = (bf16[1056,128]{1,0:T(8,128)(2,1)S(1)}, bf16[1056,128]{1,0:T(8,128)(2,1)S(1)}, u32[]{:S(2)}, u32[]{:S(2)}) collective-permute-start(bf16[1056,128]{1,0:T(8,128)(2,1)S(1)} %shard_map.68), channel_id=1, source_target_pairs={{0,2},{2,4},{4,6},{6,7},{7,5},{5,3},{3,1},{1,0},{8,10},{10,12},{12... | collective-permute-start | bytes 811016 | tf_op jit(solution)/shard_map/ppermute | solution.py:376
  53.5 8.2 %collective-permute-start.16 = (bf16[1056,128]{1,0:T(8,128)(2,1)S(1)}, bf16[1056,128]{1,0:T(8,128)(2,1)S(1)}, u32[]{:S(2)}, u32[]{:S(2)}) collective-permute-start(bf16[1056,128]{1,0:T(8,128)(2,1)S(1)} %shard_map.75), channel_id=1, source_target_pairs={{2,0},{4,2},{6,4},{7,6},{5,7},{3,5},{1,3},{0,1},{10,8},{12,10},{14... | collective-permute-start | bytes 811016 | tf_op jit(solution)/shard_map/ppermute | solution.py:377
  61.4 9.3 %collective-permute-start.12 = (bf16[1056,128]{1,0:T(8,128)(2,1)S(1)}, bf16[1056,128]{1,0:T(8,128)(2,1)S(1)}, u32[]{:S(2)}, u32[]{:S(2)}) collective-permute-start(bf16[1056,128]{1,0:T(8,128)(2,1)S(1)} %shard_map.70), channel_id=1, source_target_pairs={{0,2},{2,4},{4,6},{6,7},{7,5},{5,3},{3,1},{1,0},{8,10},{10,12},{12... | collective-permute-start | bytes 811016 | tf_op jit(solution)/shard_map/ppermute | solution.py:376
  62.4 9.4 %collective-permute-start.17 = (bf16[1056,128]{1,0:T(8,128)(2,1)S(1)}, bf16[1056,128]{1,0:T(8,128)(2,1)S(1)}, u32[]{:S(2)}, u32[]{:S(2)}) collective-permute-start(bf16[1056,128]{1,0:T(8,128)(2,1)S(1)} %shard_map.77), channel_id=1, source_target_pairs={{2,0},{4,2},{6,4},{7,6},{5,7},{3,5},{1,3},{0,1},{10,8},{12,10},{14... | collective-permute-start | bytes 811016 | tf_op jit(solution)/shard_map/ppermute | solution.py:377
  66.3 15.7 %copy-start.3 = (bf16[4,4,2048]{2,1,0:T(4,128)(2,1)S(1)}, bf16[4,4,2048]{2,1,0:T(4,128)(2,1)}, u32[]{:S(2)}) copy-start(bf16[4,4,2048]{2,1,0:T(4,128)(2,1)} %refs_4_.1) | copy-start | bytes 196612
  71.4 6.5 %collective-permute-start.13 = (bf16[1056,128]{1,0:T(8,128)(2,1)S(1)}, bf16[1056,128]{1,0:T(8,128)(2,1)S(1)}, u32[]{:S(2)}, u32[]{:S(2)}) collective-permute-start(bf16[1056,128]{1,0:T(8,128)(2,1)S(1)} %shard_map.72), channel_id=1, source_target_pairs={{0,2},{2,4},{4,6},{6,7},{7,5},{5,3},{3,1},{1,0},{8,10},{10,12},{12... | collective-permute-start | bytes 811016 | tf_op jit(solution)/shard_map/ppermute | solution.py:376
  72.4 6.7 %collective-permute-start.18 = (bf16[1056,128]{1,0:T(8,128)(2,1)S(1)}, bf16[1056,128]{1,0:T(8,128)(2,1)S(1)}, u32[]{:S(2)}, u32[]{:S(2)}) collective-permute-start(bf16[1056,128]{1,0:T(8,128)(2,1)S(1)} %shard_map.79), channel_id=1, source_target_pairs={{2,0},{4,2},{6,4},{7,6},{5,7},{3,5},{1,3},{0,1},{10,8},{12,10},{14... | collective-permute-start | bytes 811016 | tf_op jit(solution)/shard_map/ppermute | solution.py:377
  80.0 3.6 %collective-permute-start.19 = (bf16[272,128]{1,0:T(8,128)(2,1)S(1)}, bf16[272,128]{1,0:T(8,128)(2,1)S(1)}, u32[]{:S(2)}, u32[]{:S(2)}) collective-permute-start(bf16[272,128]{1,0:T(8,128)(2,1)S(1)} %get-tuple-element.20), channel_id=1, source_target_pairs={{0,8},{8,0},{16,24},{24,16},{1,9},{9,1},{17,25},{25,17},{2,10},{10... | collective-permute-start | bytes 208904 | tf_op jit(solution)/shard_map/ppermute | solution.py:354
  80.1 5.0 %collective-permute-start.20 = (bf16[272,128]{1,0:T(8,128)(2,1)S(1)}, bf16[272,128]{1,0:T(8,128)(2,1)S(1)}, u32[]{:S(2)}, u32[]{:S(2)}) collective-permute-start(bf16[272,128]{1,0:T(8,128)(2,1)S(1)} %get-tuple-element.21), channel_id=1, source_target_pairs={{0,16},{8,24},{16,0},{24,8},{1,17},{9,25},{17,1},{25,9},{2,18},{10... | collective-permute-start | bytes 208904 | tf_op jit(solution)/shard_map/ppermute | solution.py:354
  81.1 4.6 %collective-permute-start.21 = (bf16[272,128]{1,0:T(8,128)(2,1)S(1)}, bf16[272,128]{1,0:T(8,128)(2,1)S(1)}, u32[]{:S(2)}, u32[]{:S(2)}) collective-permute-start(bf16[272,128]{1,0:T(8,128)(2,1)S(1)} %get-tuple-element.22), channel_id=1, source_target_pairs={{0,24},{8,16},{16,8},{24,0},{1,25},{9,17},{17,9},{25,1},{2,26},{10... | collective-permute-start | bytes 208904 | tf_op jit(solution)/shard_map/ppermute | solution.py:354
  (5 other events, 6.4 us)

commit v3 on v2

--- a/solution.py
+++ b/solution.py
@@ -142,39 +142,58 @@
     )(place, *queries, new_kv)
 
 
-def payload_kernel(place_ref, owner_ref, index_ref, length_ref, *refs):
-    visits, out = refs[:-1], refs[-1]
-    cut = len(visits) // 2
-    lists = list_rows(len(visits))
+def list_kernel(place_ref, owner_ref, index_ref, length_ref, out):
+    requests = owner_ref.shape[0]
+    lists = list_rows(requests)
     rows = lax.broadcasted_iota(jnp.int32, (lists, LANES), 0)
     lanes = lane_ids(lists)
     tile = jnp.zeros((lists, LANES), F32)
-    for d, visit in enumerate(visits):
-        start = d * BODY + (lists if d >= cut else 0)
-        out[start : start + BODY, :] = visit[...]
+    for d in range(requests):
         row = place_ref[0] ^ d
         for s in range(SEL):
             count = jnp.clip(length_ref[row] - s * PAGE, 0, PAGE).astype(F32)
             mine = lanes == owner_ref[row, s]
             tile = jnp.where(mine & (rows == 2 * d), count, tile)
             tile = jnp.where(mine & (rows == 2 * d + 1), index_ref[row, s].astype(F32), tile)
-    out[cut * BODY : cut * BODY + lists, :] = tile.astype(BF16)
-
-
-def payload(place, page_owner, page_index, lengths, visits):
-    groups = len(visits)
-    rows = groups * BODY + list_rows(groups)
-    return pl.pallas_call(
-        payload_kernel,
+    out[...] = tile.astype(BF16)
+
+
+def page_lists(place, page_owner, page_index, lengths):
+    lists = list_rows(page_owner.shape[0])
+    return pl.pallas_call(
+        list_kernel,
+        out_shape=jax.ShapeDtypeStruct((lists, LANES), BF16),
+        in_specs=[IN_SMEM] * 4,
+        out_specs=IN_VMEM,
+        compiler_params=params(),
+        cost_estimate=cost(0, 4 * lists * HD),
+    )(place, page_owner, page_index, lengths)
+
+
+def payload_kernel(after, *refs):
+    lists_ref, visits, out = refs[0], refs[1 : len(refs) - 1 - after], refs[-1]
+    cut = len(visits) // 2
+    lists = lists_ref.shape[0]
+    for d, visit in enumerate(visits):
+        start = d * BODY + (lists if d >= cut else 0)
+        out[start : start + BODY, :] = visit[...]
+    out[cut * BODY : cut * BODY + lists, :] = lists_ref[...]
+
+
+def payload(lists, visits, after):
+    rows = len(visits) * BODY + lists.shape[0]
+    return pl.pallas_call(
+        functools.partial(payload_kernel, len(after)),
         out_shape=jax.ShapeDtypeStruct((rows, HD), BF16),
-        in_specs=[IN_SMEM] * 4 + [IN_VMEM] * groups,
+        in_specs=[IN_VMEM] * (1 + len(visits) + len(after)),
         out_specs=IN_VMEM,
         compiler_params=params(),
         cost_estimate=cost(0, 4 * rows * HD),
-    )(place, page_owner, page_index, lengths, *visits)
-
-
-def item_kernel(slots, list_start, first, gap_at, lists, place_ref, query_ref, cache_ref, out_ref, level_ref, code_ref):
+    )(lists, *visits, *after)
+
+
+def item_kernel(slots, list_start, first, gap_at, lists, outs, place_ref, query_ref, cache_ref, *refs):
+    out_refs, (level_ref, code_ref) = refs[-2 - outs : -2], refs[-2:]
     owner = place_ref[1]
     table = query_ref[list_start : list_start + lists, :].astype(F32)
     rows = lax.broadcasted_iota(jnp.int32, (lists, LANES), 0)
@@ -183,13 +202,13 @@
         code = jnp.where(rows == 2 * slot, table, jnp.where(rows == 2 * slot + 1, table * 256.0, 0.0))
         code_ref[entry] = jnp.sum(code).astype(jnp.int32)
     tokens = lax.broadcasted_iota(jnp.int32, (ROWS, PAGE), 1)
-
-    @pl.loop(0, len(slots))
-    def _(entry):
+    each = len(slots) // outs
+
+    def one(entry, out_ref, inner):
         code = code_ref[entry]
         count, page = code & 255, code >> 8
         start = first + entry * BODY + jnp.where(entry >= gap_at, lists, 0)
-        out = (entry // 2) * PAIR + (entry % 2) * BODY
+        out = (inner // 2) * PAIR + (inner % 2) * BODY
 
         @pl.when(count > 0)
         def _():
@@ -207,13 +226,20 @@
             level_ref[entry] = jnp.full((HALF, LANES), EMPTY, F32)
 
     lanes = lane_ids()
-    for pair in range(len(slots) // 2):
-        level = jnp.where(lanes < COLS, level_ref[2 * pair], pltpu.roll(level_ref[2 * pair + 1], SECOND, 1))
-        start = pair * PAIR + 2 * BODY
-        out_ref[start : start + HALF, :] = pack_stats(level)
-
-
-def items(place, queries, kv_cache, requests, slots):
+    for number, out_ref in enumerate(out_refs):
+
+        @pl.loop(0, each)
+        def _(inner):
+            one(number * each + inner, out_ref, inner)
+
+        for pair in range(each // 2):
+            entry = number * each + 2 * pair
+            level = jnp.where(lanes < COLS, level_ref[entry], pltpu.roll(level_ref[entry + 1], SECOND, 1))
+            start = pair * PAIR + 2 * BODY
+            out_ref[start : start + HALF, :] = pack_stats(level)
+
+
+def items(place, queries, pages, requests, slots, after=()):
     lists = list_rows(requests)
     cut = requests // 2
     if len(slots) == requests:
@@ -223,16 +249,16 @@
     else:
         list_start, first, gap_at = 0, lists, requests
     count = len(slots)
-    out_rows = count // 2 * PAIR
-    return pl.pallas_call(
-        functools.partial(item_kernel, slots, list_start, first, gap_at, lists),
-        out_shape=jax.ShapeDtypeStruct((out_rows, HD), BF16),
-        in_specs=[IN_SMEM, IN_VMEM, IN_VMEM],
-        out_specs=IN_VMEM,
+    outs = count // cut
+    return pl.pallas_call(
+        functools.partial(item_kernel, slots, list_start, first, gap_at, lists, outs),
+        out_shape=[jax.ShapeDtypeStruct((cut // 2 * PAIR, HD), BF16)] * outs,
+        in_specs=[IN_SMEM] + [IN_VMEM] * (2 + len(after)),
+        out_specs=[IN_VMEM] * outs,
         scratch_shapes=[pltpu.VMEM((count, HALF, LANES), F32), pltpu.SMEM((count,), jnp.int32)],
         compiler_params=params(),
-        cost_estimate=cost(count * KVH * 4 * ROWS * HD * PAGE, count * PAGE * kv_cache.shape[2] * 2),
-    )(place, queries, kv_cache)
+        cost_estimate=cost(count * KVH * 4 * ROWS * HD * PAGE, count * PAGE * pages.shape[2] * 2),
+    )(place, queries, pages, *after)
 
 
 def blend(levels):
@@ -246,24 +272,19 @@
     values = []
     for index in range(COLS):
         row, lane = start + tile_start(index), first_lane + index
-        parts = [share[:, lane : lane + 1] * ref[row : row + HALF, :].astype(F32) for share, ref in zip(shares, refs)]
-        values.append(functools.reduce(jnp.add, parts))
+        tiles = [ref[row : row + HALF, :].astype(F32) for ref in refs]
+        total = tiles[0]
+        for share, tile in zip(shares[1:], tiles[1:]):
+            total = total + share[:, lane : lane + 1] * (tile - tiles[0])
+        values.append(total)
     return values
 
 
-def merge_kernel(base, arrived_ref, own_ref, out_ref):
-    pairs = out_ref.shape[0] // PAIR
-    arrived_pairs = arrived_ref.shape[0] // PAIR
-    for pair in range(pairs):
-        start = pair * PAIR
-        if not base <= pair < base + arrived_pairs:
-            out_ref[start : start + PAIR, :] = own_ref[start : start + PAIR, :]
-            continue
-        arrived = arrived_ref.at[(pair - base) * PAIR : (pair - base + 1) * PAIR]
-        own = own_ref.at[start : start + PAIR]
-        out = out_ref.at[start : start + PAIR]
-        levels = [unpack_stats(ref[2 * BODY : PAIR, :]) for ref in (arrived, own)]
-        shares, level = blend(levels)
+def merge_kernel(arrived_ref, own_ref, out_ref):
+    for pair in range(out_ref.shape[0] // PAIR):
+        part = slice(pair * PAIR, (pair + 1) * PAIR)
+        arrived, own, out = arrived_ref.at[part], own_ref.at[part], out_ref.at[part]
+        shares, level = blend([unpack_stats(ref[2 * BODY : PAIR, :]) for ref in (arrived, own)])
         values = [mix(shares, (arrived, own), second * BODY, second * SECOND) for second in range(2)]
         for second in range(2):
             for index in range(COLS):
@@ -272,9 +293,9 @@
         out[2 * BODY : PAIR, :] = pack_stats(level)
 
 
-def merge(arrived, own, base):
-    return pl.pallas_call(
-        functools.partial(merge_kernel, base),
+def merge(arrived, own):
+    return pl.pallas_call(
+        merge_kernel,
         out_shape=jax.ShapeDtypeStruct(own.shape, BF16),
         in_specs=[IN_VMEM, IN_VMEM],
         out_specs=IN_VMEM,
@@ -283,25 +304,25 @@
     )(arrived, own)
 
 
-def gather_kernel(ahead_base, behind_base, ahead_ref, behind_ref, own_ref, *outs):
+def gather_kernel(ahead_ref, behind_ref, own_ref, *outs):
     for pair in range(len(outs) // 2):
-        sources = [own_ref.at[pair * PAIR : (pair + 1) * PAIR]]
-        for ref, base in ((ahead_ref, ahead_base), (behind_ref, behind_base)):
-            if base <= pair < base + ref.shape[0] // PAIR:
-                sources.append(ref.at[(pair - base) * PAIR : (pair - base + 1) * PAIR])
+        part = slice(pair * PAIR, (pair + 1) * PAIR)
+        sources = [ref.at[part] for ref in (own_ref, ahead_ref, behind_ref)]
         shares, level = blend([unpack_stats(ref[2 * BODY : PAIR, :]) for ref in sources])
+        values = [mix(shares, sources, second * BODY, second * SECOND) for second in range(2)]
         for second in range(2):
             out = outs[2 * pair + second]
-            for index, values in enumerate(mix(shares, sources, second * BODY, second * SECOND)):
+            for index in range(COLS):
                 row = tile_start(index)
-                out[row : row + HALF, :] = values.astype(BF16)
+                out[row : row + HALF, :] = values[second][index].astype(BF16)
             here = pltpu.roll(level, LANES - SECOND, 1) if second else level
             out[BODY:LONE, :] = pack_stats(here)
 
 
-def gather(ahead, behind, own, requests, ahead_base, behind_base):
-    return pl.pallas_call(
-        functools.partial(gather_kernel, ahead_base, behind_base),
+def gather(ahead, behind, own):
+    requests = own.shape[0] // PAIR * 2
+    return pl.pallas_call(
+        gather_kernel,
         out_shape=[jax.ShapeDtypeStruct((LONE, HD), BF16)] * requests,
         in_specs=[IN_VMEM] * 3,
         out_specs=[IN_VMEM] * requests,
@@ -311,16 +332,17 @@
 
 
 def final_kernel(place_ref, *refs):
-    parts, (new_ref, level_ref, out_ref) = refs[:-3], refs[-3:]
+    parts, (new_ref, level_ref, out_ref, rows_ref) = refs[:-4], refs[-4:]
     for d, part in enumerate(parts):
+        shares, _ = blend([unpack_stats(part[BODY:LONE, :]), level_ref[d]])
+        for index, tile in enumerate(mix(shares, (part, new_ref.at[d]), 0, 0)):
+            row = tile_start(index)
+            rows_ref[d, row : row + HALF, :] = tile
+    for d in range(len(parts)):
         row = place_ref[0] ^ d
-        shares, _ = blend([unpack_stats(part[BODY:LONE, :]), level_ref[d]])
-        values = mix(shares, (part, new_ref.at[d]), 0, 0)
-        for index, tile in enumerate(values):
-            first = tile_start(index) // STEPS
-            for g in range(HALF // STEPS):
-                head = first + g
-                out_ref[row, :, head * HD : (head + 1) * HD] = tile[g * STEPS : (g + 1) * STEPS, :].astype(BF16)
+        for head in range(KVH * GQ):
+            tile = rows_ref[d, head * STEPS : (head + 1) * STEPS, :]
+            out_ref[row, :, head * HD : (head + 1) * HD] = tile.astype(BF16)
 
 
 def final(place, parts, new_out, new_level):
@@ -330,6 +352,7 @@
         out_shape=jax.ShapeDtypeStruct((groups, STEPS, KVH * GQ * HD), BF16),
         in_specs=[IN_SMEM] + [IN_VMEM] * (groups + 2),
         out_specs=IN_VMEM,
+        scratch_shapes=[pltpu.VMEM((groups, BODY, HD), F32)],
         compiler_params=params(),
         cost_estimate=cost(0, groups * BODY * HD * 8),
     )(place, *parts, new_out, new_level)
@@ -354,33 +377,51 @@
         return lax.ppermute(array, "grp", [(g, g ^ d) for g in range(groups)]) if d else array
 
     rows = relayout(place, queries)
-    visits = [swap(rows[d], d) for d in range(groups)]
+    visits = [rows[0]] + [None] * (groups - 1)
+    for d in range(groups - 1, 0, -1):
+        visits[d] = swap(rows[d], d)
     new_out, new_level = new_tokens(place, rows, new_kv)
-    block = payload(place, page_owner, page_index[:, :, 0], lengths, visits)
+    lists = page_lists(place, page_owner, page_index[:, :, 0], lengths)
+    block = payload(lists, visits, (new_level,))
 
     slots = list(range(requests))
     cut = requests // 2
-    lists = list_rows(requests)
-    ahead = behind = block
+    middle = cut * BODY
+    below = above = block
     parts = {0: items(place, block, kv_cache, requests, slots)}
     for step in range(1, reach + 1):
         if step == reach:
-            ahead, behind = ahead[: cut * BODY + lists], behind[cut * BODY :]
-        ahead = lax.ppermute(ahead, "cache", forward)
-        behind = lax.ppermute(behind, "cache", backward)
-        parts[-step] = items(place, ahead, kv_cache, requests, slots if step < reach else slots[:cut])
-        parts[step] = items(place, behind, kv_cache, requests, slots if step < reach else slots[cut:])
-
-    ahead, behind = parts[-reach], parts[reach]
-    for step in range(reach - 1, -1, -1):
-        ahead = lax.ppermute(ahead, "cache", forward)
-        behind = lax.ppermute(behind, "cache", backward)
-        base = cut // 2 if step == reach - 1 else 0
-        if step > 0:
-            ahead, behind = merge(ahead, parts[step], 0), merge(behind, parts[-step], base)
-        else:
-            returned = gather(ahead, behind, parts[0], requests, 0, base)
-    home = [swap(returned[d], d) for d in range(groups)]
+            below, above = below[: middle + lists.shape[0]], above[middle:]
+        below = lax.ppermute(below, "cache", forward)
+        above = lax.ppermute(above, "cache", backward)
+        if step < reach:
+            done = parts[0] if step == 1 else parts[1 - step] + parts[step - 1]
+            below, above = lax.optimization_barrier((below, done))[0], lax.optimization_barrier((above, done))[0]
+            parts[-step] = items(place, below, kv_cache, requests, slots)
+            parts[step] = items(place, above, kv_cache, requests, slots)
+    far_ahead = items(place, below, kv_cache, requests, slots[:cut])
+    far_behind = items(place, above, kv_cache, requests, slots[cut:])
+
+    arrived = []
+    for half in range(2):
+        for ring, sign in ((forward, 1), (backward, -1)):
+            if half == 0 and sign == 1:
+                chain, steps = far_ahead[0], range(reach - 1, -1, -1)
+            elif half == 1 and sign == -1:
+                chain, steps = far_behind[0], range(reach - 1, -1, -1)
+            else:
+                chain, steps = parts[sign * (reach - 1)][half], range(reach - 2, -1, -1)
+            for step in steps:
+                chain = lax.ppermute(chain, "cache", ring)
+                if step > 0:
+                    chain = merge(chain, parts[sign * step][half])
+            arrived.append(chain)
+    back = gather(arrived[2], arrived[3], parts[0][1])
+    front = gather(arrived[0], arrived[1], parts[0][0])
+    returned = list(front) + list(back)
+    home = [returned[0]] + [None] * (groups - 1)
+    for d in range(groups - 1, 0, -1):
+        home[d] = swap(returned[d], d)
     return final(place, home, new_out, new_level)
 
 

time: 88.4 us -> 75.3 us (0.85)
  waiting for transfers between devices: 34.4 us -> 13.5 us
  Pallas kernels: 20.9 us -> 27.9 us
  starting transfers between devices: 25.1 us -> 26.5 us
    ppermute x16 -> x22, waiting for transfers between devices: 28.2 us -> 11.7 us  [the longest x14 6.6 us: per_device(): chain = lax.ppermute(chain, 'cache', ring)]
    pallas_call x9, Pallas kernels: 11.6 us -> 19.7 us  [items(): pl.pallas_call(functools.partial(item_kernel, slots, list_start, first, g...]
    ppermute x6, waiting for transfers between devices: 6.11 us -> 1.72 us  [swap(): lax.ppermute(array, 'grp', [(g, g ^ d) for g in range(groups)])]
    ppermute x16 -> x22, starting transfers between devices: 20 us -> 21.8 us  [the longest x14 13.5 us: per_device(): chain = lax.ppermute(chain, 'cache', ring)]
    pallas_call x8 -> x14, Pallas kernels: 4.92 us -> 4.11 us  [the longest x10 2.66 us: merge(): pl.pallas_call(merge_kernel, out_shape=jax.ShapeDtypeStruct(own.shape, BF...]
  transfers between devices with their start and end apart: 22 -> 28, of which waited for: 15 -> 12; matrix products, arithmetic and copies ran while one was open for 0% -> 0% of each run, Pallas kernels for 19% -> 34%
where the time goes in v3:
time: 75.3 us
  Pallas kernels  27.9 us (37%)
  starting transfers between devices  26.5 us (35%)
  waiting for transfers between devices  13.5 us (18%)
  local copies, waits for them, and re-layouts  7.21 us (10%)
    pallas_call x9, Pallas kernels, items(): pl.pallas_call(functools.partial(item_kernel, slots, list_start, first, g...  19.7 us
    ppermute x14, starting transfers between devices, per_device(): chain = lax.ppermute(chain, 'cache', ring)  13.5 us
    unnamed x14, local copies, waits for them, and re-layouts  7.19 us
    ppermute x4, starting transfers between devices, per_device(): above = lax.ppermute(above, 'cache', backward)  6.63 us
    ppermute x14, waiting for transfers between devices, per_device(): chain = lax.ppermute(chain, 'cache', ring)  6.6 us
    ppermute x4, waiting for transfers between devices, per_device(): above = lax.ppermute(above, 'cache', backward)  5.13 us
    ppermute x6, starting transfers between devices, swap(): lax.ppermute(array, 'grp', [(g, g ^ d) for g in range(groups)])  4.72 us
    pallas_call x10, Pallas kernels, merge(): pl.pallas_call(merge_kernel, out_shape=jax.ShapeDtypeStruct(own.shape, BF...  2.66 us
  transfers between devices with their start and end apart: 28, of which 12 were waited for; matrix products, arithmetic and copies ran while one was open for 0% of the time, Pallas kernels for 34%

profile of v3, /device:TPU:0, one launch (start us, length us, event | category | flops | bytes accessed | tf_op | source)
XLA Modules:
  0.0 75.3 jit_solution(1071753333309648168)
XLA Ops:
  2.1 2.6 %collective-permute-start.1 = (bf16[256,128]{1,0:T(8,128)(2,1)S(1)}, bf16[256,128]{1,0:T(8,128)(2,1)S(1)}, u32[]{:S(2)}, u32[]{:S(2)}) collective-permute-start(bf16[256,128]{1,0:T(8,128)(2,1)S(1)} %get-tuple-element.37.refs_2_), channel_id=1, source_target_pairs={{0,16},{8,24},{16,0},{24,8},{1,17},{9,25},{17,1},{25,9},{2,18},{10... | collective-permute-start | bytes 196616 | tf_op jit(solution)/shard_map/ppermute | solution.py:377
  8.3 1.6 %shard_map.66 = (f32[4,256,128]{2,1,0:T(8,128)S(1)}, f32[4,16,128]{2,1,0:T(8,128)S(1)}) custom-call(s32[2]{0:T(128)S(1)} %pad_add_fusion.place_ref, bf16[256,128]{1,0:T(8,128)(2,1)S(1)} %get-tuple-element.35.refs_0_.refs_1_, bf16[256,128]{1,0:T(8,128)(2,1)S(1)} %get-tuple-element.36.refs_1_, bf16[256,128]{1,0:T(8,128)(2,1)S(1)} %get-tuple-element.37.refs_2_, ...), custom_call_target="tpu_custom_call" | custom-call | flops 67108864 | bytes 786432 | tf_op jit(solution)/shard_map/pallas_call | solution.py:132
  10.0 1.8 %collective-permute-start.5 = (bf16[1040,128]{1,0:T(8,128)(2,1)S(1)}, bf16[1040,128]{1,0:T(8,128)(2,1)S(1)}, u32[]{:S(2)}, u32[]{:S(2)}) collective-permute-start(bf16[1040,128]{1,0:T(8,128)(2,1)S(1)} %shard_map.67.query_ref), channel_id=1, source_target_pairs={{2,0},{4,2},{6,4},{7,6},{5,7},{3,5},{1,3},{0,1},{10,8},{12,10},{14... | collective-permute-start | bytes 798728 | tf_op jit(solution)/shard_map/ppermute | solution.py:396
  12.1 3.4 %copy-done = bf16[16,128,2048]{2,1,0:T(8,128)(2,1)S(1)} copy-done((bf16[16,128,2048]{2,1,0:T(8,128)(2,1)S(1)}, bf16[16,128,2048]{2,1,0:T(8,128)(2,1)}, u32[]{:S(2)}) %copy-start) | copy-done | bytes 8388632
  15.5 2.8 %shard_map.68 = (bf16[528,128]{1,0:T(8,128)(2,1)S(1)}, bf16[528,128]{1,0:T(8,128)(2,1)S(1)}) custom-call(s32[2]{0:T(128)S(1)} %pad_add_fusion.place_ref, bf16[1040,128]{1,0:T(8,128)(2,1)S(1)} %shard_map.67.query_ref, bf16[16,128,2048]{2,1,0:T(8,128)(2,1)S(1)} %copy-done), custom_call_target="tpu_custom_call" | custom-call | flops 67108864 | bytes 2097152 | tf_op jit(solution)/shard_map/pallas_call | solution.py:253
  18.8 1.7 %collective-permute-start.7 = (bf16[1040,128]{1,0:T(8,128)(2,1)S(1)}, bf16[1040,128]{1,0:T(8,128)(2,1)S(1)}, u32[]{:S(2)}, u32[]{:S(2)}) collective-permute-start(bf16[1040,128]{1,0:T(8,128)(2,1)S(1)} %collective-permute-done.5.query_ref), channel_id=1, source_target_pairs={{2,0},{4,2},{6,4},{7,6},{5,7},{3,5},{1,3},{0,1},{10,8},{12,10},{14... | collective-permute-start | bytes 798728 | tf_op jit(solution)/shard_map/ppermute | solution.py:396
  20.8 2.4 %shard_map.70 = (bf16[528,128]{1,0:T(8,128)(2,1)S(1)}, bf16[528,128]{1,0:T(8,128)(2,1)S(1)}) custom-call(s32[2]{0:T(128)S(1)} %pad_add_fusion.place_ref, bf16[1040,128]{1,0:T(8,128)(2,1)S(1)} %collective-permute-done.5.query_ref, bf16[16,128,2048]{2,1,0:T(8,128)(2,1)S(1)} %copy-done.1), custom_call_target="tpu_custom_call" | custom-call | flops 67108864 | bytes 2097152 | tf_op jit(solution)/shard_map/pallas_call | solution.py:253
  23.2 2.4 %shard_map.69 = (bf16[528,128]{1,0:T(8,128)(2,1)S(1)}, bf16[528,128]{1,0:T(8,128)(2,1)S(1)}) custom-call(s32[2]{0:T(128)S(1)} %pad_add_fusion.place_ref, bf16[1040,128]{1,0:T(8,128)(2,1)S(1)} %collective-permute-done.3.query_ref, bf16[16,128,2048]{2,1,0:T(8,128)(2,1)S(1)} %copy-done.1), custom_call_target="tpu_custom_call" | custom-call | flops 67108864 | bytes 2097152 | tf_op jit(solution)/shard_map/pallas_call | solution.py:253
  26.6 1.6 %collective-permute-start.10 = (bf16[1040,128]{1,0:T(8,128)(2,1)S(1)}, bf16[1040,128]{1,0:T(8,128)(2,1)S(1)}, u32[]{:S(2)}, u32[]{:S(2)}) collective-permute-start(bf16[1040,128]{1,0:T(8,128)(2,1)S(1)} %collective-permute-done.7.query_ref), channel_id=1, source_target_pairs={{2,0},{4,2},{6,4},{7,6},{5,7},{3,5},{1,3},{0,1},{10,8},{12,10},{14... | collective-permute-start | bytes 798728 | tf_op jit(solution)/shard_map/ppermute | solution.py:396
  28.7 2.4 %shard_map.72 = (bf16[528,128]{1,0:T(8,128)(2,1)S(1)}, bf16[528,128]{1,0:T(8,128)(2,1)S(1)}) custom-call(s32[2]{0:T(128)S(1)} %pad_add_fusion.place_ref, bf16[1040,128]{1,0:T(8,128)(2,1)S(1)} %collective-permute-done.7.query_ref, bf16[16,128,2048]{2,1,0:T(8,128)(2,1)S(1)} %copy-done.1), custom_call_target="tpu_custom_call" | custom-call | flops 67108864 | bytes 2097152 | tf_op jit(solution)/shard_map/pallas_call | solution.py:253
  31.0 1.9 %shard_map.71 = (bf16[528,128]{1,0:T(8,128)(2,1)S(1)}, bf16[528,128]{1,0:T(8,128)(2,1)S(1)}) custom-call(s32[2]{0:T(128)S(1)} %pad_add_fusion.place_ref, bf16[1040,128]{1,0:T(8,128)(2,1)S(1)} %collective-permute-done.4.query_ref, bf16[16,128,2048]{2,1,0:T(8,128)(2,1)S(1)} %copy-done.1), custom_call_target="tpu_custom_call" | custom-call | flops 67108864 | bytes 2097152 | tf_op jit(solution)/shard_map/pallas_call | solution.py:253
  33.6 1.6 %collective-permute-start.21 = (bf16[528,128]{1,0:T(8,128)(2,1)S(1)}, bf16[528,128]{1,0:T(8,128)(2,1)S(1)}, u32[]{:S(2)}, u32[]{:S(2)}) collective-permute-start(bf16[528,128]{1,0:T(8,128)(2,1)S(1)} %slice.7), channel_id=1, source_target_pairs={{2,0},{4,2},{6,4},{7,6},{5,7},{3,5},{1,3},{0,1},{10,8},{12,10},{14... | collective-permute-start | bytes 405512 | tf_op jit(solution)/shard_map/ppermute | solution.py:396
  35.8 2.9 %collective-permute-done.21.query_ref = bf16[528,128]{1,0:T(8,128)(2,1)S(1)} collective-permute-done((bf16[528,128]{1,0:T(8,128)(2,1)S(1)}, bf16[528,128]{1,0:T(8,128)(2,1)S(1)}, u32[]{:S(2)}, u32[]{:S(2)}) %collective-permute-start.21) | collective-permute-done | bytes 135200 | tf_op jit(solution)/shard_map/ppermute | solution.py:396
  38.7 1.7 %shard_map.84 = bf16[528,128]{1,0:T(8,128)(2,1)S(1)} custom-call(s32[2]{0:T(128)S(1)} %pad_add_fusion.place_ref, bf16[528,128]{1,0:T(8,128)(2,1)S(1)} %collective-permute-done.21.query_ref, bf16[16,128,2048]{2,1,0:T(8,128)(2,1)S(1)} %copy-done.1), custom_call_target="tpu_custom_call" | custom-call | flops 33554432 | bytes 1048576 | tf_op jit(solution)/shard_map/pallas_call | solution.py:253
  41.1 1.7 %shard_map.73 = bf16[528,128]{1,0:T(8,128)(2,1)S(1)} custom-call(s32[2]{0:T(128)S(1)} %pad_add_fusion.place_ref, bf16[528,128]{1,0:T(8,128)(2,1)S(1)} %collective-permute-done.8.query_ref, bf16[16,128,2048]{2,1,0:T(8,128)(2,1)S(1)} %copy-done.1), custom_call_target="tpu_custom_call" | custom-call | flops 33554432 | bytes 1048576 | tf_op jit(solution)/shard_map/pallas_call | solution.py:253
  43.8 1.9 %shard_map.74 = (bf16[528,128]{1,0:T(8,128)(2,1)S(1)}, bf16[528,128]{1,0:T(8,128)(2,1)S(1)}) custom-call(s32[2]{0:T(128)S(1)} %pad_add_fusion.place_ref, bf16[1040,128]{1,0:T(8,128)(2,1)S(1)} %collective-permute-done.10.query_ref, bf16[16,128,2048]{2,1,0:T(8,128)(2,1)S(1)} %copy-done.1), custom_call_target="tpu_custom_call" | custom-call | flops 67108864 | bytes 2097152 | tf_op jit(solution)/shard_map/pallas_call | solution.py:253
  46.5 2.4 %shard_map.78 = (bf16[528,128]{1,0:T(8,128)(2,1)S(1)}, bf16[528,128]{1,0:T(8,128)(2,1)S(1)}) custom-call(s32[2]{0:T(128)S(1)} %pad_add_fusion.place_ref, bf16[1040,128]{1,0:T(8,128)(2,1)S(1)} %collective-permute-done.6.query_ref, bf16[16,128,2048]{2,1,0:T(8,128)(2,1)S(1)} %copy-done.1), custom_call_target="tpu_custom_call" | custom-call | flops 67108864 | bytes 2097152 | tf_op jit(solution)/shard_map/pallas_call | solution.py:253
  50.5 1.8 %collective-permute-start.11 = (bf16[528,128]{1,0:T(8,128)(2,1)S(1)}, bf16[528,128]{1,0:T(8,128)(2,1)S(1)}, u32[]{:S(2)}, u32[]{:S(2)}) collective-permute-start(bf16[528,128]{1,0:T(8,128)(2,1)S(1)} %shard_map.75), channel_id=1, source_target_pairs={{0,2},{2,4},{4,6},{6,7},{7,5},{5,3},{3,1},{1,0},{8,10},{10,12},{12... | collective-permute-start | bytes 405512 | tf_op jit(solution)/shard_map/ppermute | solution.py:415
  53.9 1.8 %collective-permute-done.23.arrived_ref = bf16[528,128]{1,0:T(8,128)(2,1)S(1)} collective-permute-done((bf16[528,128]{1,0:T(8,128)(2,1)S(1)}, bf16[528,128]{1,0:T(8,128)(2,1)S(1)}, u32[]{:S(2)}, u32[]{:S(2)}) %collective-permute-start.23) | collective-permute-done | bytes 135200 | tf_op jit(solution)/shard_map/ppermute | solution.py:415
  56.5 1.9 %collective-permute-done.14.arrived_ref = bf16[528,128]{1,0:T(8,128)(2,1)S(1)} collective-permute-done((bf16[528,128]{1,0:T(8,128)(2,1)S(1)}, bf16[528,128]{1,0:T(8,128)(2,1)S(1)}, u32[]{:S(2)}, u32[]{:S(2)}) %collective-permute-start.14) | collective-permute-done | bytes 135200 | tf_op jit(solution)/shard_map/ppermute | solution.py:415
  62.1 1.7 %collective-permute-start.25 = (bf16[528,128]{1,0:T(8,128)(2,1)S(1)}, bf16[528,128]{1,0:T(8,128)(2,1)S(1)}, u32[]{:S(2)}, u32[]{:S(2)}) collective-permute-start(bf16[528,128]{1,0:T(8,128)(2,1)S(1)} %shard_map.87), channel_id=1, source_target_pairs={{2,0},{4,2},{6,4},{7,6},{5,7},{3,5},{1,3},{0,1},{10,8},{12,10},{14... | collective-permute-start | bytes 405512 | tf_op jit(solution)/shard_map/ppermute | solution.py:415
  69.6 1.7 %collective-permute-done.13.ahead_ref = bf16[528,128]{1,0:T(8,128)(2,1)S(1)} collective-permute-done((bf16[528,128]{1,0:T(8,128)(2,1)S(1)}, bf16[528,128]{1,0:T(8,128)(2,1)S(1)}, u32[]{:S(2)}, u32[]{:S(2)}) %collective-permute-start.13) | collective-permute-done | bytes 135200 | tf_op jit(solution)/shard_map/ppermute | solution.py:415
  71.9 1.5 %collective-permute-done.27.refs_3_ = bf16[272,128]{1,0:T(8,128)(2,1)S(1)} collective-permute-done((bf16[272,128]{1,0:T(8,128)(2,1)S(1)}, bf16[272,128]{1,0:T(8,128)(2,1)S(1)}, u32[]{:S(2)}, u32[]{:S(2)}) %collective-permute-start.27) | collective-permute-done | bytes 69664 | tf_op jit(solution)/shard_map/ppermute | solution.py:377
  73.4 1.9 %shard_map.89 = bf16[4,4,8192]{2,1,0:T(4,128)(2,1)} custom-call(s32[2]{0:T(128)S(1)} %pad_add_fusion.place_ref, bf16[272,128]{1,0:T(8,128)(2,1)S(1)} %get-tuple-element.58.refs_0_, bf16[272,128]{1,0:T(8,128)(2,1)S(1)} %collective-permute-done.17.refs_1_, bf16[272,128]{1,0:T(8,128)(2,1)S(1)} %collective-permute-done.26.refs_2_, ...), custom_call_target="tpu_custom_call" | custom-call | bytes 1048576 | tf_op jit(solution)/shard_map/pallas_call | solution.py:350
  (75 shorter events, 26.1 us)
Async XLA Ops:
  1.6 8.3 %collective-permute-start = (bf16[256,128]{1,0:T(8,128)(2,1)S(1)}, bf16[256,128]{1,0:T(8,128)(2,1)S(1)}, u32[]{:S(2)}, u32[]{:S(2)}) collective-permute-start(bf16[256,128]{1,0:T(8,128)(2,1)S(1)} %get-tuple-element.36.refs_1_), channel_id=1, source_target_pairs={{0,8},{8,0},{16,24},{24,16},{1,9},{9,1},{17,25},{25,17},{2,10},{10... | collective-permute-start | bytes 196616 | tf_op jit(solution)/shard_map/ppermute | solution.py:377
  2.1 7.8 %collective-permute-start.1 = (bf16[256,128]{1,0:T(8,128)(2,1)S(1)}, bf16[256,128]{1,0:T(8,128)(2,1)S(1)}, u32[]{:S(2)}, u32[]{:S(2)}) collective-permute-start(bf16[256,128]{1,0:T(8,128)(2,1)S(1)} %get-tuple-element.37.refs_2_), channel_id=1, source_target_pairs={{0,16},{8,24},{16,0},{24,8},{1,17},{9,25},{17,1},{25,9},{2,18},{10... | collective-permute-start | bytes 196616 | tf_op jit(solution)/shard_map/ppermute | solution.py:377
  4.7 5.3 %collective-permute-start.2 = (bf16[256,128]{1,0:T(8,128)(2,1)S(1)}, bf16[256,128]{1,0:T(8,128)(2,1)S(1)}, u32[]{:S(2)}, u32[]{:S(2)}) collective-permute-start(bf16[256,128]{1,0:T(8,128)(2,1)S(1)} %get-tuple-element.38.refs_3_), channel_id=1, source_target_pairs={{0,24},{8,16},{16,8},{24,0},{1,25},{9,17},{17,9},{25,1},{2,26},{10... | collective-permute-start | bytes 196616 | tf_op jit(solution)/shard_map/ppermute | solution.py:377
  10.0 8.7 %collective-permute-start.5 = (bf16[1040,128]{1,0:T(8,128)(2,1)S(1)}, bf16[1040,128]{1,0:T(8,128)(2,1)S(1)}, u32[]{:S(2)}, u32[]{:S(2)}) collective-permute-start(bf16[1040,128]{1,0:T(8,128)(2,1)S(1)} %shard_map.67.query_ref), channel_id=1, source_target_pairs={{2,0},{4,2},{6,4},{7,6},{5,7},{3,5},{1,3},{0,1},{10,8},{12,10},{14... | collective-permute-start | bytes 798728 | tf_op jit(solution)/shard_map/ppermute | solution.py:396
  11.8 8.7 %collective-permute-start.3 = (bf16[1040,128]{1,0:T(8,128)(2,1)S(1)}, bf16[1040,128]{1,0:T(8,128)(2,1)S(1)}, u32[]{:S(2)}, u32[]{:S(2)}) collective-permute-start(bf16[1040,128]{1,0:T(8,128)(2,1)S(1)} %shard_map.67.query_ref), channel_id=1, source_target_pairs={{0,2},{2,4},{4,6},{6,7},{7,5},{5,3},{3,1},{1,0},{8,10},{10,12},{12... | collective-permute-start | bytes 798728 | tf_op jit(solution)/shard_map/ppermute | solution.py:395
  18.8 7.9 %collective-permute-start.7 = (bf16[1040,128]{1,0:T(8,128)(2,1)S(1)}, bf16[1040,128]{1,0:T(8,128)(2,1)S(1)}, u32[]{:S(2)}, u32[]{:S(2)}) collective-permute-start(bf16[1040,128]{1,0:T(8,128)(2,1)S(1)} %collective-permute-done.5.query_ref), channel_id=1, source_target_pairs={{2,0},{4,2},{6,4},{7,6},{5,7},{3,5},{1,3},{0,1},{10,8},{12,10},{14... | collective-permute-start | bytes 798728 | tf_op jit(solution)/shard_map/ppermute | solution.py:396
  20.4 7.8 %collective-permute-start.4 = (bf16[1040,128]{1,0:T(8,128)(2,1)S(1)}, bf16[1040,128]{1,0:T(8,128)(2,1)S(1)}, u32[]{:S(2)}, u32[]{:S(2)}) collective-permute-start(bf16[1040,128]{1,0:T(8,128)(2,1)S(1)} %collective-permute-done.3.query_ref), channel_id=1, source_target_pairs={{0,2},{2,4},{4,6},{6,7},{7,5},{5,3},{3,1},{1,0},{8,10},{10,12},{12... | collective-permute-start | bytes 798728 | tf_op jit(solution)/shard_map/ppermute | solution.py:395
  26.6 7.0 %collective-permute-start.10 = (bf16[1040,128]{1,0:T(8,128)(2,1)S(1)}, bf16[1040,128]{1,0:T(8,128)(2,1)S(1)}, u32[]{:S(2)}, u32[]{:S(2)}) collective-permute-start(bf16[1040,128]{1,0:T(8,128)(2,1)S(1)} %collective-permute-done.7.query_ref), channel_id=1, source_target_pairs={{2,0},{4,2},{6,4},{7,6},{5,7},{3,5},{1,3},{0,1},{10,8},{12,10},{14... | collective-permute-start | bytes 798728 | tf_op jit(solution)/shard_map/ppermute | solution.py:396
  28.3 7.0 %collective-permute-start.6 = (bf16[1040,128]{1,0:T(8,128)(2,1)S(1)}, bf16[1040,128]{1,0:T(8,128)(2,1)S(1)}, u32[]{:S(2)}, u32[]{:S(2)}) collective-permute-start(bf16[1040,128]{1,0:T(8,128)(2,1)S(1)} %collective-permute-done.4.query_ref), channel_id=1, source_target_pairs={{0,2},{2,4},{4,6},{6,7},{7,5},{5,3},{3,1},{1,0},{8,10},{10,12},{12... | collective-permute-start | bytes 798728 | tf_op jit(solution)/shard_map/ppermute | solution.py:395
  33.6 5.1 %collective-permute-start.21 = (bf16[528,128]{1,0:T(8,128)(2,1)S(1)}, bf16[528,128]{1,0:T(8,128)(2,1)S(1)}, u32[]{:S(2)}, u32[]{:S(2)}) collective-permute-start(bf16[528,128]{1,0:T(8,128)(2,1)S(1)} %slice.7), channel_id=1, source_target_pairs={{2,0},{4,2},{6,4},{7,6},{5,7},{3,5},{1,3},{0,1},{10,8},{12,10},{14... | collective-permute-start | bytes 405512 | tf_op jit(solution)/shard_map/ppermute | solution.py:396
  35.3 5.9 %collective-permute-start.8 = (bf16[528,128]{1,0:T(8,128)(2,1)S(1)}, bf16[528,128]{1,0:T(8,128)(2,1)S(1)}, u32[]{:S(2)}, u32[]{:S(2)}) collective-permute-start(bf16[528,128]{1,0:T(8,128)(2,1)S(1)} %slice.6), channel_id=1, source_target_pairs={{0,2},{2,4},{4,6},{6,7},{7,5},{5,3},{3,1},{1,0},{8,10},{10,12},{12... | collective-permute-start | bytes 405512 | tf_op jit(solution)/shard_map/ppermute | solution.py:395
  40.5 8.4 %collective-permute-start.22 = (bf16[528,128]{1,0:T(8,128)(2,1)S(1)}, bf16[528,128]{1,0:T(8,128)(2,1)S(1)}, u32[]{:S(2)}, u32[]{:S(2)}) collective-permute-start(bf16[528,128]{1,0:T(8,128)(2,1)S(1)} %shard_map.84), channel_id=1, source_target_pairs={{2,0},{4,2},{6,4},{7,6},{5,7},{3,5},{1,3},{0,1},{10,8},{12,10},{14... | collective-permute-start | bytes 405512 | tf_op jit(solution)/shard_map/ppermute | solution.py:415
  42.9 7.4 %collective-permute-start.9 = (bf16[528,128]{1,0:T(8,128)(2,1)S(1)}, bf16[528,128]{1,0:T(8,128)(2,1)S(1)}, u32[]{:S(2)}, u32[]{:S(2)}) collective-permute-start(bf16[528,128]{1,0:T(8,128)(2,1)S(1)} %shard_map.73), channel_id=1, source_target_pairs={{0,2},{2,4},{4,6},{6,7},{7,5},{5,3},{3,1},{1,0},{8,10},{10,12},{12... | collective-permute-start | bytes 405512 | tf_op jit(solution)/shard_map/ppermute | solution.py:415
  45.7 6.6 %collective-permute-start.18 = (bf16[528,128]{1,0:T(8,128)(2,1)S(1)}, bf16[528,128]{1,0:T(8,128)(2,1)S(1)}, u32[]{:S(2)}, u32[]{:S(2)}) collective-permute-start(bf16[528,128]{1,0:T(8,128)(2,1)S(1)} %get-tuple-element.60), channel_id=1, source_target_pairs={{0,2},{2,4},{4,6},{6,7},{7,5},{5,3},{3,1},{1,0},{8,10},{10,12},{12... | collective-permute-start | bytes 405512 | tf_op jit(solution)/shard_map/ppermute | solution.py:415
  49.1 6.5 %collective-permute-start.23 = (bf16[528,128]{1,0:T(8,128)(2,1)S(1)}, bf16[528,128]{1,0:T(8,128)(2,1)S(1)}, u32[]{:S(2)}, u32[]{:S(2)}) collective-permute-start(bf16[528,128]{1,0:T(8,128)(2,1)S(1)} %shard_map.85), channel_id=1, source_target_pairs={{2,0},{4,2},{6,4},{7,6},{5,7},{3,5},{1,3},{0,1},{10,8},{12,10},{14... | collective-permute-start | bytes 405512 | tf_op jit(solution)/shard_map/ppermute | solution.py:415
  50.0 8.4 %collective-permute-start.14 = (bf16[528,128]{1,0:T(8,128)(2,1)S(1)}, bf16[528,128]{1,0:T(8,128)(2,1)S(1)}, u32[]{:S(2)}, u32[]{:S(2)}) collective-permute-start(bf16[528,128]{1,0:T(8,128)(2,1)S(1)} %get-tuple-element.57), channel_id=1, source_target_pairs={{2,0},{4,2},{6,4},{7,6},{5,7},{3,5},{1,3},{0,1},{10,8},{12,10},{14... | collective-permute-start | bytes 405512 | tf_op jit(solution)/shard_map/ppermute | solution.py:415
  50.5 8.9 %collective-permute-start.11 = (bf16[528,128]{1,0:T(8,128)(2,1)S(1)}, bf16[528,128]{1,0:T(8,128)(2,1)S(1)}, u32[]{:S(2)}, u32[]{:S(2)}) collective-permute-start(bf16[528,128]{1,0:T(8,128)(2,1)S(1)} %shard_map.75), channel_id=1, source_target_pairs={{0,2},{2,4},{4,6},{6,7},{7,5},{5,3},{3,1},{1,0},{8,10},{10,12},{12... | collective-permute-start | bytes 405512 | tf_op jit(solution)/shard_map/ppermute | solution.py:415
  52.6 8.5 %collective-permute-start.19 = (bf16[528,128]{1,0:T(8,128)(2,1)S(1)}, bf16[528,128]{1,0:T(8,128)(2,1)S(1)}, u32[]{:S(2)}, u32[]{:S(2)}) collective-permute-start(bf16[528,128]{1,0:T(8,128)(2,1)S(1)} %shard_map.82), channel_id=1, source_target_pairs={{0,2},{2,4},{4,6},{6,7},{7,5},{5,3},{3,1},{1,0},{8,10},{10,12},{12... | collective-permute-start | bytes 405512 | tf_op jit(solution)/shard_map/ppermute | solution.py:415
  55.9 5.9 %collective-permute-start.24 = (bf16[528,128]{1,0:T(8,128)(2,1)S(1)}, bf16[528,128]{1,0:T(8,128)(2,1)S(1)}, u32[]{:S(2)}, u32[]{:S(2)}) collective-permute-start(bf16[528,128]{1,0:T(8,128)(2,1)S(1)} %shard_map.86), channel_id=1, source_target_pairs={{2,0},{4,2},{6,4},{7,6},{5,7},{3,5},{1,3},{0,1},{10,8},{12,10},{14... | collective-permute-start | bytes 405512 | tf_op jit(solution)/shard_map/ppermute | solution.py:415
  58.7 5.5 %collective-permute-start.15 = (bf16[528,128]{1,0:T(8,128)(2,1)S(1)}, bf16[528,128]{1,0:T(8,128)(2,1)S(1)}, u32[]{:S(2)}, u32[]{:S(2)}) collective-permute-start(bf16[528,128]{1,0:T(8,128)(2,1)S(1)} %shard_map.79), channel_id=1, source_target_pairs={{2,0},{4,2},{6,4},{7,6},{5,7},{3,5},{1,3},{0,1},{10,8},{12,10},{14... | collective-permute-start | bytes 405512 | tf_op jit(solution)/shard_map/ppermute | solution.py:415
  59.7 6.2 %collective-permute-start.12 = (bf16[528,128]{1,0:T(8,128)(2,1)S(1)}, bf16[528,128]{1,0:T(8,128)(2,1)S(1)}, u32[]{:S(2)}, u32[]{:S(2)}) collective-permute-start(bf16[528,128]{1,0:T(8,128)(2,1)S(1)} %shard_map.76), channel_id=1, source_target_pairs={{0,2},{2,4},{4,6},{6,7},{7,5},{5,3},{3,1},{1,0},{8,10},{10,12},{12... | collective-permute-start | bytes 405512 | tf_op jit(solution)/shard_map/ppermute | solution.py:415
  61.4 5.5 %collective-permute-start.20 = (bf16[528,128]{1,0:T(8,128)(2,1)S(1)}, bf16[528,128]{1,0:T(8,128)(2,1)S(1)}, u32[]{:S(2)}, u32[]{:S(2)}) collective-permute-start(bf16[528,128]{1,0:T(8,128)(2,1)S(1)} %shard_map.83), channel_id=1, source_target_pairs={{0,2},{2,4},{4,6},{6,7},{7,5},{5,3},{3,1},{1,0},{8,10},{10,12},{12... | collective-permute-start | bytes 405512 | tf_op jit(solution)/shard_map/ppermute | solution.py:415
  62.1 5.1 %collective-permute-start.25 = (bf16[528,128]{1,0:T(8,128)(2,1)S(1)}, bf16[528,128]{1,0:T(8,128)(2,1)S(1)}, u32[]{:S(2)}, u32[]{:S(2)}) collective-permute-start(bf16[528,128]{1,0:T(8,128)(2,1)S(1)} %shard_map.87), channel_id=1, source_target_pairs={{2,0},{4,2},{6,4},{7,6},{5,7},{3,5},{1,3},{0,1},{10,8},{12,10},{14... | collective-permute-start | bytes 405512 | tf_op jit(solution)/shard_map/ppermute | solution.py:415
  64.5 5.1 %collective-permute-start.16 = (bf16[528,128]{1,0:T(8,128)(2,1)S(1)}, bf16[528,128]{1,0:T(8,128)(2,1)S(1)}, u32[]{:S(2)}, u32[]{:S(2)}) collective-permute-start(bf16[528,128]{1,0:T(8,128)(2,1)S(1)} %shard_map.80), channel_id=1, source_target_pairs={{2,0},{4,2},{6,4},{7,6},{5,7},{3,5},{1,3},{0,1},{10,8},{12,10},{14... | collective-permute-start | bytes 405512 | tf_op jit(solution)/shard_map/ppermute | solution.py:415
  (11 other events, 28.1 us)

commit v4 on v3

--- a/solution.py
+++ b/solution.py
@@ -82,12 +82,16 @@
 def attend(queries, keys, values, usable):
     across = (((1,), (1,)), ((), ()))
     along = (((1,), (0,)), ((), ()))
+    ones = jnp.ones(values[0].shape, BF16)
     scores = [lax.dot_general(q, k, across, preferred_element_type=F32) for q, k in zip(queries, keys)]
     scores = [jnp.where(usable, s * SCALE, EMPTY) for s in scores]
     tops = [jnp.max(s, axis=1, keepdims=True) for s in scores]
-    weights = [jnp.exp2(s - t) for s, t in zip(scores, tops)]
-    totals = [jnp.sum(w, axis=1, keepdims=True) for w in weights]
-    mixed = [lax.dot_general(w.astype(BF16), v, along, preferred_element_type=F32) for w, v in zip(weights, values)]
+    weights = [jnp.exp2(s - t).astype(BF16) for s, t in zip(scores, tops)]
+    both = [
+        lax.dot_general(w, jnp.concatenate([v, ones], axis=1), along, preferred_element_type=F32)
+        for w, v in zip(weights, values)
+    ]
+    mixed, totals = [b[:, :HD] for b in both], [b[:, HD:] for b in both]
     level = by_lane(tops) + jnp.log2(jnp.maximum(by_lane(totals), 1.0))
     return [m / t for m, t in zip(mixed, totals)], level
 
@@ -142,73 +146,60 @@
     )(place, *queries, new_kv)
 
 
-def list_kernel(place_ref, owner_ref, index_ref, length_ref, out):
-    requests = owner_ref.shape[0]
-    lists = list_rows(requests)
-    rows = lax.broadcasted_iota(jnp.int32, (lists, LANES), 0)
-    lanes = lane_ids(lists)
-    tile = jnp.zeros((lists, LANES), F32)
-    for d in range(requests):
-        row = place_ref[0] ^ d
-        for s in range(SEL):
-            count = jnp.clip(length_ref[row] - s * PAGE, 0, PAGE).astype(F32)
-            mine = lanes == owner_ref[row, s]
-            tile = jnp.where(mine & (rows == 2 * d), count, tile)
-            tile = jnp.where(mine & (rows == 2 * d + 1), index_ref[row, s].astype(F32), tile)
-    out[...] = tile.astype(BF16)
-
-
-def page_lists(place, page_owner, page_index, lengths):
-    lists = list_rows(page_owner.shape[0])
-    return pl.pallas_call(
-        list_kernel,
-        out_shape=jax.ShapeDtypeStruct((lists, LANES), BF16),
-        in_specs=[IN_SMEM] * 4,
+def page_lists(page_owner, page_index, lengths):
+    visitors = page_owner.shape[0]
+    lanes = jnp.arange(LANES, dtype=jnp.int32)[None, None, :]
+    first = jnp.arange(2, dtype=jnp.int32)[None, :, None] == 0
+    table = jnp.zeros((visitors, 2, LANES), jnp.int32)
+    for s in range(SEL):
+        count = jnp.clip(lengths - s * PAGE, 0, PAGE)[:, None, None]
+        value = jnp.where(first, count, page_index[:, s, 0][:, None, None])
+        table = table + jnp.where(page_owner[:, s][:, None, None] == lanes, value, 0)
+    table = table.reshape(2 * visitors, LANES).astype(BF16)
+    return jnp.pad(table, ((0, list_rows(visitors) - 2 * visitors), (0, 0)))
+
+
+def payload_kernel(lists_ref, *refs):
+    visits, out = refs[:-1], refs[-1]
+    for number, visit in enumerate(visits):
+        out[number * BODY : (number + 1) * BODY, :] = visit[...]
+    out[len(visits) * BODY :, :] = lists_ref[...]
+
+
+def payload(lists, visits):
+    rows = len(visits) * BODY + lists.shape[0]
+    return pl.pallas_call(
+        payload_kernel,
+        out_shape=jax.ShapeDtypeStruct((rows, HD), BF16),
+        in_specs=[IN_VMEM] * (1 + len(visits)),
         out_specs=IN_VMEM,
         compiler_params=params(),
-        cost_estimate=cost(0, 4 * lists * HD),
-    )(place, page_owner, page_index, lengths)
-
-
-def payload_kernel(after, *refs):
-    lists_ref, visits, out = refs[0], refs[1 : len(refs) - 1 - after], refs[-1]
-    cut = len(visits) // 2
-    lists = lists_ref.shape[0]
-    for d, visit in enumerate(visits):
-        start = d * BODY + (lists if d >= cut else 0)
-        out[start : start + BODY, :] = visit[...]
-    out[cut * BODY : cut * BODY + lists, :] = lists_ref[...]
-
-
-def payload(lists, visits, after):
-    rows = len(visits) * BODY + lists.shape[0]
-    return pl.pallas_call(
-        functools.partial(payload_kernel, len(after)),
-        out_shape=jax.ShapeDtypeStruct((rows, HD), BF16),
-        in_specs=[IN_VMEM] * (1 + len(visits) + len(after)),
-        out_specs=IN_VMEM,
-        compiler_params=params(),
         cost_estimate=cost(0, 4 * rows * HD),
-    )(lists, *visits, *after)
-
-
-def item_kernel(slots, list_start, first, gap_at, lists, outs, place_ref, query_ref, cache_ref, *refs):
-    out_refs, (level_ref, code_ref) = refs[-2 - outs : -2], refs[-2:]
-    owner = place_ref[1]
-    table = query_ref[list_start : list_start + lists, :].astype(F32)
-    rows = lax.broadcasted_iota(jnp.int32, (lists, LANES), 0)
-    table = jnp.where(lane_ids(lists) == owner, table, 0.0)
-    for entry, slot in enumerate(slots):
-        code = jnp.where(rows == 2 * slot, table, jnp.where(rows == 2 * slot + 1, table * 256.0, 0.0))
-        code_ref[entry] = jnp.sum(code).astype(jnp.int32)
+    )(lists, *visits)
+
+
+def item_kernel(slots, place_ref, cache_ref, *refs):
+    sides = len(slots)
+    query_refs, out_refs, (level_ref, code_ref) = refs[:sides], refs[sides : 2 * sides], refs[2 * sides :]
+    each = len(slots[0])
+    for side, query_ref in enumerate(query_refs):
+        lists = query_ref.shape[0] - each * BODY
+        rows = lax.broadcasted_iota(jnp.int32, (lists, LANES), 0)
+        table = query_ref[each * BODY :, :].astype(F32)
+        table = jnp.where(lane_ids(lists) == place_ref[1], table, 0.0)
+        table = jnp.where((rows & 1) == 0, table, table * 256.0)
+        for number, slot in enumerate(slots[side]):
+            code = jnp.where(rows >> 1 == (place_ref[0] ^ slot), table, 0.0)
+            code_ref[side * each + number] = jnp.sum(code).astype(jnp.int32)
     tokens = lax.broadcasted_iota(jnp.int32, (ROWS, PAGE), 1)
-    each = len(slots) // outs
-
-    def one(entry, out_ref, inner):
+
+    def one(side, number):
+        entry = side * each + number
+        query_ref, out_ref = query_refs[side], out_refs[side]
         code = code_ref[entry]
         count, page = code & 255, code >> 8
-        start = first + entry * BODY + jnp.where(entry >= gap_at, lists, 0)
-        out = (inner // 2) * PAIR + (inner % 2) * BODY
+        start = number * BODY
+        out = (number // 2) * PAIR + (number % 2) * BODY
 
         @pl.when(count > 0)
         def _():
@@ -226,39 +217,32 @@
             level_ref[entry] = jnp.full((HALF, LANES), EMPTY, F32)
 
     lanes = lane_ids()
-    for number, out_ref in enumerate(out_refs):
+    for side, out_ref in enumerate(out_refs):
 
         @pl.loop(0, each)
-        def _(inner):
-            one(number * each + inner, out_ref, inner)
-
+        def _(number):
+            one(side, number)
+
+    for side, out_ref in enumerate(out_refs):
         for pair in range(each // 2):
-            entry = number * each + 2 * pair
+            entry = side * each + 2 * pair
             level = jnp.where(lanes < COLS, level_ref[entry], pltpu.roll(level_ref[entry + 1], SECOND, 1))
             start = pair * PAIR + 2 * BODY
             out_ref[start : start + HALF, :] = pack_stats(level)
 
 
-def items(place, queries, pages, requests, slots, after=()):
-    lists = list_rows(requests)
-    cut = requests // 2
-    if len(slots) == requests:
-        list_start, first, gap_at = cut * BODY, 0, cut
-    elif slots[0] == 0:
-        list_start, first, gap_at = cut * BODY, 0, requests
-    else:
-        list_start, first, gap_at = 0, lists, requests
-    count = len(slots)
-    outs = count // cut
-    return pl.pallas_call(
-        functools.partial(item_kernel, slots, list_start, first, gap_at, lists, outs),
-        out_shape=[jax.ShapeDtypeStruct((cut // 2 * PAIR, HD), BF16)] * outs,
-        in_specs=[IN_SMEM] + [IN_VMEM] * (2 + len(after)),
-        out_specs=[IN_VMEM] * outs,
+def items(place, kv_cache, payloads, slots):
+    count = sum(len(row) for row in slots)
+    rows = len(slots[0]) // 2 * PAIR
+    return pl.pallas_call(
+        functools.partial(item_kernel, slots),
+        out_shape=[jax.ShapeDtypeStruct((rows, HD), BF16)] * len(slots),
+        in_specs=[IN_SMEM] + [IN_VMEM] * (1 + len(slots)),
+        out_specs=[IN_VMEM] * len(slots),
         scratch_shapes=[pltpu.VMEM((count, HALF, LANES), F32), pltpu.SMEM((count,), jnp.int32)],
         compiler_params=params(),
-        cost_estimate=cost(count * KVH * 4 * ROWS * HD * PAGE, count * PAGE * pages.shape[2] * 2),
-    )(place, queries, pages, *after)
+        cost_estimate=cost(count * KVH * 4 * ROWS * HD * PAGE, count * PAGE * kv_cache.shape[2] * 2),
+    )(place, kv_cache, *payloads)
 
 
 def blend(levels):
@@ -381,43 +365,45 @@
     for d in range(groups - 1, 0, -1):
         visits[d] = swap(rows[d], d)
     new_out, new_level = new_tokens(place, rows, new_kv)
-    lists = page_lists(place, page_owner, page_index[:, :, 0], lengths)
-    block = payload(lists, visits, (new_level,))
-
-    slots = list(range(requests))
+    lists = page_lists(page_owner, page_index, lengths)
+
     cut = requests // 2
-    middle = cut * BODY
-    below = above = block
-    parts = {0: items(place, block, kv_cache, requests, slots)}
+    slots = [list(range(cut)), list(range(cut, requests))]
+    blocks = [payload(lists, visits[:cut])]
+    blocks.append(payload(lax.optimization_barrier((lists, blocks[0]))[0], visits[cut:]))
+    below, above = list(blocks), list(blocks)
+    parts = {(half, 0): part for half, part in enumerate(items(place, kv_cache, blocks, slots))}
+    far = [None, None]
     for step in range(1, reach + 1):
-        if step == reach:
-            below, above = below[: middle + lists.shape[0]], above[middle:]
-        below = lax.ppermute(below, "cache", forward)
-        above = lax.ppermute(above, "cache", backward)
-        if step < reach:
-            done = parts[0] if step == 1 else parts[1 - step] + parts[step - 1]
-            below, above = lax.optimization_barrier((below, done))[0], lax.optimization_barrier((above, done))[0]
-            parts[-step] = items(place, below, kv_cache, requests, slots)
-            parts[step] = items(place, above, kv_cache, requests, slots)
-    far_ahead = items(place, below, kv_cache, requests, slots[:cut])
-    far_behind = items(place, above, kv_cache, requests, slots[cut:])
+        for half in range(2):
+            if step < reach or half == 0:
+                below[half] = lax.ppermute(below[half], "cache", forward)
+            if step < reach or half == 1:
+                above[half] = lax.ppermute(above[half], "cache", backward)
+            if step == reach:
+                far[half] = items(place, kv_cache, [(below, above)[half][half]], [slots[half]])[0]
+                continue
+            done = [parts[half, 0]] if step == 1 else [parts[half, 1 - step], parts[half, step - 1]]
+            below[half] = lax.optimization_barrier((below[half], done))[0]
+            above[half] = lax.optimization_barrier((above[half], done))[0]
+            parts[half, -step], parts[half, step] = items(
+                place, kv_cache, [below[half], above[half]], [slots[half]] * 2
+            )
 
     arrived = []
     for half in range(2):
         for ring, sign in ((forward, 1), (backward, -1)):
-            if half == 0 and sign == 1:
-                chain, steps = far_ahead[0], range(reach - 1, -1, -1)
-            elif half == 1 and sign == -1:
-                chain, steps = far_behind[0], range(reach - 1, -1, -1)
+            if half == (0 if sign == 1 else 1):
+                chain, steps = far[half], range(reach - 1, -1, -1)
             else:
-                chain, steps = parts[sign * (reach - 1)][half], range(reach - 2, -1, -1)
+                chain, steps = parts[half, sign * (reach - 1)], range(reach - 2, -1, -1)
             for step in steps:
                 chain = lax.ppermute(chain, "cache", ring)
                 if step > 0:
-                    chain = merge(chain, parts[sign * step][half])
+                    chain = merge(chain, parts[half, sign * step])
             arrived.append(chain)
-    back = gather(arrived[2], arrived[3], parts[0][1])
-    front = gather(arrived[0], arrived[1], parts[0][0])
+    back = gather(arrived[2], arrived[3], parts[1, 0])
+    front = gather(arrived[0], arrived[1], parts[0, 0])
     returned = list(front) + list(back)
     home = [returned[0]] + [None] * (groups - 1)
     for d in range(groups - 1, 0, -1):

time: 75.3 us -> 74.1 us (0.984)
  starting transfers between devices: 26.5 us -> 36.7 us
  Pallas kernels: 27.9 us -> 20 us
  waiting for transfers between devices: 13.5 us -> 7.66 us
  other arithmetic: 0.07 us -> 0.98 us
  local copies, waits for them, and re-layouts: 7.21 us -> 8.06 us
    pallas_call x11, Pallas kernels: 20.4 us -> 12.5 us  [the longest x9 12.5 us: items(): pl.pallas_call(functools.partial(item_kernel, slots), out_shape=[jax.Shap...]
    ppermute x8 -> x14, starting transfers between devices: 8.26 us -> 15.1 us  [the longest x7 8.77 us: per_device(): below[half] = lax.ppermute(below[half], 'cache', forward)]
    ppermute x8 -> x14, waiting for transfers between devices: 5.14 us -> 2.19 us  [the longest x7 1.31 us: per_device(): below[half] = lax.ppermute(below[half], 'cache', forward)]
    unnamed x14 -> x8, local copies, waits for them, and re-layouts: 7.19 us -> 4.34 us
    ppermute x14, waiting for transfers between devices: 6.6 us -> 4.01 us  [per_device(): chain = lax.ppermute(chain, 'cache', ring)]
    ppermute x6, starting transfers between devices: 4.72 us -> 7 us  [swap(): lax.ppermute(array, 'grp', [(g, g ^ d) for g in range(groups)])]
    slice x2, local copies, waits for them, and re-layouts: 0.02 us -> 2.28 us  [the longest x1 1.23 us: page_lists(): value = jnp.where(first, count, page_index[:, s, 0][:, None, None])]
    broadcast_in_dim x0 -> x26, local copies, waits for them, and re-layouts: none -> 1.43 us  [the longest x18 1.33 us: page_lists(): value = jnp.where(first, count, page_index[:, s, 0][:, None, None])]
  transfers between devices with their start and end apart: 28 -> 34, of which waited for: 12 -> 10; matrix products, arithmetic and copies ran while one was open for 0% -> 6% of each run, Pallas kernels for 34% -> 24%
where the time goes in v4:
time: 74.1 us; the launch traced here: 73.6 us
  starting transfers between devices  36.7 us (50%)
  Pallas kernels  20 us (27%)
  local copies, waits for them, and re-layouts  8.06 us (11%)
  waiting for transfers between devices  7.66 us (10%)
  other arithmetic  0.98 us (1%)
    ppermute x14, starting transfers between devices, per_device(): chain = lax.ppermute(chain, 'cache', ring)  14.6 us
    pallas_call x9, Pallas kernels, items(): pl.pallas_call(functools.partial(item_kernel, slots), out_shape=[jax.Shap...  12.5 us
    ppermute x7, starting transfers between devices, per_device(): below[half] = lax.ppermute(below[half], 'cache', forward)  8.77 us
    ppermute x6, starting transfers between devices, swap(): lax.ppermute(array, 'grp', [(g, g ^ d) for g in range(groups)])  7 us
    ppermute x7, starting transfers between devices, per_device(): above[half] = lax.ppermute(above[half], 'cache', backward)  6.31 us
    unnamed x8, local copies, waits for them, and re-layouts  4.34 us
    ppermute x14, waiting for transfers between devices, per_device(): chain = lax.ppermute(chain, 'cache', ring)  4.01 us
    pallas_call x10, Pallas kernels, merge(): pl.pallas_call(merge_kernel, out_shape=jax.ShapeDtypeStruct(own.shape, BF...  2.65 us
  transfers between devices with their start and end apart: 34, of which 10 were waited for; matrix products, arithmetic and copies ran while one was open for 6% of the time, Pallas kernels for 24%

profile of v4, /device:TPU:0, one launch (start us, length us, event | category | flops | bytes accessed | tf_op | source)
XLA Modules:
  0.0 73.6 jit_solution(7213938997739277897)
XLA Ops:
  2.1 2.6 %collective-permute-start.2 = (bf16[256,128]{1,0:T(8,128)(2,1)S(1)}, bf16[256,128]{1,0:T(8,128)(2,1)S(1)}, u32[]{:S(2)}, u32[]{:S(2)}) collective-permute-start(bf16[256,128]{1,0:T(8,128)(2,1)S(1)} %get-tuple-element.45.refs_2_), channel_id=1, source_target_pairs={{0,16},{8,24},{16,0},{24,8},{1,17},{9,25},{17,1},{25,9},{2,18},{10... | collective-permute-start | bytes 196616 | tf_op jit(solution)/shard_map/ppermute | solution.py:361
  9.5 1.8 %collective-permute-start.20 = (bf16[528,128]{1,0:T(8,128)(2,1)S(1)}, bf16[528,128]{1,0:T(8,128)(2,1)S(1)}, u32[]{:S(2)}, u32[]{:S(2)}) collective-permute-start(bf16[528,128]{1,0:T(8,128)(2,1)S(1)} %shard_map.66.refs_1_), channel_id=1, source_target_pairs={{2,0},{4,2},{6,4},{7,6},{5,7},{3,5},{1,3},{0,1},{10,8},{12,10},{14... | collective-permute-start | bytes 405512 | tf_op jit(solution)/shard_map/ppermute | solution.py:382
  11.6 1.8 %collective-permute-start.18 = (bf16[528,128]{1,0:T(8,128)(2,1)S(1)}, bf16[528,128]{1,0:T(8,128)(2,1)S(1)}, u32[]{:S(2)}, u32[]{:S(2)}) collective-permute-start(bf16[528,128]{1,0:T(8,128)(2,1)S(1)} %shard_map.66.refs_1_), channel_id=1, source_target_pairs={{0,2},{2,4},{4,6},{6,7},{7,5},{5,3},{3,1},{1,0},{8,10},{10,12},{12... | collective-permute-start | bytes 405512 | tf_op jit(solution)/shard_map/ppermute | solution.py:380
  13.6 3.4 %copy-done = bf16[16,128,2048]{2,1,0:T(8,128)(2,1)S(1)} copy-done((bf16[16,128,2048]{2,1,0:T(8,128)(2,1)S(1)}, bf16[16,128,2048]{2,1,0:T(8,128)(2,1)}, u32[]{:S(2)}) %copy-start) | copy-done | bytes 8388632
  17.0 1.4 %shard_map.67 = (bf16[528,128]{1,0:T(8,128)(2,1)S(1)}, bf16[528,128]{1,0:T(8,128)(2,1)S(1)}) custom-call(s32[2]{0:T(128)S(1)} %pad_add_fusion.place_ref, bf16[16,128,2048]{2,1,0:T(8,128)(2,1)S(1)} %copy-done, bf16[528,128]{1,0:T(8,128)(2,1)S(1)} %shard_map.65.refs_0_, bf16[528,128]{1,0:T(8,128)(2,1)S(1)} %shard_map.66.refs_1_), custom_call_target="tpu_custom_call" | custom-call | flops 67108864 | bytes 2097152 | tf_op jit(solution)/shard_map/pallas_call | solution.py:237
  20.5 1.9 %collective-permute-start.19 = (bf16[528,128]{1,0:T(8,128)(2,1)S(1)}, bf16[528,128]{1,0:T(8,128)(2,1)S(1)}, u32[]{:S(2)}, u32[]{:S(2)}) collective-permute-start(bf16[528,128]{1,0:T(8,128)(2,1)S(1)} %collective-permute-done.18.refs_0_), channel_id=1, source_target_pairs={{0,2},{2,4},{4,6},{6,7},{7,5},{5,3},{3,1},{1,0},{8,10},{10,12},{12... | collective-permute-start | bytes 405512 | tf_op jit(solution)/shard_map/ppermute | solution.py:380
  22.5 1.4 %shard_map.78 = (bf16[528,128]{1,0:T(8,128)(2,1)S(1)}, bf16[528,128]{1,0:T(8,128)(2,1)S(1)}) custom-call(s32[2]{0:T(128)S(1)} %pad_add_fusion.place_ref, bf16[16,128,2048]{2,1,0:T(8,128)(2,1)S(1)} %copy-done.1, bf16[528,128]{1,0:T(8,128)(2,1)S(1)} %collective-permute-done.18.refs_0_, bf16[528,128]{1,0:T(8,128)(2,1)S(1)} %collective-permute-done.20.refs_1_), custom_call_target="tpu_custom_call" | custom-call | flops 67108864 | bytes 2097152 | tf_op jit(solution)/shard_map/pallas_call | solution.py:237
  23.9 1.8 %collective-permute-start.23 = (bf16[528,128]{1,0:T(8,128)(2,1)S(1)}, bf16[528,128]{1,0:T(8,128)(2,1)S(1)}, u32[]{:S(2)}, u32[]{:S(2)}) collective-permute-start(bf16[528,128]{1,0:T(8,128)(2,1)S(1)} %collective-permute-done.22.refs_1_), channel_id=1, source_target_pairs={{2,0},{4,2},{6,4},{7,6},{5,7},{3,5},{1,3},{0,1},{10,8},{12,10},{14... | collective-permute-start | bytes 405512 | tf_op jit(solution)/shard_map/ppermute | solution.py:382
  25.7 1.4 %shard_map.68 = (bf16[528,128]{1,0:T(8,128)(2,1)S(1)}, bf16[528,128]{1,0:T(8,128)(2,1)S(1)}) custom-call(s32[2]{0:T(128)S(1)} %pad_add_fusion.place_ref, bf16[16,128,2048]{2,1,0:T(8,128)(2,1)S(1)} %copy-done.1, bf16[528,128]{1,0:T(8,128)(2,1)S(1)} %collective-permute-done.1.refs_0_, bf16[528,128]{1,0:T(8,128)(2,1)S(1)} %collective-permute-done.5.refs_1_), custom_call_target="tpu_custom_call" | custom-call | flops 67108864 | bytes 2097152 | tf_op jit(solution)/shard_map/pallas_call | solution.py:237
  28.6 1.4 %shard_map.79 = (bf16[528,128]{1,0:T(8,128)(2,1)S(1)}, bf16[528,128]{1,0:T(8,128)(2,1)S(1)}) custom-call(s32[2]{0:T(128)S(1)} %pad_add_fusion.place_ref, bf16[16,128,2048]{2,1,0:T(8,128)(2,1)S(1)} %copy-done.1, bf16[528,128]{1,0:T(8,128)(2,1)S(1)} %collective-permute-done.19.refs_0_, bf16[528,128]{1,0:T(8,128)(2,1)S(1)} %collective-permute-done.22.refs_1_), custom_call_target="tpu_custom_call" | custom-call | flops 67108864 | bytes 2097152 | tf_op jit(solution)/shard_map/pallas_call | solution.py:237
  31.2 1.4 %shard_map.69 = (bf16[528,128]{1,0:T(8,128)(2,1)S(1)}, bf16[528,128]{1,0:T(8,128)(2,1)S(1)}) custom-call(s32[2]{0:T(128)S(1)} %pad_add_fusion.place_ref, bf16[16,128,2048]{2,1,0:T(8,128)(2,1)S(1)} %copy-done.1, bf16[528,128]{1,0:T(8,128)(2,1)S(1)} %collective-permute-done.4.refs_0_, bf16[528,128]{1,0:T(8,128)(2,1)S(1)} %collective-permute-done.7.refs_1_), custom_call_target="tpu_custom_call" | custom-call | flops 67108864 | bytes 2097152 | tf_op jit(solution)/shard_map/pallas_call | solution.py:237
  33.7 3.3 %collective-permute-start.21 = (bf16[528,128]{1,0:T(8,128)(2,1)S(1)}, bf16[528,128]{1,0:T(8,128)(2,1)S(1)}, u32[]{:S(2)}, u32[]{:S(2)}) collective-permute-start(bf16[528,128]{1,0:T(8,128)(2,1)S(1)} %collective-permute-done.19.refs_0_), channel_id=1, source_target_pairs={{0,2},{2,4},{4,6},{6,7},{7,5},{5,3},{3,1},{1,0},{8,10},{10,12},{12... | collective-permute-start | bytes 405512 | tf_op jit(solution)/shard_map/ppermute | solution.py:380
  37.1 1.8 %shard_map.83 = bf16[528,128]{1,0:T(8,128)(2,1)S(1)} custom-call(s32[2]{0:T(128)S(1)} %pad_add_fusion.place_ref, bf16[16,128,2048]{2,1,0:T(8,128)(2,1)S(1)} %copy-done.1, bf16[528,128]{1,0:T(8,128)(2,1)S(1)} %collective-permute-done.27.refs_0_), custom_call_target="tpu_custom_call" | custom-call | flops 33554432 | bytes 1048576 | tf_op jit(solution)/shard_map/pallas_call | solution.py:237
  39.9 1.9 %collective-permute-start.9 = (bf16[528,128]{1,0:T(8,128)(2,1)S(1)}, bf16[528,128]{1,0:T(8,128)(2,1)S(1)}, u32[]{:S(2)}, u32[]{:S(2)}) collective-permute-start(bf16[528,128]{1,0:T(8,128)(2,1)S(1)} %shard_map.70), channel_id=1, source_target_pairs={{0,2},{2,4},{4,6},{6,7},{7,5},{5,3},{3,1},{1,0},{8,10},{10,12},{12... | collective-permute-start | bytes 405512 | tf_op jit(solution)/shard_map/ppermute | solution.py:401
  41.8 1.9 %shard_map.80 = (bf16[528,128]{1,0:T(8,128)(2,1)S(1)}, bf16[528,128]{1,0:T(8,128)(2,1)S(1)}) custom-call(s32[2]{0:T(128)S(1)} %pad_add_fusion.place_ref, bf16[16,128,2048]{2,1,0:T(8,128)(2,1)S(1)} %copy-done.1, bf16[528,128]{1,0:T(8,128)(2,1)S(1)} %collective-permute-done.21.refs_0_, bf16[528,128]{1,0:T(8,128)(2,1)S(1)} %collective-permute-done.23.refs_1_), custom_call_target="tpu_custom_call" | custom-call | flops 67108864 | bytes 2097152 | tf_op jit(solution)/shard_map/pallas_call | solution.py:237
  43.7 1.6 %collective-permute-start.24 = (bf16[528,128]{1,0:T(8,128)(2,1)S(1)}, bf16[528,128]{1,0:T(8,128)(2,1)S(1)}, u32[]{:S(2)}, u32[]{:S(2)}) collective-permute-start(bf16[528,128]{1,0:T(8,128)(2,1)S(1)} %get-tuple-element.73), channel_id=1, source_target_pairs={{0,2},{2,4},{4,6},{6,7},{7,5},{5,3},{3,1},{1,0},{8,10},{10,12},{12... | collective-permute-start | bytes 405512 | tf_op jit(solution)/shard_map/ppermute | solution.py:401
  50.2 1.7 %collective-permute-start.25 = (bf16[528,128]{1,0:T(8,128)(2,1)S(1)}, bf16[528,128]{1,0:T(8,128)(2,1)S(1)}, u32[]{:S(2)}, u32[]{:S(2)}) collective-permute-start(bf16[528,128]{1,0:T(8,128)(2,1)S(1)} %shard_map.81), channel_id=1, source_target_pairs={{0,2},{2,4},{4,6},{6,7},{7,5},{5,3},{3,1},{1,0},{8,10},{10,12},{12... | collective-permute-start | bytes 405512 | tf_op jit(solution)/shard_map/ppermute | solution.py:401
  52.6 1.3 %collective-permute-done.14.arrived_ref = bf16[528,128]{1,0:T(8,128)(2,1)S(1)} collective-permute-done((bf16[528,128]{1,0:T(8,128)(2,1)S(1)}, bf16[528,128]{1,0:T(8,128)(2,1)S(1)}, u32[]{:S(2)}, u32[]{:S(2)}) %collective-permute-start.14) | collective-permute-done | bytes 135200 | tf_op jit(solution)/shard_map/ppermute | solution.py:401
  57.2 1.5 %collective-permute-start.26 = (bf16[528,128]{1,0:T(8,128)(2,1)S(1)}, bf16[528,128]{1,0:T(8,128)(2,1)S(1)}, u32[]{:S(2)}, u32[]{:S(2)}) collective-permute-start(bf16[528,128]{1,0:T(8,128)(2,1)S(1)} %shard_map.82), channel_id=1, source_target_pairs={{0,2},{2,4},{4,6},{6,7},{7,5},{5,3},{3,1},{1,0},{8,10},{10,12},{12... | collective-permute-start | bytes 405512 | tf_op jit(solution)/shard_map/ppermute | solution.py:401
  59.6 1.4 %collective-permute-done.15.arrived_ref = bf16[528,128]{1,0:T(8,128)(2,1)S(1)} collective-permute-done((bf16[528,128]{1,0:T(8,128)(2,1)S(1)}, bf16[528,128]{1,0:T(8,128)(2,1)S(1)}, u32[]{:S(2)}, u32[]{:S(2)}) %collective-permute-start.15) | collective-permute-done | bytes 135200 | tf_op jit(solution)/shard_map/ppermute | solution.py:401
  64.4 3.6 %collective-permute-start.32 = (bf16[272,128]{1,0:T(8,128)(2,1)S(1)}, bf16[272,128]{1,0:T(8,128)(2,1)S(1)}, u32[]{:S(2)}, u32[]{:S(2)}) collective-permute-start(bf16[272,128]{1,0:T(8,128)(2,1)S(1)} %get-tuple-element.75), channel_id=1, source_target_pairs={{0,16},{8,24},{16,0},{24,8},{1,17},{9,25},{17,1},{25,9},{2,18},{10... | collective-permute-start | bytes 208904 | tf_op jit(solution)/shard_map/ppermute | solution.py:361
  68.6 1.7 %shard_map.88 = (f32[4,256,128]{2,1,0:T(8,128)S(1)}, f32[4,16,128]{2,1,0:T(8,128)S(1)}) custom-call(s32[2]{0:T(128)S(1)} %pad_add_fusion.place_ref, bf16[256,128]{1,0:T(8,128)(2,1)S(1)} %get-tuple-element.42.refs_0_, bf16[256,128]{1,0:T(8,128)(2,1)S(1)} %get-tuple-element.43.refs_1_, bf16[256,128]{1,0:T(8,128)(2,1)S(1)} %get-tuple-element.45.refs_2_, ...), custom_call_target="tpu_custom_call" | custom-call | flops 67108864 | bytes 786432 | tf_op jit(solution)/shard_map/pallas_call | solution.py:136
  70.3 1.5 %collective-permute-done.33.refs_3_ = bf16[272,128]{1,0:T(8,128)(2,1)S(1)} collective-permute-done((bf16[272,128]{1,0:T(8,128)(2,1)S(1)}, bf16[272,128]{1,0:T(8,128)(2,1)S(1)}, u32[]{:S(2)}, u32[]{:S(2)}) %collective-permute-start.33) | collective-permute-done | bytes 69664 | tf_op jit(solution)/shard_map/ppermute | solution.py:361
  71.8 1.9 %shard_map.89 = bf16[4,4,8192]{2,1,0:T(4,128)(2,1)} custom-call(s32[2]{0:T(128)S(1)} %pad_add_fusion.place_ref, bf16[272,128]{1,0:T(8,128)(2,1)S(1)} %get-tuple-element.60.refs_0_, bf16[272,128]{1,0:T(8,128)(2,1)S(1)} %collective-permute-done.17.refs_1_, bf16[272,128]{1,0:T(8,128)(2,1)S(1)} %collective-permute-done.32.refs_2_, ...), custom_call_target="tpu_custom_call" | custom-call | bytes 1048576 | tf_op jit(solution)/shard_map/pallas_call | solution.py:334
  (114 shorter events, 28.2 us)
Async XLA Ops:
  1.6 7.9 %collective-permute-start = (bf16[256,128]{1,0:T(8,128)(2,1)S(1)}, bf16[256,128]{1,0:T(8,128)(2,1)S(1)}, u32[]{:S(2)}, u32[]{:S(2)}) collective-permute-start(bf16[256,128]{1,0:T(8,128)(2,1)S(1)} %get-tuple-element.43.refs_1_), channel_id=1, source_target_pairs={{0,8},{8,0},{16,24},{24,16},{1,9},{9,1},{17,25},{25,17},{2,10},{10... | collective-permute-start | bytes 196616 | tf_op jit(solution)/shard_map/ppermute | solution.py:361
  2.1 7.4 %collective-permute-start.2 = (bf16[256,128]{1,0:T(8,128)(2,1)S(1)}, bf16[256,128]{1,0:T(8,128)(2,1)S(1)}, u32[]{:S(2)}, u32[]{:S(2)}) collective-permute-start(bf16[256,128]{1,0:T(8,128)(2,1)S(1)} %get-tuple-element.45.refs_2_), channel_id=1, source_target_pairs={{0,16},{8,24},{16,0},{24,8},{1,17},{9,25},{17,1},{25,9},{2,18},{10... | collective-permute-start | bytes 196616 | tf_op jit(solution)/shard_map/ppermute | solution.py:361
  9.5 8.9 %collective-permute-start.20 = (bf16[528,128]{1,0:T(8,128)(2,1)S(1)}, bf16[528,128]{1,0:T(8,128)(2,1)S(1)}, u32[]{:S(2)}, u32[]{:S(2)}) collective-permute-start(bf16[528,128]{1,0:T(8,128)(2,1)S(1)} %shard_map.66.refs_1_), channel_id=1, source_target_pairs={{2,0},{4,2},{6,4},{7,6},{5,7},{3,5},{1,3},{0,1},{10,8},{12,10},{14... | collective-permute-start | bytes 405512 | tf_op jit(solution)/shard_map/ppermute | solution.py:382
  11.3 8.4 %collective-permute-start.1 = (bf16[528,128]{1,0:T(8,128)(2,1)S(1)}, bf16[528,128]{1,0:T(8,128)(2,1)S(1)}, u32[]{:S(2)}, u32[]{:S(2)}) collective-permute-start(bf16[528,128]{1,0:T(8,128)(2,1)S(1)} %shard_map.65.refs_0_), channel_id=1, source_target_pairs={{0,2},{2,4},{4,6},{6,7},{7,5},{5,3},{3,1},{1,0},{8,10},{10,12},{12... | collective-permute-start | bytes 405512 | tf_op jit(solution)/shard_map/ppermute | solution.py:380
  11.6 8.9 %collective-permute-start.18 = (bf16[528,128]{1,0:T(8,128)(2,1)S(1)}, bf16[528,128]{1,0:T(8,128)(2,1)S(1)}, u32[]{:S(2)}, u32[]{:S(2)}) collective-permute-start(bf16[528,128]{1,0:T(8,128)(2,1)S(1)} %shard_map.66.refs_1_), channel_id=1, source_target_pairs={{0,2},{2,4},{4,6},{6,7},{7,5},{5,3},{3,1},{1,0},{8,10},{10,12},{12... | collective-permute-start | bytes 405512 | tf_op jit(solution)/shard_map/ppermute | solution.py:380
  13.4 9.0 %collective-permute-start.5 = (bf16[528,128]{1,0:T(8,128)(2,1)S(1)}, bf16[528,128]{1,0:T(8,128)(2,1)S(1)}, u32[]{:S(2)}, u32[]{:S(2)}) collective-permute-start(bf16[528,128]{1,0:T(8,128)(2,1)S(1)} %shard_map.65.refs_0_), channel_id=1, source_target_pairs={{2,0},{4,2},{6,4},{7,6},{5,7},{3,5},{1,3},{0,1},{10,8},{12,10},{14... | collective-permute-start | bytes 405512 | tf_op jit(solution)/shard_map/ppermute | solution.py:382
  19.7 7.5 %collective-permute-start.4 = (bf16[528,128]{1,0:T(8,128)(2,1)S(1)}, bf16[528,128]{1,0:T(8,128)(2,1)S(1)}, u32[]{:S(2)}, u32[]{:S(2)}) collective-permute-start(bf16[528,128]{1,0:T(8,128)(2,1)S(1)} %collective-permute-done.1.refs_0_), channel_id=1, source_target_pairs={{0,2},{2,4},{4,6},{6,7},{7,5},{5,3},{3,1},{1,0},{8,10},{10,12},{12... | collective-permute-start | bytes 405512 | tf_op jit(solution)/shard_map/ppermute | solution.py:380
  20.5 7.3 %collective-permute-start.19 = (bf16[528,128]{1,0:T(8,128)(2,1)S(1)}, bf16[528,128]{1,0:T(8,128)(2,1)S(1)}, u32[]{:S(2)}, u32[]{:S(2)}) collective-permute-start(bf16[528,128]{1,0:T(8,128)(2,1)S(1)} %collective-permute-done.18.refs_0_), channel_id=1, source_target_pairs={{0,2},{2,4},{4,6},{6,7},{7,5},{5,3},{3,1},{1,0},{8,10},{10,12},{12... | collective-permute-start | bytes 405512 | tf_op jit(solution)/shard_map/ppermute | solution.py:380
  22.4 6.2 %collective-permute-start.7 = (bf16[528,128]{1,0:T(8,128)(2,1)S(1)}, bf16[528,128]{1,0:T(8,128)(2,1)S(1)}, u32[]{:S(2)}, u32[]{:S(2)}) collective-permute-start(bf16[528,128]{1,0:T(8,128)(2,1)S(1)} %collective-permute-done.5.refs_1_), channel_id=1, source_target_pairs={{2,0},{4,2},{6,4},{7,6},{5,7},{3,5},{1,3},{0,1},{10,8},{12,10},{14... | collective-permute-start | bytes 405512 | tf_op jit(solution)/shard_map/ppermute | solution.py:382
  30.1 7.0 %collective-permute-start.27 = (bf16[528,128]{1,0:T(8,128)(2,1)S(1)}, bf16[528,128]{1,0:T(8,128)(2,1)S(1)}, u32[]{:S(2)}, u32[]{:S(2)}) collective-permute-start(bf16[528,128]{1,0:T(8,128)(2,1)S(1)} %collective-permute-done.23.refs_1_), channel_id=1, source_target_pairs={{2,0},{4,2},{6,4},{7,6},{5,7},{3,5},{1,3},{0,1},{10,8},{12,10},{14... | collective-permute-start | bytes 405512 | tf_op jit(solution)/shard_map/ppermute | solution.py:382
  33.7 8.0 %collective-permute-start.21 = (bf16[528,128]{1,0:T(8,128)(2,1)S(1)}, bf16[528,128]{1,0:T(8,128)(2,1)S(1)}, u32[]{:S(2)}, u32[]{:S(2)}) collective-permute-start(bf16[528,128]{1,0:T(8,128)(2,1)S(1)} %collective-permute-done.19.refs_0_), channel_id=1, source_target_pairs={{0,2},{2,4},{4,6},{6,7},{7,5},{5,3},{3,1},{1,0},{8,10},{10,12},{12... | collective-permute-start | bytes 405512 | tf_op jit(solution)/shard_map/ppermute | solution.py:380
  37.1 8.3 %collective-permute-start.10 = (bf16[528,128]{1,0:T(8,128)(2,1)S(1)}, bf16[528,128]{1,0:T(8,128)(2,1)S(1)}, u32[]{:S(2)}, u32[]{:S(2)}) collective-permute-start(bf16[528,128]{1,0:T(8,128)(2,1)S(1)} %collective-permute-done.7.refs_1_), channel_id=1, source_target_pairs={{2,0},{4,2},{6,4},{7,6},{5,7},{3,5},{1,3},{0,1},{10,8},{12,10},{14... | collective-permute-start | bytes 405512 | tf_op jit(solution)/shard_map/ppermute | solution.py:382
  38.9 6.4 %collective-permute-start.28 = (bf16[528,128]{1,0:T(8,128)(2,1)S(1)}, bf16[528,128]{1,0:T(8,128)(2,1)S(1)}, u32[]{:S(2)}, u32[]{:S(2)}) collective-permute-start(bf16[528,128]{1,0:T(8,128)(2,1)S(1)} %shard_map.83), channel_id=1, source_target_pairs={{2,0},{4,2},{6,4},{7,6},{5,7},{3,5},{1,3},{0,1},{10,8},{12,10},{14... | collective-permute-start | bytes 405512 | tf_op jit(solution)/shard_map/ppermute | solution.py:401
  39.9 8.4 %collective-permute-start.9 = (bf16[528,128]{1,0:T(8,128)(2,1)S(1)}, bf16[528,128]{1,0:T(8,128)(2,1)S(1)}, u32[]{:S(2)}, u32[]{:S(2)}) collective-permute-start(bf16[528,128]{1,0:T(8,128)(2,1)S(1)} %shard_map.70), channel_id=1, source_target_pairs={{0,2},{2,4},{4,6},{6,7},{7,5},{5,3},{3,1},{1,0},{8,10},{10,12},{12... | collective-permute-start | bytes 405512 | tf_op jit(solution)/shard_map/ppermute | solution.py:401
  43.7 6.2 %collective-permute-start.24 = (bf16[528,128]{1,0:T(8,128)(2,1)S(1)}, bf16[528,128]{1,0:T(8,128)(2,1)S(1)}, u32[]{:S(2)}, u32[]{:S(2)}) collective-permute-start(bf16[528,128]{1,0:T(8,128)(2,1)S(1)} %get-tuple-element.73), channel_id=1, source_target_pairs={{0,2},{2,4},{4,6},{6,7},{7,5},{5,3},{3,1},{1,0},{8,10},{10,12},{12... | collective-permute-start | bytes 405512 | tf_op jit(solution)/shard_map/ppermute | solution.py:401
  45.6 6.2 %collective-permute-start.29 = (bf16[528,128]{1,0:T(8,128)(2,1)S(1)}, bf16[528,128]{1,0:T(8,128)(2,1)S(1)}, u32[]{:S(2)}, u32[]{:S(2)}) collective-permute-start(bf16[528,128]{1,0:T(8,128)(2,1)S(1)} %shard_map.84), channel_id=1, source_target_pairs={{2,0},{4,2},{6,4},{7,6},{5,7},{3,5},{1,3},{0,1},{10,8},{12,10},{14... | collective-permute-start | bytes 405512 | tf_op jit(solution)/shard_map/ppermute | solution.py:401
  47.0 6.9 %collective-permute-start.14 = (bf16[528,128]{1,0:T(8,128)(2,1)S(1)}, bf16[528,128]{1,0:T(8,128)(2,1)S(1)}, u32[]{:S(2)}, u32[]{:S(2)}) collective-permute-start(bf16[528,128]{1,0:T(8,128)(2,1)S(1)} %get-tuple-element.59), channel_id=1, source_target_pairs={{2,0},{4,2},{6,4},{7,6},{5,7},{3,5},{1,3},{0,1},{10,8},{12,10},{14... | collective-permute-start | bytes 405512 | tf_op jit(solution)/shard_map/ppermute | solution.py:401
  48.5 6.5 %collective-permute-start.11 = (bf16[528,128]{1,0:T(8,128)(2,1)S(1)}, bf16[528,128]{1,0:T(8,128)(2,1)S(1)}, u32[]{:S(2)}, u32[]{:S(2)}) collective-permute-start(bf16[528,128]{1,0:T(8,128)(2,1)S(1)} %shard_map.72), channel_id=1, source_target_pairs={{0,2},{2,4},{4,6},{6,7},{7,5},{5,3},{3,1},{1,0},{8,10},{10,12},{12... | collective-permute-start | bytes 405512 | tf_op jit(solution)/shard_map/ppermute | solution.py:401
  50.2 6.8 %collective-permute-start.25 = (bf16[528,128]{1,0:T(8,128)(2,1)S(1)}, bf16[528,128]{1,0:T(8,128)(2,1)S(1)}, u32[]{:S(2)}, u32[]{:S(2)}) collective-permute-start(bf16[528,128]{1,0:T(8,128)(2,1)S(1)} %shard_map.81), channel_id=1, source_target_pairs={{0,2},{2,4},{4,6},{6,7},{7,5},{5,3},{3,1},{1,0},{8,10},{10,12},{12... | collective-permute-start | bytes 405512 | tf_op jit(solution)/shard_map/ppermute | solution.py:401
  52.1 6.6 %collective-permute-start.30 = (bf16[528,128]{1,0:T(8,128)(2,1)S(1)}, bf16[528,128]{1,0:T(8,128)(2,1)S(1)}, u32[]{:S(2)}, u32[]{:S(2)}) collective-permute-start(bf16[528,128]{1,0:T(8,128)(2,1)S(1)} %shard_map.85), channel_id=1, source_target_pairs={{2,0},{4,2},{6,4},{7,6},{5,7},{3,5},{1,3},{0,1},{10,8},{12,10},{14... | collective-permute-start | bytes 405512 | tf_op jit(solution)/shard_map/ppermute | solution.py:401
  54.1 6.9 %collective-permute-start.15 = (bf16[528,128]{1,0:T(8,128)(2,1)S(1)}, bf16[528,128]{1,0:T(8,128)(2,1)S(1)}, u32[]{:S(2)}, u32[]{:S(2)}) collective-permute-start(bf16[528,128]{1,0:T(8,128)(2,1)S(1)} %shard_map.75), channel_id=1, source_target_pairs={{2,0},{4,2},{6,4},{7,6},{5,7},{3,5},{1,3},{0,1},{10,8},{12,10},{14... | collective-permute-start | bytes 405512 | tf_op jit(solution)/shard_map/ppermute | solution.py:401
  55.3 6.8 %collective-permute-start.12 = (bf16[528,128]{1,0:T(8,128)(2,1)S(1)}, bf16[528,128]{1,0:T(8,128)(2,1)S(1)}, u32[]{:S(2)}, u32[]{:S(2)}) collective-permute-start(bf16[528,128]{1,0:T(8,128)(2,1)S(1)} %shard_map.73), channel_id=1, source_target_pairs={{0,2},{2,4},{4,6},{6,7},{7,5},{5,3},{3,1},{1,0},{8,10},{10,12},{12... | collective-permute-start | bytes 405512 | tf_op jit(solution)/shard_map/ppermute | solution.py:401
  57.2 6.5 %collective-permute-start.26 = (bf16[528,128]{1,0:T(8,128)(2,1)S(1)}, bf16[528,128]{1,0:T(8,128)(2,1)S(1)}, u32[]{:S(2)}, u32[]{:S(2)}) collective-permute-start(bf16[528,128]{1,0:T(8,128)(2,1)S(1)} %shard_map.82), channel_id=1, source_target_pairs={{0,2},{2,4},{4,6},{6,7},{7,5},{5,3},{3,1},{1,0},{8,10},{10,12},{12... | collective-permute-start | bytes 405512 | tf_op jit(solution)/shard_map/ppermute | solution.py:401
  61.3 6.7 %collective-permute-start.16 = (bf16[528,128]{1,0:T(8,128)(2,1)S(1)}, bf16[528,128]{1,0:T(8,128)(2,1)S(1)}, u32[]{:S(2)}, u32[]{:S(2)}) collective-permute-start(bf16[528,128]{1,0:T(8,128)(2,1)S(1)} %shard_map.76), channel_id=1, source_target_pairs={{2,0},{4,2},{6,4},{7,6},{5,7},{3,5},{1,3},{0,1},{10,8},{12,10},{14... | collective-permute-start | bytes 405512 | tf_op jit(solution)/shard_map/ppermute | solution.py:401
  (14 other events, 86.8 us)

commit v5 on v4

--- a/solution.py
+++ b/solution.py
@@ -147,59 +147,75 @@
 
 
 def page_lists(page_owner, page_index, lengths):
-    visitors = page_owner.shape[0]
     lanes = jnp.arange(LANES, dtype=jnp.int32)[None, None, :]
-    first = jnp.arange(2, dtype=jnp.int32)[None, :, None] == 0
-    table = jnp.zeros((visitors, 2, LANES), jnp.int32)
-    for s in range(SEL):
-        count = jnp.clip(lengths - s * PAGE, 0, PAGE)[:, None, None]
-        value = jnp.where(first, count, page_index[:, s, 0][:, None, None])
-        table = table + jnp.where(page_owner[:, s][:, None, None] == lanes, value, 0)
-    table = table.reshape(2 * visitors, LANES).astype(BF16)
-    return jnp.pad(table, ((0, list_rows(visitors) - 2 * visitors), (0, 0)))
-
-
-def payload_kernel(lists_ref, *refs):
-    visits, out = refs[:-1], refs[-1]
+    counts = jnp.clip(lengths[:, None] - jnp.arange(SEL, dtype=jnp.int32)[None, :] * PAGE, 0, PAGE)
+    named = page_owner[:, :, None] == lanes
+    return (
+        jnp.sum(jnp.where(named, counts[:, :, None], 0), axis=1),
+        jnp.sum(jnp.where(named, page_index, 0), axis=1),
+    )
+
+
+def payload_kernel(after, counts_ref, pages_ref, *refs):
+    visits, out = refs[: len(refs) - 1 - after], refs[-1]
     for number, visit in enumerate(visits):
         out[number * BODY : (number + 1) * BODY, :] = visit[...]
-    out[len(visits) * BODY :, :] = lists_ref[...]
-
-
-def payload(lists, visits):
-    rows = len(visits) * BODY + lists.shape[0]
-    return pl.pallas_call(
-        payload_kernel,
+    tables = [counts_ref[...].astype(F32), pages_ref[...].astype(F32)]
+    short = out.shape[0] - len(visits) * BODY - 2 * tables[0].shape[0]
+    if short:
+        tables.append(jnp.zeros((short, LANES), F32))
+    out[len(visits) * BODY :, :] = jnp.concatenate(tables, axis=0).astype(BF16)
+
+
+def payload(lists, visits, after=()):
+    rows = len(visits) * BODY + list_rows(lists[0].shape[0])
+    return pl.pallas_call(
+        functools.partial(payload_kernel, len(after)),
         out_shape=jax.ShapeDtypeStruct((rows, HD), BF16),
-        in_specs=[IN_VMEM] * (1 + len(visits)),
+        in_specs=[IN_VMEM] * (2 + len(visits) + len(after)),
         out_specs=IN_VMEM,
         compiler_params=params(),
         cost_estimate=cost(0, 4 * rows * HD),
-    )(lists, *visits)
-
-
-def item_kernel(slots, place_ref, cache_ref, *refs):
+    )(*lists, *visits, *after)
+
+
+def touch_kernel(after_ref, cache_ref, out_ref):
+    out_ref[...] = cache_ref[0, :HALF, :HD]
+
+
+def touch(kv_cache, after):
+    return pl.pallas_call(
+        touch_kernel,
+        out_shape=jax.ShapeDtypeStruct((HALF, HD), BF16),
+        in_specs=[IN_VMEM, IN_VMEM],
+        out_specs=IN_VMEM,
+        compiler_params=params(),
+        cost_estimate=cost(0, 2 * HALF * HD),
+    )(after, kv_cache)
+
+
+def item_kernel(slots, visitors, place_ref, cache_ref, *refs):
     sides = len(slots)
-    query_refs, out_refs, (level_ref, code_ref) = refs[:sides], refs[sides : 2 * sides], refs[2 * sides :]
+    query_refs, (out_ref, level_ref, code_ref) = refs[:sides], refs[sides:]
     each = len(slots[0])
     for side, query_ref in enumerate(query_refs):
         lists = query_ref.shape[0] - each * BODY
         rows = lax.broadcasted_iota(jnp.int32, (lists, LANES), 0)
         table = query_ref[each * BODY :, :].astype(F32)
         table = jnp.where(lane_ids(lists) == place_ref[1], table, 0.0)
-        table = jnp.where((rows & 1) == 0, table, table * 256.0)
         for number, slot in enumerate(slots[side]):
-            code = jnp.where(rows >> 1 == (place_ref[0] ^ slot), table, 0.0)
+            row = place_ref[0] ^ slot
+            code = jnp.where(rows == row, table, jnp.where(rows == row + visitors, table * 256.0, 0.0))
             code_ref[side * each + number] = jnp.sum(code).astype(jnp.int32)
     tokens = lax.broadcasted_iota(jnp.int32, (ROWS, PAGE), 1)
 
     def one(side, number):
         entry = side * each + number
-        query_ref, out_ref = query_refs[side], out_refs[side]
+        query_ref = query_refs[side]
         code = code_ref[entry]
         count, page = code & 255, code >> 8
         start = number * BODY
-        out = (number // 2) * PAIR + (number % 2) * BODY
+        out = (entry // 2) * PAIR + (entry % 2) * BODY
 
         @pl.when(count > 0)
         def _():
@@ -216,29 +232,26 @@
             out_ref[pl.ds(pl.multiple_of(out, HALF), BODY), :] = jnp.zeros((BODY, HD), BF16)
             level_ref[entry] = jnp.full((HALF, LANES), EMPTY, F32)
 
-    lanes = lane_ids()
-    for side, out_ref in enumerate(out_refs):
+    for side in range(sides):
 
         @pl.loop(0, each)
         def _(number):
             one(side, number)
 
-    for side, out_ref in enumerate(out_refs):
-        for pair in range(each // 2):
-            entry = side * each + 2 * pair
-            level = jnp.where(lanes < COLS, level_ref[entry], pltpu.roll(level_ref[entry + 1], SECOND, 1))
-            start = pair * PAIR + 2 * BODY
-            out_ref[start : start + HALF, :] = pack_stats(level)
-
-
-def items(place, kv_cache, payloads, slots):
+    lanes = lane_ids()
+    for pair in range(sides * each // 2):
+        level = jnp.where(lanes < COLS, level_ref[2 * pair], pltpu.roll(level_ref[2 * pair + 1], SECOND, 1))
+        start = pair * PAIR + 2 * BODY
+        out_ref[start : start + HALF, :] = pack_stats(level)
+
+
+def items(place, kv_cache, payloads, slots, visitors):
     count = sum(len(row) for row in slots)
-    rows = len(slots[0]) // 2 * PAIR
-    return pl.pallas_call(
-        functools.partial(item_kernel, slots),
-        out_shape=[jax.ShapeDtypeStruct((rows, HD), BF16)] * len(slots),
+    return pl.pallas_call(
+        functools.partial(item_kernel, slots, visitors),
+        out_shape=jax.ShapeDtypeStruct((count // 2 * PAIR, HD), BF16),
         in_specs=[IN_SMEM] + [IN_VMEM] * (1 + len(slots)),
-        out_specs=[IN_VMEM] * len(slots),
+        out_specs=IN_VMEM,
         scratch_shapes=[pltpu.VMEM((count, HALF, LANES), F32), pltpu.SMEM((count,), jnp.int32)],
         compiler_params=params(),
         cost_estimate=cost(count * KVH * 4 * ROWS * HD * PAGE, count * PAGE * kv_cache.shape[2] * 2),
@@ -264,10 +277,15 @@
     return values
 
 
-def merge_kernel(arrived_ref, own_ref, out_ref):
+def merge_kernel(base, arrived_ref, own_ref, out_ref):
+    arrived_pairs = arrived_ref.shape[0] // PAIR
     for pair in range(out_ref.shape[0] // PAIR):
         part = slice(pair * PAIR, (pair + 1) * PAIR)
-        arrived, own, out = arrived_ref.at[part], own_ref.at[part], out_ref.at[part]
+        own, out = own_ref.at[part], out_ref.at[part]
+        if not base <= pair < base + arrived_pairs:
+            out[...] = own[...]
+            continue
+        arrived = arrived_ref.at[(pair - base) * PAIR : (pair - base + 1) * PAIR]
         shares, level = blend([unpack_stats(ref[2 * BODY : PAIR, :]) for ref in (arrived, own)])
         values = [mix(shares, (arrived, own), second * BODY, second * SECOND) for second in range(2)]
         for second in range(2):
@@ -277,9 +295,9 @@
         out[2 * BODY : PAIR, :] = pack_stats(level)
 
 
-def merge(arrived, own):
-    return pl.pallas_call(
-        merge_kernel,
+def merge(arrived, own, base):
+    return pl.pallas_call(
+        functools.partial(merge_kernel, base),
         out_shape=jax.ShapeDtypeStruct(own.shape, BF16),
         in_specs=[IN_VMEM, IN_VMEM],
         out_specs=IN_VMEM,
@@ -288,9 +306,9 @@
     )(arrived, own)
 
 
-def gather_kernel(ahead_ref, behind_ref, own_ref, *outs):
+def gather_kernel(base, ahead_ref, behind_ref, own_ref, *outs):
     for pair in range(len(outs) // 2):
-        part = slice(pair * PAIR, (pair + 1) * PAIR)
+        part = slice((base + pair) * PAIR, (base + pair + 1) * PAIR)
         sources = [ref.at[part] for ref in (own_ref, ahead_ref, behind_ref)]
         shares, level = blend([unpack_stats(ref[2 * BODY : PAIR, :]) for ref in sources])
         values = [mix(shares, sources, second * BODY, second * SECOND) for second in range(2)]
@@ -303,43 +321,47 @@
             out[BODY:LONE, :] = pack_stats(here)
 
 
-def gather(ahead, behind, own):
-    requests = own.shape[0] // PAIR * 2
-    return pl.pallas_call(
-        gather_kernel,
-        out_shape=[jax.ShapeDtypeStruct((LONE, HD), BF16)] * requests,
+def gather(ahead, behind, own, base, pairs):
+    return pl.pallas_call(
+        functools.partial(gather_kernel, base),
+        out_shape=[jax.ShapeDtypeStruct((LONE, HD), BF16)] * (2 * pairs),
         in_specs=[IN_VMEM] * 3,
-        out_specs=[IN_VMEM] * requests,
-        compiler_params=params(),
-        cost_estimate=cost(0, 8 * own.size),
+        out_specs=[IN_VMEM] * (2 * pairs),
+        compiler_params=params(),
+        cost_estimate=cost(0, 8 * pairs * PAIR * HD),
     )(ahead, behind, own)
 
 
-def final_kernel(place_ref, *refs):
-    parts, (new_ref, level_ref, out_ref, rows_ref) = refs[:-4], refs[-4:]
-    for d, part in enumerate(parts):
+def final_kernel(first, early, place_ref, *refs):
+    earlier, parts = refs[:early], refs[early:-4]
+    new_ref, level_ref, out_ref, rows_ref = refs[-4:]
+    for number, part in enumerate(parts):
+        d = first + number
         shares, _ = blend([unpack_stats(part[BODY:LONE, :]), level_ref[d]])
         for index, tile in enumerate(mix(shares, (part, new_ref.at[d]), 0, 0)):
             row = tile_start(index)
-            rows_ref[d, row : row + HALF, :] = tile
-    for d in range(len(parts)):
-        row = place_ref[0] ^ d
+            rows_ref[number, row : row + HALF, :] = tile
+    for number in range(len(parts)):
+        row = place_ref[0] ^ (first + number) if early else number
         for head in range(KVH * GQ):
-            tile = rows_ref[d, head * STEPS : (head + 1) * STEPS, :]
+            tile = rows_ref[number, head * STEPS : (head + 1) * STEPS, :]
             out_ref[row, :, head * HD : (head + 1) * HD] = tile.astype(BF16)
-
-
-def final(place, parts, new_out, new_level):
-    groups = len(parts)
-    return pl.pallas_call(
-        final_kernel,
-        out_shape=jax.ShapeDtypeStruct((groups, STEPS, KVH * GQ * HD), BF16),
-        in_specs=[IN_SMEM] + [IN_VMEM] * (groups + 2),
+    for ref in earlier:
+        for d in range(ref.shape[0]):
+            out_ref[place_ref[0] ^ d] = ref[d]
+
+
+def final(place, parts, first, new_out, new_level, earlier=()):
+    requests = len(parts) + sum(e.shape[0] for e in earlier)
+    return pl.pallas_call(
+        functools.partial(final_kernel, first, len(earlier)),
+        out_shape=jax.ShapeDtypeStruct((requests, STEPS, KVH * GQ * HD), BF16),
+        in_specs=[IN_SMEM] + [IN_VMEM] * (len(earlier) + len(parts) + 2),
         out_specs=IN_VMEM,
-        scratch_shapes=[pltpu.VMEM((groups, BODY, HD), F32)],
-        compiler_params=params(),
-        cost_estimate=cost(0, groups * BODY * HD * 8),
-    )(place, *parts, new_out, new_level)
+        scratch_shapes=[pltpu.VMEM((len(parts), BODY, HD), F32)],
+        compiler_params=params(),
+        cost_estimate=cost(0, len(parts) * BODY * HD * 8),
+    )(place, *earlier, *parts, new_out, new_level)
 
 
 def ring_order(owners):
@@ -369,46 +391,35 @@
 
     cut = requests // 2
     slots = [list(range(cut)), list(range(cut, requests))]
-    blocks = [payload(lists, visits[:cut])]
-    blocks.append(payload(lax.optimization_barrier((lists, blocks[0]))[0], visits[cut:]))
-    below, above = list(blocks), list(blocks)
-    parts = {(half, 0): part for half, part in enumerate(items(place, kv_cache, blocks, slots))}
-    far = [None, None]
-    for step in range(1, reach + 1):
-        for half in range(2):
-            if step < reach or half == 0:
-                below[half] = lax.ppermute(below[half], "cache", forward)
-            if step < reach or half == 1:
-                above[half] = lax.ppermute(above[half], "cache", backward)
-            if step == reach:
-                far[half] = items(place, kv_cache, [(below, above)[half][half]], [slots[half]])[0]
-                continue
-            done = [parts[half, 0]] if step == 1 else [parts[half, 1 - step], parts[half, step - 1]]
-            below[half] = lax.optimization_barrier((below[half], done))[0]
-            above[half] = lax.optimization_barrier((above[half], done))[0]
-            parts[half, -step], parts[half, step] = items(
-                place, kv_cache, [below[half], above[half]], [slots[half]] * 2
-            )
-
-    arrived = []
-    for half in range(2):
-        for ring, sign in ((forward, 1), (backward, -1)):
-            if half == (0 if sign == 1 else 1):
-                chain, steps = far[half], range(reach - 1, -1, -1)
-            else:
-                chain, steps = parts[half, sign * (reach - 1)], range(reach - 2, -1, -1)
-            for step in steps:
-                chain = lax.ppermute(chain, "cache", ring)
-                if step > 0:
-                    chain = merge(chain, parts[half, sign * step])
-            arrived.append(chain)
-    back = gather(arrived[2], arrived[3], parts[1, 0])
-    front = gather(arrived[0], arrived[1], parts[0, 0])
-    returned = list(front) + list(back)
-    home = [returned[0]] + [None] * (groups - 1)
-    for d in range(groups - 1, 0, -1):
-        home[d] = swap(returned[d], d)
-    return final(place, home, new_out, new_level)
+    owned = functools.partial(items, place, kv_cache, visitors=requests)
+
+    def exchange(both, half, last=False):
+        below = lax.ppermute(both[0], "cache", forward) if half == 0 or not last else None
+        above = lax.ppermute(both[1], "cache", backward) if half == 1 or not last else None
+        return (below, above) if last else lax.optimization_barrier((below, above))
+
+    first = payload(lists, visits[:cut])
+    halves = [exchange((first, first), 0)]
+    second = payload(lists, visits[cut:], [touch(kv_cache, first), *halves[0]])
+    halves.append(exchange((second, second), 1))
+    parts = {0: owned([first, second], slots)}
+    for step in range(1, reach):
+        parts[-step] = owned([halves[0][0], halves[1][0]], slots)
+        parts[step] = owned([halves[0][1], halves[1][1]], slots)
+        halves = [exchange(halves[half], half, step == reach - 1) for half in range(2)]
+
+    ahead, behind = owned([halves[0][0]], slots[:1]), owned([halves[1][1]], slots[1:])
+    for step in range(reach - 1, -1, -1):
+        ahead = lax.ppermute(ahead, "cache", forward)
+        behind = lax.ppermute(behind, "cache", backward)
+        if step > 0:
+            base = cut // 2 if step == reach - 1 else 0
+            ahead, behind = merge(ahead, parts[step], 0), merge(behind, parts[-step], base)
+    back = gather(ahead, behind, parts[0], cut // 2, cut // 2)
+    front = gather(ahead, behind, parts[0], 0, cut // 2)
+    home = [swap(part, d) for d, part in enumerate(list(front) + list(back))]
+    early = final(place, home[:cut], 0, new_out, new_level)
+    return final(place, home[cut:], cut, new_out, new_level, [early])
 
 
 def solution(mesh):

time: 74.1 us -> 80.9 us (1.092)
  waiting for transfers between devices: 7.66 us -> 28.7 us
  starting transfers between devices: 36.7 us -> 24.3 us
  local copies, waits for them, and re-layouts: 8.06 us -> 4.34 us
  Pallas kernels: 20 us -> 21.7 us
    ppermute x28 -> x22, waiting for transfers between devices: 6.19 us -> 26.8 us  [the longest x4 7.98 us: per_device(): behind = lax.ppermute(behind, 'cache', backward)]
    ppermute x28 -> x22, starting transfers between devices: 29.7 us -> 19.9 us  [the longest x7 8.09 us: exchange(): lax.ppermute(both[1], 'cache', backward)]
    ppermute x6, starting transfers between devices: 7 us -> 4.37 us  [swap(): lax.ppermute(array, 'grp', [(g, g ^ d) for g in range(groups)])]
    slice x2 -> x0, local copies, waits for them, and re-layouts: 2.28 us -> none  [the longest x1 1.23 us: page_lists(): value = jnp.where(first, count, page_index[:, s, 0][:, None, None])]
    pallas_call x24 -> x22, Pallas kernels: 17.8 us -> 19.5 us  [the longest x9 13.9 us: items(): pl.pallas_call(functools.partial(item_kernel, slots, visitors), out_shape...]
    broadcast_in_dim x26 -> x0, local copies, waits for them, and re-layouts: 1.43 us -> none  [the longest x18 1.33 us: page_lists(): value = jnp.where(first, count, page_index[:, s, 0][:, None, None])]
  transfers between devices with their start and end apart: 34 -> 28, of which waited for: 10 -> 21; matrix products, arithmetic and copies ran while one was open for 6% -> 2% of each run, Pallas kernels for 24% -> 24%
where the time goes in v5:
time: 80.9 us; the launch traced here: 80.8 us
  waiting for transfers between devices  28.7 us (35%)
  starting transfers between devices  24.3 us (30%)
  Pallas kernels  21.7 us (27%)
  local copies, waits for them, and re-layouts  4.34 us (5%)
  other arithmetic  1.59 us (2%)
    pallas_call x9, Pallas kernels, items(): pl.pallas_call(functools.partial(item_kernel, slots, visitors), out_shape...  13.9 us
    ppermute x7, starting transfers between devices, exchange(): lax.ppermute(both[1], 'cache', backward)  8.09 us
    ppermute x4, waiting for transfers between devices, per_device(): behind = lax.ppermute(behind, 'cache', backward)  7.98 us
    ppermute x7, waiting for transfers between devices, exchange(): lax.ppermute(both[0], 'cache', forward)  7.48 us
    ppermute x7, waiting for transfers between devices, exchange(): lax.ppermute(both[1], 'cache', backward)  6.34 us
    ppermute x7, starting transfers between devices, exchange(): lax.ppermute(both[0], 'cache', forward)  6.1 us
    ppermute x4, waiting for transfers between devices, per_device(): ahead = lax.ppermute(ahead, 'cache', forward)  5.04 us
    ppermute x4, starting transfers between devices, per_device(): ahead = lax.ppermute(ahead, 'cache', forward)  4.85 us
  transfers between devices with their start and end apart: 28, of which 21 were waited for; matrix products, arithmetic and copies ran while one was open for 2% of the time, Pallas kernels for 24%

profile of v5, /device:TPU:0, one launch (start us, length us, event | category | flops | bytes accessed | tf_op | source)
XLA Modules:
  0.0 80.8 jit_solution(2911642423928457911)
XLA Ops:
  3.7 2.6 %collective-permute-start.2 = (bf16[528,128]{1,0:T(8,128)(2,1)S(1)}, bf16[528,128]{1,0:T(8,128)(2,1)S(1)}, u32[]{:S(2)}, u32[]{:S(2)}) collective-permute-start(bf16[528,128]{1,0:T(8,128)(2,1)S(1)} %shard_map.65.after_ref.refs_0_), channel_id=1, source_target_pairs={{2,0},{4,2},{6,4},{7,6},{5,7},{3,5},{1,3},{0,1},{10,8},{12,10},{14... | collective-permute-start | bytes 405512 | tf_op jit(solution)/shard_map/ppermute | solution.py:398
  6.4 1.9 %collective-permute-start.9 = (bf16[256,128]{1,0:T(8,128)(2,1)S(1)}, bf16[256,128]{1,0:T(8,128)(2,1)S(1)}, u32[]{:S(2)}, u32[]{:S(2)}) collective-permute-start(bf16[256,128]{1,0:T(8,128)(2,1)S(1)} %get-tuple-element.35.refs_2_), channel_id=1, source_target_pairs={{0,16},{8,24},{16,0},{24,8},{1,17},{9,25},{17,1},{25,9},{2,18},{10... | collective-permute-start | bytes 196616 | tf_op jit(solution)/shard_map/ppermute | solution.py:383
  8.3 3.4 %copy-done = bf16[16,128,2048]{2,1,0:T(8,128)(2,1)S(1)} copy-done((bf16[16,128,2048]{2,1,0:T(8,128)(2,1)S(1)}, bf16[16,128,2048]{2,1,0:T(8,128)(2,1)}, u32[]{:S(2)}) %copy-start) | copy-done | bytes 8388632
  12.5 1.5 %collective-permute-start.12 = (bf16[528,128]{1,0:T(8,128)(2,1)S(1)}, bf16[528,128]{1,0:T(8,128)(2,1)S(1)}, u32[]{:S(2)}, u32[]{:S(2)}) collective-permute-start(bf16[528,128]{1,0:T(8,128)(2,1)S(1)} %shard_map.68.refs_1_), channel_id=1, source_target_pairs={{2,0},{4,2},{6,4},{7,6},{5,7},{3,5},{1,3},{0,1},{10,8},{12,10},{14... | collective-permute-start | bytes 405512 | tf_op jit(solution)/shard_map/ppermute | solution.py:398
  14.6 1.6 %collective-permute-start.3 = (bf16[528,128]{1,0:T(8,128)(2,1)S(1)}, bf16[528,128]{1,0:T(8,128)(2,1)S(1)}, u32[]{:S(2)}, u32[]{:S(2)}) collective-permute-start(bf16[528,128]{1,0:T(8,128)(2,1)S(1)} %collective-permute-done.1.refs_3_.refs_0_), channel_id=1, source_target_pairs={{0,2},{2,4},{4,6},{6,7},{7,5},{5,3},{3,1},{1,0},{8,10},{10,12},{12... | collective-permute-start | bytes 405512 | tf_op jit(solution)/shard_map/ppermute | solution.py:397
  18.1 2.5 %collective-permute-done.11.refs_1_ = bf16[528,128]{1,0:T(8,128)(2,1)S(1)} collective-permute-done((bf16[528,128]{1,0:T(8,128)(2,1)S(1)}, bf16[528,128]{1,0:T(8,128)(2,1)S(1)}, u32[]{:S(2)}, u32[]{:S(2)}) %collective-permute-start.11) | collective-permute-done | bytes 135200 | tf_op jit(solution)/shard_map/ppermute | solution.py:397
  26.8 1.6 %collective-permute-start.15 = (bf16[528,128]{1,0:T(8,128)(2,1)S(1)}, bf16[528,128]{1,0:T(8,128)(2,1)S(1)}, u32[]{:S(2)}, u32[]{:S(2)}) collective-permute-start(bf16[528,128]{1,0:T(8,128)(2,1)S(1)} %collective-permute-done.13.refs_1_), channel_id=1, source_target_pairs={{0,2},{2,4},{4,6},{6,7},{7,5},{5,3},{3,1},{1,0},{8,10},{10,12},{12... | collective-permute-start | bytes 405512 | tf_op jit(solution)/shard_map/ppermute | solution.py:397
  32.3 2.2 %collective-permute-done.16.refs_1_ = bf16[528,128]{1,0:T(8,128)(2,1)S(1)} collective-permute-done((bf16[528,128]{1,0:T(8,128)(2,1)S(1)}, bf16[528,128]{1,0:T(8,128)(2,1)S(1)}, u32[]{:S(2)}, u32[]{:S(2)}) %collective-permute-start.16) | collective-permute-done | bytes 135200 | tf_op jit(solution)/shard_map/ppermute | solution.py:398
  34.9 1.8 %shard_map.66 = bf16[528,128]{1,0:T(8,128)(2,1)S(1)} custom-call(s32[2]{0:T(128)S(1)} %pad_add_fusion.place_ref, bf16[16,128,2048]{2,1,0:T(8,128)(2,1)S(1)} %copy-done.1, bf16[528,128]{1,0:T(8,128)(2,1)S(1)} %collective-permute-done.7.refs_0_), custom_call_target="tpu_custom_call" | custom-call | flops 33554432 | bytes 1048576 | tf_op jit(solution)/shard_map/pallas_call | solution.py:250
  38.0 2.7 %collective-permute-done.20.refs_0_ = bf16[528,128]{1,0:T(8,128)(2,1)S(1)} collective-permute-done((bf16[528,128]{1,0:T(8,128)(2,1)S(1)}, bf16[528,128]{1,0:T(8,128)(2,1)S(1)}, u32[]{:S(2)}, u32[]{:S(2)}) %collective-permute-start.20) | collective-permute-done | bytes 135200 | tf_op jit(solution)/shard_map/ppermute | solution.py:398
  41.6 1.9 %shard_map.69.own_ref = bf16[1056,128]{1,0:T(8,128)(2,1)S(1)} custom-call(s32[2]{0:T(128)S(1)} %pad_add_fusion.place_ref, bf16[16,128,2048]{2,1,0:T(8,128)(2,1)S(1)} %copy-done.1, bf16[528,128]{1,0:T(8,128)(2,1)S(1)} %collective-permute-done.6.refs_0_, bf16[528,128]{1,0:T(8,128)(2,1)S(1)} %collective-permute-done.16.refs_1_), custom_call_target="tpu_custom_call" | custom-call | flops 67108864 | bytes 2097152 | tf_op jit(solution)/shard_map/pallas_call | solution.py:250
  44.7 2.0 %collective-permute-start.17 = (bf16[1056,128]{1,0:T(8,128)(2,1)S(1)}, bf16[1056,128]{1,0:T(8,128)(2,1)S(1)}, u32[]{:S(2)}, u32[]{:S(2)}) collective-permute-start(bf16[1056,128]{1,0:T(8,128)(2,1)S(1)} %shard_map.70), channel_id=1, source_target_pairs={{0,2},{2,4},{4,6},{6,7},{7,5},{5,3},{3,1},{1,0},{8,10},{10,12},{12... | collective-permute-start | bytes 811016 | tf_op jit(solution)/shard_map/ppermute | solution.py:413
  48.4 1.9 %shard_map.78.own_ref = bf16[1056,128]{1,0:T(8,128)(2,1)S(1)} custom-call(s32[2]{0:T(128)S(1)} %pad_add_fusion.place_ref, bf16[16,128,2048]{2,1,0:T(8,128)(2,1)S(1)} %copy-done.1, bf16[528,128]{1,0:T(8,128)(2,1)S(1)} %collective-permute-done.3.refs_0_, bf16[528,128]{1,0:T(8,128)(2,1)S(1)} %collective-permute-done.13.refs_1_), custom_call_target="tpu_custom_call" | custom-call | flops 67108864 | bytes 2097152 | tf_op jit(solution)/shard_map/pallas_call | solution.py:250
  50.3 1.9 %shard_map.71.own_ref = bf16[1056,128]{1,0:T(8,128)(2,1)S(1)} custom-call(s32[2]{0:T(128)S(1)} %pad_add_fusion.place_ref, bf16[16,128,2048]{2,1,0:T(8,128)(2,1)S(1)} %copy-done.1, bf16[528,128]{1,0:T(8,128)(2,1)S(1)} %collective-permute-done.4.refs_0_, bf16[528,128]{1,0:T(8,128)(2,1)S(1)} %collective-permute-done.14.refs_1_), custom_call_target="tpu_custom_call" | custom-call | flops 67108864 | bytes 2097152 | tf_op jit(solution)/shard_map/pallas_call | solution.py:250
  52.2 1.7 %collective-permute-done.17.arrived_ref = bf16[1056,128]{1,0:T(8,128)(2,1)S(1)} collective-permute-done((bf16[1056,128]{1,0:T(8,128)(2,1)S(1)}, bf16[1056,128]{1,0:T(8,128)(2,1)S(1)}, u32[]{:S(2)}, u32[]{:S(2)}) %collective-permute-start.17) | collective-permute-done | bytes 270368 | tf_op jit(solution)/shard_map/ppermute | solution.py:413
  55.2 1.8 %collective-permute-done.22.arrived_ref = bf16[1056,128]{1,0:T(8,128)(2,1)S(1)} collective-permute-done((bf16[1056,128]{1,0:T(8,128)(2,1)S(1)}, bf16[1056,128]{1,0:T(8,128)(2,1)S(1)}, u32[]{:S(2)}, u32[]{:S(2)}) %collective-permute-start.22) | collective-permute-done | bytes 270368 | tf_op jit(solution)/shard_map/ppermute | solution.py:414
  57.9 1.9 %shard_map.80.own_ref = bf16[1056,128]{1,0:T(8,128)(2,1)S(1)} custom-call(s32[2]{0:T(128)S(1)} %pad_add_fusion.place_ref, bf16[16,128,2048]{2,1,0:T(8,128)(2,1)S(1)} %copy-done.1, bf16[528,128]{1,0:T(8,128)(2,1)S(1)} %collective-permute-done.1.refs_3_.refs_0_, bf16[528,128]{1,0:T(8,128)(2,1)S(1)} %collective-permute-done.11.refs_1_), custom_call_target="tpu_custom_call" | custom-call | flops 67108864 | bytes 2097152 | tf_op jit(solution)/shard_map/pallas_call | solution.py:250
  60.7 2.1 %collective-permute-done.18.arrived_ref = bf16[1056,128]{1,0:T(8,128)(2,1)S(1)} collective-permute-done((bf16[1056,128]{1,0:T(8,128)(2,1)S(1)}, bf16[1056,128]{1,0:T(8,128)(2,1)S(1)}, u32[]{:S(2)}, u32[]{:S(2)}) %collective-permute-start.18) | collective-permute-done | bytes 270368 | tf_op jit(solution)/shard_map/ppermute | solution.py:413
  63.9 1.8 %collective-permute-done.23.arrived_ref = bf16[1056,128]{1,0:T(8,128)(2,1)S(1)} collective-permute-done((bf16[1056,128]{1,0:T(8,128)(2,1)S(1)}, bf16[1056,128]{1,0:T(8,128)(2,1)S(1)}, u32[]{:S(2)}, u32[]{:S(2)}) %collective-permute-start.23) | collective-permute-done | bytes 270368 | tf_op jit(solution)/shard_map/ppermute | solution.py:414
  66.5 1.9 %shard_map.82.own_ref = bf16[1056,128]{1,0:T(8,128)(2,1)S(1)} custom-call(s32[2]{0:T(128)S(1)} %pad_add_fusion.place_ref, bf16[16,128,2048]{2,1,0:T(8,128)(2,1)S(1)} %copy-done.1, bf16[528,128]{1,0:T(8,128)(2,1)S(1)} %shard_map.65.after_ref.refs_0_, bf16[528,128]{1,0:T(8,128)(2,1)S(1)} %shard_map.68.refs_1_), custom_call_target="tpu_custom_call" | custom-call | flops 67108864 | bytes 2097152 | tf_op jit(solution)/shard_map/pallas_call | solution.py:250
  69.7 3.0 %collective-permute-done.24.behind_ref = bf16[1056,128]{1,0:T(8,128)(2,1)S(1)} collective-permute-done((bf16[1056,128]{1,0:T(8,128)(2,1)S(1)}, bf16[1056,128]{1,0:T(8,128)(2,1)S(1)}, u32[]{:S(2)}, u32[]{:S(2)}) %collective-permute-start.24) | collective-permute-done | bytes 270368 | tf_op jit(solution)/shard_map/ppermute | solution.py:414
  73.6 1.8 %collective-permute-start.27 = (bf16[272,128]{1,0:T(8,128)(2,1)S(1)}, bf16[272,128]{1,0:T(8,128)(2,1)S(1)}, u32[]{:S(2)}, u32[]{:S(2)}) collective-permute-start(bf16[272,128]{1,0:T(8,128)(2,1)S(1)} %get-tuple-element.48), channel_id=1, source_target_pairs={{0,24},{8,16},{16,8},{24,0},{1,25},{9,17},{17,9},{25,1},{2,26},{10... | collective-permute-start | bytes 208904 | tf_op jit(solution)/shard_map/ppermute | solution.py:383
  75.4 1.7 %shard_map.84 = (f32[4,256,128]{2,1,0:T(8,128)S(1)}, f32[4,16,128]{2,1,0:T(8,128)S(1)}) custom-call(s32[2]{0:T(128)S(1)} %pad_add_fusion.place_ref, bf16[256,128]{1,0:T(8,128)(2,1)S(1)} %get-tuple-element.27.refs_0_, bf16[256,128]{1,0:T(8,128)(2,1)S(1)} %get-tuple-element.28.refs_1_, bf16[256,128]{1,0:T(8,128)(2,1)S(1)} %get-tuple-element.35.refs_2_, ...), custom_call_target="tpu_custom_call" | custom-call | flops 67108864 | bytes 786432 | tf_op jit(solution)/shard_map/pallas_call | solution.py:136
  79.3 1.6 %shard_map.87 = bf16[4,4,8192]{2,1,0:T(4,128)(2,1)} custom-call(s32[2]{0:T(128)S(1)} %pad_add_fusion.place_ref, bf16[2,4,8192]{2,1,0:T(4,128)(2,1)S(1)} %shard_map.85.refs_0_, bf16[272,128]{1,0:T(8,128)(2,1)S(1)} %collective-permute-done.26.refs_1_, bf16[272,128]{1,0:T(8,128)(2,1)S(1)} %collective-permute-done.27.refs_2_, ...), custom_call_target="tpu_custom_call" | custom-call | bytes 524288 | tf_op jit(solution)/shard_map/pallas_call | solution.py:356
  (68 shorter events, 32.2 us)
Async XLA Ops:
  3.7 8.0 %collective-permute-start.2 = (bf16[528,128]{1,0:T(8,128)(2,1)S(1)}, bf16[528,128]{1,0:T(8,128)(2,1)S(1)}, u32[]{:S(2)}, u32[]{:S(2)}) collective-permute-start(bf16[528,128]{1,0:T(8,128)(2,1)S(1)} %shard_map.65.after_ref.refs_0_), channel_id=1, source_target_pairs={{2,0},{4,2},{6,4},{7,6},{5,7},{3,5},{1,3},{0,1},{10,8},{12,10},{14... | collective-permute-start | bytes 405512 | tf_op jit(solution)/shard_map/ppermute | solution.py:398
  6.2 5.7 %collective-permute-start.1 = (bf16[528,128]{1,0:T(8,128)(2,1)S(1)}, bf16[528,128]{1,0:T(8,128)(2,1)S(1)}, u32[]{:S(2)}, u32[]{:S(2)}) collective-permute-start(bf16[528,128]{1,0:T(8,128)(2,1)S(1)} %shard_map.65.after_ref.refs_0_), channel_id=1, source_target_pairs={{0,2},{2,4},{4,6},{6,7},{7,5},{5,3},{3,1},{1,0},{8,10},{10,12},{12... | collective-permute-start | bytes 405512 | tf_op jit(solution)/shard_map/ppermute | solution.py:397
  6.4 5.5 %collective-permute-start.9 = (bf16[256,128]{1,0:T(8,128)(2,1)S(1)}, bf16[256,128]{1,0:T(8,128)(2,1)S(1)}, u32[]{:S(2)}, u32[]{:S(2)}) collective-permute-start(bf16[256,128]{1,0:T(8,128)(2,1)S(1)} %get-tuple-element.35.refs_2_), channel_id=1, source_target_pairs={{0,16},{8,24},{16,0},{24,8},{1,17},{9,25},{17,1},{25,9},{2,18},{10... | collective-permute-start | bytes 196616 | tf_op jit(solution)/shard_map/ppermute | solution.py:383
  12.5 5.5 %collective-permute-start.12 = (bf16[528,128]{1,0:T(8,128)(2,1)S(1)}, bf16[528,128]{1,0:T(8,128)(2,1)S(1)}, u32[]{:S(2)}, u32[]{:S(2)}) collective-permute-start(bf16[528,128]{1,0:T(8,128)(2,1)S(1)} %shard_map.68.refs_1_), channel_id=1, source_target_pairs={{2,0},{4,2},{6,4},{7,6},{5,7},{3,5},{1,3},{0,1},{10,8},{12,10},{14... | collective-permute-start | bytes 405512 | tf_op jit(solution)/shard_map/ppermute | solution.py:398
  14.1 6.5 %collective-permute-start.11 = (bf16[528,128]{1,0:T(8,128)(2,1)S(1)}, bf16[528,128]{1,0:T(8,128)(2,1)S(1)}, u32[]{:S(2)}, u32[]{:S(2)}) collective-permute-start(bf16[528,128]{1,0:T(8,128)(2,1)S(1)} %shard_map.68.refs_1_), channel_id=1, source_target_pairs={{0,2},{2,4},{4,6},{6,7},{7,5},{5,3},{3,1},{1,0},{8,10},{10,12},{12... | collective-permute-start | bytes 405512 | tf_op jit(solution)/shard_map/ppermute | solution.py:397
  14.6 8.9 %collective-permute-start.3 = (bf16[528,128]{1,0:T(8,128)(2,1)S(1)}, bf16[528,128]{1,0:T(8,128)(2,1)S(1)}, u32[]{:S(2)}, u32[]{:S(2)}) collective-permute-start(bf16[528,128]{1,0:T(8,128)(2,1)S(1)} %collective-permute-done.1.refs_3_.refs_0_), channel_id=1, source_target_pairs={{0,2},{2,4},{4,6},{6,7},{7,5},{5,3},{3,1},{1,0},{8,10},{10,12},{12... | collective-permute-start | bytes 405512 | tf_op jit(solution)/shard_map/ppermute | solution.py:397
  16.2 7.3 %collective-permute-start.4 = (bf16[528,128]{1,0:T(8,128)(2,1)S(1)}, bf16[528,128]{1,0:T(8,128)(2,1)S(1)}, u32[]{:S(2)}, u32[]{:S(2)}) collective-permute-start(bf16[528,128]{1,0:T(8,128)(2,1)S(1)} %collective-permute-done.2.refs_4_.refs_0_), channel_id=1, source_target_pairs={{2,0},{4,2},{6,4},{7,6},{5,7},{3,5},{1,3},{0,1},{10,8},{12,10},{14... | collective-permute-start | bytes 405512 | tf_op jit(solution)/shard_map/ppermute | solution.py:398
  20.6 6.1 %collective-permute-start.13 = (bf16[528,128]{1,0:T(8,128)(2,1)S(1)}, bf16[528,128]{1,0:T(8,128)(2,1)S(1)}, u32[]{:S(2)}, u32[]{:S(2)}) collective-permute-start(bf16[528,128]{1,0:T(8,128)(2,1)S(1)} %collective-permute-done.11.refs_1_), channel_id=1, source_target_pairs={{0,2},{2,4},{4,6},{6,7},{7,5},{5,3},{3,1},{1,0},{8,10},{10,12},{12... | collective-permute-start | bytes 405512 | tf_op jit(solution)/shard_map/ppermute | solution.py:397
  21.1 5.6 %collective-permute-start.14 = (bf16[528,128]{1,0:T(8,128)(2,1)S(1)}, bf16[528,128]{1,0:T(8,128)(2,1)S(1)}, u32[]{:S(2)}, u32[]{:S(2)}) collective-permute-start(bf16[528,128]{1,0:T(8,128)(2,1)S(1)} %collective-permute-done.12.refs_1_), channel_id=1, source_target_pairs={{2,0},{4,2},{6,4},{7,6},{5,7},{3,5},{1,3},{0,1},{10,8},{12,10},{14... | collective-permute-start | bytes 405512 | tf_op jit(solution)/shard_map/ppermute | solution.py:398
  23.5 6.4 %collective-permute-start.5 = (bf16[528,128]{1,0:T(8,128)(2,1)S(1)}, bf16[528,128]{1,0:T(8,128)(2,1)S(1)}, u32[]{:S(2)}, u32[]{:S(2)}) collective-permute-start(bf16[528,128]{1,0:T(8,128)(2,1)S(1)} %collective-permute-done.3.refs_0_), channel_id=1, source_target_pairs={{0,2},{2,4},{4,6},{6,7},{7,5},{5,3},{3,1},{1,0},{8,10},{10,12},{12... | collective-permute-start | bytes 405512 | tf_op jit(solution)/shard_map/ppermute | solution.py:397
  24.0 5.9 %collective-permute-start.6 = (bf16[528,128]{1,0:T(8,128)(2,1)S(1)}, bf16[528,128]{1,0:T(8,128)(2,1)S(1)}, u32[]{:S(2)}, u32[]{:S(2)}) collective-permute-start(bf16[528,128]{1,0:T(8,128)(2,1)S(1)} %collective-permute-done.4.refs_0_), channel_id=1, source_target_pairs={{2,0},{4,2},{6,4},{7,6},{5,7},{3,5},{1,3},{0,1},{10,8},{12,10},{14... | collective-permute-start | bytes 405512 | tf_op jit(solution)/shard_map/ppermute | solution.py:398
  26.8 5.5 %collective-permute-start.15 = (bf16[528,128]{1,0:T(8,128)(2,1)S(1)}, bf16[528,128]{1,0:T(8,128)(2,1)S(1)}, u32[]{:S(2)}, u32[]{:S(2)}) collective-permute-start(bf16[528,128]{1,0:T(8,128)(2,1)S(1)} %collective-permute-done.13.refs_1_), channel_id=1, source_target_pairs={{0,2},{2,4},{4,6},{6,7},{7,5},{5,3},{3,1},{1,0},{8,10},{10,12},{12... | collective-permute-start | bytes 405512 | tf_op jit(solution)/shard_map/ppermute | solution.py:397
  28.3 6.1 %collective-permute-start.16 = (bf16[528,128]{1,0:T(8,128)(2,1)S(1)}, bf16[528,128]{1,0:T(8,128)(2,1)S(1)}, u32[]{:S(2)}, u32[]{:S(2)}) collective-permute-start(bf16[528,128]{1,0:T(8,128)(2,1)S(1)} %collective-permute-done.14.refs_1_), channel_id=1, source_target_pairs={{2,0},{4,2},{6,4},{7,6},{5,7},{3,5},{1,3},{0,1},{10,8},{12,10},{14... | collective-permute-start | bytes 405512 | tf_op jit(solution)/shard_map/ppermute | solution.py:398
  34.4 6.3 %collective-permute-start.20 = (bf16[528,128]{1,0:T(8,128)(2,1)S(1)}, bf16[528,128]{1,0:T(8,128)(2,1)S(1)}, u32[]{:S(2)}, u32[]{:S(2)}) collective-permute-start(bf16[528,128]{1,0:T(8,128)(2,1)S(1)} %collective-permute-done.16.refs_1_), channel_id=1, source_target_pairs={{2,0},{4,2},{6,4},{7,6},{5,7},{3,5},{1,3},{0,1},{10,8},{12,10},{14... | collective-permute-start | bytes 405512 | tf_op jit(solution)/shard_map/ppermute | solution.py:398
  36.8 7.7 %collective-permute-start.8 = (bf16[528,128]{1,0:T(8,128)(2,1)S(1)}, bf16[528,128]{1,0:T(8,128)(2,1)S(1)}, u32[]{:S(2)}, u32[]{:S(2)}) collective-permute-start(bf16[528,128]{1,0:T(8,128)(2,1)S(1)} %shard_map.66), channel_id=1, source_target_pairs={{0,2},{2,4},{4,6},{6,7},{7,5},{5,3},{3,1},{1,0},{8,10},{10,12},{12... | collective-permute-start | bytes 405512 | tf_op jit(solution)/shard_map/ppermute | solution.py:413
  41.5 6.5 %collective-permute-start.21 = (bf16[528,128]{1,0:T(8,128)(2,1)S(1)}, bf16[528,128]{1,0:T(8,128)(2,1)S(1)}, u32[]{:S(2)}, u32[]{:S(2)}) collective-permute-start(bf16[528,128]{1,0:T(8,128)(2,1)S(1)} %shard_map.75), channel_id=1, source_target_pairs={{2,0},{4,2},{6,4},{7,6},{5,7},{3,5},{1,3},{0,1},{10,8},{12,10},{14... | collective-permute-start | bytes 405512 | tf_op jit(solution)/shard_map/ppermute | solution.py:414
  44.7 9.1 %collective-permute-start.17 = (bf16[1056,128]{1,0:T(8,128)(2,1)S(1)}, bf16[1056,128]{1,0:T(8,128)(2,1)S(1)}, u32[]{:S(2)}, u32[]{:S(2)}) collective-permute-start(bf16[1056,128]{1,0:T(8,128)(2,1)S(1)} %shard_map.70), channel_id=1, source_target_pairs={{0,2},{2,4},{4,6},{6,7},{7,5},{5,3},{3,1},{1,0},{8,10},{10,12},{12... | collective-permute-start | bytes 811016 | tf_op jit(solution)/shard_map/ppermute | solution.py:413
  48.3 8.8 %collective-permute-start.22 = (bf16[1056,128]{1,0:T(8,128)(2,1)S(1)}, bf16[1056,128]{1,0:T(8,128)(2,1)S(1)}, u32[]{:S(2)}, u32[]{:S(2)}) collective-permute-start(bf16[1056,128]{1,0:T(8,128)(2,1)S(1)} %shard_map.77), channel_id=1, source_target_pairs={{2,0},{4,2},{6,4},{7,6},{5,7},{3,5},{1,3},{0,1},{10,8},{12,10},{14... | collective-permute-start | bytes 811016 | tf_op jit(solution)/shard_map/ppermute | solution.py:414
  54.3 8.4 %collective-permute-start.18 = (bf16[1056,128]{1,0:T(8,128)(2,1)S(1)}, bf16[1056,128]{1,0:T(8,128)(2,1)S(1)}, u32[]{:S(2)}, u32[]{:S(2)}) collective-permute-start(bf16[1056,128]{1,0:T(8,128)(2,1)S(1)} %shard_map.72), channel_id=1, source_target_pairs={{0,2},{2,4},{4,6},{6,7},{7,5},{5,3},{3,1},{1,0},{8,10},{10,12},{12... | collective-permute-start | bytes 811016 | tf_op jit(solution)/shard_map/ppermute | solution.py:413
  57.5 8.2 %collective-permute-start.23 = (bf16[1056,128]{1,0:T(8,128)(2,1)S(1)}, bf16[1056,128]{1,0:T(8,128)(2,1)S(1)}, u32[]{:S(2)}, u32[]{:S(2)}) collective-permute-start(bf16[1056,128]{1,0:T(8,128)(2,1)S(1)} %shard_map.79), channel_id=1, source_target_pairs={{2,0},{4,2},{6,4},{7,6},{5,7},{3,5},{1,3},{0,1},{10,8},{12,10},{14... | collective-permute-start | bytes 811016 | tf_op jit(solution)/shard_map/ppermute | solution.py:414
  63.2 6.5 %collective-permute-start.19 = (bf16[1056,128]{1,0:T(8,128)(2,1)S(1)}, bf16[1056,128]{1,0:T(8,128)(2,1)S(1)}, u32[]{:S(2)}, u32[]{:S(2)}) collective-permute-start(bf16[1056,128]{1,0:T(8,128)(2,1)S(1)} %shard_map.74), channel_id=1, source_target_pairs={{0,2},{2,4},{4,6},{6,7},{7,5},{5,3},{3,1},{1,0},{8,10},{10,12},{12... | collective-permute-start | bytes 811016 | tf_op jit(solution)/shard_map/ppermute | solution.py:413
  66.2 6.5 %collective-permute-start.24 = (bf16[1056,128]{1,0:T(8,128)(2,1)S(1)}, bf16[1056,128]{1,0:T(8,128)(2,1)S(1)}, u32[]{:S(2)}, u32[]{:S(2)}) collective-permute-start(bf16[1056,128]{1,0:T(8,128)(2,1)S(1)} %shard_map.81), channel_id=1, source_target_pairs={{2,0},{4,2},{6,4},{7,6},{5,7},{3,5},{1,3},{0,1},{10,8},{12,10},{14... | collective-permute-start | bytes 811016 | tf_op jit(solution)/shard_map/ppermute | solution.py:414
  73.5 5.0 %collective-permute-start.26 = (bf16[272,128]{1,0:T(8,128)(2,1)S(1)}, bf16[272,128]{1,0:T(8,128)(2,1)S(1)}, u32[]{:S(2)}, u32[]{:S(2)}) collective-permute-start(bf16[272,128]{1,0:T(8,128)(2,1)S(1)} %get-tuple-element.47), channel_id=1, source_target_pairs={{0,16},{8,24},{16,0},{24,8},{1,17},{9,25},{17,1},{25,9},{2,18},{10... | collective-permute-start | bytes 208904 | tf_op jit(solution)/shard_map/ppermute | solution.py:383
  73.6 5.7 %collective-permute-start.27 = (bf16[272,128]{1,0:T(8,128)(2,1)S(1)}, bf16[272,128]{1,0:T(8,128)(2,1)S(1)}, u32[]{:S(2)}, u32[]{:S(2)}) collective-permute-start(bf16[272,128]{1,0:T(8,128)(2,1)S(1)} %get-tuple-element.48), channel_id=1, source_target_pairs={{0,24},{8,16},{16,8},{24,0},{1,25},{9,17},{17,9},{25,1},{2,26},{10... | collective-permute-start | bytes 208904 | tf_op jit(solution)/shard_map/ppermute | solution.py:383
  (8 other events, 58.6 us)

commit v6 on v5

--- a/solution.py
+++ b/solution.py
@@ -156,8 +156,8 @@
     )
 
 
-def payload_kernel(after, counts_ref, pages_ref, *refs):
-    visits, out = refs[: len(refs) - 1 - after], refs[-1]
+def payload_kernel(counts_ref, pages_ref, *refs):
+    visits, out = refs[:-1], refs[-1]
     for number, visit in enumerate(visits):
         out[number * BODY : (number + 1) * BODY, :] = visit[...]
     tables = [counts_ref[...].astype(F32), pages_ref[...].astype(F32)]
@@ -167,16 +167,35 @@
     out[len(visits) * BODY :, :] = jnp.concatenate(tables, axis=0).astype(BF16)
 
 
-def payload(lists, visits, after=()):
+def payload(lists, visits):
     rows = len(visits) * BODY + list_rows(lists[0].shape[0])
     return pl.pallas_call(
-        functools.partial(payload_kernel, len(after)),
+        payload_kernel,
         out_shape=jax.ShapeDtypeStruct((rows, HD), BF16),
-        in_specs=[IN_VMEM] * (2 + len(visits) + len(after)),
+        in_specs=[IN_VMEM] * (2 + len(visits)),
         out_specs=IN_VMEM,
         compiler_params=params(),
         cost_estimate=cost(0, 4 * rows * HD),
-    )(*lists, *visits, *after)
+    )(*lists, *visits)
+
+
+def join_kernel(count, *refs):
+    out, start = refs[-1], 0
+    for ref in refs[:count]:
+        out[start : start + ref.shape[0], :] = ref[...]
+        start += ref.shape[0]
+
+
+def join(arrays, after):
+    rows = sum(array.shape[0] for array in arrays)
+    return pl.pallas_call(
+        functools.partial(join_kernel, len(arrays)),
+        out_shape=jax.ShapeDtypeStruct((rows, HD), BF16),
+        in_specs=[IN_VMEM] * (len(arrays) + len(after)),
+        out_specs=IN_VMEM,
+        compiler_params=params(),
+        cost_estimate=cost(0, 4 * rows * HD),
+    )(*arrays, *after)
 
 
 def touch_kernel(after_ref, cache_ref, out_ref):
@@ -196,8 +215,10 @@
 
 def item_kernel(slots, visitors, place_ref, cache_ref, *refs):
     sides = len(slots)
-    query_refs, (out_ref, level_ref, code_ref) = refs[:sides], refs[sides:]
+    arrays, (out_ref, level_ref, code_ref) = refs[:-3], refs[-3:]
     each = len(slots[0])
+    unit = sum(ref.shape[0] for ref in arrays) // sides
+    query_refs = [ref.at[at : at + unit] for ref in arrays for at in range(0, ref.shape[0], unit)]
     for side, query_ref in enumerate(query_refs):
         lists = query_ref.shape[0] - each * BODY
         rows = lax.broadcasted_iota(jnp.int32, (lists, LANES), 0)
@@ -250,7 +271,7 @@
     return pl.pallas_call(
         functools.partial(item_kernel, slots, visitors),
         out_shape=jax.ShapeDtypeStruct((count // 2 * PAIR, HD), BF16),
-        in_specs=[IN_SMEM] + [IN_VMEM] * (1 + len(slots)),
+        in_specs=[IN_SMEM] + [IN_VMEM] * (1 + len(payloads)),
         out_specs=IN_VMEM,
         scratch_shapes=[pltpu.VMEM((count, HALF, LANES), F32), pltpu.SMEM((count,), jnp.int32)],
         compiler_params=params(),
@@ -277,11 +298,12 @@
     return values
 
 
-def merge_kernel(base, arrived_ref, own_ref, out_ref):
+def merge_kernel(base, arrived_ref, own_ref, *outs):
     arrived_pairs = arrived_ref.shape[0] // PAIR
-    for pair in range(out_ref.shape[0] // PAIR):
-        part = slice(pair * PAIR, (pair + 1) * PAIR)
-        own, out = own_ref.at[part], out_ref.at[part]
+    each = outs[0].shape[0] // PAIR
+    for pair in range(own_ref.shape[0] // PAIR):
+        own = own_ref.at[pair * PAIR : (pair + 1) * PAIR]
+        out = outs[pair // each].at[pair % each * PAIR : (pair % each + 1) * PAIR]
         if not base <= pair < base + arrived_pairs:
             out[...] = own[...]
             continue
@@ -295,12 +317,13 @@
         out[2 * BODY : PAIR, :] = pack_stats(level)
 
 
-def merge(arrived, own, base):
+def merge(arrived, own, base, outs=1):
+    rows = own.shape[0] // outs
     return pl.pallas_call(
         functools.partial(merge_kernel, base),
-        out_shape=jax.ShapeDtypeStruct(own.shape, BF16),
+        out_shape=[jax.ShapeDtypeStruct((rows, HD), BF16)] * outs,
         in_specs=[IN_VMEM, IN_VMEM],
-        out_specs=IN_VMEM,
+        out_specs=[IN_VMEM] * outs,
         compiler_params=params(),
         cost_estimate=cost(0, 6 * own.size),
     )(arrived, own)
@@ -308,8 +331,8 @@
 
 def gather_kernel(base, ahead_ref, behind_ref, own_ref, *outs):
     for pair in range(len(outs) // 2):
-        part = slice((base + pair) * PAIR, (base + pair + 1) * PAIR)
-        sources = [ref.at[part] for ref in (own_ref, ahead_ref, behind_ref)]
+        part = slice(pair * PAIR, (pair + 1) * PAIR)
+        sources = [own_ref.at[(base + pair) * PAIR : (base + pair + 1) * PAIR], ahead_ref.at[part], behind_ref.at[part]]
         shares, level = blend([unpack_stats(ref[2 * BODY : PAIR, :]) for ref in sources])
         values = [mix(shares, sources, second * BODY, second * SECOND) for second in range(2)]
         for second in range(2):
@@ -321,7 +344,8 @@
             out[BODY:LONE, :] = pack_stats(here)
 
 
-def gather(ahead, behind, own, base, pairs):
+def gather(ahead, behind, own, base):
+    pairs = ahead.shape[0] // PAIR
     return pl.pallas_call(
         functools.partial(gather_kernel, base),
         out_shape=[jax.ShapeDtypeStruct((LONE, HD), BF16)] * (2 * pairs),
@@ -348,7 +372,7 @@
             out_ref[row, :, head * HD : (head + 1) * HD] = tile.astype(BF16)
     for ref in earlier:
         for d in range(ref.shape[0]):
-            out_ref[place_ref[0] ^ d] = ref[d]
+            out_ref[place_ref[0] ^ (len(parts) + d)] = ref[d]
 
 
 def final(place, parts, first, new_out, new_level, earlier=()):
@@ -393,33 +417,43 @@
     slots = [list(range(cut)), list(range(cut, requests))]
     owned = functools.partial(items, place, kv_cache, visitors=requests)
 
-    def exchange(both, half, last=False):
-        below = lax.ppermute(both[0], "cache", forward) if half == 0 or not last else None
-        above = lax.ppermute(both[1], "cache", backward) if half == 1 or not last else None
-        return (below, above) if last else lax.optimization_barrier((below, above))
-
-    first = payload(lists, visits[:cut])
-    halves = [exchange((first, first), 0)]
-    second = payload(lists, visits[cut:], [touch(kv_cache, first), *halves[0]])
-    halves.append(exchange((second, second), 1))
-    parts = {0: owned([first, second], slots)}
+    def up(array):
+        return lax.ppermute(array, "cache", forward)
+
+    def down(array):
+        return lax.ppermute(array, "cache", backward)
+
+    def after(array, *others):
+        return lax.optimization_barrier((array, others))[0]
+
+    blocks = [payload(lists, visits[:cut])]
+    front = up(blocks[0])
+    blocks.append(payload(lists, visits[cut:]))
+    below = join([front, up(after(blocks[1], front))], [touch(kv_cache, blocks[1])])
+    above = down(join(blocks, []))
+    parts = {0: owned(blocks, slots)}
+    unit = blocks[0].shape[0]
     for step in range(1, reach):
-        parts[-step] = owned([halves[0][0], halves[1][0]], slots)
-        parts[step] = owned([halves[0][1], halves[1][1]], slots)
-        halves = [exchange(halves[half], half, step == reach - 1) for half in range(2)]
-
-    ahead, behind = owned([halves[0][0]], slots[:1]), owned([halves[1][1]], slots[1:])
-    for step in range(reach - 1, -1, -1):
-        ahead = lax.ppermute(ahead, "cache", forward)
-        behind = lax.ppermute(behind, "cache", backward)
-        if step > 0:
-            base = cut // 2 if step == reach - 1 else 0
-            ahead, behind = merge(ahead, parts[step], 0), merge(behind, parts[-step], base)
-    back = gather(ahead, behind, parts[0], cut // 2, cut // 2)
-    front = gather(ahead, behind, parts[0], 0, cut // 2)
-    home = [swap(part, d) for d, part in enumerate(list(front) + list(back))]
-    early = final(place, home[:cut], 0, new_out, new_level)
-    return final(place, home[cut:], cut, new_out, new_level, [early])
+        last = step == reach - 1
+        parts[-step] = owned([below], slots)
+        parts[step] = owned([above], slots)
+        ready = [] if step == 1 else [parts[step - 1], parts[0]]
+        below, above = after(below, *ready), after(above, parts[-step])
+        below, above = up(below[:unit] if last else below), down(above[unit:] if last else above)
+
+    ahead, behind = [owned([below], slots[:1])], [owned([above], slots[1:])]
+    for step in range(reach - 1, 0, -1):
+        base = cut // 2 if step == reach - 1 else 0
+        outs = 2 if step == 1 else 1
+        own = after(parts[step], new_level) if step == 1 else parts[step]
+        ahead = merge(up(ahead[0]), own, 0, outs)
+        behind = merge(down(behind[0]), parts[-step], base, outs)
+    back = gather(up(ahead[1]), down(behind[1]), parts[0], cut // 2)
+    front = gather(up(ahead[0]), down(behind[0]), after(parts[0], *back), 0)
+    home = [swap(part, d) for d, part in enumerate(front)]
+    home = home + [swap(part, cut + d) for d, part in enumerate(back)]
+    early = final(place, home[cut:], cut, new_out, new_level)
+    return final(place, home[:cut], 0, new_out, new_level, [early])
 
 
 def solution(mesh):

time: 80.9 us -> 85.7 us (1.059)
  the two profiles are of different devices: /device:TPU:0 before, /device:TPU:17 now
where the time goes in v6:
time: 85.7 us; the launch traced here: 84 us
  starting transfers between devices  36.5 us (43%)
  waiting for transfers between devices  20.4 us (24%)
  Pallas kernels  18.9 us (22%)
  local copies, waits for them, and re-layouts  6.44 us (8%)
  other arithmetic  1.59 us (2%)
    ppermute x10, starting transfers between devices, up(): return lax.ppermute(array, 'cache', forward)  20.6 us
    ppermute x6, starting transfers between devices, swap(): lax.ppermute(array, 'grp', [(g, g ^ d) for g in range(groups)])  14.6 us
    pallas_call x9, Pallas kernels, items(): pl.pallas_call(functools.partial(item_kernel, slots, visitors), out_shape...  11 us
    ppermute x10, waiting for transfers between devices, up(): return lax.ppermute(array, 'cache', forward)  9.73 us
    ppermute x9, waiting for transfers between devices, down(): return lax.ppermute(array, 'cache', backward)  7.36 us
    unnamed x8, local copies, waits for them, and re-layouts  6.42 us
    ppermute x6, waiting for transfers between devices, swap(): lax.ppermute(array, 'grp', [(g, g ^ d) for g in range(groups)])  3.35 us
    pallas_call x2, Pallas kernels, final(): pl.pallas_call(functools.partial(final_kernel, first, len(earlier)), out_...  2.4 us
  transfers between devices with their start and end apart: 25, of which 14 were waited for; matrix products, arithmetic and copies ran while one was open for 2% of the time, Pallas kernels for 20%

profile of v6, /device:TPU:17, one launch (start us, length us, event | category | flops | bytes accessed | tf_op | source)
XLA Modules:
  0.0 84.0 jit_solution(2780377771202593245)
XLA Ops:
  5.6 1.3 %collective-permute-start.1 = (bf16[528,128]{1,0:T(8,128)(2,1)S(1)}, bf16[528,128]{1,0:T(8,128)(2,1)S(1)}, u32[]{:S(2)}, u32[]{:S(2)}) collective-permute-start(bf16[528,128]{1,0:T(8,128)(2,1)S(1)} %shard_map.65.refs_0_), channel_id=1, source_target_pairs={{0,2},{2,4},{4,6},{6,7},{7,5},{5,3},{3,1},{1,0},{8,10},{10,12},{12... | collective-permute-start | bytes 405512 | tf_op jit(solution)/shard_map/ppermute | solution.py:421
  7.9 2.8 %collective-permute-done.1.refs_0_ = bf16[528,128]{1,0:T(8,128)(2,1)S(1)} collective-permute-done((bf16[528,128]{1,0:T(8,128)(2,1)S(1)}, bf16[528,128]{1,0:T(8,128)(2,1)S(1)}, u32[]{:S(2)}, u32[]{:S(2)}) %collective-permute-start.1) | collective-permute-done | bytes 135200 | tf_op jit(solution)/shard_map/ppermute | solution.py:421
  12.0 3.4 %copy-done = bf16[16,128,2048]{2,1,0:T(8,128)(2,1)S(1)} copy-done((bf16[16,128,2048]{2,1,0:T(8,128)(2,1)S(1)}, bf16[16,128,2048]{2,1,0:T(8,128)(2,1)}, u32[]{:S(2)}) %copy-start) | copy-done | bytes 8388632
  16.7 2.1 %copy-done.1 = bf16[16,128,2048]{2,1,0:T(8,128)(2,1)S(1)} copy-done((bf16[16,128,2048]{2,1,0:T(8,128)(2,1)S(1)}, bf16[16,128,2048]{2,1,0:T(8,128)(2,1)}, u32[]{:S(2)}) %copy-start.1) | copy-done | bytes 8388632
  18.8 1.4 %shard_map.72.own_ref = bf16[1056,128]{1,0:T(8,128)(2,1)S(1)} custom-call(s32[2]{0:T(128)S(1)} %pad_add_fusion.place_ref, bf16[16,128,2048]{2,1,0:T(8,128)(2,1)S(1)} %copy-done.1, bf16[1056,128]{1,0:T(8,128)(2,1)S(1)} %shard_map.68.refs_0_), custom_call_target="tpu_custom_call" | custom-call | flops 67108864 | bytes 2097152 | tf_op jit(solution)/shard_map/pallas_call | solution.py:271
  20.4 1.4 %shard_map.71.own_ref = bf16[1056,128]{1,0:T(8,128)(2,1)S(1)} custom-call(s32[2]{0:T(128)S(1)} %pad_add_fusion.place_ref, bf16[16,128,2048]{2,1,0:T(8,128)(2,1)S(1)} %copy-done.1, bf16[528,128]{1,0:T(8,128)(2,1)S(1)} %shard_map.65.refs_0_, bf16[528,128]{1,0:T(8,128)(2,1)S(1)} %shard_map.66.after_ref.refs_1_), custom_call_target="tpu_custom_call" | custom-call | flops 67108864 | bytes 2097152 | tf_op jit(solution)/shard_map/pallas_call | solution.py:271
  22.7 3.5 %collective-permute-start.7 = (bf16[1056,128]{1,0:T(8,128)(2,1)S(1)}, bf16[1056,128]{1,0:T(8,128)(2,1)S(1)}, u32[]{:S(2)}, u32[]{:S(2)}) collective-permute-start(bf16[1056,128]{1,0:T(8,128)(2,1)S(1)} %collective-permute-done.5.refs_0_), channel_id=1, source_target_pairs={{0,2},{2,4},{4,6},{6,7},{7,5},{5,3},{3,1},{1,0},{8,10},{10,12},{12... | collective-permute-start | bytes 811016 | tf_op jit(solution)/shard_map/ppermute | solution.py:421
  27.9 2.8 %collective-permute-done.7.refs_0_ = bf16[1056,128]{1,0:T(8,128)(2,1)S(1)} collective-permute-done((bf16[1056,128]{1,0:T(8,128)(2,1)S(1)}, bf16[1056,128]{1,0:T(8,128)(2,1)S(1)}, u32[]{:S(2)}, u32[]{:S(2)}) %collective-permute-start.7) | collective-permute-done | bytes 270368 | tf_op jit(solution)/shard_map/ppermute | solution.py:421
  30.7 1.9 %shard_map.81.own_ref = bf16[1056,128]{1,0:T(8,128)(2,1)S(1)} custom-call(s32[2]{0:T(128)S(1)} %pad_add_fusion.place_ref, bf16[16,128,2048]{2,1,0:T(8,128)(2,1)S(1)} %copy-done.1, bf16[1056,128]{1,0:T(8,128)(2,1)S(1)} %collective-permute-done.7.refs_0_), custom_call_target="tpu_custom_call" | custom-call | flops 67108864 | bytes 2097152 | tf_op jit(solution)/shard_map/pallas_call | solution.py:271
  32.5 1.4 %collective-permute-done.11.refs_0_ = bf16[1056,128]{1,0:T(8,128)(2,1)S(1)} collective-permute-done((bf16[1056,128]{1,0:T(8,128)(2,1)S(1)}, bf16[1056,128]{1,0:T(8,128)(2,1)S(1)}, u32[]{:S(2)}, u32[]{:S(2)}) %collective-permute-start.11) | collective-permute-done | bytes 270368 | tf_op jit(solution)/shard_map/ppermute | solution.py:424
  35.2 2.7 %collective-permute-start.9 = (bf16[528,128]{1,0:T(8,128)(2,1)S(1)}, bf16[528,128]{1,0:T(8,128)(2,1)S(1)}, u32[]{:S(2)}, u32[]{:S(2)}) collective-permute-start(bf16[528,128]{1,0:T(8,128)(2,1)S(1)} %slice.6), channel_id=1, source_target_pairs={{0,2},{2,4},{4,6},{6,7},{7,5},{5,3},{3,1},{1,0},{8,10},{10,12},{12... | collective-permute-start | bytes 405512 | tf_op jit(solution)/shard_map/ppermute | solution.py:421
  40.7 2.6 %collective-permute-start.10 = (bf16[528,128]{1,0:T(8,128)(2,1)S(1)}, bf16[528,128]{1,0:T(8,128)(2,1)S(1)}, u32[]{:S(2)}, u32[]{:S(2)}) collective-permute-start(bf16[528,128]{1,0:T(8,128)(2,1)S(1)} %shard_map.74), channel_id=1, source_target_pairs={{0,2},{2,4},{4,6},{6,7},{7,5},{5,3},{3,1},{1,0},{8,10},{10,12},{12... | collective-permute-start | bytes 405512 | tf_op jit(solution)/shard_map/ppermute | solution.py:421
  43.8 1.4 %shard_map.76.own_ref = bf16[1056,128]{1,0:T(8,128)(2,1)S(1)} custom-call(s32[2]{0:T(128)S(1)} %pad_add_fusion.place_ref, bf16[16,128,2048]{2,1,0:T(8,128)(2,1)S(1)} %copy-done.1, bf16[1056,128]{1,0:T(8,128)(2,1)S(1)} %collective-permute-done.11.refs_0_), custom_call_target="tpu_custom_call" | custom-call | flops 67108864 | bytes 2097152 | tf_op jit(solution)/shard_map/pallas_call | solution.py:271
  45.6 2.0 %collective-permute-start.12 = (bf16[1056,128]{1,0:T(8,128)(2,1)S(1)}, bf16[1056,128]{1,0:T(8,128)(2,1)S(1)}, u32[]{:S(2)}, u32[]{:S(2)}) collective-permute-start(bf16[1056,128]{1,0:T(8,128)(2,1)S(1)} %shard_map.77), channel_id=1, source_target_pairs={{0,2},{2,4},{4,6},{6,7},{7,5},{5,3},{3,1},{1,0},{8,10},{10,12},{12... | collective-permute-start | bytes 811016 | tf_op jit(solution)/shard_map/ppermute | solution.py:421
  47.6 3.1 %collective-permute-done.17.arrived_ref = bf16[1056,128]{1,0:T(8,128)(2,1)S(1)} collective-permute-done((bf16[1056,128]{1,0:T(8,128)(2,1)S(1)}, bf16[1056,128]{1,0:T(8,128)(2,1)S(1)}, u32[]{:S(2)}, u32[]{:S(2)}) %collective-permute-start.17) | collective-permute-done | bytes 270368 | tf_op jit(solution)/shard_map/ppermute | solution.py:424
  52.9 2.3 %collective-permute-start.13 = (bf16[1056,128]{1,0:T(8,128)(2,1)S(1)}, bf16[1056,128]{1,0:T(8,128)(2,1)S(1)}, u32[]{:S(2)}, u32[]{:S(2)}) collective-permute-start(bf16[1056,128]{1,0:T(8,128)(2,1)S(1)} %shard_map.78), channel_id=1, source_target_pairs={{0,2},{2,4},{4,6},{6,7},{7,5},{5,3},{3,1},{1,0},{8,10},{10,12},{12... | collective-permute-start | bytes 811016 | tf_op jit(solution)/shard_map/ppermute | solution.py:421
  55.1 1.7 %shard_map.79 = (f32[4,256,128]{2,1,0:T(8,128)S(1)}, f32[4,16,128]{2,1,0:T(8,128)S(1)}) custom-call(s32[2]{0:T(128)S(1)} %pad_add_fusion.place_ref, bf16[256,128]{1,0:T(8,128)(2,1)S(1)} %get-tuple-element.27.refs_0_, bf16[256,128]{1,0:T(8,128)(2,1)S(1)} %get-tuple-element.28.refs_1_, bf16[256,128]{1,0:T(8,128)(2,1)S(1)} %get-tuple-element.29.refs_2_, ...), custom_call_target="tpu_custom_call" | custom-call | flops 67108864 | bytes 786432 | tf_op jit(solution)/shard_map/pallas_call | solution.py:136
  56.8 1.9 %collective-permute-done.18.arrived_ref = bf16[1056,128]{1,0:T(8,128)(2,1)S(1)} collective-permute-done((bf16[1056,128]{1,0:T(8,128)(2,1)S(1)}, bf16[1056,128]{1,0:T(8,128)(2,1)S(1)}, u32[]{:S(2)}, u32[]{:S(2)}) %collective-permute-start.18) | collective-permute-done | bytes 270368 | tf_op jit(solution)/shard_map/ppermute | solution.py:424
  59.3 1.8 %collective-permute-done.13.arrived_ref = bf16[1056,128]{1,0:T(8,128)(2,1)S(1)} collective-permute-done((bf16[1056,128]{1,0:T(8,128)(2,1)S(1)}, bf16[1056,128]{1,0:T(8,128)(2,1)S(1)}, u32[]{:S(2)}, u32[]{:S(2)}) %collective-permute-start.13) | collective-permute-done | bytes 270368 | tf_op jit(solution)/shard_map/ppermute | solution.py:421
  61.6 2.2 %collective-permute-start.14 = (bf16[528,128]{1,0:T(8,128)(2,1)S(1)}, bf16[528,128]{1,0:T(8,128)(2,1)S(1)}, u32[]{:S(2)}, u32[]{:S(2)}) collective-permute-start(bf16[528,128]{1,0:T(8,128)(2,1)S(1)} %get-tuple-element.38), channel_id=1, source_target_pairs={{0,2},{2,4},{4,6},{6,7},{7,5},{5,3},{3,1},{1,0},{8,10},{10,12},{12... | collective-permute-start | bytes 405512 | tf_op jit(solution)/shard_map/ppermute | solution.py:421
  63.8 1.5 %collective-permute-start.22 = (bf16[528,128]{1,0:T(8,128)(2,1)S(1)}, bf16[528,128]{1,0:T(8,128)(2,1)S(1)}, u32[]{:S(2)}, u32[]{:S(2)}) collective-permute-start(bf16[528,128]{1,0:T(8,128)(2,1)S(1)} %get-tuple-element.44), channel_id=1, source_target_pairs={{0,2},{2,4},{4,6},{6,7},{7,5},{5,3},{3,1},{1,0},{8,10},{10,12},{12... | collective-permute-start | bytes 405512 | tf_op jit(solution)/shard_map/ppermute | solution.py:421
  67.6 10.5 %collective-permute-start.21 = (bf16[272,128]{1,0:T(8,128)(2,1)S(1)}, bf16[272,128]{1,0:T(8,128)(2,1)S(1)}, u32[]{:S(2)}, u32[]{:S(2)}) collective-permute-start(bf16[272,128]{1,0:T(8,128)(2,1)S(1)} %get-tuple-element.42), channel_id=1, source_target_pairs={{0,24},{8,16},{16,8},{24,0},{1,25},{9,17},{17,9},{25,1},{2,26},{10... | collective-permute-start | bytes 208904 | tf_op jit(solution)/shard_map/ppermute | solution.py:407
  79.0 2.7 %collective-permute-done.21.refs_1_ = bf16[272,128]{1,0:T(8,128)(2,1)S(1)} collective-permute-done((bf16[272,128]{1,0:T(8,128)(2,1)S(1)}, bf16[272,128]{1,0:T(8,128)(2,1)S(1)}, u32[]{:S(2)}, u32[]{:S(2)}) %collective-permute-start.21) | collective-permute-done | bytes 69664 | tf_op jit(solution)/shard_map/ppermute | solution.py:407
  82.5 1.6 %shard_map.89 = bf16[4,4,8192]{2,1,0:T(4,128)(2,1)} custom-call(s32[2]{0:T(128)S(1)} %pad_add_fusion.place_ref, bf16[2,4,8192]{2,1,0:T(4,128)(2,1)S(1)} %shard_map.87.refs_0_, bf16[272,128]{1,0:T(8,128)(2,1)S(1)} %get-tuple-element.47.refs_1_, bf16[272,128]{1,0:T(8,128)(2,1)S(1)} %collective-permute-done.24.refs_2_, ...), custom_call_target="tpu_custom_call" | custom-call | bytes 524288 | tf_op jit(solution)/shard_map/pallas_call | solution.py:380
  (66 shorter events, 24.1 us)
Async XLA Ops:
  1.6 4.0 %collective-permute-start = (bf16[256,128]{1,0:T(8,128)(2,1)S(1)}, bf16[256,128]{1,0:T(8,128)(2,1)S(1)}, u32[]{:S(2)}, u32[]{:S(2)}) collective-permute-start(bf16[256,128]{1,0:T(8,128)(2,1)S(1)} %get-tuple-element.28.refs_1_), channel_id=1, source_target_pairs={{0,8},{8,0},{16,24},{24,16},{1,9},{9,1},{17,25},{25,17},{2,10},{10... | collective-permute-start | bytes 196616 | tf_op jit(solution)/shard_map/ppermute | solution.py:407
  2.4 4.6 %collective-permute-start.2 = (bf16[256,128]{1,0:T(8,128)(2,1)S(1)}, bf16[256,128]{1,0:T(8,128)(2,1)S(1)}, u32[]{:S(2)}, u32[]{:S(2)}) collective-permute-start(bf16[256,128]{1,0:T(8,128)(2,1)S(1)} %get-tuple-element.29.refs_2_), channel_id=1, source_target_pairs={{0,16},{8,24},{16,0},{24,8},{1,17},{9,25},{17,1},{25,9},{2,18},{10... | collective-permute-start | bytes 196616 | tf_op jit(solution)/shard_map/ppermute | solution.py:407
  3.6 4.0 %collective-permute-start.3 = (bf16[256,128]{1,0:T(8,128)(2,1)S(1)}, bf16[256,128]{1,0:T(8,128)(2,1)S(1)}, u32[]{:S(2)}, u32[]{:S(2)}) collective-permute-start(bf16[256,128]{1,0:T(8,128)(2,1)S(1)} %get-tuple-element.30.refs_3_), channel_id=1, source_target_pairs={{0,24},{8,16},{16,8},{24,0},{1,25},{9,17},{17,9},{25,1},{2,26},{10... | collective-permute-start | bytes 196616 | tf_op jit(solution)/shard_map/ppermute | solution.py:407
  5.6 5.1 %collective-permute-start.1 = (bf16[528,128]{1,0:T(8,128)(2,1)S(1)}, bf16[528,128]{1,0:T(8,128)(2,1)S(1)}, u32[]{:S(2)}, u32[]{:S(2)}) collective-permute-start(bf16[528,128]{1,0:T(8,128)(2,1)S(1)} %shard_map.65.refs_0_), channel_id=1, source_target_pairs={{0,2},{2,4},{4,6},{6,7},{7,5},{5,3},{3,1},{1,0},{8,10},{10,12},{12... | collective-permute-start | bytes 405512 | tf_op jit(solution)/shard_map/ppermute | solution.py:421
  7.7 12.5 %collective-permute-start.6 = (bf16[1056,128]{1,0:T(8,128)(2,1)S(1)}, bf16[1056,128]{1,0:T(8,128)(2,1)S(1)}, u32[]{:S(2)}, u32[]{:S(2)}) collective-permute-start(bf16[1056,128]{1,0:T(8,128)(2,1)S(1)} %shard_map.69), channel_id=1, source_target_pairs={{2,0},{4,2},{6,4},{7,6},{5,7},{3,5},{1,3},{0,1},{10,8},{12,10},{14... | collective-permute-start | bytes 811016 | tf_op jit(solution)/shard_map/ppermute | solution.py:424
  10.7 4.7 %collective-permute-start.4 = (bf16[528,128]{1,0:T(8,128)(2,1)S(1)}, bf16[528,128]{1,0:T(8,128)(2,1)S(1)}, u32[]{:S(2)}, u32[]{:S(2)}) collective-permute-start(bf16[528,128]{1,0:T(8,128)(2,1)S(1)} %shard_map.66.after_ref.refs_1_), channel_id=1, source_target_pairs={{0,2},{2,4},{4,6},{6,7},{7,5},{5,3},{3,1},{1,0},{8,10},{10,12},{12... | collective-permute-start | bytes 405512 | tf_op jit(solution)/shard_map/ppermute | solution.py:421
  15.4 7.3 %collective-permute-start.5 = (bf16[1056,128]{1,0:T(8,128)(2,1)S(1)}, bf16[1056,128]{1,0:T(8,128)(2,1)S(1)}, u32[]{:S(2)}, u32[]{:S(2)}) collective-permute-start(bf16[1056,128]{1,0:T(8,128)(2,1)S(1)} %shard_map.68.refs_0_), channel_id=1, source_target_pairs={{0,2},{2,4},{4,6},{6,7},{7,5},{5,3},{3,1},{1,0},{8,10},{10,12},{12... | collective-permute-start | bytes 811016 | tf_op jit(solution)/shard_map/ppermute | solution.py:421
  20.2 7.7 %collective-permute-start.8 = (bf16[1056,128]{1,0:T(8,128)(2,1)S(1)}, bf16[1056,128]{1,0:T(8,128)(2,1)S(1)}, u32[]{:S(2)}, u32[]{:S(2)}) collective-permute-start(bf16[1056,128]{1,0:T(8,128)(2,1)S(1)} %collective-permute-done.6.refs_0_), channel_id=1, source_target_pairs={{2,0},{4,2},{6,4},{7,6},{5,7},{3,5},{1,3},{0,1},{10,8},{12,10},{14... | collective-permute-start | bytes 811016 | tf_op jit(solution)/shard_map/ppermute | solution.py:424
  22.7 7.9 %collective-permute-start.7 = (bf16[1056,128]{1,0:T(8,128)(2,1)S(1)}, bf16[1056,128]{1,0:T(8,128)(2,1)S(1)}, u32[]{:S(2)}, u32[]{:S(2)}) collective-permute-start(bf16[1056,128]{1,0:T(8,128)(2,1)S(1)} %collective-permute-done.5.refs_0_), channel_id=1, source_target_pairs={{0,2},{2,4},{4,6},{6,7},{7,5},{5,3},{3,1},{1,0},{8,10},{10,12},{12... | collective-permute-start | bytes 811016 | tf_op jit(solution)/shard_map/ppermute | solution.py:421
  27.9 6.0 %collective-permute-start.11 = (bf16[1056,128]{1,0:T(8,128)(2,1)S(1)}, bf16[1056,128]{1,0:T(8,128)(2,1)S(1)}, u32[]{:S(2)}, u32[]{:S(2)}) collective-permute-start(bf16[1056,128]{1,0:T(8,128)(2,1)S(1)} %collective-permute-done.8.refs_0_), channel_id=1, source_target_pairs={{2,0},{4,2},{6,4},{7,6},{5,7},{3,5},{1,3},{0,1},{10,8},{12,10},{14... | collective-permute-start | bytes 811016 | tf_op jit(solution)/shard_map/ppermute | solution.py:424
  35.2 4.6 %collective-permute-start.9 = (bf16[528,128]{1,0:T(8,128)(2,1)S(1)}, bf16[528,128]{1,0:T(8,128)(2,1)S(1)}, u32[]{:S(2)}, u32[]{:S(2)}) collective-permute-start(bf16[528,128]{1,0:T(8,128)(2,1)S(1)} %slice.6), channel_id=1, source_target_pairs={{0,2},{2,4},{4,6},{6,7},{7,5},{5,3},{3,1},{1,0},{8,10},{10,12},{12... | collective-permute-start | bytes 405512 | tf_op jit(solution)/shard_map/ppermute | solution.py:421
  39.2 4.3 %collective-permute-start.16 = (bf16[528,128]{1,0:T(8,128)(2,1)S(1)}, bf16[528,128]{1,0:T(8,128)(2,1)S(1)}, u32[]{:S(2)}, u32[]{:S(2)}) collective-permute-start(bf16[528,128]{1,0:T(8,128)(2,1)S(1)} %shard_map.82), channel_id=1, source_target_pairs={{2,0},{4,2},{6,4},{7,6},{5,7},{3,5},{1,3},{0,1},{10,8},{12,10},{14... | collective-permute-start | bytes 405512 | tf_op jit(solution)/shard_map/ppermute | solution.py:424
  40.7 4.6 %collective-permute-start.10 = (bf16[528,128]{1,0:T(8,128)(2,1)S(1)}, bf16[528,128]{1,0:T(8,128)(2,1)S(1)}, u32[]{:S(2)}, u32[]{:S(2)}) collective-permute-start(bf16[528,128]{1,0:T(8,128)(2,1)S(1)} %shard_map.74), channel_id=1, source_target_pairs={{0,2},{2,4},{4,6},{6,7},{7,5},{5,3},{3,1},{1,0},{8,10},{10,12},{12... | collective-permute-start | bytes 405512 | tf_op jit(solution)/shard_map/ppermute | solution.py:421
  43.8 6.9 %collective-permute-start.17 = (bf16[1056,128]{1,0:T(8,128)(2,1)S(1)}, bf16[1056,128]{1,0:T(8,128)(2,1)S(1)}, u32[]{:S(2)}, u32[]{:S(2)}) collective-permute-start(bf16[1056,128]{1,0:T(8,128)(2,1)S(1)} %shard_map.83), channel_id=1, source_target_pairs={{2,0},{4,2},{6,4},{7,6},{5,7},{3,5},{1,3},{0,1},{10,8},{12,10},{14... | collective-permute-start | bytes 811016 | tf_op jit(solution)/shard_map/ppermute | solution.py:424
  45.6 6.8 %collective-permute-start.12 = (bf16[1056,128]{1,0:T(8,128)(2,1)S(1)}, bf16[1056,128]{1,0:T(8,128)(2,1)S(1)}, u32[]{:S(2)}, u32[]{:S(2)}) collective-permute-start(bf16[1056,128]{1,0:T(8,128)(2,1)S(1)} %shard_map.77), channel_id=1, source_target_pairs={{0,2},{2,4},{4,6},{6,7},{7,5},{5,3},{3,1},{1,0},{8,10},{10,12},{12... | collective-permute-start | bytes 811016 | tf_op jit(solution)/shard_map/ppermute | solution.py:421
  51.2 7.6 %collective-permute-start.18 = (bf16[1056,128]{1,0:T(8,128)(2,1)S(1)}, bf16[1056,128]{1,0:T(8,128)(2,1)S(1)}, u32[]{:S(2)}, u32[]{:S(2)}) collective-permute-start(bf16[1056,128]{1,0:T(8,128)(2,1)S(1)} %shard_map.84), channel_id=1, source_target_pairs={{2,0},{4,2},{6,4},{7,6},{5,7},{3,5},{1,3},{0,1},{10,8},{12,10},{14... | collective-permute-start | bytes 811016 | tf_op jit(solution)/shard_map/ppermute | solution.py:424
  52.9 8.2 %collective-permute-start.13 = (bf16[1056,128]{1,0:T(8,128)(2,1)S(1)}, bf16[1056,128]{1,0:T(8,128)(2,1)S(1)}, u32[]{:S(2)}, u32[]{:S(2)}) collective-permute-start(bf16[1056,128]{1,0:T(8,128)(2,1)S(1)} %shard_map.78), channel_id=1, source_target_pairs={{0,2},{2,4},{4,6},{6,7},{7,5},{5,3},{3,1},{1,0},{8,10},{10,12},{12... | collective-permute-start | bytes 811016 | tf_op jit(solution)/shard_map/ppermute | solution.py:421
  59.2 6.1 %collective-permute-start.19 = (bf16[528,128]{1,0:T(8,128)(2,1)S(1)}, bf16[528,128]{1,0:T(8,128)(2,1)S(1)}, u32[]{:S(2)}, u32[]{:S(2)}) collective-permute-start(bf16[528,128]{1,0:T(8,128)(2,1)S(1)} %get-tuple-element.40), channel_id=1, source_target_pairs={{2,0},{4,2},{6,4},{7,6},{5,7},{3,5},{1,3},{0,1},{10,8},{12,10},{14... | collective-permute-start | bytes 405512 | tf_op jit(solution)/shard_map/ppermute | solution.py:424
  61.6 4.4 %collective-permute-start.14 = (bf16[528,128]{1,0:T(8,128)(2,1)S(1)}, bf16[528,128]{1,0:T(8,128)(2,1)S(1)}, u32[]{:S(2)}, u32[]{:S(2)}) collective-permute-start(bf16[528,128]{1,0:T(8,128)(2,1)S(1)} %get-tuple-element.38), channel_id=1, source_target_pairs={{0,2},{2,4},{4,6},{6,7},{7,5},{5,3},{3,1},{1,0},{8,10},{10,12},{12... | collective-permute-start | bytes 405512 | tf_op jit(solution)/shard_map/ppermute | solution.py:421
  63.8 14.3 %collective-permute-start.23 = (bf16[528,128]{1,0:T(8,128)(2,1)S(1)}, bf16[528,128]{1,0:T(8,128)(2,1)S(1)}, u32[]{:S(2)}, u32[]{:S(2)}) collective-permute-start(bf16[528,128]{1,0:T(8,128)(2,1)S(1)} %get-tuple-element.45), channel_id=1, source_target_pairs={{2,0},{4,2},{6,4},{7,6},{5,7},{3,5},{1,3},{0,1},{10,8},{12,10},{14... | collective-permute-start | bytes 405512 | tf_op jit(solution)/shard_map/ppermute | solution.py:424
  63.8 14.3 %collective-permute-start.22 = (bf16[528,128]{1,0:T(8,128)(2,1)S(1)}, bf16[528,128]{1,0:T(8,128)(2,1)S(1)}, u32[]{:S(2)}, u32[]{:S(2)}) collective-permute-start(bf16[528,128]{1,0:T(8,128)(2,1)S(1)} %get-tuple-element.44), channel_id=1, source_target_pairs={{0,2},{2,4},{4,6},{6,7},{7,5},{5,3},{3,1},{1,0},{8,10},{10,12},{12... | collective-permute-start | bytes 405512 | tf_op jit(solution)/shard_map/ppermute | solution.py:421
  66.4 12.6 %collective-permute-start.20 = (bf16[272,128]{1,0:T(8,128)(2,1)S(1)}, bf16[272,128]{1,0:T(8,128)(2,1)S(1)}, u32[]{:S(2)}, u32[]{:S(2)}) collective-permute-start(bf16[272,128]{1,0:T(8,128)(2,1)S(1)} %get-tuple-element.41), channel_id=1, source_target_pairs={{0,16},{8,24},{16,0},{24,8},{1,17},{9,25},{17,1},{25,9},{2,18},{10... | collective-permute-start | bytes 208904 | tf_op jit(solution)/shard_map/ppermute | solution.py:407
  67.6 14.0 %collective-permute-start.21 = (bf16[272,128]{1,0:T(8,128)(2,1)S(1)}, bf16[272,128]{1,0:T(8,128)(2,1)S(1)}, u32[]{:S(2)}, u32[]{:S(2)}) collective-permute-start(bf16[272,128]{1,0:T(8,128)(2,1)S(1)} %get-tuple-element.42), channel_id=1, source_target_pairs={{0,24},{8,16},{16,8},{24,0},{1,25},{9,17},{17,9},{25,1},{2,26},{10... | collective-permute-start | bytes 208904 | tf_op jit(solution)/shard_map/ppermute | solution.py:407
  78.5 3.9 %collective-permute-start.24 = (bf16[272,128]{1,0:T(8,128)(2,1)S(1)}, bf16[272,128]{1,0:T(8,128)(2,1)S(1)}, u32[]{:S(2)}, u32[]{:S(2)}) collective-permute-start(bf16[272,128]{1,0:T(8,128)(2,1)S(1)} %get-tuple-element.48), channel_id=1, source_target_pairs={{0,8},{8,0},{16,24},{24,16},{1,9},{9,1},{17,25},{25,17},{2,10},{10... | collective-permute-start | bytes 208904 | tf_op jit(solution)/shard_map/ppermute | solution.py:407
  (5 other events, 27.6 us)

commit v7 on v5

--- a/solution.py
+++ b/solution.py
@@ -69,8 +69,8 @@
     return head * ROWS + half * HALF
 
 
-def by_lane(columns):
-    lanes = lane_ids()
+def by_lane(columns, first=0):
+    lanes = lane_ids() - first
     tile = jnp.zeros((HALF, LANES), F32)
     for head, values in enumerate(columns):
         for half in range(ROWS // HALF):
@@ -79,7 +79,7 @@
     return tile
 
 
-def attend(queries, keys, values, usable):
+def attend(queries, keys, values, usable, first=0):
     across = (((1,), (1,)), ((), ()))
     along = (((1,), (0,)), ((), ()))
     ones = jnp.ones(values[0].shape, BF16)
@@ -92,7 +92,7 @@
         for w, v in zip(weights, values)
     ]
     mixed, totals = [b[:, :HD] for b in both], [b[:, HD:] for b in both]
-    level = by_lane(tops) + jnp.log2(jnp.maximum(by_lane(totals), 1.0))
+    level = by_lane(tops, first) + jnp.log2(jnp.maximum(by_lane(totals, first), 1.0))
     return [m / t for m, t in zip(mixed, totals)], level
 
 
@@ -196,33 +196,38 @@
 
 def item_kernel(slots, visitors, place_ref, cache_ref, *refs):
     sides = len(slots)
-    query_refs, (out_ref, level_ref, code_ref) = refs[:sides], refs[sides:]
+    query_refs, out_refs, (level_ref, code_ref) = refs[:sides], refs[sides : 2 * sides], refs[2 * sides :]
     each = len(slots[0])
     for side, query_ref in enumerate(query_refs):
         lists = query_ref.shape[0] - each * BODY
         rows = lax.broadcasted_iota(jnp.int32, (lists, LANES), 0)
         table = query_ref[each * BODY :, :].astype(F32)
         table = jnp.where(lane_ids(lists) == place_ref[1], table, 0.0)
-        for number, slot in enumerate(slots[side]):
-            row = place_ref[0] ^ slot
-            code = jnp.where(rows == row, table, jnp.where(rows == row + visitors, table * 256.0, 0.0))
-            code_ref[side * each + number] = jnp.sum(code).astype(jnp.int32)
+        for pair in range(each // 2):
+            factor = jnp.zeros((lists, LANES), F32)
+            for second in range(2):
+                row = place_ref[0] ^ slots[side][2 * pair + second]
+                factor = jnp.where(rows == row, float(4096**second), factor)
+                factor = jnp.where(rows == row + visitors, float(256 * 4096**second), factor)
+            code_ref[(side * each) // 2 + pair] = jnp.sum(table * factor).astype(jnp.int32)
     tokens = lax.broadcasted_iota(jnp.int32, (ROWS, PAGE), 1)
 
     def one(side, number):
         entry = side * each + number
-        query_ref = query_refs[side]
-        code = code_ref[entry]
-        count, page = code & 255, code >> 8
+        query_ref, out_ref = query_refs[side], out_refs[side]
+        odd = number & 1
+        code = code_ref[entry >> 1] >> (12 * odd)
+        count, page = code & 255, (code >> 8) & 15
         start = number * BODY
-        out = (entry // 2) * PAIR + (entry % 2) * BODY
+        out = (number >> 1) * PAIR + odd * BODY
+        first = odd * SECOND
 
         @pl.when(count > 0)
         def _():
             queries = [query_ref[pl.ds(pl.multiple_of(start + h * ROWS, HALF), ROWS), :] for h in range(KVH)]
             keys = [cache_ref[page, :, h * HD : (h + 1) * HD] for h in range(KVH)]
             values = [cache_ref[page, :, (KVH + h) * HD : (KVH + h + 1) * HD] for h in range(KVH)]
-            mixed, level = attend(queries, keys, values, tokens < count)
+            mixed, level = attend(queries, keys, values, tokens < count, first)
             for head, part in enumerate(mixed):
                 out_ref[pl.ds(pl.multiple_of(out + head * ROWS, HALF), ROWS), :] = part.astype(BF16)
             level_ref[entry] = level
@@ -230,7 +235,8 @@
         @pl.when(count <= 0)
         def _():
             out_ref[pl.ds(pl.multiple_of(out, HALF), BODY), :] = jnp.zeros((BODY, HD), BF16)
-            level_ref[entry] = jnp.full((HALF, LANES), EMPTY, F32)
+            lanes = lane_ids() - first
+            level_ref[entry] = jnp.where((lanes >= 0) & (lanes < COLS), EMPTY, 0.0)
 
     for side in range(sides):
 
@@ -238,21 +244,22 @@
         def _(number):
             one(side, number)
 
-    lanes = lane_ids()
-    for pair in range(sides * each // 2):
-        level = jnp.where(lanes < COLS, level_ref[2 * pair], pltpu.roll(level_ref[2 * pair + 1], SECOND, 1))
-        start = pair * PAIR + 2 * BODY
-        out_ref[start : start + HALF, :] = pack_stats(level)
+    for side, out_ref in enumerate(out_refs):
+        for pair in range(each // 2):
+            entry = side * each + 2 * pair
+            start = pair * PAIR + 2 * BODY
+            out_ref[start : start + HALF, :] = pack_stats(level_ref[entry] + level_ref[entry + 1])
 
 
 def items(place, kv_cache, payloads, slots, visitors):
     count = sum(len(row) for row in slots)
+    rows = len(slots[0]) // 2 * PAIR
     return pl.pallas_call(
         functools.partial(item_kernel, slots, visitors),
-        out_shape=jax.ShapeDtypeStruct((count // 2 * PAIR, HD), BF16),
+        out_shape=[jax.ShapeDtypeStruct((rows, HD), BF16)] * len(slots),
         in_specs=[IN_SMEM] + [IN_VMEM] * (1 + len(slots)),
-        out_specs=IN_VMEM,
-        scratch_shapes=[pltpu.VMEM((count, HALF, LANES), F32), pltpu.SMEM((count,), jnp.int32)],
+        out_specs=[IN_VMEM] * len(slots),
+        scratch_shapes=[pltpu.VMEM((count, HALF, LANES), F32), pltpu.SMEM((count // 2,), jnp.int32)],
         compiler_params=params(),
         cost_estimate=cost(count * KVH * 4 * ROWS * HD * PAGE, count * PAGE * kv_cache.shape[2] * 2),
     )(place, kv_cache, *payloads)
@@ -277,15 +284,10 @@
     return values
 
 
-def merge_kernel(base, arrived_ref, own_ref, out_ref):
-    arrived_pairs = arrived_ref.shape[0] // PAIR
+def merge_kernel(arrived_ref, own_ref, out_ref):
     for pair in range(out_ref.shape[0] // PAIR):
         part = slice(pair * PAIR, (pair + 1) * PAIR)
-        own, out = own_ref.at[part], out_ref.at[part]
-        if not base <= pair < base + arrived_pairs:
-            out[...] = own[...]
-            continue
-        arrived = arrived_ref.at[(pair - base) * PAIR : (pair - base + 1) * PAIR]
+        arrived, own, out = arrived_ref.at[part], own_ref.at[part], out_ref.at[part]
         shares, level = blend([unpack_stats(ref[2 * BODY : PAIR, :]) for ref in (arrived, own)])
         values = [mix(shares, (arrived, own), second * BODY, second * SECOND) for second in range(2)]
         for second in range(2):
@@ -295,9 +297,9 @@
         out[2 * BODY : PAIR, :] = pack_stats(level)
 
 
-def merge(arrived, own, base):
-    return pl.pallas_call(
-        functools.partial(merge_kernel, base),
+def merge(arrived, own):
+    return pl.pallas_call(
+        merge_kernel,
         out_shape=jax.ShapeDtypeStruct(own.shape, BF16),
         in_specs=[IN_VMEM, IN_VMEM],
         out_specs=IN_VMEM,
@@ -306,9 +308,9 @@
     )(arrived, own)
 
 
-def gather_kernel(base, ahead_ref, behind_ref, own_ref, *outs):
+def gather_kernel(ahead_ref, behind_ref, own_ref, *outs):
     for pair in range(len(outs) // 2):
-        part = slice((base + pair) * PAIR, (base + pair + 1) * PAIR)
+        part = slice(pair * PAIR, (pair + 1) * PAIR)
         sources = [ref.at[part] for ref in (own_ref, ahead_ref, behind_ref)]
         shares, level = blend([unpack_stats(ref[2 * BODY : PAIR, :]) for ref in sources])
         values = [mix(shares, sources, second * BODY, second * SECOND) for second in range(2)]
@@ -321,9 +323,10 @@
             out[BODY:LONE, :] = pack_stats(here)
 
 
-def gather(ahead, behind, own, base, pairs):
-    return pl.pallas_call(
-        functools.partial(gather_kernel, base),
+def gather(ahead, behind, own):
+    pairs = own.shape[0] // PAIR
+    return pl.pallas_call(
+        gather_kernel,
         out_shape=[jax.ShapeDtypeStruct((LONE, HD), BF16)] * (2 * pairs),
         in_specs=[IN_VMEM] * 3,
         out_specs=[IN_VMEM] * (2 * pairs),
@@ -393,31 +396,47 @@
     slots = [list(range(cut)), list(range(cut, requests))]
     owned = functools.partial(items, place, kv_cache, visitors=requests)
 
-    def exchange(both, half, last=False):
-        below = lax.ppermute(both[0], "cache", forward) if half == 0 or not last else None
-        above = lax.ppermute(both[1], "cache", backward) if half == 1 or not last else None
-        return (below, above) if last else lax.optimization_barrier((below, above))
-
-    first = payload(lists, visits[:cut])
-    halves = [exchange((first, first), 0)]
-    second = payload(lists, visits[cut:], [touch(kv_cache, first), *halves[0]])
-    halves.append(exchange((second, second), 1))
-    parts = {0: owned([first, second], slots)}
-    for step in range(1, reach):
-        parts[-step] = owned([halves[0][0], halves[1][0]], slots)
-        parts[step] = owned([halves[0][1], halves[1][1]], slots)
-        halves = [exchange(halves[half], half, step == reach - 1) for half in range(2)]
-
-    ahead, behind = owned([halves[0][0]], slots[:1]), owned([halves[1][1]], slots[1:])
-    for step in range(reach - 1, -1, -1):
-        ahead = lax.ppermute(ahead, "cache", forward)
-        behind = lax.ppermute(behind, "cache", backward)
-        if step > 0:
-            base = cut // 2 if step == reach - 1 else 0
-            ahead, behind = merge(ahead, parts[step], 0), merge(behind, parts[-step], base)
-    back = gather(ahead, behind, parts[0], cut // 2, cut // 2)
-    front = gather(ahead, behind, parts[0], 0, cut // 2)
-    home = [swap(part, d) for d, part in enumerate(list(front) + list(back))]
+    def up(array):
+        return lax.ppermute(array, "cache", forward)
+
+    def down(array):
+        return lax.ppermute(array, "cache", backward)
+
+    def after(array, *others):
+        return lax.optimization_barrier((array, others))[0]
+
+    blocks = [payload(lists, visits[:cut])]
+    ahead, behind = up(blocks[0]), down(blocks[0])
+    blocks.append(payload(lists, visits[cut:], [touch(kv_cache, blocks[0])]))
+    second = after(blocks[1], ahead, behind)
+    below, above, far = [ahead, up(second)], [behind, down(second)], [None, None]
+    parts = {(half, 0): part for half, part in enumerate(owned(blocks, slots))}
+    for step in range(1, reach + 1):
+        for half in range(2):
+            if step == reach:
+                arrival = up(below[0]) if half == 0 else down(above[1])
+                far[half] = owned([arrival], [slots[half]])[0]
+                continue
+            done = [parts[half, 0]] if step == 1 else [parts[half, 1 - step], parts[half, step - 1]]
+            if step > 1:
+                below[half], above[half] = up(below[half]), down(above[half])
+            below[half], above[half] = after(below[half], *done), after(above[half], *done)
+            parts[half, -step], parts[half, step] = owned([below[half], above[half]], [slots[half]] * 2)
+
+    arrived = []
+    for half in range(2):
+        for move, sign in ((up, 1), (down, -1)):
+            if half == (0 if sign == 1 else 1):
+                chain, steps = far[half], range(reach - 1, -1, -1)
+            else:
+                chain, steps = parts[half, sign * (reach - 1)], range(reach - 2, -1, -1)
+            for step in steps:
+                chain = move(chain)
+                if step > 0:
+                    chain = merge(chain, parts[half, sign * step])
+            arrived.append(chain)
+    returned = gather(arrived[0], arrived[1], parts[0, 0]) + gather(arrived[2], arrived[3], parts[1, 0])
+    home = [swap(part, d) for d, part in enumerate(returned)]
     early = final(place, home[:cut], 0, new_out, new_level)
     return final(place, home[cut:], cut, new_out, new_level, [early])
 

time: 80.9 us -> 78.3 us (0.968)
  waiting for transfers between devices: 28.7 us -> 11.6 us
  starting transfers between devices: 24.3 us -> 39.2 us
  local copies, waits for them, and re-layouts: 4.34 us -> 5.3 us
    ppermute x22 -> x28, waiting for transfers between devices: 26.8 us -> 9.54 us  [the longest x14 6.6 us: up(): return lax.ppermute(array, 'cache', forward)]
    ppermute x22 -> x28, starting transfers between devices: 19.9 us -> 34.3 us  [the longest x14 24.3 us: up(): return lax.ppermute(array, 'cache', forward)]
    pallas_call x9, Pallas kernels: 13.9 us -> 12.8 us  [items(): pl.pallas_call(functools.partial(item_kernel, slots, visitors), out_shape...]
    unnamed x8, local copies, waits for them, and re-layouts: 4.34 us -> 5.3 us
    pallas_call x8 -> x12, Pallas kernels: 3.17 us -> 3.42 us  [the longest x10 2.66 us: merge(): pl.pallas_call(merge_kernel, out_shape=jax.ShapeDtypeStruct(own.shape, BF...]
  transfers between devices with their start and end apart: 28 -> 34, of which waited for: 21 -> 11; matrix products, arithmetic and copies ran while one was open for 2% -> 2% of each run, Pallas kernels for 24% -> 24%
where the time goes in v7:
time: 78.3 us; the launch traced here: 78.8 us
  starting transfers between devices  39.2 us (50%)
  Pallas kernels  20.9 us (27%)
  waiting for transfers between devices  11.6 us (15%)
  local copies, waits for them, and re-layouts  5.3 us (7%)
  other arithmetic  1.59 us (2%)
    ppermute x14, starting transfers between devices, up(): return lax.ppermute(array, 'cache', forward)  24.3 us
    pallas_call x9, Pallas kernels, items(): pl.pallas_call(functools.partial(item_kernel, slots, visitors), out_shape...  12.8 us
    ppermute x14, starting transfers between devices, down(): return lax.ppermute(array, 'cache', backward)  10 us
    ppermute x14, waiting for transfers between devices, up(): return lax.ppermute(array, 'cache', forward)  6.6 us
    unnamed x8, local copies, waits for them, and re-layouts  5.3 us
    ppermute x6, starting transfers between devices, swap(): lax.ppermute(array, 'grp', [(g, g ^ d) for g in range(groups)])  4.88 us
    ppermute x14, waiting for transfers between devices, down(): return lax.ppermute(array, 'cache', backward)  2.94 us
    pallas_call x10, Pallas kernels, merge(): pl.pallas_call(merge_kernel, out_shape=jax.ShapeDtypeStruct(own.shape, BF...  2.66 us
  transfers between devices with their start and end apart: 34, of which 11 were waited for; matrix products, arithmetic and copies ran while one was open for 2% of the time, Pallas kernels for 24%

profile of v7, /device:TPU:0, one launch (start us, length us, event | category | flops | bytes accessed | tf_op | source)
XLA Modules:
  0.0 78.8 jit_solution(9366331269362292339)
XLA Ops:
  3.7 2.6 %collective-permute-start.1 = (bf16[528,128]{1,0:T(8,128)(2,1)S(1)}, bf16[528,128]{1,0:T(8,128)(2,1)S(1)}, u32[]{:S(2)}, u32[]{:S(2)}) collective-permute-start(bf16[528,128]{1,0:T(8,128)(2,1)S(1)} %shard_map.65.after_ref.refs_0_), channel_id=1, source_target_pairs={{0,2},{2,4},{4,6},{6,7},{7,5},{5,3},{3,1},{1,0},{8,10},{10,12},{12... | collective-permute-start | bytes 405512 | tf_op jit(solution)/shard_map/ppermute | solution.py:400
  6.3 2.0 %collective-permute-start.2 = (bf16[256,128]{1,0:T(8,128)(2,1)S(1)}, bf16[256,128]{1,0:T(8,128)(2,1)S(1)}, u32[]{:S(2)}, u32[]{:S(2)}) collective-permute-start(bf16[256,128]{1,0:T(8,128)(2,1)S(1)} %get-tuple-element.44.refs_2_), channel_id=1, source_target_pairs={{0,16},{8,24},{16,0},{24,8},{1,17},{9,25},{17,1},{25,9},{2,18},{10... | collective-permute-start | bytes 196616 | tf_op jit(solution)/shard_map/ppermute | solution.py:386
  8.3 3.4 %copy-done = bf16[16,128,2048]{2,1,0:T(8,128)(2,1)S(1)} copy-done((bf16[16,128,2048]{2,1,0:T(8,128)(2,1)S(1)}, bf16[16,128,2048]{2,1,0:T(8,128)(2,1)}, u32[]{:S(2)}) %copy-start) | copy-done | bytes 8388632
  12.6 1.5 %collective-permute-start.20 = (bf16[528,128]{1,0:T(8,128)(2,1)S(1)}, bf16[528,128]{1,0:T(8,128)(2,1)S(1)}, u32[]{:S(2)}, u32[]{:S(2)}) collective-permute-start(bf16[528,128]{1,0:T(8,128)(2,1)S(1)} %shard_map.67.refs_1_), channel_id=1, source_target_pairs={{2,0},{4,2},{6,4},{7,6},{5,7},{3,5},{1,3},{0,1},{10,8},{12,10},{14... | collective-permute-start | bytes 405512 | tf_op jit(solution)/shard_map/ppermute | solution.py:403
  15.1 1.8 %shard_map.68 = (bf16[528,128]{1,0:T(8,128)(2,1)S(1)}, bf16[528,128]{1,0:T(8,128)(2,1)S(1)}) custom-call(s32[2]{0:T(128)S(1)} %pad_add_fusion.place_ref, bf16[16,128,2048]{2,1,0:T(8,128)(2,1)S(1)} %copy-done.1, bf16[528,128]{1,0:T(8,128)(2,1)S(1)} %shard_map.65.after_ref.refs_0_, bf16[528,128]{1,0:T(8,128)(2,1)S(1)} %shard_map.67.refs_1_), custom_call_target="tpu_custom_call" | custom-call | flops 67108864 | bytes 2097152 | tf_op jit(solution)/shard_map/pallas_call | solution.py:257
  17.5 2.5 %collective-permute-start.4 = (bf16[528,128]{1,0:T(8,128)(2,1)S(1)}, bf16[528,128]{1,0:T(8,128)(2,1)S(1)}, u32[]{:S(2)}, u32[]{:S(2)}) collective-permute-start(bf16[528,128]{1,0:T(8,128)(2,1)S(1)} %collective-permute-done.1.refs_0_), channel_id=1, source_target_pairs={{0,2},{2,4},{4,6},{6,7},{7,5},{5,3},{3,1},{1,0},{8,10},{10,12},{12... | collective-permute-start | bytes 405512 | tf_op jit(solution)/shard_map/ppermute | solution.py:400
  22.6 2.3 %collective-permute-start.19 = (bf16[528,128]{1,0:T(8,128)(2,1)S(1)}, bf16[528,128]{1,0:T(8,128)(2,1)S(1)}, u32[]{:S(2)}, u32[]{:S(2)}) collective-permute-start(bf16[528,128]{1,0:T(8,128)(2,1)S(1)} %collective-permute-done.18.refs_0_), channel_id=1, source_target_pairs={{0,2},{2,4},{4,6},{6,7},{7,5},{5,3},{3,1},{1,0},{8,10},{10,12},{12... | collective-permute-start | bytes 405512 | tf_op jit(solution)/shard_map/ppermute | solution.py:400
  30.9 2.2 %collective-permute-start.8 = (bf16[528,128]{1,0:T(8,128)(2,1)S(1)}, bf16[528,128]{1,0:T(8,128)(2,1)S(1)}, u32[]{:S(2)}, u32[]{:S(2)}) collective-permute-start(bf16[528,128]{1,0:T(8,128)(2,1)S(1)} %collective-permute-done.6.refs_0_), channel_id=1, source_target_pairs={{0,2},{2,4},{4,6},{6,7},{7,5},{5,3},{3,1},{1,0},{8,10},{10,12},{12... | collective-permute-start | bytes 405512 | tf_op jit(solution)/shard_map/ppermute | solution.py:400
  34.6 2.0 %collective-permute-start.10 = (bf16[528,128]{1,0:T(8,128)(2,1)S(1)}, bf16[528,128]{1,0:T(8,128)(2,1)S(1)}, u32[]{:S(2)}, u32[]{:S(2)}) collective-permute-start(bf16[528,128]{1,0:T(8,128)(2,1)S(1)} %collective-permute-done.7.refs_1_), channel_id=1, source_target_pairs={{2,0},{4,2},{6,4},{7,6},{5,7},{3,5},{1,3},{0,1},{10,8},{12,10},{14... | collective-permute-start | bytes 405512 | tf_op jit(solution)/shard_map/ppermute | solution.py:403
  37.8 2.9 %collective-permute-start.9 = (bf16[528,128]{1,0:T(8,128)(2,1)S(1)}, bf16[528,128]{1,0:T(8,128)(2,1)S(1)}, u32[]{:S(2)}, u32[]{:S(2)}) collective-permute-start(bf16[528,128]{1,0:T(8,128)(2,1)S(1)} %shard_map.71), channel_id=1, source_target_pairs={{0,2},{2,4},{4,6},{6,7},{7,5},{5,3},{3,1},{1,0},{8,10},{10,12},{12... | collective-permute-start | bytes 405512 | tf_op jit(solution)/shard_map/ppermute | solution.py:400
  40.7 1.7 %shard_map.86 = bf16[528,128]{1,0:T(8,128)(2,1)S(1)} custom-call(s32[2]{0:T(128)S(1)} %pad_add_fusion.place_ref, bf16[16,128,2048]{2,1,0:T(8,128)(2,1)S(1)} %copy-done.1, bf16[528,128]{1,0:T(8,128)(2,1)S(1)} %collective-permute-done.27.refs_0_), custom_call_target="tpu_custom_call" | custom-call | flops 33554432 | bytes 1048576 | tf_op jit(solution)/shard_map/pallas_call | solution.py:257
  43.8 2.1 %collective-permute-start.14 = (bf16[528,128]{1,0:T(8,128)(2,1)S(1)}, bf16[528,128]{1,0:T(8,128)(2,1)S(1)}, u32[]{:S(2)}, u32[]{:S(2)}) collective-permute-start(bf16[528,128]{1,0:T(8,128)(2,1)S(1)} %get-tuple-element.58), channel_id=1, source_target_pairs={{2,0},{4,2},{6,4},{7,6},{5,7},{3,5},{1,3},{0,1},{10,8},{12,10},{14... | collective-permute-start | bytes 405512 | tf_op jit(solution)/shard_map/ppermute | solution.py:403
  45.9 1.8 %shard_map.83 = (bf16[528,128]{1,0:T(8,128)(2,1)S(1)}, bf16[528,128]{1,0:T(8,128)(2,1)S(1)}) custom-call(s32[2]{0:T(128)S(1)} %pad_add_fusion.place_ref, bf16[16,128,2048]{2,1,0:T(8,128)(2,1)S(1)} %copy-done.1, bf16[528,128]{1,0:T(8,128)(2,1)S(1)} %collective-permute-done.21.refs_0_, bf16[528,128]{1,0:T(8,128)(2,1)S(1)} %collective-permute-done.23.refs_1_), custom_call_target="tpu_custom_call" | custom-call | flops 67108864 | bytes 2097152 | tf_op jit(solution)/shard_map/pallas_call | solution.py:257
  48.0 1.5 %collective-permute-start.11 = (bf16[528,128]{1,0:T(8,128)(2,1)S(1)}, bf16[528,128]{1,0:T(8,128)(2,1)S(1)}, u32[]{:S(2)}, u32[]{:S(2)}) collective-permute-start(bf16[528,128]{1,0:T(8,128)(2,1)S(1)} %shard_map.73), channel_id=1, source_target_pairs={{0,2},{2,4},{4,6},{6,7},{7,5},{5,3},{3,1},{1,0},{8,10},{10,12},{12... | collective-permute-start | bytes 405512 | tf_op jit(solution)/shard_map/ppermute | solution.py:400
  49.4 2.0 %collective-permute-start.24 = (bf16[528,128]{1,0:T(8,128)(2,1)S(1)}, bf16[528,128]{1,0:T(8,128)(2,1)S(1)}, u32[]{:S(2)}, u32[]{:S(2)}) collective-permute-start(bf16[528,128]{1,0:T(8,128)(2,1)S(1)} %get-tuple-element.75), channel_id=1, source_target_pairs={{0,2},{2,4},{4,6},{6,7},{7,5},{5,3},{3,1},{1,0},{8,10},{10,12},{12... | collective-permute-start | bytes 405512 | tf_op jit(solution)/shard_map/ppermute | solution.py:400
  52.7 1.5 %collective-permute-done.11.arrived_ref = bf16[528,128]{1,0:T(8,128)(2,1)S(1)} collective-permute-done((bf16[528,128]{1,0:T(8,128)(2,1)S(1)}, bf16[528,128]{1,0:T(8,128)(2,1)S(1)}, u32[]{:S(2)}, u32[]{:S(2)}) %collective-permute-start.11) | collective-permute-done | bytes 135200 | tf_op jit(solution)/shard_map/ppermute | solution.py:400
  55.7 1.4 %collective-permute-done.24.arrived_ref = bf16[528,128]{1,0:T(8,128)(2,1)S(1)} collective-permute-done((bf16[528,128]{1,0:T(8,128)(2,1)S(1)}, bf16[528,128]{1,0:T(8,128)(2,1)S(1)}, u32[]{:S(2)}, u32[]{:S(2)}) %collective-permute-start.24) | collective-permute-done | bytes 135200 | tf_op jit(solution)/shard_map/ppermute | solution.py:400
  61.7 2.1 %collective-permute-start.13 = (bf16[528,128]{1,0:T(8,128)(2,1)S(1)}, bf16[528,128]{1,0:T(8,128)(2,1)S(1)}, u32[]{:S(2)}, u32[]{:S(2)}) collective-permute-start(bf16[528,128]{1,0:T(8,128)(2,1)S(1)} %shard_map.75), channel_id=1, source_target_pairs={{0,2},{2,4},{4,6},{6,7},{7,5},{5,3},{3,1},{1,0},{8,10},{10,12},{12... | collective-permute-start | bytes 405512 | tf_op jit(solution)/shard_map/ppermute | solution.py:400
  64.0 1.4 %collective-permute-start.26 = (bf16[528,128]{1,0:T(8,128)(2,1)S(1)}, bf16[528,128]{1,0:T(8,128)(2,1)S(1)}, u32[]{:S(2)}, u32[]{:S(2)}) collective-permute-start(bf16[528,128]{1,0:T(8,128)(2,1)S(1)} %shard_map.85), channel_id=1, source_target_pairs={{0,2},{2,4},{4,6},{6,7},{7,5},{5,3},{3,1},{1,0},{8,10},{10,12},{12... | collective-permute-start | bytes 405512 | tf_op jit(solution)/shard_map/ppermute | solution.py:400
  67.2 1.9 %collective-permute-done.26.ahead_ref = bf16[528,128]{1,0:T(8,128)(2,1)S(1)} collective-permute-done((bf16[528,128]{1,0:T(8,128)(2,1)S(1)}, bf16[528,128]{1,0:T(8,128)(2,1)S(1)}, u32[]{:S(2)}, u32[]{:S(2)}) %collective-permute-start.26) | collective-permute-done | bytes 135200 | tf_op jit(solution)/shard_map/ppermute | solution.py:400
  69.1 1.7 %collective-permute-done.31.behind_ref = bf16[528,128]{1,0:T(8,128)(2,1)S(1)} collective-permute-done((bf16[528,128]{1,0:T(8,128)(2,1)S(1)}, bf16[528,128]{1,0:T(8,128)(2,1)S(1)}, u32[]{:S(2)}, u32[]{:S(2)}) %collective-permute-start.31) | collective-permute-done | bytes 135200 | tf_op jit(solution)/shard_map/ppermute | solution.py:403
  71.1 2.3 %collective-permute-start.32 = (bf16[272,128]{1,0:T(8,128)(2,1)S(1)}, bf16[272,128]{1,0:T(8,128)(2,1)S(1)}, u32[]{:S(2)}, u32[]{:S(2)}) collective-permute-start(bf16[272,128]{1,0:T(8,128)(2,1)S(1)} %get-tuple-element.77), channel_id=1, source_target_pairs={{0,16},{8,24},{16,0},{24,8},{1,17},{9,25},{17,1},{25,9},{2,18},{10... | collective-permute-start | bytes 208904 | tf_op jit(solution)/shard_map/ppermute | solution.py:386
  73.4 1.7 %shard_map.79 = (f32[4,256,128]{2,1,0:T(8,128)S(1)}, f32[4,16,128]{2,1,0:T(8,128)S(1)}) custom-call(s32[2]{0:T(128)S(1)} %pad_add_fusion.place_ref, bf16[256,128]{1,0:T(8,128)(2,1)S(1)} %get-tuple-element.42.refs_0_, bf16[256,128]{1,0:T(8,128)(2,1)S(1)} %get-tuple-element.43.refs_1_, bf16[256,128]{1,0:T(8,128)(2,1)S(1)} %get-tuple-element.44.refs_2_, ...), custom_call_target="tpu_custom_call" | custom-call | flops 67108864 | bytes 786432 | tf_op jit(solution)/shard_map/pallas_call | solution.py:136
  77.2 1.6 %shard_map.91 = bf16[4,4,8192]{2,1,0:T(4,128)(2,1)} custom-call(s32[2]{0:T(128)S(1)} %pad_add_fusion.place_ref, bf16[2,4,8192]{2,1,0:T(4,128)(2,1)S(1)} %shard_map.80.refs_0_, bf16[272,128]{1,0:T(8,128)(2,1)S(1)} %collective-permute-done.32.refs_1_, bf16[272,128]{1,0:T(8,128)(2,1)S(1)} %collective-permute-done.33.refs_2_, ...), custom_call_target="tpu_custom_call" | custom-call | bytes 524288 | tf_op jit(solution)/shard_map/pallas_call | solution.py:359
  (84 shorter events, 30.8 us)
Async XLA Ops:
  3.7 8.9 %collective-permute-start.1 = (bf16[528,128]{1,0:T(8,128)(2,1)S(1)}, bf16[528,128]{1,0:T(8,128)(2,1)S(1)}, u32[]{:S(2)}, u32[]{:S(2)}) collective-permute-start(bf16[528,128]{1,0:T(8,128)(2,1)S(1)} %shard_map.65.after_ref.refs_0_), channel_id=1, source_target_pairs={{0,2},{2,4},{4,6},{6,7},{7,5},{5,3},{3,1},{1,0},{8,10},{10,12},{12... | collective-permute-start | bytes 405512 | tf_op jit(solution)/shard_map/ppermute | solution.py:400
  6.3 6.2 %collective-permute-start.5 = (bf16[528,128]{1,0:T(8,128)(2,1)S(1)}, bf16[528,128]{1,0:T(8,128)(2,1)S(1)}, u32[]{:S(2)}, u32[]{:S(2)}) collective-permute-start(bf16[528,128]{1,0:T(8,128)(2,1)S(1)} %shard_map.65.after_ref.refs_0_), channel_id=1, source_target_pairs={{2,0},{4,2},{6,4},{7,6},{5,7},{3,5},{1,3},{0,1},{10,8},{12,10},{14... | collective-permute-start | bytes 405512 | tf_op jit(solution)/shard_map/ppermute | solution.py:403
  12.6 7.5 %collective-permute-start.20 = (bf16[528,128]{1,0:T(8,128)(2,1)S(1)}, bf16[528,128]{1,0:T(8,128)(2,1)S(1)}, u32[]{:S(2)}, u32[]{:S(2)}) collective-permute-start(bf16[528,128]{1,0:T(8,128)(2,1)S(1)} %shard_map.67.refs_1_), channel_id=1, source_target_pairs={{2,0},{4,2},{6,4},{7,6},{5,7},{3,5},{1,3},{0,1},{10,8},{12,10},{14... | collective-permute-start | bytes 405512 | tf_op jit(solution)/shard_map/ppermute | solution.py:403
  16.9 5.7 %collective-permute-start.18 = (bf16[528,128]{1,0:T(8,128)(2,1)S(1)}, bf16[528,128]{1,0:T(8,128)(2,1)S(1)}, u32[]{:S(2)}, u32[]{:S(2)}) collective-permute-start(bf16[528,128]{1,0:T(8,128)(2,1)S(1)} %shard_map.67.refs_1_), channel_id=1, source_target_pairs={{0,2},{2,4},{4,6},{6,7},{7,5},{5,3},{3,1},{1,0},{8,10},{10,12},{12... | collective-permute-start | bytes 405512 | tf_op jit(solution)/shard_map/ppermute | solution.py:400
  17.5 8.0 %collective-permute-start.4 = (bf16[528,128]{1,0:T(8,128)(2,1)S(1)}, bf16[528,128]{1,0:T(8,128)(2,1)S(1)}, u32[]{:S(2)}, u32[]{:S(2)}) collective-permute-start(bf16[528,128]{1,0:T(8,128)(2,1)S(1)} %collective-permute-done.1.refs_0_), channel_id=1, source_target_pairs={{0,2},{2,4},{4,6},{6,7},{7,5},{5,3},{3,1},{1,0},{8,10},{10,12},{12... | collective-permute-start | bytes 405512 | tf_op jit(solution)/shard_map/ppermute | solution.py:400
  20.0 8.1 %collective-permute-start.22 = (bf16[528,128]{1,0:T(8,128)(2,1)S(1)}, bf16[528,128]{1,0:T(8,128)(2,1)S(1)}, u32[]{:S(2)}, u32[]{:S(2)}) collective-permute-start(bf16[528,128]{1,0:T(8,128)(2,1)S(1)} %collective-permute-done.20.refs_1_), channel_id=1, source_target_pairs={{2,0},{4,2},{6,4},{7,6},{5,7},{3,5},{1,3},{0,1},{10,8},{12,10},{14... | collective-permute-start | bytes 405512 | tf_op jit(solution)/shard_map/ppermute | solution.py:403
  20.0 8.9 %collective-permute-start.7 = (bf16[528,128]{1,0:T(8,128)(2,1)S(1)}, bf16[528,128]{1,0:T(8,128)(2,1)S(1)}, u32[]{:S(2)}, u32[]{:S(2)}) collective-permute-start(bf16[528,128]{1,0:T(8,128)(2,1)S(1)} %collective-permute-done.5.refs_1_), channel_id=1, source_target_pairs={{2,0},{4,2},{6,4},{7,6},{5,7},{3,5},{1,3},{0,1},{10,8},{12,10},{14... | collective-permute-start | bytes 405512 | tf_op jit(solution)/shard_map/ppermute | solution.py:403
  22.6 7.6 %collective-permute-start.19 = (bf16[528,128]{1,0:T(8,128)(2,1)S(1)}, bf16[528,128]{1,0:T(8,128)(2,1)S(1)}, u32[]{:S(2)}, u32[]{:S(2)}) collective-permute-start(bf16[528,128]{1,0:T(8,128)(2,1)S(1)} %collective-permute-done.18.refs_0_), channel_id=1, source_target_pairs={{0,2},{2,4},{4,6},{6,7},{7,5},{5,3},{3,1},{1,0},{8,10},{10,12},{12... | collective-permute-start | bytes 405512 | tf_op jit(solution)/shard_map/ppermute | solution.py:400
  28.1 6.4 %collective-permute-start.23 = (bf16[528,128]{1,0:T(8,128)(2,1)S(1)}, bf16[528,128]{1,0:T(8,128)(2,1)S(1)}, u32[]{:S(2)}, u32[]{:S(2)}) collective-permute-start(bf16[528,128]{1,0:T(8,128)(2,1)S(1)} %collective-permute-done.22.refs_1_), channel_id=1, source_target_pairs={{2,0},{4,2},{6,4},{7,6},{5,7},{3,5},{1,3},{0,1},{10,8},{12,10},{14... | collective-permute-start | bytes 405512 | tf_op jit(solution)/shard_map/ppermute | solution.py:403
  30.9 6.0 %collective-permute-start.8 = (bf16[528,128]{1,0:T(8,128)(2,1)S(1)}, bf16[528,128]{1,0:T(8,128)(2,1)S(1)}, u32[]{:S(2)}, u32[]{:S(2)}) collective-permute-start(bf16[528,128]{1,0:T(8,128)(2,1)S(1)} %collective-permute-done.6.refs_0_), channel_id=1, source_target_pairs={{0,2},{2,4},{4,6},{6,7},{7,5},{5,3},{3,1},{1,0},{8,10},{10,12},{12... | collective-permute-start | bytes 405512 | tf_op jit(solution)/shard_map/ppermute | solution.py:400
  34.5 6.2 %collective-permute-start.27 = (bf16[528,128]{1,0:T(8,128)(2,1)S(1)}, bf16[528,128]{1,0:T(8,128)(2,1)S(1)}, u32[]{:S(2)}, u32[]{:S(2)}) collective-permute-start(bf16[528,128]{1,0:T(8,128)(2,1)S(1)} %collective-permute-done.23.refs_1_), channel_id=1, source_target_pairs={{2,0},{4,2},{6,4},{7,6},{5,7},{3,5},{1,3},{0,1},{10,8},{12,10},{14... | collective-permute-start | bytes 405512 | tf_op jit(solution)/shard_map/ppermute | solution.py:403
  34.6 7.9 %collective-permute-start.10 = (bf16[528,128]{1,0:T(8,128)(2,1)S(1)}, bf16[528,128]{1,0:T(8,128)(2,1)S(1)}, u32[]{:S(2)}, u32[]{:S(2)}) collective-permute-start(bf16[528,128]{1,0:T(8,128)(2,1)S(1)} %collective-permute-done.7.refs_1_), channel_id=1, source_target_pairs={{2,0},{4,2},{6,4},{7,6},{5,7},{3,5},{1,3},{0,1},{10,8},{12,10},{14... | collective-permute-start | bytes 405512 | tf_op jit(solution)/shard_map/ppermute | solution.py:403
  36.6 9.3 %collective-permute-start.21 = (bf16[528,128]{1,0:T(8,128)(2,1)S(1)}, bf16[528,128]{1,0:T(8,128)(2,1)S(1)}, u32[]{:S(2)}, u32[]{:S(2)}) collective-permute-start(bf16[528,128]{1,0:T(8,128)(2,1)S(1)} %collective-permute-done.19.refs_0_), channel_id=1, source_target_pairs={{0,2},{2,4},{4,6},{6,7},{7,5},{5,3},{3,1},{1,0},{8,10},{10,12},{12... | collective-permute-start | bytes 405512 | tf_op jit(solution)/shard_map/ppermute | solution.py:400
  37.8 9.9 %collective-permute-start.9 = (bf16[528,128]{1,0:T(8,128)(2,1)S(1)}, bf16[528,128]{1,0:T(8,128)(2,1)S(1)}, u32[]{:S(2)}, u32[]{:S(2)}) collective-permute-start(bf16[528,128]{1,0:T(8,128)(2,1)S(1)} %shard_map.71), channel_id=1, source_target_pairs={{0,2},{2,4},{4,6},{6,7},{7,5},{5,3},{3,1},{1,0},{8,10},{10,12},{12... | collective-permute-start | bytes 405512 | tf_op jit(solution)/shard_map/ppermute | solution.py:400
  42.5 9.0 %collective-permute-start.28 = (bf16[528,128]{1,0:T(8,128)(2,1)S(1)}, bf16[528,128]{1,0:T(8,128)(2,1)S(1)}, u32[]{:S(2)}, u32[]{:S(2)}) collective-permute-start(bf16[528,128]{1,0:T(8,128)(2,1)S(1)} %shard_map.86), channel_id=1, source_target_pairs={{2,0},{4,2},{6,4},{7,6},{5,7},{3,5},{1,3},{0,1},{10,8},{12,10},{14... | collective-permute-start | bytes 405512 | tf_op jit(solution)/shard_map/ppermute | solution.py:403
  43.8 8.0 %collective-permute-start.14 = (bf16[528,128]{1,0:T(8,128)(2,1)S(1)}, bf16[528,128]{1,0:T(8,128)(2,1)S(1)}, u32[]{:S(2)}, u32[]{:S(2)}) collective-permute-start(bf16[528,128]{1,0:T(8,128)(2,1)S(1)} %get-tuple-element.58), channel_id=1, source_target_pairs={{2,0},{4,2},{6,4},{7,6},{5,7},{3,5},{1,3},{0,1},{10,8},{12,10},{14... | collective-permute-start | bytes 405512 | tf_op jit(solution)/shard_map/ppermute | solution.py:403
  48.0 6.2 %collective-permute-start.11 = (bf16[528,128]{1,0:T(8,128)(2,1)S(1)}, bf16[528,128]{1,0:T(8,128)(2,1)S(1)}, u32[]{:S(2)}, u32[]{:S(2)}) collective-permute-start(bf16[528,128]{1,0:T(8,128)(2,1)S(1)} %shard_map.73), channel_id=1, source_target_pairs={{0,2},{2,4},{4,6},{6,7},{7,5},{5,3},{3,1},{1,0},{8,10},{10,12},{12... | collective-permute-start | bytes 405512 | tf_op jit(solution)/shard_map/ppermute | solution.py:400
  49.4 7.7 %collective-permute-start.24 = (bf16[528,128]{1,0:T(8,128)(2,1)S(1)}, bf16[528,128]{1,0:T(8,128)(2,1)S(1)}, u32[]{:S(2)}, u32[]{:S(2)}) collective-permute-start(bf16[528,128]{1,0:T(8,128)(2,1)S(1)} %get-tuple-element.75), channel_id=1, source_target_pairs={{0,2},{2,4},{4,6},{6,7},{7,5},{5,3},{3,1},{1,0},{8,10},{10,12},{12... | collective-permute-start | bytes 405512 | tf_op jit(solution)/shard_map/ppermute | solution.py:400
  51.7 6.8 %collective-permute-start.29 = (bf16[528,128]{1,0:T(8,128)(2,1)S(1)}, bf16[528,128]{1,0:T(8,128)(2,1)S(1)}, u32[]{:S(2)}, u32[]{:S(2)}) collective-permute-start(bf16[528,128]{1,0:T(8,128)(2,1)S(1)} %shard_map.87), channel_id=1, source_target_pairs={{2,0},{4,2},{6,4},{7,6},{5,7},{3,5},{1,3},{0,1},{10,8},{12,10},{14... | collective-permute-start | bytes 405512 | tf_op jit(solution)/shard_map/ppermute | solution.py:403
  52.0 9.0 %collective-permute-start.15 = (bf16[528,128]{1,0:T(8,128)(2,1)S(1)}, bf16[528,128]{1,0:T(8,128)(2,1)S(1)}, u32[]{:S(2)}, u32[]{:S(2)}) collective-permute-start(bf16[528,128]{1,0:T(8,128)(2,1)S(1)} %shard_map.76), channel_id=1, source_target_pairs={{2,0},{4,2},{6,4},{7,6},{5,7},{3,5},{1,3},{0,1},{10,8},{12,10},{14... | collective-permute-start | bytes 405512 | tf_op jit(solution)/shard_map/ppermute | solution.py:403
  54.5 6.9 %collective-permute-start.12 = (bf16[528,128]{1,0:T(8,128)(2,1)S(1)}, bf16[528,128]{1,0:T(8,128)(2,1)S(1)}, u32[]{:S(2)}, u32[]{:S(2)}) collective-permute-start(bf16[528,128]{1,0:T(8,128)(2,1)S(1)} %shard_map.74), channel_id=1, source_target_pairs={{0,2},{2,4},{4,6},{6,7},{7,5},{5,3},{3,1},{1,0},{8,10},{10,12},{12... | collective-permute-start | bytes 405512 | tf_op jit(solution)/shard_map/ppermute | solution.py:400
  57.4 6.4 %collective-permute-start.25 = (bf16[528,128]{1,0:T(8,128)(2,1)S(1)}, bf16[528,128]{1,0:T(8,128)(2,1)S(1)}, u32[]{:S(2)}, u32[]{:S(2)}) collective-permute-start(bf16[528,128]{1,0:T(8,128)(2,1)S(1)} %shard_map.84), channel_id=1, source_target_pairs={{0,2},{2,4},{4,6},{6,7},{7,5},{5,3},{3,1},{1,0},{8,10},{10,12},{12... | collective-permute-start | bytes 405512 | tf_op jit(solution)/shard_map/ppermute | solution.py:400
  58.8 6.6 %collective-permute-start.30 = (bf16[528,128]{1,0:T(8,128)(2,1)S(1)}, bf16[528,128]{1,0:T(8,128)(2,1)S(1)}, u32[]{:S(2)}, u32[]{:S(2)}) collective-permute-start(bf16[528,128]{1,0:T(8,128)(2,1)S(1)} %shard_map.88), channel_id=1, source_target_pairs={{2,0},{4,2},{6,4},{7,6},{5,7},{3,5},{1,3},{0,1},{10,8},{12,10},{14... | collective-permute-start | bytes 405512 | tf_op jit(solution)/shard_map/ppermute | solution.py:403
  67.1 8.0 %collective-permute-start.17 = (bf16[272,128]{1,0:T(8,128)(2,1)S(1)}, bf16[272,128]{1,0:T(8,128)(2,1)S(1)}, u32[]{:S(2)}, u32[]{:S(2)}) collective-permute-start(bf16[272,128]{1,0:T(8,128)(2,1)S(1)} %get-tuple-element.60), channel_id=1, source_target_pairs={{0,8},{8,0},{16,24},{24,16},{1,9},{9,1},{17,25},{25,17},{2,10},{10... | collective-permute-start | bytes 208904 | tf_op jit(solution)/shard_map/ppermute | solution.py:386
  (14 other events, 83.4 us)

commit v8 on v7

--- a/solution.py
+++ b/solution.py
@@ -96,19 +96,20 @@
     return [m / t for m, t in zip(mixed, totals)], level
 
 
-def relayout_kernel(place_ref, queries_ref, *outs):
+def relayout_kernel(owners, place_ref, queries_ref, *outs):
+    group = lax.div(place_ref[0], owners)
     for d, out in enumerate(outs):
-        values = queries_ref[place_ref[0] ^ d].astype(F32)
+        values = queries_ref[group ^ d].astype(F32)
         for head in range(KVH):
             first = head * GQ
             parts = [values[:, (first + g) * HD : (first + g + 1) * HD] for g in range(GQ)]
             out[head * ROWS : (head + 1) * ROWS, :] = jnp.concatenate(parts, axis=0).astype(BF16)
 
 
-def relayout(place, queries):
+def relayout(place, owners, queries):
     groups = queries.shape[0]
     return pl.pallas_call(
-        relayout_kernel,
+        functools.partial(relayout_kernel, owners),
         out_shape=[jax.ShapeDtypeStruct((BODY, HD), BF16)] * groups,
         in_specs=[IN_SMEM, IN_VMEM],
         out_specs=[IN_VMEM] * groups,
@@ -117,12 +118,13 @@
     )(place, queries)
 
 
-def new_kernel(place_ref, *refs):
+def new_kernel(owners, place_ref, *refs):
+    group = lax.div(place_ref[0], owners)
     queries, (new_ref, out_ref, level_ref) = refs[:-3], refs[-3:]
     step = lax.broadcasted_iota(jnp.int32, (ROWS, STEPS), 0) % STEPS
     usable = lax.broadcasted_iota(jnp.int32, (ROWS, STEPS), 1) <= step
     for d, query in enumerate(queries):
-        new = new_ref[place_ref[0] ^ d]
+        new = new_ref[group ^ d]
         heads = [new[:, head * HD : (head + 1) * HD] for head in range(2 * KVH)]
         rows = [query[head * ROWS : (head + 1) * ROWS, :] for head in range(KVH)]
         mixed, level = attend(rows, heads[:KVH], heads[KVH:], usable)
@@ -131,10 +133,10 @@
         level_ref[d] = level
 
 
-def new_tokens(place, queries, new_kv):
+def new_tokens(place, owners, queries, new_kv):
     groups = len(queries)
     return pl.pallas_call(
-        new_kernel,
+        functools.partial(new_kernel, owners),
         out_shape=[
             jax.ShapeDtypeStruct((groups, BODY, HD), F32),
             jax.ShapeDtypeStruct((groups, HALF, LANES), F32),
@@ -194,7 +196,8 @@
     )(after, kv_cache)
 
 
-def item_kernel(slots, visitors, place_ref, cache_ref, *refs):
+def item_kernel(slots, visitors, owners, place_ref, cache_ref, *refs):
+    group, owner = lax.div(place_ref[0], owners), lax.rem(place_ref[0], owners)
     sides = len(slots)
     query_refs, out_refs, (level_ref, code_ref) = refs[:sides], refs[sides : 2 * sides], refs[2 * sides :]
     each = len(slots[0])
@@ -202,11 +205,11 @@
         lists = query_ref.shape[0] - each * BODY
         rows = lax.broadcasted_iota(jnp.int32, (lists, LANES), 0)
         table = query_ref[each * BODY :, :].astype(F32)
-        table = jnp.where(lane_ids(lists) == place_ref[1], table, 0.0)
+        table = jnp.where(lane_ids(lists) == owner, table, 0.0)
         for pair in range(each // 2):
             factor = jnp.zeros((lists, LANES), F32)
             for second in range(2):
-                row = place_ref[0] ^ slots[side][2 * pair + second]
+                row = group ^ slots[side][2 * pair + second]
                 factor = jnp.where(rows == row, float(4096**second), factor)
                 factor = jnp.where(rows == row + visitors, float(256 * 4096**second), factor)
             code_ref[(side * each) // 2 + pair] = jnp.sum(table * factor).astype(jnp.int32)
@@ -251,11 +254,11 @@
             out_ref[start : start + HALF, :] = pack_stats(level_ref[entry] + level_ref[entry + 1])
 
 
-def items(place, kv_cache, payloads, slots, visitors):
+def items(place, owners, kv_cache, payloads, slots, visitors):
     count = sum(len(row) for row in slots)
     rows = len(slots[0]) // 2 * PAIR
     return pl.pallas_call(
-        functools.partial(item_kernel, slots, visitors),
+        functools.partial(item_kernel, slots, visitors, owners),
         out_shape=[jax.ShapeDtypeStruct((rows, HD), BF16)] * len(slots),
         in_specs=[IN_SMEM] + [IN_VMEM] * (1 + len(slots)),
         out_specs=[IN_VMEM] * len(slots),
@@ -335,9 +338,10 @@
     )(ahead, behind, own)
 
 
-def final_kernel(first, early, place_ref, *refs):
+def final_kernel(first, early, owners, place_ref, *refs):
     earlier, parts = refs[:early], refs[early:-4]
     new_ref, level_ref, out_ref, rows_ref = refs[-4:]
+    group = lax.div(place_ref[0], owners)
     for number, part in enumerate(parts):
         d = first + number
         shares, _ = blend([unpack_stats(part[BODY:LONE, :]), level_ref[d]])
@@ -345,19 +349,19 @@
             row = tile_start(index)
             rows_ref[number, row : row + HALF, :] = tile
     for number in range(len(parts)):
-        row = place_ref[0] ^ (first + number) if early else number
+        row = group ^ (first + number) if early else number
         for head in range(KVH * GQ):
             tile = rows_ref[number, head * STEPS : (head + 1) * STEPS, :]
             out_ref[row, :, head * HD : (head + 1) * HD] = tile.astype(BF16)
     for ref in earlier:
-        for d in range(ref.shape[0]):
-            out_ref[place_ref[0] ^ d] = ref[d]
-
-
-def final(place, parts, first, new_out, new_level, earlier=()):
+        for number in range(ref.shape[0]):
+            out_ref[group ^ (len(parts) + number)] = ref[number]
+
+
+def final(place, owners, parts, first, new_out, new_level, earlier=()):
     requests = len(parts) + sum(e.shape[0] for e in earlier)
     return pl.pallas_call(
-        functools.partial(final_kernel, first, len(earlier)),
+        functools.partial(final_kernel, first, len(earlier), owners),
         out_shape=jax.ShapeDtypeStruct((requests, STEPS, KVH * GQ * HD), BF16),
         in_specs=[IN_SMEM] + [IN_VMEM] * (len(earlier) + len(parts) + 2),
         out_specs=IN_VMEM,
@@ -380,21 +384,21 @@
     order = ring_order(owners)
     forward = [(order[i], order[(i + 1) % owners]) for i in range(owners)]
     backward = [(b, a) for a, b in forward]
-    place = jnp.stack([lax.axis_index("grp"), lax.axis_index("cache")]).astype(jnp.int32)
+    place = jnp.reshape(lax.axis_index(("grp", "cache")), (1,)).astype(jnp.int32)
 
     def swap(array, d):
         return lax.ppermute(array, "grp", [(g, g ^ d) for g in range(groups)]) if d else array
 
-    rows = relayout(place, queries)
+    rows = relayout(place, owners, queries)
     visits = [rows[0]] + [None] * (groups - 1)
     for d in range(groups - 1, 0, -1):
         visits[d] = swap(rows[d], d)
-    new_out, new_level = new_tokens(place, rows, new_kv)
+    new_out, new_level = new_tokens(place, owners, rows, new_kv)
     lists = page_lists(page_owner, page_index, lengths)
 
     cut = requests // 2
     slots = [list(range(cut)), list(range(cut, requests))]
-    owned = functools.partial(items, place, kv_cache, visitors=requests)
+    owned = functools.partial(items, place, owners, kv_cache, visitors=requests)
 
     def up(array):
         return lax.ppermute(array, "cache", forward)
@@ -406,10 +410,8 @@
         return lax.optimization_barrier((array, others))[0]
 
     blocks = [payload(lists, visits[:cut])]
-    ahead, behind = up(blocks[0]), down(blocks[0])
     blocks.append(payload(lists, visits[cut:], [touch(kv_cache, blocks[0])]))
-    second = after(blocks[1], ahead, behind)
-    below, above, far = [ahead, up(second)], [behind, down(second)], [None, None]
+    below, above, far = list(blocks), list(blocks), [None, None]
     parts = {(half, 0): part for half, part in enumerate(owned(blocks, slots))}
     for step in range(1, reach + 1):
         for half in range(2):
@@ -418,9 +420,8 @@
                 far[half] = owned([arrival], [slots[half]])[0]
                 continue
             done = [parts[half, 0]] if step == 1 else [parts[half, 1 - step], parts[half, step - 1]]
-            if step > 1:
-                below[half], above[half] = up(below[half]), down(above[half])
-            below[half], above[half] = after(below[half], *done), after(above[half], *done)
+            below[half] = after(up(below[half]), *done)
+            above[half] = after(down(above[half]), *done)
             parts[half, -step], parts[half, step] = owned([below[half], above[half]], [slots[half]] * 2)
 
     arrived = []
@@ -435,10 +436,11 @@
                 if step > 0:
                     chain = merge(chain, parts[half, sign * step])
             arrived.append(chain)
-    returned = gather(arrived[0], arrived[1], parts[0, 0]) + gather(arrived[2], arrived[3], parts[1, 0])
-    home = [swap(part, d) for d, part in enumerate(returned)]
-    early = final(place, home[:cut], 0, new_out, new_level)
-    return final(place, home[cut:], cut, new_out, new_level, [early])
+    back = gather(arrived[2], arrived[3], parts[1, 0])
+    front = gather(arrived[0], arrived[1], after(parts[0, 0], *back))
+    home = [swap(part, d) for d, part in enumerate(front + back)]
+    early = final(place, owners, home[cut:], cut, new_out, new_level)
+    return final(place, owners, home[:cut], 0, new_out, new_level, [early])
 
 
 def solution(mesh):

time: 78.3 us -> 68.8 us (0.88); the launches traced: 78.8 us -> 68 us
  Pallas kernels: 20.9 us -> 12.5 us
  starting transfers between devices: 39.2 us -> 36.7 us
  waiting for transfers between devices: 11.6 us -> 12.8 us
  local copies, waits for them, and re-layouts: 5.3 us -> 4.33 us
    ppermute x14, starting transfers between devices: 24.3 us -> 7.66 us  [up(): return lax.ppermute(array, 'cache', forward)]
    ppermute x14, starting transfers between devices: 10 us -> 24.1 us  [down(): return lax.ppermute(array, 'cache', backward)]
    pallas_call x13, Pallas kernels: 17.4 us -> 9 us  [the longest x9 6.5 us: items(): pl.pallas_call(functools.partial(item_kernel, slots, visitors, owners), o...]
    ppermute x14, waiting for transfers between devices: 2.94 us -> 6.05 us  [down(): return lax.ppermute(array, 'cache', backward)]
    ppermute x6, waiting for transfers between devices: 2.06 us -> 0.82 us  [swap(): lax.ppermute(array, 'grp', [(g, g ^ d) for g in range(groups)])]
    unnamed x8, local copies, waits for them, and re-layouts: 5.3 us -> 4.33 us
  transfers between devices with their start and end apart: 34 -> 34, of which waited for: 11 -> 12; matrix products, arithmetic and copies ran while one was open for 2% -> 2% of each run, Pallas kernels for 24% -> 17%
where the time goes in v8:
time: 68.8 us; the launch traced here: 68 us
  starting transfers between devices  36.7 us (53%)
  waiting for transfers between devices  12.8 us (19%)
  Pallas kernels  12.5 us (18%)
  local copies, waits for them, and re-layouts  4.33 us (6%)
  other arithmetic  1.52 us (2%)
    ppermute x14, starting transfers between devices, down(): return lax.ppermute(array, 'cache', backward)  24.1 us
    ppermute x14, starting transfers between devices, up(): return lax.ppermute(array, 'cache', forward)  7.66 us
    pallas_call x9, Pallas kernels, items(): pl.pallas_call(functools.partial(item_kernel, slots, visitors, owners), o...  6.5 us
    ppermute x14, waiting for transfers between devices, down(): return lax.ppermute(array, 'cache', backward)  6.05 us
    ppermute x14, waiting for transfers between devices, up(): return lax.ppermute(array, 'cache', forward)  5.97 us
    ppermute x6, starting transfers between devices, swap(): lax.ppermute(array, 'grp', [(g, g ^ d) for g in range(groups)])  4.9 us
    unnamed x8, local copies, waits for them, and re-layouts  4.33 us
    pallas_call x10, Pallas kernels, merge(): pl.pallas_call(merge_kernel, out_shape=jax.ShapeDtypeStruct(own.shape, BF...  2.65 us
  transfers between devices with their start and end apart: 34, of which 12 were waited for; matrix products, arithmetic and copies ran while one was open for 2% of the time, Pallas kernels for 17%

profile of v8, /device:TPU:0, one launch (start us, length us, event | category | flops | bytes accessed | tf_op | source)
XLA Modules:
  0.0 68.0 jit_solution(13589203313651564032)
XLA Ops:
  1.5 2.6 %collective-permute-start = (bf16[256,128]{1,0:T(8,128)(2,1)S(1)}, bf16[256,128]{1,0:T(8,128)(2,1)S(1)}, u32[]{:S(2)}, u32[]{:S(2)}) collective-permute-start(bf16[256,128]{1,0:T(8,128)(2,1)S(1)} %get-tuple-element.42.refs_2_), channel_id=1, source_target_pairs={{0,16},{8,24},{16,0},{24,8},{1,17},{9,25},{17,1},{25,9},{2,18},{10... | collective-permute-start | bytes 196616 | tf_op jit(solution)/shard_map/ppermute | solution.py:390
  5.7 3.4 %copy-done = bf16[16,128,2048]{2,1,0:T(8,128)(2,1)S(1)} copy-done((bf16[16,128,2048]{2,1,0:T(8,128)(2,1)S(1)}, bf16[16,128,2048]{2,1,0:T(8,128)(2,1)}, u32[]{:S(2)}) %copy-start) | copy-done | bytes 8388632
  9.1 1.8 %collective-permute-start.5 = (bf16[528,128]{1,0:T(8,128)(2,1)S(1)}, bf16[528,128]{1,0:T(8,128)(2,1)S(1)}, u32[]{:S(2)}, u32[]{:S(2)}) collective-permute-start(bf16[528,128]{1,0:T(8,128)(2,1)S(1)} %shard_map.67.refs_1_), channel_id=1, source_target_pairs={{2,0},{4,2},{6,4},{7,6},{5,7},{3,5},{1,3},{0,1},{10,8},{12,10},{14... | collective-permute-start | bytes 405512 | tf_op jit(solution)/shard_map/ppermute | solution.py:407
  11.2 1.8 %collective-permute-start.3 = (bf16[528,128]{1,0:T(8,128)(2,1)S(1)}, bf16[528,128]{1,0:T(8,128)(2,1)S(1)}, u32[]{:S(2)}, u32[]{:S(2)}) collective-permute-start(bf16[528,128]{1,0:T(8,128)(2,1)S(1)} %shard_map.67.refs_1_), channel_id=1, source_target_pairs={{0,2},{2,4},{4,6},{6,7},{7,5},{5,3},{3,1},{1,0},{8,10},{10,12},{12... | collective-permute-start | bytes 405512 | tf_op jit(solution)/shard_map/ppermute | solution.py:404
  13.3 1.3 %shard_map.68 = (bf16[528,128]{1,0:T(8,128)(2,1)S(1)}, bf16[528,128]{1,0:T(8,128)(2,1)S(1)}) custom-call(s32[1]{0:T(128)} %bitcast.place_ref, bf16[16,128,2048]{2,1,0:T(8,128)(2,1)S(1)} %copy-done.1, bf16[528,128]{1,0:T(8,128)(2,1)S(1)} %shard_map.65.after_ref.refs_0_, bf16[528,128]{1,0:T(8,128)(2,1)S(1)} %shard_map.67.refs_1_), custom_call_target="tpu_custom_call" | custom-call | flops 67108864 | bytes 2097152 | tf_op jit(solution)/shard_map/pallas_call | solution.py:260
  15.1 2.2 %collective-permute-start.7 = (bf16[528,128]{1,0:T(8,128)(2,1)S(1)}, bf16[528,128]{1,0:T(8,128)(2,1)S(1)}, u32[]{:S(2)}, u32[]{:S(2)}) collective-permute-start(bf16[528,128]{1,0:T(8,128)(2,1)S(1)} %collective-permute-done.5.refs_1_), channel_id=1, source_target_pairs={{2,0},{4,2},{6,4},{7,6},{5,7},{3,5},{1,3},{0,1},{10,8},{12,10},{14... | collective-permute-start | bytes 405512 | tf_op jit(solution)/shard_map/ppermute | solution.py:407
  17.7 2.4 %collective-permute-done.3.refs_0_ = bf16[528,128]{1,0:T(8,128)(2,1)S(1)} collective-permute-done((bf16[528,128]{1,0:T(8,128)(2,1)S(1)}, bf16[528,128]{1,0:T(8,128)(2,1)S(1)}, u32[]{:S(2)}, u32[]{:S(2)}) %collective-permute-start.3) | collective-permute-done | bytes 135200 | tf_op jit(solution)/shard_map/ppermute | solution.py:404
  20.5 1.6 %collective-permute-start.23 = (bf16[528,128]{1,0:T(8,128)(2,1)S(1)}, bf16[528,128]{1,0:T(8,128)(2,1)S(1)}, u32[]{:S(2)}, u32[]{:S(2)}) collective-permute-start(bf16[528,128]{1,0:T(8,128)(2,1)S(1)} %collective-permute-done.21.refs_1_), channel_id=1, source_target_pairs={{2,0},{4,2},{6,4},{7,6},{5,7},{3,5},{1,3},{0,1},{10,8},{12,10},{14... | collective-permute-start | bytes 405512 | tf_op jit(solution)/shard_map/ppermute | solution.py:407
  22.9 1.6 %collective-permute-start.8 = (bf16[528,128]{1,0:T(8,128)(2,1)S(1)}, bf16[528,128]{1,0:T(8,128)(2,1)S(1)}, u32[]{:S(2)}, u32[]{:S(2)}) collective-permute-start(bf16[528,128]{1,0:T(8,128)(2,1)S(1)} %collective-permute-done.7.refs_1_), channel_id=1, source_target_pairs={{2,0},{4,2},{6,4},{7,6},{5,7},{3,5},{1,3},{0,1},{10,8},{12,10},{14... | collective-permute-start | bytes 405512 | tf_op jit(solution)/shard_map/ppermute | solution.py:407
  26.7 1.2 %collective-permute-done.8.refs_1_ = bf16[528,128]{1,0:T(8,128)(2,1)S(1)} collective-permute-done((bf16[528,128]{1,0:T(8,128)(2,1)S(1)}, bf16[528,128]{1,0:T(8,128)(2,1)S(1)}, u32[]{:S(2)}, u32[]{:S(2)}) %collective-permute-start.8) | collective-permute-done | bytes 135200 | tf_op jit(solution)/shard_map/ppermute | solution.py:407
  27.9 1.9 %collective-permute-start.12 = (bf16[528,128]{1,0:T(8,128)(2,1)S(1)}, bf16[528,128]{1,0:T(8,128)(2,1)S(1)}, u32[]{:S(2)}, u32[]{:S(2)}) collective-permute-start(bf16[528,128]{1,0:T(8,128)(2,1)S(1)} %collective-permute-done.8.refs_1_), channel_id=1, source_target_pairs={{2,0},{4,2},{6,4},{7,6},{5,7},{3,5},{1,3},{0,1},{10,8},{12,10},{14... | collective-permute-start | bytes 405512 | tf_op jit(solution)/shard_map/ppermute | solution.py:407
  29.8 1.3 %shard_map.82 = (bf16[528,128]{1,0:T(8,128)(2,1)S(1)}, bf16[528,128]{1,0:T(8,128)(2,1)S(1)}) custom-call(s32[1]{0:T(128)} %bitcast.place_ref, bf16[16,128,2048]{2,1,0:T(8,128)(2,1)S(1)} %copy-done.1, bf16[528,128]{1,0:T(8,128)(2,1)S(1)} %collective-permute-done.20.refs_0_, bf16[528,128]{1,0:T(8,128)(2,1)S(1)} %collective-permute-done.23.refs_1_), custom_call_target="tpu_custom_call" | custom-call | flops 67108864 | bytes 2097152 | tf_op jit(solution)/shard_map/pallas_call | solution.py:260
  31.7 1.5 %collective-permute-start.26 = (bf16[528,128]{1,0:T(8,128)(2,1)S(1)}, bf16[528,128]{1,0:T(8,128)(2,1)S(1)}, u32[]{:S(2)}, u32[]{:S(2)}) collective-permute-start(bf16[528,128]{1,0:T(8,128)(2,1)S(1)} %collective-permute-done.23.refs_1_), channel_id=1, source_target_pairs={{2,0},{4,2},{6,4},{7,6},{5,7},{3,5},{1,3},{0,1},{10,8},{12,10},{14... | collective-permute-start | bytes 405512 | tf_op jit(solution)/shard_map/ppermute | solution.py:407
  34.4 3.1 %collective-permute-start.13 = (bf16[528,128]{1,0:T(8,128)(2,1)S(1)}, bf16[528,128]{1,0:T(8,128)(2,1)S(1)}, u32[]{:S(2)}, u32[]{:S(2)}) collective-permute-start(bf16[528,128]{1,0:T(8,128)(2,1)S(1)} %shard_map.74), channel_id=1, source_target_pairs={{2,0},{4,2},{6,4},{7,6},{5,7},{3,5},{1,3},{0,1},{10,8},{12,10},{14... | collective-permute-start | bytes 405512 | tf_op jit(solution)/shard_map/ppermute | solution.py:407
  39.1 2.1 %collective-permute-done.13.arrived_ref = bf16[528,128]{1,0:T(8,128)(2,1)S(1)} collective-permute-done((bf16[528,128]{1,0:T(8,128)(2,1)S(1)}, bf16[528,128]{1,0:T(8,128)(2,1)S(1)}, u32[]{:S(2)}, u32[]{:S(2)}) %collective-permute-start.13) | collective-permute-done | bytes 135200 | tf_op jit(solution)/shard_map/ppermute | solution.py:407
  41.4 2.5 %collective-permute-start.14 = (bf16[528,128]{1,0:T(8,128)(2,1)S(1)}, bf16[528,128]{1,0:T(8,128)(2,1)S(1)}, u32[]{:S(2)}, u32[]{:S(2)}) collective-permute-start(bf16[528,128]{1,0:T(8,128)(2,1)S(1)} %shard_map.75), channel_id=1, source_target_pairs={{2,0},{4,2},{6,4},{7,6},{5,7},{3,5},{1,3},{0,1},{10,8},{12,10},{14... | collective-permute-start | bytes 405512 | tf_op jit(solution)/shard_map/ppermute | solution.py:407
  43.9 1.3 %shard_map.84 = (bf16[528,128]{1,0:T(8,128)(2,1)S(1)}, bf16[528,128]{1,0:T(8,128)(2,1)S(1)}) custom-call(s32[1]{0:T(128)} %bitcast.place_ref, bf16[16,128,2048]{2,1,0:T(8,128)(2,1)S(1)} %copy-done.1, bf16[528,128]{1,0:T(8,128)(2,1)S(1)} %collective-permute-done.22.refs_0_, bf16[528,128]{1,0:T(8,128)(2,1)S(1)} %collective-permute-done.26.refs_1_), custom_call_target="tpu_custom_call" | custom-call | flops 67108864 | bytes 2097152 | tf_op jit(solution)/shard_map/pallas_call | solution.py:260
  45.5 2.1 %collective-permute-start.27 = (bf16[528,128]{1,0:T(8,128)(2,1)S(1)}, bf16[528,128]{1,0:T(8,128)(2,1)S(1)}, u32[]{:S(2)}, u32[]{:S(2)}) collective-permute-start(bf16[528,128]{1,0:T(8,128)(2,1)S(1)} %shard_map.85), channel_id=1, source_target_pairs={{0,2},{2,4},{4,6},{6,7},{7,5},{5,3},{3,1},{1,0},{8,10},{10,12},{12... | collective-permute-start | bytes 405512 | tf_op jit(solution)/shard_map/ppermute | solution.py:404
  48.2 2.5 %collective-permute-start.15 = (bf16[528,128]{1,0:T(8,128)(2,1)S(1)}, bf16[528,128]{1,0:T(8,128)(2,1)S(1)}, u32[]{:S(2)}, u32[]{:S(2)}) collective-permute-start(bf16[528,128]{1,0:T(8,128)(2,1)S(1)} %shard_map.76), channel_id=1, source_target_pairs={{2,0},{4,2},{6,4},{7,6},{5,7},{3,5},{1,3},{0,1},{10,8},{12,10},{14... | collective-permute-start | bytes 405512 | tf_op jit(solution)/shard_map/ppermute | solution.py:407
  51.0 1.8 %collective-permute-start.31 = (bf16[528,128]{1,0:T(8,128)(2,1)S(1)}, bf16[528,128]{1,0:T(8,128)(2,1)S(1)}, u32[]{:S(2)}, u32[]{:S(2)}) collective-permute-start(bf16[528,128]{1,0:T(8,128)(2,1)S(1)} %shard_map.88), channel_id=1, source_target_pairs={{2,0},{4,2},{6,4},{7,6},{5,7},{3,5},{1,3},{0,1},{10,8},{12,10},{14... | collective-permute-start | bytes 405512 | tf_op jit(solution)/shard_map/ppermute | solution.py:407
  55.4 1.9 %collective-permute-start.16 = (bf16[528,128]{1,0:T(8,128)(2,1)S(1)}, bf16[528,128]{1,0:T(8,128)(2,1)S(1)}, u32[]{:S(2)}, u32[]{:S(2)}) collective-permute-start(bf16[528,128]{1,0:T(8,128)(2,1)S(1)} %shard_map.77), channel_id=1, source_target_pairs={{2,0},{4,2},{6,4},{7,6},{5,7},{3,5},{1,3},{0,1},{10,8},{12,10},{14... | collective-permute-start | bytes 405512 | tf_op jit(solution)/shard_map/ppermute | solution.py:407
  57.6 1.4 %collective-permute-start.32 = (bf16[528,128]{1,0:T(8,128)(2,1)S(1)}, bf16[528,128]{1,0:T(8,128)(2,1)S(1)}, u32[]{:S(2)}, u32[]{:S(2)}) collective-permute-start(bf16[528,128]{1,0:T(8,128)(2,1)S(1)} %shard_map.89), channel_id=1, source_target_pairs={{2,0},{4,2},{6,4},{7,6},{5,7},{3,5},{1,3},{0,1},{10,8},{12,10},{14... | collective-permute-start | bytes 405512 | tf_op jit(solution)/shard_map/ppermute | solution.py:407
  60.8 1.7 %collective-permute-start.17 = (bf16[272,128]{1,0:T(8,128)(2,1)S(1)}, bf16[272,128]{1,0:T(8,128)(2,1)S(1)}, u32[]{:S(2)}, u32[]{:S(2)}) collective-permute-start(bf16[272,128]{1,0:T(8,128)(2,1)S(1)} %get-tuple-element.59), channel_id=1, source_target_pairs={{0,16},{8,24},{16,0},{24,8},{1,17},{9,25},{17,1},{25,9},{2,18},{10... | collective-permute-start | bytes 208904 | tf_op jit(solution)/shard_map/ppermute | solution.py:390
  62.6 1.6 %collective-permute-done.29.ahead_ref = bf16[528,128]{1,0:T(8,128)(2,1)S(1)} collective-permute-done((bf16[528,128]{1,0:T(8,128)(2,1)S(1)}, bf16[528,128]{1,0:T(8,128)(2,1)S(1)}, u32[]{:S(2)}, u32[]{:S(2)}) %collective-permute-start.29) | collective-permute-done | bytes 135200 | tf_op jit(solution)/shard_map/ppermute | solution.py:404
  (83 shorter events, 21.4 us)
Async XLA Ops:
  1.5 7.6 %collective-permute-start = (bf16[256,128]{1,0:T(8,128)(2,1)S(1)}, bf16[256,128]{1,0:T(8,128)(2,1)S(1)}, u32[]{:S(2)}, u32[]{:S(2)}) collective-permute-start(bf16[256,128]{1,0:T(8,128)(2,1)S(1)} %get-tuple-element.42.refs_2_), channel_id=1, source_target_pairs={{0,16},{8,24},{16,0},{24,8},{1,17},{9,25},{17,1},{25,9},{2,18},{10... | collective-permute-start | bytes 196616 | tf_op jit(solution)/shard_map/ppermute | solution.py:390
  9.1 5.9 %collective-permute-start.5 = (bf16[528,128]{1,0:T(8,128)(2,1)S(1)}, bf16[528,128]{1,0:T(8,128)(2,1)S(1)}, u32[]{:S(2)}, u32[]{:S(2)}) collective-permute-start(bf16[528,128]{1,0:T(8,128)(2,1)S(1)} %shard_map.67.refs_1_), channel_id=1, source_target_pairs={{2,0},{4,2},{6,4},{7,6},{5,7},{3,5},{1,3},{0,1},{10,8},{12,10},{14... | collective-permute-start | bytes 405512 | tf_op jit(solution)/shard_map/ppermute | solution.py:407
  10.9 6.4 %collective-permute-start.19 = (bf16[528,128]{1,0:T(8,128)(2,1)S(1)}, bf16[528,128]{1,0:T(8,128)(2,1)S(1)}, u32[]{:S(2)}, u32[]{:S(2)}) collective-permute-start(bf16[528,128]{1,0:T(8,128)(2,1)S(1)} %shard_map.65.after_ref.refs_0_), channel_id=1, source_target_pairs={{0,2},{2,4},{4,6},{6,7},{7,5},{5,3},{3,1},{1,0},{8,10},{10,12},{12... | collective-permute-start | bytes 405512 | tf_op jit(solution)/shard_map/ppermute | solution.py:404
  11.2 8.8 %collective-permute-start.3 = (bf16[528,128]{1,0:T(8,128)(2,1)S(1)}, bf16[528,128]{1,0:T(8,128)(2,1)S(1)}, u32[]{:S(2)}, u32[]{:S(2)}) collective-permute-start(bf16[528,128]{1,0:T(8,128)(2,1)S(1)} %shard_map.67.refs_1_), channel_id=1, source_target_pairs={{0,2},{2,4},{4,6},{6,7},{7,5},{5,3},{3,1},{1,0},{8,10},{10,12},{12... | collective-permute-start | bytes 405512 | tf_op jit(solution)/shard_map/ppermute | solution.py:404
  13.0 7.5 %collective-permute-start.21 = (bf16[528,128]{1,0:T(8,128)(2,1)S(1)}, bf16[528,128]{1,0:T(8,128)(2,1)S(1)}, u32[]{:S(2)}, u32[]{:S(2)}) collective-permute-start(bf16[528,128]{1,0:T(8,128)(2,1)S(1)} %shard_map.65.after_ref.refs_0_), channel_id=1, source_target_pairs={{2,0},{4,2},{6,4},{7,6},{5,7},{3,5},{1,3},{0,1},{10,8},{12,10},{14... | collective-permute-start | bytes 405512 | tf_op jit(solution)/shard_map/ppermute | solution.py:407
  15.1 7.8 %collective-permute-start.7 = (bf16[528,128]{1,0:T(8,128)(2,1)S(1)}, bf16[528,128]{1,0:T(8,128)(2,1)S(1)}, u32[]{:S(2)}, u32[]{:S(2)}) collective-permute-start(bf16[528,128]{1,0:T(8,128)(2,1)S(1)} %collective-permute-done.5.refs_1_), channel_id=1, source_target_pairs={{2,0},{4,2},{6,4},{7,6},{5,7},{3,5},{1,3},{0,1},{10,8},{12,10},{14... | collective-permute-start | bytes 405512 | tf_op jit(solution)/shard_map/ppermute | solution.py:407
  17.3 7.9 %collective-permute-start.20 = (bf16[528,128]{1,0:T(8,128)(2,1)S(1)}, bf16[528,128]{1,0:T(8,128)(2,1)S(1)}, u32[]{:S(2)}, u32[]{:S(2)}) collective-permute-start(bf16[528,128]{1,0:T(8,128)(2,1)S(1)} %collective-permute-done.19.refs_0_), channel_id=1, source_target_pairs={{0,2},{2,4},{4,6},{6,7},{7,5},{5,3},{3,1},{1,0},{8,10},{10,12},{12... | collective-permute-start | bytes 405512 | tf_op jit(solution)/shard_map/ppermute | solution.py:404
  20.0 5.7 %collective-permute-start.4 = (bf16[528,128]{1,0:T(8,128)(2,1)S(1)}, bf16[528,128]{1,0:T(8,128)(2,1)S(1)}, u32[]{:S(2)}, u32[]{:S(2)}) collective-permute-start(bf16[528,128]{1,0:T(8,128)(2,1)S(1)} %collective-permute-done.3.refs_0_), channel_id=1, source_target_pairs={{0,2},{2,4},{4,6},{6,7},{7,5},{5,3},{3,1},{1,0},{8,10},{10,12},{12... | collective-permute-start | bytes 405512 | tf_op jit(solution)/shard_map/ppermute | solution.py:404
  20.5 5.9 %collective-permute-start.23 = (bf16[528,128]{1,0:T(8,128)(2,1)S(1)}, bf16[528,128]{1,0:T(8,128)(2,1)S(1)}, u32[]{:S(2)}, u32[]{:S(2)}) collective-permute-start(bf16[528,128]{1,0:T(8,128)(2,1)S(1)} %collective-permute-done.21.refs_1_), channel_id=1, source_target_pairs={{2,0},{4,2},{6,4},{7,6},{5,7},{3,5},{1,3},{0,1},{10,8},{12,10},{14... | collective-permute-start | bytes 405512 | tf_op jit(solution)/shard_map/ppermute | solution.py:407
  25.3 5.8 %collective-permute-start.22 = (bf16[528,128]{1,0:T(8,128)(2,1)S(1)}, bf16[528,128]{1,0:T(8,128)(2,1)S(1)}, u32[]{:S(2)}, u32[]{:S(2)}) collective-permute-start(bf16[528,128]{1,0:T(8,128)(2,1)S(1)} %collective-permute-done.20.refs_0_), channel_id=1, source_target_pairs={{0,2},{2,4},{4,6},{6,7},{7,5},{5,3},{3,1},{1,0},{8,10},{10,12},{12... | collective-permute-start | bytes 405512 | tf_op jit(solution)/shard_map/ppermute | solution.py:404
  27.9 6.3 %collective-permute-start.12 = (bf16[528,128]{1,0:T(8,128)(2,1)S(1)}, bf16[528,128]{1,0:T(8,128)(2,1)S(1)}, u32[]{:S(2)}, u32[]{:S(2)}) collective-permute-start(bf16[528,128]{1,0:T(8,128)(2,1)S(1)} %collective-permute-done.8.refs_1_), channel_id=1, source_target_pairs={{2,0},{4,2},{6,4},{7,6},{5,7},{3,5},{1,3},{0,1},{10,8},{12,10},{14... | collective-permute-start | bytes 405512 | tf_op jit(solution)/shard_map/ppermute | solution.py:407
  31.1 6.4 %collective-permute-start.24 = (bf16[528,128]{1,0:T(8,128)(2,1)S(1)}, bf16[528,128]{1,0:T(8,128)(2,1)S(1)}, u32[]{:S(2)}, u32[]{:S(2)}) collective-permute-start(bf16[528,128]{1,0:T(8,128)(2,1)S(1)} %collective-permute-done.22.refs_0_), channel_id=1, source_target_pairs={{0,2},{2,4},{4,6},{6,7},{7,5},{5,3},{3,1},{1,0},{8,10},{10,12},{12... | collective-permute-start | bytes 405512 | tf_op jit(solution)/shard_map/ppermute | solution.py:404
  31.2 7.5 %collective-permute-start.6 = (bf16[528,128]{1,0:T(8,128)(2,1)S(1)}, bf16[528,128]{1,0:T(8,128)(2,1)S(1)}, u32[]{:S(2)}, u32[]{:S(2)}) collective-permute-start(bf16[528,128]{1,0:T(8,128)(2,1)S(1)} %collective-permute-done.4.refs_0_), channel_id=1, source_target_pairs={{0,2},{2,4},{4,6},{6,7},{7,5},{5,3},{3,1},{1,0},{8,10},{10,12},{12... | collective-permute-start | bytes 405512 | tf_op jit(solution)/shard_map/ppermute | solution.py:404
  31.7 7.3 %collective-permute-start.26 = (bf16[528,128]{1,0:T(8,128)(2,1)S(1)}, bf16[528,128]{1,0:T(8,128)(2,1)S(1)}, u32[]{:S(2)}, u32[]{:S(2)}) collective-permute-start(bf16[528,128]{1,0:T(8,128)(2,1)S(1)} %collective-permute-done.23.refs_1_), channel_id=1, source_target_pairs={{2,0},{4,2},{6,4},{7,6},{5,7},{3,5},{1,3},{0,1},{10,8},{12,10},{14... | collective-permute-start | bytes 405512 | tf_op jit(solution)/shard_map/ppermute | solution.py:407
  34.4 6.7 %collective-permute-start.13 = (bf16[528,128]{1,0:T(8,128)(2,1)S(1)}, bf16[528,128]{1,0:T(8,128)(2,1)S(1)}, u32[]{:S(2)}, u32[]{:S(2)}) collective-permute-start(bf16[528,128]{1,0:T(8,128)(2,1)S(1)} %shard_map.74), channel_id=1, source_target_pairs={{2,0},{4,2},{6,4},{7,6},{5,7},{3,5},{1,3},{0,1},{10,8},{12,10},{14... | collective-permute-start | bytes 405512 | tf_op jit(solution)/shard_map/ppermute | solution.py:407
  37.8 7.4 %collective-permute-start.25 = (bf16[528,128]{1,0:T(8,128)(2,1)S(1)}, bf16[528,128]{1,0:T(8,128)(2,1)S(1)}, u32[]{:S(2)}, u32[]{:S(2)}) collective-permute-start(bf16[528,128]{1,0:T(8,128)(2,1)S(1)} %shard_map.83), channel_id=1, source_target_pairs={{0,2},{2,4},{4,6},{6,7},{7,5},{5,3},{3,1},{1,0},{8,10},{10,12},{12... | collective-permute-start | bytes 405512 | tf_op jit(solution)/shard_map/ppermute | solution.py:404
  39.0 8.5 %collective-permute-start.9 = (bf16[528,128]{1,0:T(8,128)(2,1)S(1)}, bf16[528,128]{1,0:T(8,128)(2,1)S(1)}, u32[]{:S(2)}, u32[]{:S(2)}) collective-permute-start(bf16[528,128]{1,0:T(8,128)(2,1)S(1)} %get-tuple-element.57), channel_id=1, source_target_pairs={{0,2},{2,4},{4,6},{6,7},{7,5},{5,3},{3,1},{1,0},{8,10},{10,12},{12... | collective-permute-start | bytes 405512 | tf_op jit(solution)/shard_map/ppermute | solution.py:404
  41.4 6.5 %collective-permute-start.14 = (bf16[528,128]{1,0:T(8,128)(2,1)S(1)}, bf16[528,128]{1,0:T(8,128)(2,1)S(1)}, u32[]{:S(2)}, u32[]{:S(2)}) collective-permute-start(bf16[528,128]{1,0:T(8,128)(2,1)S(1)} %shard_map.75), channel_id=1, source_target_pairs={{2,0},{4,2},{6,4},{7,6},{5,7},{3,5},{1,3},{0,1},{10,8},{12,10},{14... | collective-permute-start | bytes 405512 | tf_op jit(solution)/shard_map/ppermute | solution.py:407
  45.2 5.5 %collective-permute-start.30 = (bf16[528,128]{1,0:T(8,128)(2,1)S(1)}, bf16[528,128]{1,0:T(8,128)(2,1)S(1)}, u32[]{:S(2)}, u32[]{:S(2)}) collective-permute-start(bf16[528,128]{1,0:T(8,128)(2,1)S(1)} %get-tuple-element.75), channel_id=1, source_target_pairs={{2,0},{4,2},{6,4},{7,6},{5,7},{3,5},{1,3},{0,1},{10,8},{12,10},{14... | collective-permute-start | bytes 405512 | tf_op jit(solution)/shard_map/ppermute | solution.py:407
  45.5 7.3 %collective-permute-start.27 = (bf16[528,128]{1,0:T(8,128)(2,1)S(1)}, bf16[528,128]{1,0:T(8,128)(2,1)S(1)}, u32[]{:S(2)}, u32[]{:S(2)}) collective-permute-start(bf16[528,128]{1,0:T(8,128)(2,1)S(1)} %shard_map.85), channel_id=1, source_target_pairs={{0,2},{2,4},{4,6},{6,7},{7,5},{5,3},{3,1},{1,0},{8,10},{10,12},{12... | collective-permute-start | bytes 405512 | tf_op jit(solution)/shard_map/ppermute | solution.py:404
  47.8 6.8 %collective-permute-start.10 = (bf16[528,128]{1,0:T(8,128)(2,1)S(1)}, bf16[528,128]{1,0:T(8,128)(2,1)S(1)}, u32[]{:S(2)}, u32[]{:S(2)}) collective-permute-start(bf16[528,128]{1,0:T(8,128)(2,1)S(1)} %shard_map.72), channel_id=1, source_target_pairs={{0,2},{2,4},{4,6},{6,7},{7,5},{5,3},{3,1},{1,0},{8,10},{10,12},{12... | collective-permute-start | bytes 405512 | tf_op jit(solution)/shard_map/ppermute | solution.py:404
  48.2 6.9 %collective-permute-start.15 = (bf16[528,128]{1,0:T(8,128)(2,1)S(1)}, bf16[528,128]{1,0:T(8,128)(2,1)S(1)}, u32[]{:S(2)}, u32[]{:S(2)}) collective-permute-start(bf16[528,128]{1,0:T(8,128)(2,1)S(1)} %shard_map.76), channel_id=1, source_target_pairs={{2,0},{4,2},{6,4},{7,6},{5,7},{3,5},{1,3},{0,1},{10,8},{12,10},{14... | collective-permute-start | bytes 405512 | tf_op jit(solution)/shard_map/ppermute | solution.py:407
  51.0 6.3 %collective-permute-start.31 = (bf16[528,128]{1,0:T(8,128)(2,1)S(1)}, bf16[528,128]{1,0:T(8,128)(2,1)S(1)}, u32[]{:S(2)}, u32[]{:S(2)}) collective-permute-start(bf16[528,128]{1,0:T(8,128)(2,1)S(1)} %shard_map.88), channel_id=1, source_target_pairs={{2,0},{4,2},{6,4},{7,6},{5,7},{3,5},{1,3},{0,1},{10,8},{12,10},{14... | collective-permute-start | bytes 405512 | tf_op jit(solution)/shard_map/ppermute | solution.py:407
  53.1 5.8 %collective-permute-start.28 = (bf16[528,128]{1,0:T(8,128)(2,1)S(1)}, bf16[528,128]{1,0:T(8,128)(2,1)S(1)}, u32[]{:S(2)}, u32[]{:S(2)}) collective-permute-start(bf16[528,128]{1,0:T(8,128)(2,1)S(1)} %shard_map.86), channel_id=1, source_target_pairs={{0,2},{2,4},{4,6},{6,7},{7,5},{5,3},{3,1},{1,0},{8,10},{10,12},{12... | collective-permute-start | bytes 405512 | tf_op jit(solution)/shard_map/ppermute | solution.py:404
  (14 other events, 80.8 us)

commit v9 on v8

--- a/solution.py
+++ b/solution.py
@@ -79,21 +79,27 @@
     return tile
 
 
-def attend(queries, keys, values, usable, first=0):
+def attend(requests):
     across = (((1,), (1,)), ((), ()))
     along = (((1,), (0,)), ((), ()))
-    ones = jnp.ones(values[0].shape, BF16)
-    scores = [lax.dot_general(q, k, across, preferred_element_type=F32) for q, k in zip(queries, keys)]
-    scores = [jnp.where(usable, s * SCALE, EMPTY) for s in scores]
+    heads = [(q, k, v, r[3]) for r in requests for q, k, v in zip(*r[:3])]
+    ones = jnp.ones(heads[0][2].shape, BF16)
+    scores = [lax.dot_general(q, k, across, preferred_element_type=F32) for q, k, _, _ in heads]
+    scores = [jnp.where(head[3], s * SCALE, EMPTY) for s, head in zip(scores, heads)]
     tops = [jnp.max(s, axis=1, keepdims=True) for s in scores]
     weights = [jnp.exp2(s - t).astype(BF16) for s, t in zip(scores, tops)]
     both = [
-        lax.dot_general(w, jnp.concatenate([v, ones], axis=1), along, preferred_element_type=F32)
-        for w, v in zip(weights, values)
+        lax.dot_general(w, jnp.concatenate([head[2], ones], axis=1), along, preferred_element_type=F32)
+        for w, head in zip(weights, heads)
     ]
     mixed, totals = [b[:, :HD] for b in both], [b[:, HD:] for b in both]
-    level = by_lane(tops, first) + jnp.log2(jnp.maximum(by_lane(totals, first), 1.0))
-    return [m / t for m, t in zip(mixed, totals)], level
+    results = []
+    for number, request in enumerate(requests):
+        mine = slice(number * KVH, (number + 1) * KVH)
+        first = request[4]
+        level = by_lane(tops[mine], first) + jnp.log2(jnp.maximum(by_lane(totals[mine], first), 1.0))
+        results.append(([m / t for m, t in zip(mixed[mine], totals[mine])], level))
+    return results
 
 
 def relayout_kernel(owners, place_ref, queries_ref, *outs):
@@ -127,7 +133,7 @@
         new = new_ref[group ^ d]
         heads = [new[:, head * HD : (head + 1) * HD] for head in range(2 * KVH)]
         rows = [query[head * ROWS : (head + 1) * ROWS, :] for head in range(KVH)]
-        mixed, level = attend(rows, heads[:KVH], heads[KVH:], usable)
+        [(mixed, level)] = attend([(rows, heads[:KVH], heads[KVH:], usable, 0)])
         for head, values in enumerate(mixed):
             out_ref[d, head * ROWS : (head + 1) * ROWS, :] = values
         level_ref[d] = level
@@ -197,13 +203,15 @@
 
 
 def item_kernel(slots, visitors, owners, place_ref, cache_ref, *refs):
+    sides, each = len(slots), len(slots[0])
+    entries = sides * each
+    query_refs, (out_ref, rows_ref, level_ref, code_ref, order_ref) = refs[:sides], refs[sides:]
     group, owner = lax.div(place_ref[0], owners), lax.rem(place_ref[0], owners)
-    sides = len(slots)
-    query_refs, out_refs, (level_ref, code_ref) = refs[:sides], refs[sides : 2 * sides], refs[2 * sides :]
-    each = len(slots[0])
+    lists = list_rows(visitors)
+    rows = lax.broadcasted_iota(jnp.int32, (lists, LANES), 0)
+    lanes = lane_ids()
+    codes = []
     for side, query_ref in enumerate(query_refs):
-        lists = query_ref.shape[0] - each * BODY
-        rows = lax.broadcasted_iota(jnp.int32, (lists, LANES), 0)
         table = query_ref[each * BODY :, :].astype(F32)
         table = jnp.where(lane_ids(lists) == owner, table, 0.0)
         for pair in range(each // 2):
@@ -212,57 +220,59 @@
                 row = group ^ slots[side][2 * pair + second]
                 factor = jnp.where(rows == row, float(4096**second), factor)
                 factor = jnp.where(rows == row + visitors, float(256 * 4096**second), factor)
-            code_ref[(side * each) // 2 + pair] = jnp.sum(table * factor).astype(jnp.int32)
+            codes.append(jnp.sum(table * factor).astype(jnp.int32))
+        rows_ref[side * each * BODY : (side + 1) * each * BODY, :] = query_ref[: each * BODY, :]
+
+    for entry in range(entries):
+        out = entry // 2 * PAIR + entry % 2 * BODY
+        out_ref[out : out + BODY, :] = jnp.zeros((BODY, HD), BF16)
+        first = entry % 2 * SECOND
+        level_ref[entry] = jnp.where((lanes >= first) & (lanes < first + COLS), EMPTY, 0.0)
+    found = jnp.int32(0)
+    for entry in range(entries):
+        code = (codes[entry // 2] >> (12 * (entry % 2))) & 4095
+        code_ref[entry] = code
+        order_ref[found] = entry
+        found = found + jnp.where((code & 255) > 0, 1, 0)
+    order_ref[found] = order_ref[jnp.maximum(found - 1, 0)]
     tokens = lax.broadcasted_iota(jnp.int32, (ROWS, PAGE), 1)
 
-    def one(side, number):
-        entry = side * each + number
-        query_ref, out_ref = query_refs[side], out_refs[side]
-        odd = number & 1
-        code = code_ref[entry >> 1] >> (12 * odd)
-        count, page = code & 255, (code >> 8) & 15
-        start = number * BODY
-        out = (number >> 1) * PAIR + odd * BODY
-        first = odd * SECOND
-
-        @pl.when(count > 0)
-        def _():
-            queries = [query_ref[pl.ds(pl.multiple_of(start + h * ROWS, HALF), ROWS), :] for h in range(KVH)]
+    @pl.loop(0, (found + 1) >> 1)
+    def _(two):
+        requests, places = [], []
+        for number in range(2):
+            entry = order_ref[2 * two + number]
+            code = code_ref[entry]
+            page, odd = code >> 8, entry & 1
+            start = entry * BODY
+            queries = [rows_ref[pl.ds(pl.multiple_of(start + h * ROWS, HALF), ROWS), :] for h in range(KVH)]
             keys = [cache_ref[page, :, h * HD : (h + 1) * HD] for h in range(KVH)]
             values = [cache_ref[page, :, (KVH + h) * HD : (KVH + h + 1) * HD] for h in range(KVH)]
-            mixed, level = attend(queries, keys, values, tokens < count, first)
+            requests.append((queries, keys, values, tokens < (code & 255), odd * SECOND))
+            places.append((entry, (entry >> 1) * PAIR + odd * BODY))
+        for (mixed, level), (entry, out) in zip(attend(requests), places):
             for head, part in enumerate(mixed):
                 out_ref[pl.ds(pl.multiple_of(out + head * ROWS, HALF), ROWS), :] = part.astype(BF16)
             level_ref[entry] = level
 
-        @pl.when(count <= 0)
-        def _():
-            out_ref[pl.ds(pl.multiple_of(out, HALF), BODY), :] = jnp.zeros((BODY, HD), BF16)
-            lanes = lane_ids() - first
-            level_ref[entry] = jnp.where((lanes >= 0) & (lanes < COLS), EMPTY, 0.0)
-
-    for side in range(sides):
-
-        @pl.loop(0, each)
-        def _(number):
-            one(side, number)
-
-    for side, out_ref in enumerate(out_refs):
-        for pair in range(each // 2):
-            entry = side * each + 2 * pair
-            start = pair * PAIR + 2 * BODY
-            out_ref[start : start + HALF, :] = pack_stats(level_ref[entry] + level_ref[entry + 1])
+    for pair in range(entries // 2):
+        start = pair * PAIR + 2 * BODY
+        out_ref[start : start + HALF, :] = pack_stats(level_ref[2 * pair] + level_ref[2 * pair + 1])
 
 
 def items(place, owners, kv_cache, payloads, slots, visitors):
     count = sum(len(row) for row in slots)
-    rows = len(slots[0]) // 2 * PAIR
     return pl.pallas_call(
         functools.partial(item_kernel, slots, visitors, owners),
-        out_shape=[jax.ShapeDtypeStruct((rows, HD), BF16)] * len(slots),
+        out_shape=jax.ShapeDtypeStruct((count // 2 * PAIR, HD), BF16),
         in_specs=[IN_SMEM] + [IN_VMEM] * (1 + len(slots)),
-        out_specs=[IN_VMEM] * len(slots),
-        scratch_shapes=[pltpu.VMEM((count, HALF, LANES), F32), pltpu.SMEM((count // 2,), jnp.int32)],
+        out_specs=IN_VMEM,
+        scratch_shapes=[
+            pltpu.VMEM((count * BODY, HD), BF16),
+            pltpu.VMEM((count, HALF, LANES), F32),
+            pltpu.SMEM((count,), jnp.int32),
+            pltpu.SMEM((count + 1,), jnp.int32),
+        ],
         compiler_params=params(),
         cost_estimate=cost(count * KVH * 4 * ROWS * HD * PAGE, count * PAGE * kv_cache.shape[2] * 2),
     )(place, kv_cache, *payloads)
@@ -287,10 +297,10 @@
     return values
 
 
-def merge_kernel(arrived_ref, own_ref, out_ref):
+def merge_kernel(first, arrived_ref, own_ref, out_ref):
     for pair in range(out_ref.shape[0] // PAIR):
         part = slice(pair * PAIR, (pair + 1) * PAIR)
-        arrived, own, out = arrived_ref.at[part], own_ref.at[part], out_ref.at[part]
+        arrived, own, out = arrived_ref.at[part], own_ref.at[first + pair * PAIR : first + (pair + 1) * PAIR], out_ref.at[part]
         shares, level = blend([unpack_stats(ref[2 * BODY : PAIR, :]) for ref in (arrived, own)])
         values = [mix(shares, (arrived, own), second * BODY, second * SECOND) for second in range(2)]
         for second in range(2):
@@ -301,20 +311,22 @@
 
 
 def merge(arrived, own):
-    return pl.pallas_call(
-        merge_kernel,
-        out_shape=jax.ShapeDtypeStruct(own.shape, BF16),
+    own, first = own
+    return pl.pallas_call(
+        functools.partial(merge_kernel, first),
+        out_shape=jax.ShapeDtypeStruct(arrived.shape, BF16),
         in_specs=[IN_VMEM, IN_VMEM],
         out_specs=IN_VMEM,
         compiler_params=params(),
-        cost_estimate=cost(0, 6 * own.size),
+        cost_estimate=cost(0, 6 * arrived.size),
     )(arrived, own)
 
 
-def gather_kernel(ahead_ref, behind_ref, own_ref, *outs):
+def gather_kernel(first, ahead_ref, behind_ref, own_ref, *outs):
     for pair in range(len(outs) // 2):
         part = slice(pair * PAIR, (pair + 1) * PAIR)
-        sources = [ref.at[part] for ref in (own_ref, ahead_ref, behind_ref)]
+        own = own_ref.at[first + pair * PAIR : first + (pair + 1) * PAIR]
+        sources = [own, ahead_ref.at[part], behind_ref.at[part]]
         shares, level = blend([unpack_stats(ref[2 * BODY : PAIR, :]) for ref in sources])
         values = [mix(shares, sources, second * BODY, second * SECOND) for second in range(2)]
         for second in range(2):
@@ -327,9 +339,10 @@
 
 
 def gather(ahead, behind, own):
-    pairs = own.shape[0] // PAIR
-    return pl.pallas_call(
-        gather_kernel,
+    pairs = ahead.shape[0] // PAIR
+    own, first = own
+    return pl.pallas_call(
+        functools.partial(gather_kernel, first),
         out_shape=[jax.ShapeDtypeStruct((LONE, HD), BF16)] * (2 * pairs),
         in_specs=[IN_VMEM] * 3,
         out_specs=[IN_VMEM] * (2 * pairs),
@@ -411,18 +424,20 @@
 
     blocks = [payload(lists, visits[:cut])]
     blocks.append(payload(lists, visits[cut:], [touch(kv_cache, blocks[0])]))
-    below, above, far = list(blocks), list(blocks), [None, None]
-    parts = {(half, 0): part for half, part in enumerate(owned(blocks, slots))}
-    for step in range(1, reach + 1):
+    below, above = [up(block) for block in blocks], [down(block) for block in blocks]
+    size = cut // 2 * PAIR
+    both = owned(blocks, slots)
+    parts = {(0, 0): (both, 0), (1, 0): (both, size)}
+    done = [[both], [both]]
+    for step in range(1, reach):
         for half in range(2):
-            if step == reach:
-                arrival = up(below[0]) if half == 0 else down(above[1])
-                far[half] = owned([arrival], [slots[half]])[0]
-                continue
-            done = [parts[half, 0]] if step == 1 else [parts[half, 1 - step], parts[half, step - 1]]
-            below[half] = after(up(below[half]), *done)
-            above[half] = after(down(above[half]), *done)
-            parts[half, -step], parts[half, step] = owned([below[half], above[half]], [slots[half]] * 2)
+            if step > 1:
+                below[half], above[half] = up(below[half]), down(above[half])
+            below[half], above[half] = after(below[half], *done[half]), after(above[half], *done[half])
+            both = owned([below[half], above[half]], [slots[half]] * 2)
+            parts[half, -step], parts[half, step] = (both, 0), (both, size)
+            done[half] = [both]
+    far = owned([up(below[0])], slots[:1]), owned([down(above[1])], slots[1:])
 
     arrived = []
     for half in range(2):
@@ -430,14 +445,15 @@
             if half == (0 if sign == 1 else 1):
                 chain, steps = far[half], range(reach - 1, -1, -1)
             else:
-                chain, steps = parts[half, sign * (reach - 1)], range(reach - 2, -1, -1)
+                own, first = parts[half, sign * (reach - 1)]
+                chain, steps = own[first : first + size], range(reach - 2, -1, -1)
             for step in steps:
                 chain = move(chain)
                 if step > 0:
                     chain = merge(chain, parts[half, sign * step])
             arrived.append(chain)
     back = gather(arrived[2], arrived[3], parts[1, 0])
-    front = gather(arrived[0], arrived[1], after(parts[0, 0], *back))
+    front = gather(arrived[0], arrived[1], (after(parts[0, 0][0], *back), 0))
     home = [swap(part, d) for d, part in enumerate(front + back)]
     early = final(place, owners, home[cut:], cut, new_out, new_level)
     return final(place, owners, home[:cut], 0, new_out, new_level, [early])

time: 68.8 us -> 68.4 us (level)
  waiting for transfers between devices: 12.8 us -> 13.6 us
  Pallas kernels: 12.5 us -> 11.8 us
    ppermute x14, starting transfers between devices: 7.66 us -> 13.3 us  [up(): return lax.ppermute(array, 'cache', forward)]
    ppermute x14, starting transfers between devices: 24.1 us -> 18.7 us  [down(): return lax.ppermute(array, 'cache', backward)]
  transfers between devices with their start and end apart: 34 -> 34, of which waited for: 12 -> 16; matrix products, arithmetic and copies ran while one was open for 2% -> 2% of each run, Pallas kernels for 17% -> 16%
where the time goes in v9:
time: 68.4 us; the launch traced here: 68.2 us
  starting transfers between devices  36.7 us (54%)
  waiting for transfers between devices  13.6 us (20%)
  Pallas kernels  11.8 us (17%)
  local copies, waits for them, and re-layouts  4.36 us (6%)
  other arithmetic  1.52 us (2%)
    ppermute x14, starting transfers between devices, down(): return lax.ppermute(array, 'cache', backward)  18.7 us
    ppermute x14, starting transfers between devices, up(): return lax.ppermute(array, 'cache', forward)  13.3 us
    ppermute x14, waiting for transfers between devices, down(): return lax.ppermute(array, 'cache', backward)  6.39 us
    ppermute x14, waiting for transfers between devices, up(): return lax.ppermute(array, 'cache', forward)  6.26 us
    pallas_call x9, Pallas kernels, items(): pl.pallas_call(functools.partial(item_kernel, slots, visitors, owners), o...  5.84 us
    ppermute x6, starting transfers between devices, swap(): lax.ppermute(array, 'grp', [(g, g ^ d) for g in range(groups)])  4.62 us
    unnamed x8, local copies, waits for them, and re-layouts  4.33 us
    pallas_call x10, Pallas kernels, merge(): pl.pallas_call(functools.partial(merge_kernel, first), out_shape=jax.Shap...  2.65 us
  transfers between devices with their start and end apart: 34, of which 16 were waited for; matrix products, arithmetic and copies ran while one was open for 2% of the time, Pallas kernels for 16%

profile of v9, /device:TPU:0, one launch (start us, length us, event | category | flops | bytes accessed | tf_op | source)
XLA Modules:
  0.0 68.2 jit_solution(17336312679604908742)
XLA Ops:
  1.5 2.6 %collective-permute-start = (bf16[256,128]{1,0:T(8,128)(2,1)S(1)}, bf16[256,128]{1,0:T(8,128)(2,1)S(1)}, u32[]{:S(2)}, u32[]{:S(2)}) collective-permute-start(bf16[256,128]{1,0:T(8,128)(2,1)S(1)} %get-tuple-element.28.refs_2_), channel_id=1, source_target_pairs={{0,16},{8,24},{16,0},{24,8},{1,17},{9,25},{17,1},{25,9},{2,18},{10... | collective-permute-start | bytes 196616 | tf_op jit(solution)/shard_map/ppermute | solution.py:403
  5.7 3.4 %copy-done = bf16[16,128,2048]{2,1,0:T(8,128)(2,1)S(1)} copy-done((bf16[16,128,2048]{2,1,0:T(8,128)(2,1)S(1)}, bf16[16,128,2048]{2,1,0:T(8,128)(2,1)}, u32[]{:S(2)}) %copy-start) | copy-done | bytes 8388632
  9.1 1.8 %collective-permute-start.5 = (bf16[528,128]{1,0:T(8,128)(2,1)S(1)}, bf16[528,128]{1,0:T(8,128)(2,1)S(1)}, u32[]{:S(2)}, u32[]{:S(2)}) collective-permute-start(bf16[528,128]{1,0:T(8,128)(2,1)S(1)} %shard_map.67.refs_1_), channel_id=1, source_target_pairs={{2,0},{4,2},{6,4},{7,6},{5,7},{3,5},{1,3},{0,1},{10,8},{12,10},{14... | collective-permute-start | bytes 405512 | tf_op jit(solution)/shard_map/ppermute | solution.py:420
  11.2 1.8 %collective-permute-start.3 = (bf16[528,128]{1,0:T(8,128)(2,1)S(1)}, bf16[528,128]{1,0:T(8,128)(2,1)S(1)}, u32[]{:S(2)}, u32[]{:S(2)}) collective-permute-start(bf16[528,128]{1,0:T(8,128)(2,1)S(1)} %shard_map.67.refs_1_), channel_id=1, source_target_pairs={{0,2},{2,4},{4,6},{6,7},{7,5},{5,3},{3,1},{1,0},{8,10},{10,12},{12... | collective-permute-start | bytes 405512 | tf_op jit(solution)/shard_map/ppermute | solution.py:417
  15.1 2.2 %collective-permute-start.7 = (bf16[528,128]{1,0:T(8,128)(2,1)S(1)}, bf16[528,128]{1,0:T(8,128)(2,1)S(1)}, u32[]{:S(2)}, u32[]{:S(2)}) collective-permute-start(bf16[528,128]{1,0:T(8,128)(2,1)S(1)} %collective-permute-done.5.refs_1_), channel_id=1, source_target_pairs={{2,0},{4,2},{6,4},{7,6},{5,7},{3,5},{1,3},{0,1},{10,8},{12,10},{14... | collective-permute-start | bytes 405512 | tf_op jit(solution)/shard_map/ppermute | solution.py:420
  17.7 2.4 %collective-permute-done.3.refs_0_ = bf16[528,128]{1,0:T(8,128)(2,1)S(1)} collective-permute-done((bf16[528,128]{1,0:T(8,128)(2,1)S(1)}, bf16[528,128]{1,0:T(8,128)(2,1)S(1)}, u32[]{:S(2)}, u32[]{:S(2)}) %collective-permute-start.3) | collective-permute-done | bytes 135200 | tf_op jit(solution)/shard_map/ppermute | solution.py:417
  20.5 1.6 %collective-permute-start.23 = (bf16[528,128]{1,0:T(8,128)(2,1)S(1)}, bf16[528,128]{1,0:T(8,128)(2,1)S(1)}, u32[]{:S(2)}, u32[]{:S(2)}) collective-permute-start(bf16[528,128]{1,0:T(8,128)(2,1)S(1)} %collective-permute-done.21.refs_1_), channel_id=1, source_target_pairs={{2,0},{4,2},{6,4},{7,6},{5,7},{3,5},{1,3},{0,1},{10,8},{12,10},{14... | collective-permute-start | bytes 405512 | tf_op jit(solution)/shard_map/ppermute | solution.py:420
  22.9 1.6 %collective-permute-start.8 = (bf16[528,128]{1,0:T(8,128)(2,1)S(1)}, bf16[528,128]{1,0:T(8,128)(2,1)S(1)}, u32[]{:S(2)}, u32[]{:S(2)}) collective-permute-start(bf16[528,128]{1,0:T(8,128)(2,1)S(1)} %collective-permute-done.7.refs_1_), channel_id=1, source_target_pairs={{2,0},{4,2},{6,4},{7,6},{5,7},{3,5},{1,3},{0,1},{10,8},{12,10},{14... | collective-permute-start | bytes 405512 | tf_op jit(solution)/shard_map/ppermute | solution.py:420
  24.8 1.1 %collective-permute-start.22 = (bf16[528,128]{1,0:T(8,128)(2,1)S(1)}, bf16[528,128]{1,0:T(8,128)(2,1)S(1)}, u32[]{:S(2)}, u32[]{:S(2)}) collective-permute-start(bf16[528,128]{1,0:T(8,128)(2,1)S(1)} %collective-permute-done.20.refs_0_), channel_id=1, source_target_pairs={{0,2},{2,4},{4,6},{6,7},{7,5},{5,3},{3,1},{1,0},{8,10},{10,12},{12... | collective-permute-start | bytes 405512 | tf_op jit(solution)/shard_map/ppermute | solution.py:417
  28.0 1.6 %collective-permute-start.12 = (bf16[528,128]{1,0:T(8,128)(2,1)S(1)}, bf16[528,128]{1,0:T(8,128)(2,1)S(1)}, u32[]{:S(2)}, u32[]{:S(2)}) collective-permute-start(bf16[528,128]{1,0:T(8,128)(2,1)S(1)} %collective-permute-done.8.refs_1_), channel_id=1, source_target_pairs={{2,0},{4,2},{6,4},{7,6},{5,7},{3,5},{1,3},{0,1},{10,8},{12,10},{14... | collective-permute-start | bytes 405512 | tf_op jit(solution)/shard_map/ppermute | solution.py:420
  30.9 2.1 %collective-permute-start.6 = (bf16[528,128]{1,0:T(8,128)(2,1)S(1)}, bf16[528,128]{1,0:T(8,128)(2,1)S(1)}, u32[]{:S(2)}, u32[]{:S(2)}) collective-permute-start(bf16[528,128]{1,0:T(8,128)(2,1)S(1)} %collective-permute-done.4.refs_0_), channel_id=1, source_target_pairs={{0,2},{2,4},{4,6},{6,7},{7,5},{5,3},{3,1},{1,0},{8,10},{10,12},{12... | collective-permute-start | bytes 405512 | tf_op jit(solution)/shard_map/ppermute | solution.py:417
  33.0 1.5 %collective-permute-done.12.refs_0_ = bf16[528,128]{1,0:T(8,128)(2,1)S(1)} collective-permute-done((bf16[528,128]{1,0:T(8,128)(2,1)S(1)}, bf16[528,128]{1,0:T(8,128)(2,1)S(1)}, u32[]{:S(2)}, u32[]{:S(2)}) %collective-permute-start.12) | collective-permute-done | bytes 135200 | tf_op jit(solution)/shard_map/ppermute | solution.py:420
  36.5 1.7 %collective-permute-start.25 = (bf16[528,128]{1,0:T(8,128)(2,1)S(1)}, bf16[528,128]{1,0:T(8,128)(2,1)S(1)}, u32[]{:S(2)}, u32[]{:S(2)}) collective-permute-start(bf16[528,128]{1,0:T(8,128)(2,1)S(1)} %shard_map.83), channel_id=1, source_target_pairs={{0,2},{2,4},{4,6},{6,7},{7,5},{5,3},{3,1},{1,0},{8,10},{10,12},{12... | collective-permute-start | bytes 405512 | tf_op jit(solution)/shard_map/ppermute | solution.py:417
  39.1 2.0 %collective-permute-start.9 = (bf16[528,128]{1,0:T(8,128)(2,1)S(1)}, bf16[528,128]{1,0:T(8,128)(2,1)S(1)}, u32[]{:S(2)}, u32[]{:S(2)}) collective-permute-start(bf16[528,128]{1,0:T(8,128)(2,1)S(1)} %slice.8), channel_id=1, source_target_pairs={{0,2},{2,4},{4,6},{6,7},{7,5},{5,3},{3,1},{1,0},{8,10},{10,12},{12... | collective-permute-start | bytes 405512 | tf_op jit(solution)/shard_map/ppermute | solution.py:417
  43.7 2.5 %collective-permute-start.30 = (bf16[528,128]{1,0:T(8,128)(2,1)S(1)}, bf16[528,128]{1,0:T(8,128)(2,1)S(1)}, u32[]{:S(2)}, u32[]{:S(2)}) collective-permute-start(bf16[528,128]{1,0:T(8,128)(2,1)S(1)} %slice.9), channel_id=1, source_target_pairs={{2,0},{4,2},{6,4},{7,6},{5,7},{3,5},{1,3},{0,1},{10,8},{12,10},{14... | collective-permute-start | bytes 405512 | tf_op jit(solution)/shard_map/ppermute | solution.py:420
  46.8 1.6 %collective-permute-start.10 = (bf16[528,128]{1,0:T(8,128)(2,1)S(1)}, bf16[528,128]{1,0:T(8,128)(2,1)S(1)}, u32[]{:S(2)}, u32[]{:S(2)}) collective-permute-start(bf16[528,128]{1,0:T(8,128)(2,1)S(1)} %shard_map.72), channel_id=1, source_target_pairs={{0,2},{2,4},{4,6},{6,7},{7,5},{5,3},{3,1},{1,0},{8,10},{10,12},{12... | collective-permute-start | bytes 405512 | tf_op jit(solution)/shard_map/ppermute | solution.py:417
  50.7 1.7 %collective-permute-start.31 = (bf16[528,128]{1,0:T(8,128)(2,1)S(1)}, bf16[528,128]{1,0:T(8,128)(2,1)S(1)}, u32[]{:S(2)}, u32[]{:S(2)}) collective-permute-start(bf16[528,128]{1,0:T(8,128)(2,1)S(1)} %shard_map.88), channel_id=1, source_target_pairs={{2,0},{4,2},{6,4},{7,6},{5,7},{3,5},{1,3},{0,1},{10,8},{12,10},{14... | collective-permute-start | bytes 405512 | tf_op jit(solution)/shard_map/ppermute | solution.py:420
  53.3 1.4 %collective-permute-done.10.arrived_ref = bf16[528,128]{1,0:T(8,128)(2,1)S(1)} collective-permute-done((bf16[528,128]{1,0:T(8,128)(2,1)S(1)}, bf16[528,128]{1,0:T(8,128)(2,1)S(1)}, u32[]{:S(2)}, u32[]{:S(2)}) %collective-permute-start.10) | collective-permute-done | bytes 135200 | tf_op jit(solution)/shard_map/ppermute | solution.py:417
  55.5 1.8 %collective-permute-start.16 = (bf16[528,128]{1,0:T(8,128)(2,1)S(1)}, bf16[528,128]{1,0:T(8,128)(2,1)S(1)}, u32[]{:S(2)}, u32[]{:S(2)}) collective-permute-start(bf16[528,128]{1,0:T(8,128)(2,1)S(1)} %shard_map.77), channel_id=1, source_target_pairs={{2,0},{4,2},{6,4},{7,6},{5,7},{3,5},{1,3},{0,1},{10,8},{12,10},{14... | collective-permute-start | bytes 405512 | tf_op jit(solution)/shard_map/ppermute | solution.py:420
  57.6 1.3 %collective-permute-start.32 = (bf16[528,128]{1,0:T(8,128)(2,1)S(1)}, bf16[528,128]{1,0:T(8,128)(2,1)S(1)}, u32[]{:S(2)}, u32[]{:S(2)}) collective-permute-start(bf16[528,128]{1,0:T(8,128)(2,1)S(1)} %shard_map.89), channel_id=1, source_target_pairs={{2,0},{4,2},{6,4},{7,6},{5,7},{3,5},{1,3},{0,1},{10,8},{12,10},{14... | collective-permute-start | bytes 405512 | tf_op jit(solution)/shard_map/ppermute | solution.py:420
  61.0 1.4 %collective-permute-start.17 = (bf16[272,128]{1,0:T(8,128)(2,1)S(1)}, bf16[272,128]{1,0:T(8,128)(2,1)S(1)}, u32[]{:S(2)}, u32[]{:S(2)}) collective-permute-start(bf16[272,128]{1,0:T(8,128)(2,1)S(1)} %get-tuple-element.38), channel_id=1, source_target_pairs={{0,16},{8,24},{16,0},{24,8},{1,17},{9,25},{17,1},{25,9},{2,18},{10... | collective-permute-start | bytes 208904 | tf_op jit(solution)/shard_map/ppermute | solution.py:403
  62.7 1.6 %collective-permute-done.29.ahead_ref = bf16[528,128]{1,0:T(8,128)(2,1)S(1)} collective-permute-done((bf16[528,128]{1,0:T(8,128)(2,1)S(1)}, bf16[528,128]{1,0:T(8,128)(2,1)S(1)}, u32[]{:S(2)}, u32[]{:S(2)}) %collective-permute-start.29) | collective-permute-done | bytes 135200 | tf_op jit(solution)/shard_map/ppermute | solution.py:417
  64.7 1.1 %shard_map.79 = (f32[4,256,128]{2,1,0:T(8,128)S(1)}, f32[4,16,128]{2,1,0:T(8,128)S(1)}) custom-call(s32[1]{0:T(128)} %bitcast.place_ref, bf16[256,128]{1,0:T(8,128)(2,1)S(1)} %get-tuple-element.30.refs_0_, bf16[256,128]{1,0:T(8,128)(2,1)S(1)} %get-tuple-element.31.refs_1_, bf16[256,128]{1,0:T(8,128)(2,1)S(1)} %get-tuple-element.28.refs_2_, ...), custom_call_target="tpu_custom_call" | custom-call | flops 67108864 | bytes 786432 | tf_op jit(solution)/shard_map/pallas_call | solution.py:144
  67.1 1.0 %shard_map.91 = bf16[4,4,8192]{2,1,0:T(4,128)(2,1)} custom-call(s32[1]{0:T(128)} %bitcast.place_ref, bf16[2,4,8192]{2,1,0:T(4,128)(2,1)S(1)} %shard_map.80.refs_0_, bf16[272,128]{1,0:T(8,128)(2,1)S(1)} %get-tuple-element.49.refs_1_, bf16[272,128]{1,0:T(8,128)(2,1)S(1)} %collective-permute-done.33.refs_2_, ...), custom_call_target="tpu_custom_call" | custom-call | bytes 524288 | tf_op jit(solution)/shard_map/pallas_call | solution.py:376
  (85 shorter events, 25.3 us)
Async XLA Ops:
  1.5 7.6 %collective-permute-start = (bf16[256,128]{1,0:T(8,128)(2,1)S(1)}, bf16[256,128]{1,0:T(8,128)(2,1)S(1)}, u32[]{:S(2)}, u32[]{:S(2)}) collective-permute-start(bf16[256,128]{1,0:T(8,128)(2,1)S(1)} %get-tuple-element.28.refs_2_), channel_id=1, source_target_pairs={{0,16},{8,24},{16,0},{24,8},{1,17},{9,25},{17,1},{25,9},{2,18},{10... | collective-permute-start | bytes 196616 | tf_op jit(solution)/shard_map/ppermute | solution.py:403
  9.1 5.9 %collective-permute-start.5 = (bf16[528,128]{1,0:T(8,128)(2,1)S(1)}, bf16[528,128]{1,0:T(8,128)(2,1)S(1)}, u32[]{:S(2)}, u32[]{:S(2)}) collective-permute-start(bf16[528,128]{1,0:T(8,128)(2,1)S(1)} %shard_map.67.refs_1_), channel_id=1, source_target_pairs={{2,0},{4,2},{6,4},{7,6},{5,7},{3,5},{1,3},{0,1},{10,8},{12,10},{14... | collective-permute-start | bytes 405512 | tf_op jit(solution)/shard_map/ppermute | solution.py:420
  10.9 6.4 %collective-permute-start.19 = (bf16[528,128]{1,0:T(8,128)(2,1)S(1)}, bf16[528,128]{1,0:T(8,128)(2,1)S(1)}, u32[]{:S(2)}, u32[]{:S(2)}) collective-permute-start(bf16[528,128]{1,0:T(8,128)(2,1)S(1)} %shard_map.65.after_ref.refs_0_), channel_id=1, source_target_pairs={{0,2},{2,4},{4,6},{6,7},{7,5},{5,3},{3,1},{1,0},{8,10},{10,12},{12... | collective-permute-start | bytes 405512 | tf_op jit(solution)/shard_map/ppermute | solution.py:417
  11.2 8.8 %collective-permute-start.3 = (bf16[528,128]{1,0:T(8,128)(2,1)S(1)}, bf16[528,128]{1,0:T(8,128)(2,1)S(1)}, u32[]{:S(2)}, u32[]{:S(2)}) collective-permute-start(bf16[528,128]{1,0:T(8,128)(2,1)S(1)} %shard_map.67.refs_1_), channel_id=1, source_target_pairs={{0,2},{2,4},{4,6},{6,7},{7,5},{5,3},{3,1},{1,0},{8,10},{10,12},{12... | collective-permute-start | bytes 405512 | tf_op jit(solution)/shard_map/ppermute | solution.py:417
  13.0 7.5 %collective-permute-start.21 = (bf16[528,128]{1,0:T(8,128)(2,1)S(1)}, bf16[528,128]{1,0:T(8,128)(2,1)S(1)}, u32[]{:S(2)}, u32[]{:S(2)}) collective-permute-start(bf16[528,128]{1,0:T(8,128)(2,1)S(1)} %shard_map.65.after_ref.refs_0_), channel_id=1, source_target_pairs={{2,0},{4,2},{6,4},{7,6},{5,7},{3,5},{1,3},{0,1},{10,8},{12,10},{14... | collective-permute-start | bytes 405512 | tf_op jit(solution)/shard_map/ppermute | solution.py:420
  15.1 7.9 %collective-permute-start.7 = (bf16[528,128]{1,0:T(8,128)(2,1)S(1)}, bf16[528,128]{1,0:T(8,128)(2,1)S(1)}, u32[]{:S(2)}, u32[]{:S(2)}) collective-permute-start(bf16[528,128]{1,0:T(8,128)(2,1)S(1)} %collective-permute-done.5.refs_1_), channel_id=1, source_target_pairs={{2,0},{4,2},{6,4},{7,6},{5,7},{3,5},{1,3},{0,1},{10,8},{12,10},{14... | collective-permute-start | bytes 405512 | tf_op jit(solution)/shard_map/ppermute | solution.py:420
  17.3 7.4 %collective-permute-start.20 = (bf16[528,128]{1,0:T(8,128)(2,1)S(1)}, bf16[528,128]{1,0:T(8,128)(2,1)S(1)}, u32[]{:S(2)}, u32[]{:S(2)}) collective-permute-start(bf16[528,128]{1,0:T(8,128)(2,1)S(1)} %collective-permute-done.19.refs_0_), channel_id=1, source_target_pairs={{0,2},{2,4},{4,6},{6,7},{7,5},{5,3},{3,1},{1,0},{8,10},{10,12},{12... | collective-permute-start | bytes 405512 | tf_op jit(solution)/shard_map/ppermute | solution.py:417
  20.0 5.8 %collective-permute-start.4 = (bf16[528,128]{1,0:T(8,128)(2,1)S(1)}, bf16[528,128]{1,0:T(8,128)(2,1)S(1)}, u32[]{:S(2)}, u32[]{:S(2)}) collective-permute-start(bf16[528,128]{1,0:T(8,128)(2,1)S(1)} %collective-permute-done.3.refs_0_), channel_id=1, source_target_pairs={{0,2},{2,4},{4,6},{6,7},{7,5},{5,3},{3,1},{1,0},{8,10},{10,12},{12... | collective-permute-start | bytes 405512 | tf_op jit(solution)/shard_map/ppermute | solution.py:417
  20.5 5.9 %collective-permute-start.23 = (bf16[528,128]{1,0:T(8,128)(2,1)S(1)}, bf16[528,128]{1,0:T(8,128)(2,1)S(1)}, u32[]{:S(2)}, u32[]{:S(2)}) collective-permute-start(bf16[528,128]{1,0:T(8,128)(2,1)S(1)} %collective-permute-done.21.refs_1_), channel_id=1, source_target_pairs={{2,0},{4,2},{6,4},{7,6},{5,7},{3,5},{1,3},{0,1},{10,8},{12,10},{14... | collective-permute-start | bytes 405512 | tf_op jit(solution)/shard_map/ppermute | solution.py:420
  24.8 5.2 %collective-permute-start.22 = (bf16[528,128]{1,0:T(8,128)(2,1)S(1)}, bf16[528,128]{1,0:T(8,128)(2,1)S(1)}, u32[]{:S(2)}, u32[]{:S(2)}) collective-permute-start(bf16[528,128]{1,0:T(8,128)(2,1)S(1)} %collective-permute-done.20.refs_0_), channel_id=1, source_target_pairs={{0,2},{2,4},{4,6},{6,7},{7,5},{5,3},{3,1},{1,0},{8,10},{10,12},{12... | collective-permute-start | bytes 405512 | tf_op jit(solution)/shard_map/ppermute | solution.py:417
  28.0 6.5 %collective-permute-start.12 = (bf16[528,128]{1,0:T(8,128)(2,1)S(1)}, bf16[528,128]{1,0:T(8,128)(2,1)S(1)}, u32[]{:S(2)}, u32[]{:S(2)}) collective-permute-start(bf16[528,128]{1,0:T(8,128)(2,1)S(1)} %collective-permute-done.8.refs_1_), channel_id=1, source_target_pairs={{2,0},{4,2},{6,4},{7,6},{5,7},{3,5},{1,3},{0,1},{10,8},{12,10},{14... | collective-permute-start | bytes 405512 | tf_op jit(solution)/shard_map/ppermute | solution.py:420
  30.0 6.2 %collective-permute-start.24 = (bf16[528,128]{1,0:T(8,128)(2,1)S(1)}, bf16[528,128]{1,0:T(8,128)(2,1)S(1)}, u32[]{:S(2)}, u32[]{:S(2)}) collective-permute-start(bf16[528,128]{1,0:T(8,128)(2,1)S(1)} %collective-permute-done.22.refs_0_), channel_id=1, source_target_pairs={{0,2},{2,4},{4,6},{6,7},{7,5},{5,3},{3,1},{1,0},{8,10},{10,12},{12... | collective-permute-start | bytes 405512 | tf_op jit(solution)/shard_map/ppermute | solution.py:417
  30.9 7.3 %collective-permute-start.6 = (bf16[528,128]{1,0:T(8,128)(2,1)S(1)}, bf16[528,128]{1,0:T(8,128)(2,1)S(1)}, u32[]{:S(2)}, u32[]{:S(2)}) collective-permute-start(bf16[528,128]{1,0:T(8,128)(2,1)S(1)} %collective-permute-done.4.refs_0_), channel_id=1, source_target_pairs={{0,2},{2,4},{4,6},{6,7},{7,5},{5,3},{3,1},{1,0},{8,10},{10,12},{12... | collective-permute-start | bytes 405512 | tf_op jit(solution)/shard_map/ppermute | solution.py:417
  33.0 8.1 %collective-permute-start.26 = (bf16[528,128]{1,0:T(8,128)(2,1)S(1)}, bf16[528,128]{1,0:T(8,128)(2,1)S(1)}, u32[]{:S(2)}, u32[]{:S(2)}) collective-permute-start(bf16[528,128]{1,0:T(8,128)(2,1)S(1)} %collective-permute-done.23.refs_1_), channel_id=1, source_target_pairs={{2,0},{4,2},{6,4},{7,6},{5,7},{3,5},{1,3},{0,1},{10,8},{12,10},{14... | collective-permute-start | bytes 405512 | tf_op jit(solution)/shard_map/ppermute | solution.py:420
  35.3 6.5 %collective-permute-start.13 = (bf16[528,128]{1,0:T(8,128)(2,1)S(1)}, bf16[528,128]{1,0:T(8,128)(2,1)S(1)}, u32[]{:S(2)}, u32[]{:S(2)}) collective-permute-start(bf16[528,128]{1,0:T(8,128)(2,1)S(1)} %shard_map.74), channel_id=1, source_target_pairs={{2,0},{4,2},{6,4},{7,6},{5,7},{3,5},{1,3},{0,1},{10,8},{12,10},{14... | collective-permute-start | bytes 405512 | tf_op jit(solution)/shard_map/ppermute | solution.py:420
  36.5 9.7 %collective-permute-start.25 = (bf16[528,128]{1,0:T(8,128)(2,1)S(1)}, bf16[528,128]{1,0:T(8,128)(2,1)S(1)}, u32[]{:S(2)}, u32[]{:S(2)}) collective-permute-start(bf16[528,128]{1,0:T(8,128)(2,1)S(1)} %shard_map.83), channel_id=1, source_target_pairs={{0,2},{2,4},{4,6},{6,7},{7,5},{5,3},{3,1},{1,0},{8,10},{10,12},{12... | collective-permute-start | bytes 405512 | tf_op jit(solution)/shard_map/ppermute | solution.py:417
  39.1 7.5 %collective-permute-start.9 = (bf16[528,128]{1,0:T(8,128)(2,1)S(1)}, bf16[528,128]{1,0:T(8,128)(2,1)S(1)}, u32[]{:S(2)}, u32[]{:S(2)}) collective-permute-start(bf16[528,128]{1,0:T(8,128)(2,1)S(1)} %slice.8), channel_id=1, source_target_pairs={{0,2},{2,4},{4,6},{6,7},{7,5},{5,3},{3,1},{1,0},{8,10},{10,12},{12... | collective-permute-start | bytes 405512 | tf_op jit(solution)/shard_map/ppermute | solution.py:417
  42.0 6.5 %collective-permute-start.14 = (bf16[528,128]{1,0:T(8,128)(2,1)S(1)}, bf16[528,128]{1,0:T(8,128)(2,1)S(1)}, u32[]{:S(2)}, u32[]{:S(2)}) collective-permute-start(bf16[528,128]{1,0:T(8,128)(2,1)S(1)} %shard_map.75), channel_id=1, source_target_pairs={{2,0},{4,2},{6,4},{7,6},{5,7},{3,5},{1,3},{0,1},{10,8},{12,10},{14... | collective-permute-start | bytes 405512 | tf_op jit(solution)/shard_map/ppermute | solution.py:420
  43.7 6.8 %collective-permute-start.30 = (bf16[528,128]{1,0:T(8,128)(2,1)S(1)}, bf16[528,128]{1,0:T(8,128)(2,1)S(1)}, u32[]{:S(2)}, u32[]{:S(2)}) collective-permute-start(bf16[528,128]{1,0:T(8,128)(2,1)S(1)} %slice.9), channel_id=1, source_target_pairs={{2,0},{4,2},{6,4},{7,6},{5,7},{3,5},{1,3},{0,1},{10,8},{12,10},{14... | collective-permute-start | bytes 405512 | tf_op jit(solution)/shard_map/ppermute | solution.py:420
  46.5 6.5 %collective-permute-start.27 = (bf16[528,128]{1,0:T(8,128)(2,1)S(1)}, bf16[528,128]{1,0:T(8,128)(2,1)S(1)}, u32[]{:S(2)}, u32[]{:S(2)}) collective-permute-start(bf16[528,128]{1,0:T(8,128)(2,1)S(1)} %shard_map.85), channel_id=1, source_target_pairs={{0,2},{2,4},{4,6},{6,7},{7,5},{5,3},{3,1},{1,0},{8,10},{10,12},{12... | collective-permute-start | bytes 405512 | tf_op jit(solution)/shard_map/ppermute | solution.py:417
  46.8 7.9 %collective-permute-start.10 = (bf16[528,128]{1,0:T(8,128)(2,1)S(1)}, bf16[528,128]{1,0:T(8,128)(2,1)S(1)}, u32[]{:S(2)}, u32[]{:S(2)}) collective-permute-start(bf16[528,128]{1,0:T(8,128)(2,1)S(1)} %shard_map.72), channel_id=1, source_target_pairs={{0,2},{2,4},{4,6},{6,7},{7,5},{5,3},{3,1},{1,0},{8,10},{10,12},{12... | collective-permute-start | bytes 405512 | tf_op jit(solution)/shard_map/ppermute | solution.py:417
  48.8 6.5 %collective-permute-start.15 = (bf16[528,128]{1,0:T(8,128)(2,1)S(1)}, bf16[528,128]{1,0:T(8,128)(2,1)S(1)}, u32[]{:S(2)}, u32[]{:S(2)}) collective-permute-start(bf16[528,128]{1,0:T(8,128)(2,1)S(1)} %shard_map.76), channel_id=1, source_target_pairs={{2,0},{4,2},{6,4},{7,6},{5,7},{3,5},{1,3},{0,1},{10,8},{12,10},{14... | collective-permute-start | bytes 405512 | tf_op jit(solution)/shard_map/ppermute | solution.py:420
  50.7 6.7 %collective-permute-start.31 = (bf16[528,128]{1,0:T(8,128)(2,1)S(1)}, bf16[528,128]{1,0:T(8,128)(2,1)S(1)}, u32[]{:S(2)}, u32[]{:S(2)}) collective-permute-start(bf16[528,128]{1,0:T(8,128)(2,1)S(1)} %shard_map.88), channel_id=1, source_target_pairs={{2,0},{4,2},{6,4},{7,6},{5,7},{3,5},{1,3},{0,1},{10,8},{12,10},{14... | collective-permute-start | bytes 405512 | tf_op jit(solution)/shard_map/ppermute | solution.py:420
  53.2 5.7 %collective-permute-start.28 = (bf16[528,128]{1,0:T(8,128)(2,1)S(1)}, bf16[528,128]{1,0:T(8,128)(2,1)S(1)}, u32[]{:S(2)}, u32[]{:S(2)}) collective-permute-start(bf16[528,128]{1,0:T(8,128)(2,1)S(1)} %shard_map.86), channel_id=1, source_target_pairs={{0,2},{2,4},{4,6},{6,7},{7,5},{5,3},{3,1},{1,0},{8,10},{10,12},{12... | collective-permute-start | bytes 405512 | tf_op jit(solution)/shard_map/ppermute | solution.py:417
  (14 other events, 81.0 us)

commit v10 on v9

--- a/solution.py
+++ b/solution.py
@@ -26,6 +26,7 @@
 EMPTY = -1e30
 SCALE = math.log2(math.e) / math.sqrt(HD)
 VMEM_BYTES = 24 * 1024 * 1024
+LOAD_BYTES = 44 * 1024 * 1024
 BF16 = jnp.bfloat16
 F32 = jnp.float32
 IN_VMEM = pl.BlockSpec(memory_space=pltpu.VMEM)
@@ -166,17 +167,22 @@
 
 def payload_kernel(after, counts_ref, pages_ref, *refs):
     visits, out = refs[: len(refs) - 1 - after], refs[-1]
+    tables = [counts_ref[...].astype(F32), pages_ref[...].astype(F32)]
+    lists = list_rows(len(visits))
+    if lists > 2 * len(visits):
+        tables.append(jnp.zeros((lists - 2 * len(visits), LANES), F32))
+    table = jnp.concatenate(tables, axis=0).astype(BF16)
+    cut = len(visits) // 2
     for number, visit in enumerate(visits):
-        out[number * BODY : (number + 1) * BODY, :] = visit[...]
-    tables = [counts_ref[...].astype(F32), pages_ref[...].astype(F32)]
-    short = out.shape[0] - len(visits) * BODY - 2 * tables[0].shape[0]
-    if short:
-        tables.append(jnp.zeros((short, LANES), F32))
-    out[len(visits) * BODY :, :] = jnp.concatenate(tables, axis=0).astype(BF16)
-
-
-def payload(lists, visits, after=()):
-    rows = len(visits) * BODY + list_rows(lists[0].shape[0])
+        start = number * BODY + number // cut * lists
+        out[start : start + BODY, :] = visit[...]
+    for half in range(2):
+        start = (half + 1) * cut * BODY + half * lists
+        out[start : start + lists, :] = table
+
+
+def payload(lists, visits, after):
+    rows = len(visits) * BODY + 2 * list_rows(len(visits))
     return pl.pallas_call(
         functools.partial(payload_kernel, len(after)),
         out_shape=jax.ShapeDtypeStruct((rows, HD), BF16),
@@ -187,25 +193,41 @@
     )(*lists, *visits, *after)
 
 
-def touch_kernel(after_ref, cache_ref, out_ref):
-    out_ref[...] = cache_ref[0, :HALF, :HD]
-
-
-def touch(kv_cache, after):
-    return pl.pallas_call(
-        touch_kernel,
-        out_shape=jax.ShapeDtypeStruct((HALF, HD), BF16),
-        in_specs=[IN_VMEM, IN_VMEM],
+def load_kernel(owners, parity, place_ref, cache_ref, *refs):
+    out_ref, sems = refs[-2:]
+
+    @pl.when((lax.div(place_ref[0], owners) & 1) == parity)
+    def _():
+        copies = [
+            pltpu.make_async_copy(cache_ref.at[page], out_ref.at[page], sems.at[page])
+            for page in range(cache_ref.shape[0])
+        ]
+        for copy in copies:
+            copy.start()
+        for copy in copies:
+            copy.wait()
+
+
+def load_pages(place, owners, kv_cache, parity, pages=None, after=()):
+    given = [] if pages is None else [pages]
+    return pl.pallas_call(
+        functools.partial(load_kernel, owners, parity),
+        out_shape=jax.ShapeDtypeStruct(kv_cache.shape, BF16),
+        in_specs=[IN_SMEM, pl.BlockSpec(memory_space=pl.ANY)] + [IN_VMEM] * (len(given) + len(after)),
         out_specs=IN_VMEM,
-        compiler_params=params(),
-        cost_estimate=cost(0, 2 * HALF * HD),
-    )(after, kv_cache)
+        scratch_shapes=[pltpu.SemaphoreType.DMA((kv_cache.shape[0],))],
+        input_output_aliases={2: 0} if given else {},
+        compiler_params=pltpu.CompilerParams(vmem_limit_bytes=LOAD_BYTES),
+        cost_estimate=cost(0, 2 * kv_cache.size),
+    )(place, kv_cache, *given, *after)
 
 
 def item_kernel(slots, visitors, owners, place_ref, cache_ref, *refs):
     sides, each = len(slots), len(slots[0])
     entries = sides * each
-    query_refs, (out_ref, rows_ref, level_ref, code_ref, order_ref) = refs[:sides], refs[sides:]
+    arrays, (out_ref, rows_ref, level_ref, code_ref, order_ref) = refs[:-5], refs[-5:]
+    unit = each * BODY + list_rows(visitors)
+    query_refs = [ref.at[at : at + unit] for ref in arrays for at in range(0, ref.shape[0], unit)]
     group, owner = lax.div(place_ref[0], owners), lax.rem(place_ref[0], owners)
     lists = list_rows(visitors)
     rows = lax.broadcasted_iota(jnp.int32, (lists, LANES), 0)
@@ -265,7 +287,7 @@
     return pl.pallas_call(
         functools.partial(item_kernel, slots, visitors, owners),
         out_shape=jax.ShapeDtypeStruct((count // 2 * PAIR, HD), BF16),
-        in_specs=[IN_SMEM] + [IN_VMEM] * (1 + len(slots)),
+        in_specs=[IN_SMEM] + [IN_VMEM] * (1 + len(payloads)),
         out_specs=IN_VMEM,
         scratch_shapes=[
             pltpu.VMEM((count * BODY, HD), BF16),
@@ -297,10 +319,16 @@
     return values
 
 
-def merge_kernel(first, arrived_ref, own_ref, out_ref):
-    for pair in range(out_ref.shape[0] // PAIR):
-        part = slice(pair * PAIR, (pair + 1) * PAIR)
-        arrived, own, out = arrived_ref.at[part], own_ref.at[first + pair * PAIR : first + (pair + 1) * PAIR], out_ref.at[part]
+def merge_kernel(first, base, arrived_ref, own_ref, *outs):
+    arrived_pairs = arrived_ref.shape[0] // PAIR
+    each = outs[0].shape[0] // PAIR
+    for pair in range(len(outs) * each):
+        own = own_ref.at[first + pair * PAIR : first + (pair + 1) * PAIR]
+        out = outs[pair // each].at[pair % each * PAIR : (pair % each + 1) * PAIR]
+        if not base <= pair < base + arrived_pairs:
+            out[...] = own[...]
+            continue
+        arrived = arrived_ref.at[(pair - base) * PAIR : (pair - base + 1) * PAIR]
         shares, level = blend([unpack_stats(ref[2 * BODY : PAIR, :]) for ref in (arrived, own)])
         values = [mix(shares, (arrived, own), second * BODY, second * SECOND) for second in range(2)]
         for second in range(2):
@@ -310,15 +338,15 @@
         out[2 * BODY : PAIR, :] = pack_stats(level)
 
 
-def merge(arrived, own):
+def merge(arrived, own, base, rows, outs):
     own, first = own
     return pl.pallas_call(
-        functools.partial(merge_kernel, first),
-        out_shape=jax.ShapeDtypeStruct(arrived.shape, BF16),
+        functools.partial(merge_kernel, first, base),
+        out_shape=[jax.ShapeDtypeStruct((rows // outs, HD), BF16)] * outs,
         in_specs=[IN_VMEM, IN_VMEM],
-        out_specs=IN_VMEM,
-        compiler_params=params(),
-        cost_estimate=cost(0, 6 * arrived.size),
+        out_specs=[IN_VMEM] * outs,
+        compiler_params=params(),
+        cost_estimate=cost(0, 6 * rows * HD),
     )(arrived, own)
 
 
@@ -411,8 +439,6 @@
 
     cut = requests // 2
     slots = [list(range(cut)), list(range(cut, requests))]
-    owned = functools.partial(items, place, owners, kv_cache, visitors=requests)
-
     def up(array):
         return lax.ppermute(array, "cache", forward)
 
@@ -422,38 +448,34 @@
     def after(array, *others):
         return lax.optimization_barrier((array, others))[0]
 
-    blocks = [payload(lists, visits[:cut])]
-    blocks.append(payload(lists, visits[cut:], [touch(kv_cache, blocks[0])]))
-    below, above = [up(block) for block in blocks], [down(block) for block in blocks]
-    size = cut // 2 * PAIR
-    both = owned(blocks, slots)
-    parts = {(0, 0): (both, 0), (1, 0): (both, size)}
-    done = [[both], [both]]
+    pages = load_pages(place, owners, kv_cache, 1, after=[visits[1]])
+    block = payload(lists, visits, [pages])
+    below, above = up(block), down(block)
+    pages = load_pages(place, owners, kv_cache, 0, pages, [block])
+    owned = functools.partial(items, place, owners, pages, visitors=requests)
+
+    size = requests // 2 * PAIR
+    parts = {0: (owned([block], slots), 0)}
+    unit = block.shape[0] // 2
     for step in range(1, reach):
-        for half in range(2):
-            if step > 1:
-                below[half], above[half] = up(below[half]), down(above[half])
-            below[half], above[half] = after(below[half], *done[half]), after(above[half], *done[half])
-            both = owned([below[half], above[half]], [slots[half]] * 2)
-            parts[half, -step], parts[half, step] = (both, 0), (both, size)
-            done[half] = [both]
-    far = owned([up(below[0])], slots[:1]), owned([down(above[1])], slots[1:])
-
-    arrived = []
-    for half in range(2):
-        for move, sign in ((up, 1), (down, -1)):
-            if half == (0 if sign == 1 else 1):
-                chain, steps = far[half], range(reach - 1, -1, -1)
-            else:
-                own, first = parts[half, sign * (reach - 1)]
-                chain, steps = own[first : first + size], range(reach - 2, -1, -1)
-            for step in steps:
-                chain = move(chain)
-                if step > 0:
-                    chain = merge(chain, parts[half, sign * step])
-            arrived.append(chain)
-    back = gather(arrived[2], arrived[3], parts[1, 0])
-    front = gather(arrived[0], arrived[1], (after(parts[0, 0][0], *back), 0))
+        below, above = after(below, parts[1 - step][0]), after(above, parts[1 - step][0])
+        both = owned([below, above], slots * 2)
+        parts[-step], parts[step] = (both, 0), (both, size)
+        last = step == reach - 1
+        below, above = up(below[:unit] if last else below), down(above[unit:] if last else above)
+    ahead, behind = [owned([below], slots[:1])], [owned([above], slots[1:])]
+
+    for step in range(reach - 1, 0, -1):
+        base = cut // 2 if step == reach - 1 else 0
+        own = parts[step]
+        if step == 1:
+            own = (after(own[0], new_level), own[1])
+        outs = 2 if step == 1 else 1
+        ahead = merge(up(ahead[0]), own, 0, size, outs)
+        behind = merge(down(behind[0]), parts[-step], base, size, outs)
+    both = parts[0][0]
+    back = gather(up(ahead[1]), down(behind[1]), (both, size // 2))
+    front = gather(up(ahead[0]), down(behind[0]), (after(both, *back), 0))
     home = [swap(part, d) for d, part in enumerate(front + back)]
     early = final(place, owners, home[cut:], cut, new_out, new_level)
     return final(place, owners, home[:cut], 0, new_out, new_level, [early])

time: 68.4 us -> 79 us (1.15)
  waiting for transfers between devices: 13.6 us -> 39.3 us
  starting transfers between devices: 36.7 us -> 24.9 us
  local copies, waits for them, and re-layouts: 4.36 us -> 0.97 us
    ppermute x14 -> x9, waiting for transfers between devices: 6.39 us -> 28 us  [down(): return lax.ppermute(array, 'cache', backward)]
    ppermute x14 -> x9, starting transfers between devices: 13.3 us -> 3.46 us  [up(): return lax.ppermute(array, 'cache', forward)]
    pallas_call x11 -> x8, Pallas kernels: 2.65 us -> 6.1 us  [the longest x2 3.7 us: load_pages(): pl.pallas_call(functools.partial(load_kernel, owners, parity), out_shape=...]
    unnamed x8 -> x4, local copies, waits for them, and re-layouts: 4.33 us -> 0.95 us
    ppermute x6, waiting for transfers between devices: 0.92 us -> 4.24 us  [swap(): lax.ppermute(array, 'grp', [(g, g ^ d) for g in range(groups)])]
    pallas_call x9 -> x6, Pallas kernels: 5.84 us -> 2.73 us  [items(): pl.pallas_call(functools.partial(item_kernel, slots, visitors, owners), o...]
    ppermute x14 -> x9, starting transfers between devices: 18.7 us -> 17.6 us  [down(): return lax.ppermute(array, 'cache', backward)]
    ppermute x14 -> x9, waiting for transfers between devices: 6.26 us -> 7.13 us  [up(): return lax.ppermute(array, 'cache', forward)]
  transfers between devices with their start and end apart: 34 -> 24, of which waited for: 16 -> 15; matrix products, arithmetic and copies ran while one was open for 2% -> 2% of each run, Pallas kernels for 16% -> 14%
where the time goes in v10:
time: 79 us
  waiting for transfers between devices  39.3 us (50%)
  starting transfers between devices  24.9 us (32%)
  Pallas kernels  12.1 us (15%)
  other arithmetic  1.52 us (2%)
  local copies, waits for them, and re-layouts  0.97 us (1%)
    ppermute x9, waiting for transfers between devices, down(): return lax.ppermute(array, 'cache', backward)  28 us
    ppermute x9, starting transfers between devices, down(): return lax.ppermute(array, 'cache', backward)  17.6 us
    ppermute x9, waiting for transfers between devices, up(): return lax.ppermute(array, 'cache', forward)  7.13 us
    ppermute x6, waiting for transfers between devices, swap(): lax.ppermute(array, 'grp', [(g, g ^ d) for g in range(groups)])  4.24 us
    ppermute x6, starting transfers between devices, swap(): lax.ppermute(array, 'grp', [(g, g ^ d) for g in range(groups)])  3.84 us
    pallas_call x2, Pallas kernels, load_pages(): pl.pallas_call(functools.partial(load_kernel, owners, parity), out_shape=...  3.7 us
    ppermute x9, starting transfers between devices, up(): return lax.ppermute(array, 'cache', forward)  3.46 us
    pallas_call x6, Pallas kernels, items(): pl.pallas_call(functools.partial(item_kernel, slots, visitors, owners), o...  2.73 us
  transfers between devices with their start and end apart: 24, of which 15 were waited for; matrix products, arithmetic and copies ran while one was open for 2% of the time, Pallas kernels for 14%

profile of v10, /device:TPU:0, one launch (start us, length us, event | category | flops | bytes accessed | tf_op | source)
XLA Modules:
  0.0 79.0 jit_solution(17727049261985145240)
XLA Ops:
  1.5 2.6 %collective-permute-start.1 = (bf16[256,128]{1,0:T(8,128)(2,1)S(1)}, bf16[256,128]{1,0:T(8,128)(2,1)S(1)}, u32[]{:S(2)}, u32[]{:S(2)}) collective-permute-start(bf16[256,128]{1,0:T(8,128)(2,1)S(1)} %get-tuple-element.29.refs_2_), channel_id=1, source_target_pairs={{0,16},{8,24},{16,0},{24,8},{1,17},{9,25},{17,1},{25,9},{2,18},{10... | collective-permute-start | bytes 196616 | tf_op jit(solution)/shard_map/ppermute | solution.py:431
  6.8 1.4 %collective-permute-done.2.refs_3_ = bf16[256,128]{1,0:T(8,128)(2,1)S(1)} collective-permute-done((bf16[256,128]{1,0:T(8,128)(2,1)S(1)}, bf16[256,128]{1,0:T(8,128)(2,1)S(1)}, u32[]{:S(2)}, u32[]{:S(2)}) %collective-permute-start.2) | collective-permute-done | bytes 65568 | tf_op jit(solution)/shard_map/ppermute | solution.py:431
  8.2 1.5 %collective-permute-start.5 = (bf16[1056,128]{1,0:T(8,128)(2,1)S(1)}, bf16[1056,128]{1,0:T(8,128)(2,1)S(1)}, u32[]{:S(2)}, u32[]{:S(2)}) collective-permute-start(bf16[1056,128]{1,0:T(8,128)(2,1)S(1)} %shard_map.66.refs_1_.refs_0_), channel_id=1, source_target_pairs={{2,0},{4,2},{6,4},{7,6},{5,7},{3,5},{1,3},{0,1},{10,8},{12,10},{14... | collective-permute-start | bytes 811016 | tf_op jit(solution)/shard_map/ppermute | solution.py:446
  10.3 3.5 %shard_map.67.cache_ref = bf16[16,128,2048]{2,1,0:T(8,128)(2,1)S(1)} custom-call(s32[1]{0:T(128)} %bitcast.place_ref, bf16[16,128,2048]{2,1,0:T(8,128)(2,1)} %cache_ref.3, bf16[16,128,2048]{2,1,0:T(8,128)(2,1)S(1)} %shard_map.65.refs_4_.refs_0_, bf16[1056,128]{1,0:T(8,128)(2,1)S(1)} %shard_map.66.refs_1_.refs_0_), custom_call_target="tpu_custom_call", output_to_operand_aliasing={{}: (2, {})} | custom-call | bytes 8388608 | tf_op jit(solution)/shard_map/pallas_call | solution.py:213
  14.0 3.1 %collective-permute-done.5.refs_1_ = bf16[1056,128]{1,0:T(8,128)(2,1)S(1)} collective-permute-done((bf16[1056,128]{1,0:T(8,128)(2,1)S(1)}, bf16[1056,128]{1,0:T(8,128)(2,1)S(1)}, u32[]{:S(2)}, u32[]{:S(2)}) %collective-permute-start.5) | collective-permute-done | bytes 270368 | tf_op jit(solution)/shard_map/ppermute | solution.py:446
  17.1 1.3 %collective-permute-start.7 = (bf16[1056,128]{1,0:T(8,128)(2,1)S(1)}, bf16[1056,128]{1,0:T(8,128)(2,1)S(1)}, u32[]{:S(2)}, u32[]{:S(2)}) collective-permute-start(bf16[1056,128]{1,0:T(8,128)(2,1)S(1)} %collective-permute-done.5.refs_1_), channel_id=1, source_target_pairs={{2,0},{4,2},{6,4},{7,6},{5,7},{3,5},{1,3},{0,1},{10,8},{12,10},{14... | collective-permute-start | bytes 811016 | tf_op jit(solution)/shard_map/ppermute | solution.py:446
  19.6 6.5 %collective-permute-done.7.refs_1_ = bf16[1056,128]{1,0:T(8,128)(2,1)S(1)} collective-permute-done((bf16[1056,128]{1,0:T(8,128)(2,1)S(1)}, bf16[1056,128]{1,0:T(8,128)(2,1)S(1)}, u32[]{:S(2)}, u32[]{:S(2)}) %collective-permute-start.7) | collective-permute-done | bytes 270368 | tf_op jit(solution)/shard_map/ppermute | solution.py:446
  26.1 1.5 %collective-permute-start.10 = (bf16[1056,128]{1,0:T(8,128)(2,1)S(1)}, bf16[1056,128]{1,0:T(8,128)(2,1)S(1)}, u32[]{:S(2)}, u32[]{:S(2)}) collective-permute-start(bf16[1056,128]{1,0:T(8,128)(2,1)S(1)} %collective-permute-done.7.refs_1_), channel_id=1, source_target_pairs={{2,0},{4,2},{6,4},{7,6},{5,7},{3,5},{1,3},{0,1},{10,8},{12,10},{14... | collective-permute-start | bytes 811016 | tf_op jit(solution)/shard_map/ppermute | solution.py:446
  29.0 5.3 %collective-permute-done.10.refs_1_ = bf16[1056,128]{1,0:T(8,128)(2,1)S(1)} collective-permute-done((bf16[1056,128]{1,0:T(8,128)(2,1)S(1)}, bf16[1056,128]{1,0:T(8,128)(2,1)S(1)}, u32[]{:S(2)}, u32[]{:S(2)}) %collective-permute-start.10) | collective-permute-done | bytes 270368 | tf_op jit(solution)/shard_map/ppermute | solution.py:446
  34.3 1.6 %collective-permute-start.14 = (bf16[528,128]{1,0:T(8,128)(2,1)S(1)}, bf16[528,128]{1,0:T(8,128)(2,1)S(1)}, u32[]{:S(2)}, u32[]{:S(2)}) collective-permute-start(bf16[528,128]{1,0:T(8,128)(2,1)S(1)} %slice.7), channel_id=1, source_target_pairs={{2,0},{4,2},{6,4},{7,6},{5,7},{3,5},{1,3},{0,1},{10,8},{12,10},{14... | collective-permute-start | bytes 405512 | tf_op jit(solution)/shard_map/ppermute | solution.py:446
  36.4 2.9 %collective-permute-done.14.refs_0_ = bf16[528,128]{1,0:T(8,128)(2,1)S(1)} collective-permute-done((bf16[528,128]{1,0:T(8,128)(2,1)S(1)}, bf16[528,128]{1,0:T(8,128)(2,1)S(1)}, u32[]{:S(2)}, u32[]{:S(2)}) %collective-permute-start.14) | collective-permute-done | bytes 135200 | tf_op jit(solution)/shard_map/ppermute | solution.py:446
  39.6 2.2 %collective-permute-start.15 = (bf16[528,128]{1,0:T(8,128)(2,1)S(1)}, bf16[528,128]{1,0:T(8,128)(2,1)S(1)}, u32[]{:S(2)}, u32[]{:S(2)}) collective-permute-start(bf16[528,128]{1,0:T(8,128)(2,1)S(1)} %shard_map.77), channel_id=1, source_target_pairs={{2,0},{4,2},{6,4},{7,6},{5,7},{3,5},{1,3},{0,1},{10,8},{12,10},{14... | collective-permute-start | bytes 405512 | tf_op jit(solution)/shard_map/ppermute | solution.py:446
  43.7 1.4 %collective-permute-done.15.arrived_ref = bf16[528,128]{1,0:T(8,128)(2,1)S(1)} collective-permute-done((bf16[528,128]{1,0:T(8,128)(2,1)S(1)}, bf16[528,128]{1,0:T(8,128)(2,1)S(1)}, u32[]{:S(2)}, u32[]{:S(2)}) %collective-permute-start.15) | collective-permute-done | bytes 135200 | tf_op jit(solution)/shard_map/ppermute | solution.py:446
  45.3 2.1 %collective-permute-start.16 = (bf16[1056,128]{1,0:T(8,128)(2,1)S(1)}, bf16[1056,128]{1,0:T(8,128)(2,1)S(1)}, u32[]{:S(2)}, u32[]{:S(2)}) collective-permute-start(bf16[1056,128]{1,0:T(8,128)(2,1)S(1)} %shard_map.78), channel_id=1, source_target_pairs={{2,0},{4,2},{6,4},{7,6},{5,7},{3,5},{1,3},{0,1},{10,8},{12,10},{14... | collective-permute-start | bytes 811016 | tf_op jit(solution)/shard_map/ppermute | solution.py:446
  48.2 5.1 %collective-permute-done.16.arrived_ref = bf16[1056,128]{1,0:T(8,128)(2,1)S(1)} collective-permute-done((bf16[1056,128]{1,0:T(8,128)(2,1)S(1)}, bf16[1056,128]{1,0:T(8,128)(2,1)S(1)}, u32[]{:S(2)}, u32[]{:S(2)}) %collective-permute-start.16) | collective-permute-done | bytes 270368 | tf_op jit(solution)/shard_map/ppermute | solution.py:446
  53.8 2.4 %collective-permute-start.17 = (bf16[1056,128]{1,0:T(8,128)(2,1)S(1)}, bf16[1056,128]{1,0:T(8,128)(2,1)S(1)}, u32[]{:S(2)}, u32[]{:S(2)}) collective-permute-start(bf16[1056,128]{1,0:T(8,128)(2,1)S(1)} %shard_map.79), channel_id=1, source_target_pairs={{2,0},{4,2},{6,4},{7,6},{5,7},{3,5},{1,3},{0,1},{10,8},{12,10},{14... | collective-permute-start | bytes 811016 | tf_op jit(solution)/shard_map/ppermute | solution.py:446
  57.6 1.1 %shard_map.75 = (f32[4,256,128]{2,1,0:T(8,128)S(1)}, f32[4,16,128]{2,1,0:T(8,128)S(1)}) custom-call(s32[1]{0:T(128)} %bitcast.place_ref, bf16[256,128]{1,0:T(8,128)(2,1)S(1)} %get-tuple-element.28.refs_0_, bf16[256,128]{1,0:T(8,128)(2,1)S(1)} %get-tuple-element.27.refs_1_, bf16[256,128]{1,0:T(8,128)(2,1)S(1)} %get-tuple-element.29.refs_2_, ...), custom_call_target="tpu_custom_call" | custom-call | flops 67108864 | bytes 786432 | tf_op jit(solution)/shard_map/pallas_call | solution.py:145
  58.7 3.7 %collective-permute-done.17.arrived_ref = bf16[1056,128]{1,0:T(8,128)(2,1)S(1)} collective-permute-done((bf16[1056,128]{1,0:T(8,128)(2,1)S(1)}, bf16[1056,128]{1,0:T(8,128)(2,1)S(1)}, u32[]{:S(2)}, u32[]{:S(2)}) %collective-permute-start.17) | collective-permute-done | bytes 270368 | tf_op jit(solution)/shard_map/ppermute | solution.py:446
  62.9 2.6 %collective-permute-start.18 = (bf16[528,128]{1,0:T(8,128)(2,1)S(1)}, bf16[528,128]{1,0:T(8,128)(2,1)S(1)}, u32[]{:S(2)}, u32[]{:S(2)}) collective-permute-start(bf16[528,128]{1,0:T(8,128)(2,1)S(1)} %get-tuple-element.40), channel_id=1, source_target_pairs={{2,0},{4,2},{6,4},{7,6},{5,7},{3,5},{1,3},{0,1},{10,8},{12,10},{14... | collective-permute-start | bytes 405512 | tf_op jit(solution)/shard_map/ppermute | solution.py:446
  65.4 1.5 %collective-permute-done.12.arrived_ref = bf16[1056,128]{1,0:T(8,128)(2,1)S(1)} collective-permute-done((bf16[1056,128]{1,0:T(8,128)(2,1)S(1)}, bf16[1056,128]{1,0:T(8,128)(2,1)S(1)}, u32[]{:S(2)}, u32[]{:S(2)}) %collective-permute-start.12) | collective-permute-done | bytes 270368 | tf_op jit(solution)/shard_map/ppermute | solution.py:443
  67.4 2.4 %collective-permute-start.22 = (bf16[528,128]{1,0:T(8,128)(2,1)S(1)}, bf16[528,128]{1,0:T(8,128)(2,1)S(1)}, u32[]{:S(2)}, u32[]{:S(2)}) collective-permute-start(bf16[528,128]{1,0:T(8,128)(2,1)S(1)} %get-tuple-element.45), channel_id=1, source_target_pairs={{2,0},{4,2},{6,4},{7,6},{5,7},{3,5},{1,3},{0,1},{10,8},{12,10},{14... | collective-permute-start | bytes 405512 | tf_op jit(solution)/shard_map/ppermute | solution.py:446
  69.8 2.9 %collective-permute-done.13.ahead_ref = bf16[528,128]{1,0:T(8,128)(2,1)S(1)} collective-permute-done((bf16[528,128]{1,0:T(8,128)(2,1)S(1)}, bf16[528,128]{1,0:T(8,128)(2,1)S(1)}, u32[]{:S(2)}, u32[]{:S(2)}) %collective-permute-start.13) | collective-permute-done | bytes 135200 | tf_op jit(solution)/shard_map/ppermute | solution.py:443
  73.2 1.6 %collective-permute-done.21.ahead_ref = bf16[528,128]{1,0:T(8,128)(2,1)S(1)} collective-permute-done((bf16[528,128]{1,0:T(8,128)(2,1)S(1)}, bf16[528,128]{1,0:T(8,128)(2,1)S(1)}, u32[]{:S(2)}, u32[]{:S(2)}) %collective-permute-start.21) | collective-permute-done | bytes 135200 | tf_op jit(solution)/shard_map/ppermute | solution.py:443
  75.7 2.0 %collective-permute-done.19.refs_0_ = bf16[272,128]{1,0:T(8,128)(2,1)S(1)} collective-permute-done((bf16[272,128]{1,0:T(8,128)(2,1)S(1)}, bf16[272,128]{1,0:T(8,128)(2,1)S(1)}, u32[]{:S(2)}, u32[]{:S(2)}) %collective-permute-start.19) | collective-permute-done | bytes 69664 | tf_op jit(solution)/shard_map/ppermute | solution.py:431
  (54 shorter events, 16.8 us)
Async XLA Ops:
  1.0 4.7 %collective-permute-start = (bf16[256,128]{1,0:T(8,128)(2,1)S(1)}, bf16[256,128]{1,0:T(8,128)(2,1)S(1)}, u32[]{:S(2)}, u32[]{:S(2)}) collective-permute-start(bf16[256,128]{1,0:T(8,128)(2,1)S(1)} %get-tuple-element.27.refs_1_), channel_id=1, source_target_pairs={{0,8},{8,0},{16,24},{24,16},{1,9},{9,1},{17,25},{25,17},{2,10},{10... | collective-permute-start | bytes 196616 | tf_op jit(solution)/shard_map/ppermute | solution.py:431
  1.5 5.3 %collective-permute-start.1 = (bf16[256,128]{1,0:T(8,128)(2,1)S(1)}, bf16[256,128]{1,0:T(8,128)(2,1)S(1)}, u32[]{:S(2)}, u32[]{:S(2)}) collective-permute-start(bf16[256,128]{1,0:T(8,128)(2,1)S(1)} %get-tuple-element.29.refs_2_), channel_id=1, source_target_pairs={{0,16},{8,24},{16,0},{24,8},{1,17},{9,25},{17,1},{25,9},{2,18},{10... | collective-permute-start | bytes 196616 | tf_op jit(solution)/shard_map/ppermute | solution.py:431
  4.1 4.0 %collective-permute-start.2 = (bf16[256,128]{1,0:T(8,128)(2,1)S(1)}, bf16[256,128]{1,0:T(8,128)(2,1)S(1)}, u32[]{:S(2)}, u32[]{:S(2)}) collective-permute-start(bf16[256,128]{1,0:T(8,128)(2,1)S(1)} %get-tuple-element.30.refs_3_), channel_id=1, source_target_pairs={{0,24},{8,16},{16,8},{24,0},{1,25},{9,17},{17,9},{25,1},{2,26},{10... | collective-permute-start | bytes 196616 | tf_op jit(solution)/shard_map/ppermute | solution.py:431
  8.2 8.9 %collective-permute-start.5 = (bf16[1056,128]{1,0:T(8,128)(2,1)S(1)}, bf16[1056,128]{1,0:T(8,128)(2,1)S(1)}, u32[]{:S(2)}, u32[]{:S(2)}) collective-permute-start(bf16[1056,128]{1,0:T(8,128)(2,1)S(1)} %shard_map.66.refs_1_.refs_0_), channel_id=1, source_target_pairs={{2,0},{4,2},{6,4},{7,6},{5,7},{3,5},{1,3},{0,1},{10,8},{12,10},{14... | collective-permute-start | bytes 811016 | tf_op jit(solution)/shard_map/ppermute | solution.py:446
  9.7 9.0 %collective-permute-start.3 = (bf16[1056,128]{1,0:T(8,128)(2,1)S(1)}, bf16[1056,128]{1,0:T(8,128)(2,1)S(1)}, u32[]{:S(2)}, u32[]{:S(2)}) collective-permute-start(bf16[1056,128]{1,0:T(8,128)(2,1)S(1)} %shard_map.66.refs_1_.refs_0_), channel_id=1, source_target_pairs={{0,2},{2,4},{4,6},{6,7},{7,5},{5,3},{3,1},{1,0},{8,10},{10,12},{12... | collective-permute-start | bytes 811016 | tf_op jit(solution)/shard_map/ppermute | solution.py:443
  17.1 9.0 %collective-permute-start.7 = (bf16[1056,128]{1,0:T(8,128)(2,1)S(1)}, bf16[1056,128]{1,0:T(8,128)(2,1)S(1)}, u32[]{:S(2)}, u32[]{:S(2)}) collective-permute-start(bf16[1056,128]{1,0:T(8,128)(2,1)S(1)} %collective-permute-done.5.refs_1_), channel_id=1, source_target_pairs={{2,0},{4,2},{6,4},{7,6},{5,7},{3,5},{1,3},{0,1},{10,8},{12,10},{14... | collective-permute-start | bytes 811016 | tf_op jit(solution)/shard_map/ppermute | solution.py:446
  18.7 8.8 %collective-permute-start.4 = (bf16[1056,128]{1,0:T(8,128)(2,1)S(1)}, bf16[1056,128]{1,0:T(8,128)(2,1)S(1)}, u32[]{:S(2)}, u32[]{:S(2)}) collective-permute-start(bf16[1056,128]{1,0:T(8,128)(2,1)S(1)} %collective-permute-done.3.refs_0_), channel_id=1, source_target_pairs={{0,2},{2,4},{4,6},{6,7},{7,5},{5,3},{3,1},{1,0},{8,10},{10,12},{12... | collective-permute-start | bytes 811016 | tf_op jit(solution)/shard_map/ppermute | solution.py:443
  26.1 8.2 %collective-permute-start.10 = (bf16[1056,128]{1,0:T(8,128)(2,1)S(1)}, bf16[1056,128]{1,0:T(8,128)(2,1)S(1)}, u32[]{:S(2)}, u32[]{:S(2)}) collective-permute-start(bf16[1056,128]{1,0:T(8,128)(2,1)S(1)} %collective-permute-done.7.refs_1_), channel_id=1, source_target_pairs={{2,0},{4,2},{6,4},{7,6},{5,7},{3,5},{1,3},{0,1},{10,8},{12,10},{14... | collective-permute-start | bytes 811016 | tf_op jit(solution)/shard_map/ppermute | solution.py:446
  27.6 8.4 %collective-permute-start.6 = (bf16[1056,128]{1,0:T(8,128)(2,1)S(1)}, bf16[1056,128]{1,0:T(8,128)(2,1)S(1)}, u32[]{:S(2)}, u32[]{:S(2)}) collective-permute-start(bf16[1056,128]{1,0:T(8,128)(2,1)S(1)} %collective-permute-done.4.refs_0_), channel_id=1, source_target_pairs={{0,2},{2,4},{4,6},{6,7},{7,5},{5,3},{3,1},{1,0},{8,10},{10,12},{12... | collective-permute-start | bytes 811016 | tf_op jit(solution)/shard_map/ppermute | solution.py:443
  34.3 5.1 %collective-permute-start.14 = (bf16[528,128]{1,0:T(8,128)(2,1)S(1)}, bf16[528,128]{1,0:T(8,128)(2,1)S(1)}, u32[]{:S(2)}, u32[]{:S(2)}) collective-permute-start(bf16[528,128]{1,0:T(8,128)(2,1)S(1)} %slice.7), channel_id=1, source_target_pairs={{2,0},{4,2},{6,4},{7,6},{5,7},{3,5},{1,3},{0,1},{10,8},{12,10},{14... | collective-permute-start | bytes 405512 | tf_op jit(solution)/shard_map/ppermute | solution.py:446
  36.0 5.9 %collective-permute-start.8 = (bf16[528,128]{1,0:T(8,128)(2,1)S(1)}, bf16[528,128]{1,0:T(8,128)(2,1)S(1)}, u32[]{:S(2)}, u32[]{:S(2)}) collective-permute-start(bf16[528,128]{1,0:T(8,128)(2,1)S(1)} %slice.6), channel_id=1, source_target_pairs={{0,2},{2,4},{4,6},{6,7},{7,5},{5,3},{3,1},{1,0},{8,10},{10,12},{12... | collective-permute-start | bytes 405512 | tf_op jit(solution)/shard_map/ppermute | solution.py:443
  39.6 5.5 %collective-permute-start.15 = (bf16[528,128]{1,0:T(8,128)(2,1)S(1)}, bf16[528,128]{1,0:T(8,128)(2,1)S(1)}, u32[]{:S(2)}, u32[]{:S(2)}) collective-permute-start(bf16[528,128]{1,0:T(8,128)(2,1)S(1)} %shard_map.77), channel_id=1, source_target_pairs={{2,0},{4,2},{6,4},{7,6},{5,7},{3,5},{1,3},{0,1},{10,8},{12,10},{14... | collective-permute-start | bytes 405512 | tf_op jit(solution)/shard_map/ppermute | solution.py:446
  42.0 5.4 %collective-permute-start.9 = (bf16[528,128]{1,0:T(8,128)(2,1)S(1)}, bf16[528,128]{1,0:T(8,128)(2,1)S(1)}, u32[]{:S(2)}, u32[]{:S(2)}) collective-permute-start(bf16[528,128]{1,0:T(8,128)(2,1)S(1)} %shard_map.71), channel_id=1, source_target_pairs={{0,2},{2,4},{4,6},{6,7},{7,5},{5,3},{3,1},{1,0},{8,10},{10,12},{12... | collective-permute-start | bytes 405512 | tf_op jit(solution)/shard_map/ppermute | solution.py:443
  45.3 7.9 %collective-permute-start.16 = (bf16[1056,128]{1,0:T(8,128)(2,1)S(1)}, bf16[1056,128]{1,0:T(8,128)(2,1)S(1)}, u32[]{:S(2)}, u32[]{:S(2)}) collective-permute-start(bf16[1056,128]{1,0:T(8,128)(2,1)S(1)} %shard_map.78), channel_id=1, source_target_pairs={{2,0},{4,2},{6,4},{7,6},{5,7},{3,5},{1,3},{0,1},{10,8},{12,10},{14... | collective-permute-start | bytes 811016 | tf_op jit(solution)/shard_map/ppermute | solution.py:446
  47.7 9.3 %collective-permute-start.11 = (bf16[1056,128]{1,0:T(8,128)(2,1)S(1)}, bf16[1056,128]{1,0:T(8,128)(2,1)S(1)}, u32[]{:S(2)}, u32[]{:S(2)}) collective-permute-start(bf16[1056,128]{1,0:T(8,128)(2,1)S(1)} %shard_map.73), channel_id=1, source_target_pairs={{0,2},{2,4},{4,6},{6,7},{7,5},{5,3},{3,1},{1,0},{8,10},{10,12},{12... | collective-permute-start | bytes 811016 | tf_op jit(solution)/shard_map/ppermute | solution.py:443
  53.8 8.6 %collective-permute-start.17 = (bf16[1056,128]{1,0:T(8,128)(2,1)S(1)}, bf16[1056,128]{1,0:T(8,128)(2,1)S(1)}, u32[]{:S(2)}, u32[]{:S(2)}) collective-permute-start(bf16[1056,128]{1,0:T(8,128)(2,1)S(1)} %shard_map.79), channel_id=1, source_target_pairs={{2,0},{4,2},{6,4},{7,6},{5,7},{3,5},{1,3},{0,1},{10,8},{12,10},{14... | collective-permute-start | bytes 811016 | tf_op jit(solution)/shard_map/ppermute | solution.py:446
  57.5 9.4 %collective-permute-start.12 = (bf16[1056,128]{1,0:T(8,128)(2,1)S(1)}, bf16[1056,128]{1,0:T(8,128)(2,1)S(1)}, u32[]{:S(2)}, u32[]{:S(2)}) collective-permute-start(bf16[1056,128]{1,0:T(8,128)(2,1)S(1)} %shard_map.74), channel_id=1, source_target_pairs={{0,2},{2,4},{4,6},{6,7},{7,5},{5,3},{3,1},{1,0},{8,10},{10,12},{12... | collective-permute-start | bytes 811016 | tf_op jit(solution)/shard_map/ppermute | solution.py:443
  62.9 6.9 %collective-permute-start.18 = (bf16[528,128]{1,0:T(8,128)(2,1)S(1)}, bf16[528,128]{1,0:T(8,128)(2,1)S(1)}, u32[]{:S(2)}, u32[]{:S(2)}) collective-permute-start(bf16[528,128]{1,0:T(8,128)(2,1)S(1)} %get-tuple-element.40), channel_id=1, source_target_pairs={{2,0},{4,2},{6,4},{7,6},{5,7},{3,5},{1,3},{0,1},{10,8},{12,10},{14... | collective-permute-start | bytes 405512 | tf_op jit(solution)/shard_map/ppermute | solution.py:446
  67.3 5.3 %collective-permute-start.13 = (bf16[528,128]{1,0:T(8,128)(2,1)S(1)}, bf16[528,128]{1,0:T(8,128)(2,1)S(1)}, u32[]{:S(2)}, u32[]{:S(2)}) collective-permute-start(bf16[528,128]{1,0:T(8,128)(2,1)S(1)} %get-tuple-element.39), channel_id=1, source_target_pairs={{0,2},{2,4},{4,6},{6,7},{7,5},{5,3},{3,1},{1,0},{8,10},{10,12},{12... | collective-permute-start | bytes 405512 | tf_op jit(solution)/shard_map/ppermute | solution.py:443
  67.4 5.8 %collective-permute-start.22 = (bf16[528,128]{1,0:T(8,128)(2,1)S(1)}, bf16[528,128]{1,0:T(8,128)(2,1)S(1)}, u32[]{:S(2)}, u32[]{:S(2)}) collective-permute-start(bf16[528,128]{1,0:T(8,128)(2,1)S(1)} %get-tuple-element.45), channel_id=1, source_target_pairs={{2,0},{4,2},{6,4},{7,6},{5,7},{3,5},{1,3},{0,1},{10,8},{12,10},{14... | collective-permute-start | bytes 405512 | tf_op jit(solution)/shard_map/ppermute | solution.py:446
  69.8 5.0 %collective-permute-start.21 = (bf16[528,128]{1,0:T(8,128)(2,1)S(1)}, bf16[528,128]{1,0:T(8,128)(2,1)S(1)}, u32[]{:S(2)}, u32[]{:S(2)}) collective-permute-start(bf16[528,128]{1,0:T(8,128)(2,1)S(1)} %get-tuple-element.44), channel_id=1, source_target_pairs={{0,2},{2,4},{4,6},{6,7},{7,5},{5,3},{3,1},{1,0},{8,10},{10,12},{12... | collective-permute-start | bytes 405512 | tf_op jit(solution)/shard_map/ppermute | solution.py:443
  73.1 4.6 %collective-permute-start.19 = (bf16[272,128]{1,0:T(8,128)(2,1)S(1)}, bf16[272,128]{1,0:T(8,128)(2,1)S(1)}, u32[]{:S(2)}, u32[]{:S(2)}) collective-permute-start(bf16[272,128]{1,0:T(8,128)(2,1)S(1)} %get-tuple-element.41), channel_id=1, source_target_pairs={{0,16},{8,24},{16,0},{24,8},{1,17},{9,25},{17,1},{25,9},{2,18},{10... | collective-permute-start | bytes 208904 | tf_op jit(solution)/shard_map/ppermute | solution.py:431
  73.1 4.5 %collective-permute-start.20 = (bf16[272,128]{1,0:T(8,128)(2,1)S(1)}, bf16[272,128]{1,0:T(8,128)(2,1)S(1)}, u32[]{:S(2)}, u32[]{:S(2)}) collective-permute-start(bf16[272,128]{1,0:T(8,128)(2,1)S(1)} %get-tuple-element.42), channel_id=1, source_target_pairs={{0,24},{8,16},{16,8},{24,0},{1,25},{9,17},{17,9},{25,1},{2,26},{10... | collective-permute-start | bytes 208904 | tf_op jit(solution)/shard_map/ppermute | solution.py:431
  75.2 2.8 %collective-permute-start.23 = (bf16[272,128]{1,0:T(8,128)(2,1)S(1)}, bf16[272,128]{1,0:T(8,128)(2,1)S(1)}, u32[]{:S(2)}, u32[]{:S(2)}) collective-permute-start(bf16[272,128]{1,0:T(8,128)(2,1)S(1)} %get-tuple-element.48), channel_id=1, source_target_pairs={{0,8},{8,0},{16,24},{24,16},{1,9},{9,1},{17,25},{25,17},{2,10},{10... | collective-permute-start | bytes 208904 | tf_op jit(solution)/shard_map/ppermute | solution.py:431
  (2 other events, 16.5 us)

commit v11 on v9

--- a/solution.py
+++ b/solution.py
@@ -83,16 +83,14 @@
     across = (((1,), (1,)), ((), ()))
     along = (((1,), (0,)), ((), ()))
     heads = [(q, k, v, r[3]) for r in requests for q, k, v in zip(*r[:3])]
-    ones = jnp.ones(heads[0][2].shape, BF16)
     scores = [lax.dot_general(q, k, across, preferred_element_type=F32) for q, k, _, _ in heads]
     scores = [jnp.where(head[3], s * SCALE, EMPTY) for s, head in zip(scores, heads)]
     tops = [jnp.max(s, axis=1, keepdims=True) for s in scores]
     weights = [jnp.exp2(s - t).astype(BF16) for s, t in zip(scores, tops)]
-    both = [
-        lax.dot_general(w, jnp.concatenate([head[2], ones], axis=1), along, preferred_element_type=F32)
-        for w, head in zip(weights, heads)
-    ]
-    mixed, totals = [b[:, :HD] for b in both], [b[:, HD:] for b in both]
+    mixed = [lax.dot_general(w, head[2], along, preferred_element_type=F32) for w, head in zip(weights, heads)]
+    ones = jnp.ones((weights[0].shape[1], LANES), BF16)
+    total = lax.dot_general(jnp.concatenate(weights, axis=0), ones, along, preferred_element_type=F32)
+    totals = [total[number * ROWS : (number + 1) * ROWS, :] for number in range(len(heads))]
     results = []
     for number, request in enumerate(requests):
         mine = slice(number * KVH, (number + 1) * KVH)
@@ -406,7 +404,6 @@
     visits = [rows[0]] + [None] * (groups - 1)
     for d in range(groups - 1, 0, -1):
         visits[d] = swap(rows[d], d)
-    new_out, new_level = new_tokens(place, owners, rows, new_kv)
     lists = page_lists(page_owner, page_index, lengths)
 
     cut = requests // 2
@@ -428,7 +425,8 @@
     size = cut // 2 * PAIR
     both = owned(blocks, slots)
     parts = {(0, 0): (both, 0), (1, 0): (both, size)}
-    done = [[both], [both]]
+    new_out, new_level = new_tokens(place, owners, [after(rows[0], both), *rows[1:]], new_kv)
+    done = [[both], [both, new_level]]
     for step in range(1, reach):
         for half in range(2):
             if step > 1:

time: 68.4 us -> 67.6 us (0.988)
  waiting for transfers between devices: 13.6 us -> 9.94 us
  starting transfers between devices: 36.7 us -> 39.4 us
    ppermute x14, starting transfers between devices: 13.3 us -> 18.1 us  [up(): return lax.ppermute(array, 'cache', forward)]
    ppermute x14, starting transfers between devices: 18.7 us -> 15.9 us  [down(): return lax.ppermute(array, 'cache', backward)]
    ppermute x14, waiting for transfers between devices: 6.26 us -> 3.79 us  [up(): return lax.ppermute(array, 'cache', forward)]
    ppermute x14, waiting for transfers between devices: 6.39 us -> 3.93 us  [down(): return lax.ppermute(array, 'cache', backward)]
    ppermute x6, waiting for transfers between devices: 0.92 us -> 2.22 us  [swap(): lax.ppermute(array, 'grp', [(g, g ^ d) for g in range(groups)])]
    ppermute x6, starting transfers between devices: 4.62 us -> 5.41 us  [swap(): lax.ppermute(array, 'grp', [(g, g ^ d) for g in range(groups)])]
  transfers between devices with their start and end apart: 34 -> 34, of which waited for: 16 -> 12; matrix products, arithmetic and copies ran while one was open for 2% -> 2% of each run, Pallas kernels for 16% -> 16%
where the time goes in v11:
time: 67.6 us; the launch traced here: 67.3 us
  starting transfers between devices  39.4 us (58%)
  Pallas kernels  11.9 us (18%)
  waiting for transfers between devices  9.94 us (15%)
  local copies, waits for them, and re-layouts  4.36 us (6%)
  other arithmetic  1.52 us (2%)
    ppermute x14, starting transfers between devices, up(): return lax.ppermute(array, 'cache', forward)  18.1 us
    ppermute x14, starting transfers between devices, down(): return lax.ppermute(array, 'cache', backward)  15.9 us
    pallas_call x9, Pallas kernels, items(): pl.pallas_call(functools.partial(item_kernel, slots, visitors, owners), o...  5.97 us
    ppermute x6, starting transfers between devices, swap(): lax.ppermute(array, 'grp', [(g, g ^ d) for g in range(groups)])  5.41 us
    unnamed x8, local copies, waits for them, and re-layouts  4.33 us
    ppermute x14, waiting for transfers between devices, down(): return lax.ppermute(array, 'cache', backward)  3.93 us
    ppermute x14, waiting for transfers between devices, up(): return lax.ppermute(array, 'cache', forward)  3.79 us
    pallas_call x10, Pallas kernels, merge(): pl.pallas_call(functools.partial(merge_kernel, first), out_shape=jax.Shap...  2.65 us
  transfers between devices with their start and end apart: 34, of which 12 were waited for; matrix products, arithmetic and copies ran while one was open for 2% of the time, Pallas kernels for 16%

profile of v11, /device:TPU:0, one launch (start us, length us, event | category | flops | bytes accessed | tf_op | source)
XLA Modules:
  0.0 67.3 jit_solution(1967183074310762041)
XLA Ops:
  1.5 2.6 %collective-permute-start = (bf16[256,128]{1,0:T(8,128)(2,1)S(1)}, bf16[256,128]{1,0:T(8,128)(2,1)S(1)}, u32[]{:S(2)}, u32[]{:S(2)}) collective-permute-start(bf16[256,128]{1,0:T(8,128)(2,1)S(1)} %get-tuple-element.29.refs_2_), channel_id=1, source_target_pairs={{0,16},{8,24},{16,0},{24,8},{1,17},{9,25},{17,1},{25,9},{2,18},{10... | collective-permute-start | bytes 196616 | tf_op jit(solution)/shard_map/ppermute | solution.py:401
  5.7 3.4 %copy-done = bf16[16,128,2048]{2,1,0:T(8,128)(2,1)S(1)} copy-done((bf16[16,128,2048]{2,1,0:T(8,128)(2,1)S(1)}, bf16[16,128,2048]{2,1,0:T(8,128)(2,1)}, u32[]{:S(2)}) %copy-start) | copy-done | bytes 8388632
  9.2 1.8 %collective-permute-start.5 = (bf16[528,128]{1,0:T(8,128)(2,1)S(1)}, bf16[528,128]{1,0:T(8,128)(2,1)S(1)}, u32[]{:S(2)}, u32[]{:S(2)}) collective-permute-start(bf16[528,128]{1,0:T(8,128)(2,1)S(1)} %shard_map.67.refs_1_), channel_id=1, source_target_pairs={{2,0},{4,2},{6,4},{7,6},{5,7},{3,5},{1,3},{0,1},{10,8},{12,10},{14... | collective-permute-start | bytes 405512 | tf_op jit(solution)/shard_map/ppermute | solution.py:417
  11.2 1.8 %collective-permute-start.3 = (bf16[528,128]{1,0:T(8,128)(2,1)S(1)}, bf16[528,128]{1,0:T(8,128)(2,1)S(1)}, u32[]{:S(2)}, u32[]{:S(2)}) collective-permute-start(bf16[528,128]{1,0:T(8,128)(2,1)S(1)} %shard_map.67.refs_1_), channel_id=1, source_target_pairs={{0,2},{2,4},{4,6},{6,7},{7,5},{5,3},{3,1},{1,0},{8,10},{10,12},{12... | collective-permute-start | bytes 405512 | tf_op jit(solution)/shard_map/ppermute | solution.py:414
  13.9 1.2 %collective-permute-start.21 = (bf16[528,128]{1,0:T(8,128)(2,1)S(1)}, bf16[528,128]{1,0:T(8,128)(2,1)S(1)}, u32[]{:S(2)}, u32[]{:S(2)}) collective-permute-start(bf16[528,128]{1,0:T(8,128)(2,1)S(1)} %shard_map.65.after_ref.refs_0_), channel_id=1, source_target_pairs={{2,0},{4,2},{6,4},{7,6},{5,7},{3,5},{1,3},{0,1},{10,8},{12,10},{14... | collective-permute-start | bytes 405512 | tf_op jit(solution)/shard_map/ppermute | solution.py:417
  15.1 1.1 %shard_map.69 = (f32[4,256,128]{2,1,0:T(8,128)S(1)}, f32[4,16,128]{2,1,0:T(8,128)S(1)}) custom-call(s32[1]{0:T(128)} %bitcast.place_ref, bf16[256,128]{1,0:T(8,128)(2,1)S(1)} %get-tuple-element.33.refs_0_, bf16[256,128]{1,0:T(8,128)(2,1)S(1)} %get-tuple-element.32.refs_1_, bf16[256,128]{1,0:T(8,128)(2,1)S(1)} %get-tuple-element.29.refs_2_, ...), custom_call_target="tpu_custom_call" | custom-call | flops 67108864 | bytes 786432 | tf_op jit(solution)/shard_map/pallas_call | solution.py:142
  16.2 1.6 %collective-permute-start.7 = (bf16[528,128]{1,0:T(8,128)(2,1)S(1)}, bf16[528,128]{1,0:T(8,128)(2,1)S(1)}, u32[]{:S(2)}, u32[]{:S(2)}) collective-permute-start(bf16[528,128]{1,0:T(8,128)(2,1)S(1)} %collective-permute-done.5.refs_1_), channel_id=1, source_target_pairs={{2,0},{4,2},{6,4},{7,6},{5,7},{3,5},{1,3},{0,1},{10,8},{12,10},{14... | collective-permute-start | bytes 405512 | tf_op jit(solution)/shard_map/ppermute | solution.py:417
  19.8 1.6 %collective-permute-start.23 = (bf16[528,128]{1,0:T(8,128)(2,1)S(1)}, bf16[528,128]{1,0:T(8,128)(2,1)S(1)}, u32[]{:S(2)}, u32[]{:S(2)}) collective-permute-start(bf16[528,128]{1,0:T(8,128)(2,1)S(1)} %collective-permute-done.21.refs_1_), channel_id=1, source_target_pairs={{2,0},{4,2},{6,4},{7,6},{5,7},{3,5},{1,3},{0,1},{10,8},{12,10},{14... | collective-permute-start | bytes 405512 | tf_op jit(solution)/shard_map/ppermute | solution.py:417
  22.3 2.0 %collective-permute-start.8 = (bf16[528,128]{1,0:T(8,128)(2,1)S(1)}, bf16[528,128]{1,0:T(8,128)(2,1)S(1)}, u32[]{:S(2)}, u32[]{:S(2)}) collective-permute-start(bf16[528,128]{1,0:T(8,128)(2,1)S(1)} %collective-permute-done.7.refs_1_), channel_id=1, source_target_pairs={{2,0},{4,2},{6,4},{7,6},{5,7},{3,5},{1,3},{0,1},{10,8},{12,10},{14... | collective-permute-start | bytes 405512 | tf_op jit(solution)/shard_map/ppermute | solution.py:417
  24.5 1.4 %collective-permute-start.22 = (bf16[528,128]{1,0:T(8,128)(2,1)S(1)}, bf16[528,128]{1,0:T(8,128)(2,1)S(1)}, u32[]{:S(2)}, u32[]{:S(2)}) collective-permute-start(bf16[528,128]{1,0:T(8,128)(2,1)S(1)} %collective-permute-done.20.refs_0_), channel_id=1, source_target_pairs={{0,2},{2,4},{4,6},{6,7},{7,5},{5,3},{3,1},{1,0},{8,10},{10,12},{12... | collective-permute-start | bytes 405512 | tf_op jit(solution)/shard_map/ppermute | solution.py:414
  28.0 1.6 %collective-permute-start.12 = (bf16[528,128]{1,0:T(8,128)(2,1)S(1)}, bf16[528,128]{1,0:T(8,128)(2,1)S(1)}, u32[]{:S(2)}, u32[]{:S(2)}) collective-permute-start(bf16[528,128]{1,0:T(8,128)(2,1)S(1)} %collective-permute-done.8.refs_1_), channel_id=1, source_target_pairs={{2,0},{4,2},{6,4},{7,6},{5,7},{3,5},{1,3},{0,1},{10,8},{12,10},{14... | collective-permute-start | bytes 405512 | tf_op jit(solution)/shard_map/ppermute | solution.py:417
  31.1 2.7 %collective-permute-start.6 = (bf16[528,128]{1,0:T(8,128)(2,1)S(1)}, bf16[528,128]{1,0:T(8,128)(2,1)S(1)}, u32[]{:S(2)}, u32[]{:S(2)}) collective-permute-start(bf16[528,128]{1,0:T(8,128)(2,1)S(1)} %collective-permute-done.4.refs_0_), channel_id=1, source_target_pairs={{0,2},{2,4},{4,6},{6,7},{7,5},{5,3},{3,1},{1,0},{8,10},{10,12},{12... | collective-permute-start | bytes 405512 | tf_op jit(solution)/shard_map/ppermute | solution.py:414
  35.0 1.1 %collective-permute-done.24.refs_0_ = bf16[528,128]{1,0:T(8,128)(2,1)S(1)} collective-permute-done((bf16[528,128]{1,0:T(8,128)(2,1)S(1)}, bf16[528,128]{1,0:T(8,128)(2,1)S(1)}, u32[]{:S(2)}, u32[]{:S(2)}) %collective-permute-start.24) | collective-permute-done | bytes 135200 | tf_op jit(solution)/shard_map/ppermute | solution.py:414
  36.3 2.0 %collective-permute-start.25 = (bf16[528,128]{1,0:T(8,128)(2,1)S(1)}, bf16[528,128]{1,0:T(8,128)(2,1)S(1)}, u32[]{:S(2)}, u32[]{:S(2)}) collective-permute-start(bf16[528,128]{1,0:T(8,128)(2,1)S(1)} %shard_map.83), channel_id=1, source_target_pairs={{0,2},{2,4},{4,6},{6,7},{7,5},{5,3},{3,1},{1,0},{8,10},{10,12},{12... | collective-permute-start | bytes 405512 | tf_op jit(solution)/shard_map/ppermute | solution.py:414
  38.6 2.4 %collective-permute-start.9 = (bf16[528,128]{1,0:T(8,128)(2,1)S(1)}, bf16[528,128]{1,0:T(8,128)(2,1)S(1)}, u32[]{:S(2)}, u32[]{:S(2)}) collective-permute-start(bf16[528,128]{1,0:T(8,128)(2,1)S(1)} %slice.8), channel_id=1, source_target_pairs={{0,2},{2,4},{4,6},{6,7},{7,5},{5,3},{3,1},{1,0},{8,10},{10,12},{12... | collective-permute-start | bytes 405512 | tf_op jit(solution)/shard_map/ppermute | solution.py:414
  42.3 2.2 %collective-permute-start.30 = (bf16[528,128]{1,0:T(8,128)(2,1)S(1)}, bf16[528,128]{1,0:T(8,128)(2,1)S(1)}, u32[]{:S(2)}, u32[]{:S(2)}) collective-permute-start(bf16[528,128]{1,0:T(8,128)(2,1)S(1)} %slice.9), channel_id=1, source_target_pairs={{2,0},{4,2},{6,4},{7,6},{5,7},{3,5},{1,3},{0,1},{10,8},{12,10},{14... | collective-permute-start | bytes 405512 | tf_op jit(solution)/shard_map/ppermute | solution.py:417
  45.1 2.5 %collective-permute-start.10 = (bf16[528,128]{1,0:T(8,128)(2,1)S(1)}, bf16[528,128]{1,0:T(8,128)(2,1)S(1)}, u32[]{:S(2)}, u32[]{:S(2)}) collective-permute-start(bf16[528,128]{1,0:T(8,128)(2,1)S(1)} %shard_map.73), channel_id=1, source_target_pairs={{0,2},{2,4},{4,6},{6,7},{7,5},{5,3},{3,1},{1,0},{8,10},{10,12},{12... | collective-permute-start | bytes 405512 | tf_op jit(solution)/shard_map/ppermute | solution.py:414
  48.0 1.3 %collective-permute-done.30.arrived_ref = bf16[528,128]{1,0:T(8,128)(2,1)S(1)} collective-permute-done((bf16[528,128]{1,0:T(8,128)(2,1)S(1)}, bf16[528,128]{1,0:T(8,128)(2,1)S(1)}, u32[]{:S(2)}, u32[]{:S(2)}) %collective-permute-start.30) | collective-permute-done | bytes 135200 | tf_op jit(solution)/shard_map/ppermute | solution.py:417
  49.6 1.1 %collective-permute-start.31 = (bf16[528,128]{1,0:T(8,128)(2,1)S(1)}, bf16[528,128]{1,0:T(8,128)(2,1)S(1)}, u32[]{:S(2)}, u32[]{:S(2)}) collective-permute-start(bf16[528,128]{1,0:T(8,128)(2,1)S(1)} %shard_map.88), channel_id=1, source_target_pairs={{2,0},{4,2},{6,4},{7,6},{5,7},{3,5},{1,3},{0,1},{10,8},{12,10},{14... | collective-permute-start | bytes 405512 | tf_op jit(solution)/shard_map/ppermute | solution.py:417
  52.6 1.7 %collective-permute-start.11 = (bf16[528,128]{1,0:T(8,128)(2,1)S(1)}, bf16[528,128]{1,0:T(8,128)(2,1)S(1)}, u32[]{:S(2)}, u32[]{:S(2)}) collective-permute-start(bf16[528,128]{1,0:T(8,128)(2,1)S(1)} %shard_map.74), channel_id=1, source_target_pairs={{0,2},{2,4},{4,6},{6,7},{7,5},{5,3},{3,1},{1,0},{8,10},{10,12},{12... | collective-permute-start | bytes 405512 | tf_op jit(solution)/shard_map/ppermute | solution.py:414
  56.5 1.5 %collective-permute-start.32 = (bf16[528,128]{1,0:T(8,128)(2,1)S(1)}, bf16[528,128]{1,0:T(8,128)(2,1)S(1)}, u32[]{:S(2)}, u32[]{:S(2)}) collective-permute-start(bf16[528,128]{1,0:T(8,128)(2,1)S(1)} %shard_map.89), channel_id=1, source_target_pairs={{2,0},{4,2},{6,4},{7,6},{5,7},{3,5},{1,3},{0,1},{10,8},{12,10},{14... | collective-permute-start | bytes 405512 | tf_op jit(solution)/shard_map/ppermute | solution.py:417
  60.0 2.2 %collective-permute-start.17 = (bf16[272,128]{1,0:T(8,128)(2,1)S(1)}, bf16[272,128]{1,0:T(8,128)(2,1)S(1)}, u32[]{:S(2)}, u32[]{:S(2)}) collective-permute-start(bf16[272,128]{1,0:T(8,128)(2,1)S(1)} %get-tuple-element.41), channel_id=1, source_target_pairs={{0,16},{8,24},{16,0},{24,8},{1,17},{9,25},{17,1},{25,9},{2,18},{10... | collective-permute-start | bytes 208904 | tf_op jit(solution)/shard_map/ppermute | solution.py:401
  62.2 1.1 %collective-permute-done.29.ahead_ref = bf16[528,128]{1,0:T(8,128)(2,1)S(1)} collective-permute-done((bf16[528,128]{1,0:T(8,128)(2,1)S(1)}, bf16[528,128]{1,0:T(8,128)(2,1)S(1)}, u32[]{:S(2)}, u32[]{:S(2)}) %collective-permute-start.29) | collective-permute-done | bytes 135200 | tf_op jit(solution)/shard_map/ppermute | solution.py:414
  64.5 1.5 %collective-permute-done.18.refs_1_ = bf16[272,128]{1,0:T(8,128)(2,1)S(1)} collective-permute-done((bf16[272,128]{1,0:T(8,128)(2,1)S(1)}, bf16[272,128]{1,0:T(8,128)(2,1)S(1)}, u32[]{:S(2)}, u32[]{:S(2)}) %collective-permute-start.18) | collective-permute-done | bytes 69664 | tf_op jit(solution)/shard_map/ppermute | solution.py:401
  (85 shorter events, 23.7 us)
Async XLA Ops:
  1.5 7.6 %collective-permute-start = (bf16[256,128]{1,0:T(8,128)(2,1)S(1)}, bf16[256,128]{1,0:T(8,128)(2,1)S(1)}, u32[]{:S(2)}, u32[]{:S(2)}) collective-permute-start(bf16[256,128]{1,0:T(8,128)(2,1)S(1)} %get-tuple-element.29.refs_2_), channel_id=1, source_target_pairs={{0,16},{8,24},{16,0},{24,8},{1,17},{9,25},{17,1},{25,9},{2,18},{10... | collective-permute-start | bytes 196616 | tf_op jit(solution)/shard_map/ppermute | solution.py:401
  9.2 7.1 %collective-permute-start.5 = (bf16[528,128]{1,0:T(8,128)(2,1)S(1)}, bf16[528,128]{1,0:T(8,128)(2,1)S(1)}, u32[]{:S(2)}, u32[]{:S(2)}) collective-permute-start(bf16[528,128]{1,0:T(8,128)(2,1)S(1)} %shard_map.67.refs_1_), channel_id=1, source_target_pairs={{2,0},{4,2},{6,4},{7,6},{5,7},{3,5},{1,3},{0,1},{10,8},{12,10},{14... | collective-permute-start | bytes 405512 | tf_op jit(solution)/shard_map/ppermute | solution.py:417
  10.9 7.0 %collective-permute-start.19 = (bf16[528,128]{1,0:T(8,128)(2,1)S(1)}, bf16[528,128]{1,0:T(8,128)(2,1)S(1)}, u32[]{:S(2)}, u32[]{:S(2)}) collective-permute-start(bf16[528,128]{1,0:T(8,128)(2,1)S(1)} %shard_map.65.after_ref.refs_0_), channel_id=1, source_target_pairs={{0,2},{2,4},{4,6},{6,7},{7,5},{5,3},{3,1},{1,0},{8,10},{10,12},{12... | collective-permute-start | bytes 405512 | tf_op jit(solution)/shard_map/ppermute | solution.py:414
  11.2 8.1 %collective-permute-start.3 = (bf16[528,128]{1,0:T(8,128)(2,1)S(1)}, bf16[528,128]{1,0:T(8,128)(2,1)S(1)}, u32[]{:S(2)}, u32[]{:S(2)}) collective-permute-start(bf16[528,128]{1,0:T(8,128)(2,1)S(1)} %shard_map.67.refs_1_), channel_id=1, source_target_pairs={{0,2},{2,4},{4,6},{6,7},{7,5},{5,3},{3,1},{1,0},{8,10},{10,12},{12... | collective-permute-start | bytes 405512 | tf_op jit(solution)/shard_map/ppermute | solution.py:414
  13.9 5.9 %collective-permute-start.21 = (bf16[528,128]{1,0:T(8,128)(2,1)S(1)}, bf16[528,128]{1,0:T(8,128)(2,1)S(1)}, u32[]{:S(2)}, u32[]{:S(2)}) collective-permute-start(bf16[528,128]{1,0:T(8,128)(2,1)S(1)} %shard_map.65.after_ref.refs_0_), channel_id=1, source_target_pairs={{2,0},{4,2},{6,4},{7,6},{5,7},{3,5},{1,3},{0,1},{10,8},{12,10},{14... | collective-permute-start | bytes 405512 | tf_op jit(solution)/shard_map/ppermute | solution.py:417
  16.2 6.0 %collective-permute-start.7 = (bf16[528,128]{1,0:T(8,128)(2,1)S(1)}, bf16[528,128]{1,0:T(8,128)(2,1)S(1)}, u32[]{:S(2)}, u32[]{:S(2)}) collective-permute-start(bf16[528,128]{1,0:T(8,128)(2,1)S(1)} %collective-permute-done.5.refs_1_), channel_id=1, source_target_pairs={{2,0},{4,2},{6,4},{7,6},{5,7},{3,5},{1,3},{0,1},{10,8},{12,10},{14... | collective-permute-start | bytes 405512 | tf_op jit(solution)/shard_map/ppermute | solution.py:417
  17.9 6.7 %collective-permute-start.20 = (bf16[528,128]{1,0:T(8,128)(2,1)S(1)}, bf16[528,128]{1,0:T(8,128)(2,1)S(1)}, u32[]{:S(2)}, u32[]{:S(2)}) collective-permute-start(bf16[528,128]{1,0:T(8,128)(2,1)S(1)} %collective-permute-done.19.refs_0_), channel_id=1, source_target_pairs={{0,2},{2,4},{4,6},{6,7},{7,5},{5,3},{3,1},{1,0},{8,10},{10,12},{12... | collective-permute-start | bytes 405512 | tf_op jit(solution)/shard_map/ppermute | solution.py:414
  19.4 6.7 %collective-permute-start.4 = (bf16[528,128]{1,0:T(8,128)(2,1)S(1)}, bf16[528,128]{1,0:T(8,128)(2,1)S(1)}, u32[]{:S(2)}, u32[]{:S(2)}) collective-permute-start(bf16[528,128]{1,0:T(8,128)(2,1)S(1)} %collective-permute-done.3.refs_0_), channel_id=1, source_target_pairs={{0,2},{2,4},{4,6},{6,7},{7,5},{5,3},{3,1},{1,0},{8,10},{10,12},{12... | collective-permute-start | bytes 405512 | tf_op jit(solution)/shard_map/ppermute | solution.py:414
  19.8 6.2 %collective-permute-start.23 = (bf16[528,128]{1,0:T(8,128)(2,1)S(1)}, bf16[528,128]{1,0:T(8,128)(2,1)S(1)}, u32[]{:S(2)}, u32[]{:S(2)}) collective-permute-start(bf16[528,128]{1,0:T(8,128)(2,1)S(1)} %collective-permute-done.21.refs_1_), channel_id=1, source_target_pairs={{2,0},{4,2},{6,4},{7,6},{5,7},{3,5},{1,3},{0,1},{10,8},{12,10},{14... | collective-permute-start | bytes 405512 | tf_op jit(solution)/shard_map/ppermute | solution.py:417
  24.5 6.0 %collective-permute-start.22 = (bf16[528,128]{1,0:T(8,128)(2,1)S(1)}, bf16[528,128]{1,0:T(8,128)(2,1)S(1)}, u32[]{:S(2)}, u32[]{:S(2)}) collective-permute-start(bf16[528,128]{1,0:T(8,128)(2,1)S(1)} %collective-permute-done.20.refs_0_), channel_id=1, source_target_pairs={{0,2},{2,4},{4,6},{6,7},{7,5},{5,3},{3,1},{1,0},{8,10},{10,12},{12... | collective-permute-start | bytes 405512 | tf_op jit(solution)/shard_map/ppermute | solution.py:414
  28.0 5.8 %collective-permute-start.12 = (bf16[528,128]{1,0:T(8,128)(2,1)S(1)}, bf16[528,128]{1,0:T(8,128)(2,1)S(1)}, u32[]{:S(2)}, u32[]{:S(2)}) collective-permute-start(bf16[528,128]{1,0:T(8,128)(2,1)S(1)} %collective-permute-done.8.refs_1_), channel_id=1, source_target_pairs={{2,0},{4,2},{6,4},{7,6},{5,7},{3,5},{1,3},{0,1},{10,8},{12,10},{14... | collective-permute-start | bytes 405512 | tf_op jit(solution)/shard_map/ppermute | solution.py:417
  31.1 7.2 %collective-permute-start.6 = (bf16[528,128]{1,0:T(8,128)(2,1)S(1)}, bf16[528,128]{1,0:T(8,128)(2,1)S(1)}, u32[]{:S(2)}, u32[]{:S(2)}) collective-permute-start(bf16[528,128]{1,0:T(8,128)(2,1)S(1)} %collective-permute-done.4.refs_0_), channel_id=1, source_target_pairs={{0,2},{2,4},{4,6},{6,7},{7,5},{5,3},{3,1},{1,0},{8,10},{10,12},{12... | collective-permute-start | bytes 405512 | tf_op jit(solution)/shard_map/ppermute | solution.py:414
  33.8 7.2 %collective-permute-start.26 = (bf16[528,128]{1,0:T(8,128)(2,1)S(1)}, bf16[528,128]{1,0:T(8,128)(2,1)S(1)}, u32[]{:S(2)}, u32[]{:S(2)}) collective-permute-start(bf16[528,128]{1,0:T(8,128)(2,1)S(1)} %collective-permute-done.23.refs_1_), channel_id=1, source_target_pairs={{2,0},{4,2},{6,4},{7,6},{5,7},{3,5},{1,3},{0,1},{10,8},{12,10},{14... | collective-permute-start | bytes 405512 | tf_op jit(solution)/shard_map/ppermute | solution.py:417
  34.7 6.4 %collective-permute-start.13 = (bf16[528,128]{1,0:T(8,128)(2,1)S(1)}, bf16[528,128]{1,0:T(8,128)(2,1)S(1)}, u32[]{:S(2)}, u32[]{:S(2)}) collective-permute-start(bf16[528,128]{1,0:T(8,128)(2,1)S(1)} %shard_map.75), channel_id=1, source_target_pairs={{2,0},{4,2},{6,4},{7,6},{5,7},{3,5},{1,3},{0,1},{10,8},{12,10},{14... | collective-permute-start | bytes 405512 | tf_op jit(solution)/shard_map/ppermute | solution.py:417
  36.3 8.1 %collective-permute-start.25 = (bf16[528,128]{1,0:T(8,128)(2,1)S(1)}, bf16[528,128]{1,0:T(8,128)(2,1)S(1)}, u32[]{:S(2)}, u32[]{:S(2)}) collective-permute-start(bf16[528,128]{1,0:T(8,128)(2,1)S(1)} %shard_map.83), channel_id=1, source_target_pairs={{0,2},{2,4},{4,6},{6,7},{7,5},{5,3},{3,1},{1,0},{8,10},{10,12},{12... | collective-permute-start | bytes 405512 | tf_op jit(solution)/shard_map/ppermute | solution.py:414
  38.6 6.2 %collective-permute-start.9 = (bf16[528,128]{1,0:T(8,128)(2,1)S(1)}, bf16[528,128]{1,0:T(8,128)(2,1)S(1)}, u32[]{:S(2)}, u32[]{:S(2)}) collective-permute-start(bf16[528,128]{1,0:T(8,128)(2,1)S(1)} %slice.8), channel_id=1, source_target_pairs={{0,2},{2,4},{4,6},{6,7},{7,5},{5,3},{3,1},{1,0},{8,10},{10,12},{12... | collective-permute-start | bytes 405512 | tf_op jit(solution)/shard_map/ppermute | solution.py:414
  41.3 6.3 %collective-permute-start.14 = (bf16[528,128]{1,0:T(8,128)(2,1)S(1)}, bf16[528,128]{1,0:T(8,128)(2,1)S(1)}, u32[]{:S(2)}, u32[]{:S(2)}) collective-permute-start(bf16[528,128]{1,0:T(8,128)(2,1)S(1)} %shard_map.76), channel_id=1, source_target_pairs={{2,0},{4,2},{6,4},{7,6},{5,7},{3,5},{1,3},{0,1},{10,8},{12,10},{14... | collective-permute-start | bytes 405512 | tf_op jit(solution)/shard_map/ppermute | solution.py:417
  42.3 7.1 %collective-permute-start.30 = (bf16[528,128]{1,0:T(8,128)(2,1)S(1)}, bf16[528,128]{1,0:T(8,128)(2,1)S(1)}, u32[]{:S(2)}, u32[]{:S(2)}) collective-permute-start(bf16[528,128]{1,0:T(8,128)(2,1)S(1)} %slice.9), channel_id=1, source_target_pairs={{2,0},{4,2},{6,4},{7,6},{5,7},{3,5},{1,3},{0,1},{10,8},{12,10},{14... | collective-permute-start | bytes 405512 | tf_op jit(solution)/shard_map/ppermute | solution.py:417
  44.7 6.1 %collective-permute-start.27 = (bf16[528,128]{1,0:T(8,128)(2,1)S(1)}, bf16[528,128]{1,0:T(8,128)(2,1)S(1)}, u32[]{:S(2)}, u32[]{:S(2)}) collective-permute-start(bf16[528,128]{1,0:T(8,128)(2,1)S(1)} %shard_map.85), channel_id=1, source_target_pairs={{0,2},{2,4},{4,6},{6,7},{7,5},{5,3},{3,1},{1,0},{8,10},{10,12},{12... | collective-permute-start | bytes 405512 | tf_op jit(solution)/shard_map/ppermute | solution.py:414
  45.1 7.3 %collective-permute-start.10 = (bf16[528,128]{1,0:T(8,128)(2,1)S(1)}, bf16[528,128]{1,0:T(8,128)(2,1)S(1)}, u32[]{:S(2)}, u32[]{:S(2)}) collective-permute-start(bf16[528,128]{1,0:T(8,128)(2,1)S(1)} %shard_map.73), channel_id=1, source_target_pairs={{0,2},{2,4},{4,6},{6,7},{7,5},{5,3},{3,1},{1,0},{8,10},{10,12},{12... | collective-permute-start | bytes 405512 | tf_op jit(solution)/shard_map/ppermute | solution.py:414
  47.9 6.5 %collective-permute-start.15 = (bf16[528,128]{1,0:T(8,128)(2,1)S(1)}, bf16[528,128]{1,0:T(8,128)(2,1)S(1)}, u32[]{:S(2)}, u32[]{:S(2)}) collective-permute-start(bf16[528,128]{1,0:T(8,128)(2,1)S(1)} %shard_map.77), channel_id=1, source_target_pairs={{2,0},{4,2},{6,4},{7,6},{5,7},{3,5},{1,3},{0,1},{10,8},{12,10},{14... | collective-permute-start | bytes 405512 | tf_op jit(solution)/shard_map/ppermute | solution.py:417
  49.6 6.6 %collective-permute-start.31 = (bf16[528,128]{1,0:T(8,128)(2,1)S(1)}, bf16[528,128]{1,0:T(8,128)(2,1)S(1)}, u32[]{:S(2)}, u32[]{:S(2)}) collective-permute-start(bf16[528,128]{1,0:T(8,128)(2,1)S(1)} %shard_map.88), channel_id=1, source_target_pairs={{2,0},{4,2},{6,4},{7,6},{5,7},{3,5},{1,3},{0,1},{10,8},{12,10},{14... | collective-permute-start | bytes 405512 | tf_op jit(solution)/shard_map/ppermute | solution.py:417
  51.0 7.0 %collective-permute-start.28 = (bf16[528,128]{1,0:T(8,128)(2,1)S(1)}, bf16[528,128]{1,0:T(8,128)(2,1)S(1)}, u32[]{:S(2)}, u32[]{:S(2)}) collective-permute-start(bf16[528,128]{1,0:T(8,128)(2,1)S(1)} %shard_map.86), channel_id=1, source_target_pairs={{0,2},{2,4},{4,6},{6,7},{7,5},{5,3},{3,1},{1,0},{8,10},{10,12},{12... | collective-permute-start | bytes 405512 | tf_op jit(solution)/shard_map/ppermute | solution.py:414
  52.6 6.4 %collective-permute-start.11 = (bf16[528,128]{1,0:T(8,128)(2,1)S(1)}, bf16[528,128]{1,0:T(8,128)(2,1)S(1)}, u32[]{:S(2)}, u32[]{:S(2)}) collective-permute-start(bf16[528,128]{1,0:T(8,128)(2,1)S(1)} %shard_map.74), channel_id=1, source_target_pairs={{0,2},{2,4},{4,6},{6,7},{7,5},{5,3},{3,1},{1,0},{8,10},{10,12},{12... | collective-permute-start | bytes 405512 | tf_op jit(solution)/shard_map/ppermute | solution.py:414
  (14 other events, 62.0 us)

commit v12 on v11

--- a/solution.py
+++ b/solution.py
@@ -153,11 +153,11 @@
 
 
 def page_lists(page_owner, page_index, lengths):
-    lanes = jnp.arange(LANES, dtype=jnp.int32)[None, None, :]
-    counts = jnp.clip(lengths[:, None] - jnp.arange(SEL, dtype=jnp.int32)[None, :] * PAGE, 0, PAGE)
-    named = page_owner[:, :, None] == lanes
+    shape = page_owner.shape + (LANES,)
+    named = page_owner[:, :, None] == lax.broadcasted_iota(jnp.int32, shape, 2)
+    counts = jnp.clip(lengths[:, None, None] - lax.broadcasted_iota(jnp.int32, shape, 1) * PAGE, 0, PAGE)
     return (
-        jnp.sum(jnp.where(named, counts[:, :, None], 0), axis=1),
+        jnp.sum(jnp.where(named, counts, 0), axis=1),
         jnp.sum(jnp.where(named, page_index, 0), axis=1),
     )
 
@@ -320,11 +320,11 @@
     )(arrived, own)
 
 
-def gather_kernel(first, ahead_ref, behind_ref, own_ref, *outs):
+def split_kernel(firsts, *refs):
+    arrays, outs = refs[: len(firsts)], refs[len(firsts) :]
     for pair in range(len(outs) // 2):
-        part = slice(pair * PAIR, (pair + 1) * PAIR)
-        own = own_ref.at[first + pair * PAIR : first + (pair + 1) * PAIR]
-        sources = [own, ahead_ref.at[part], behind_ref.at[part]]
+        start = pair * PAIR
+        sources = [ref.at[first + start : first + start + PAIR] for ref, first in zip(arrays, firsts)]
         shares, level = blend([unpack_stats(ref[2 * BODY : PAIR, :]) for ref in sources])
         values = [mix(shares, sources, second * BODY, second * SECOND) for second in range(2)]
         for second in range(2):
@@ -336,49 +336,50 @@
             out[BODY:LONE, :] = pack_stats(here)
 
 
-def gather(ahead, behind, own):
-    pairs = ahead.shape[0] // PAIR
-    own, first = own
-    return pl.pallas_call(
-        functools.partial(gather_kernel, first),
-        out_shape=[jax.ShapeDtypeStruct((LONE, HD), BF16)] * (2 * pairs),
-        in_specs=[IN_VMEM] * 3,
-        out_specs=[IN_VMEM] * (2 * pairs),
-        compiler_params=params(),
-        cost_estimate=cost(0, 8 * pairs * PAIR * HD),
-    )(ahead, behind, own)
+def split(sources, requests):
+    return pl.pallas_call(
+        functools.partial(split_kernel, [first for _, first in sources]),
+        out_shape=[jax.ShapeDtypeStruct((LONE, HD), BF16)] * requests,
+        in_specs=[IN_VMEM] * len(sources),
+        out_specs=[IN_VMEM] * requests,
+        compiler_params=params(),
+        cost_estimate=cost(0, 6 * requests * LONE * HD),
+    )(*[array for array, _ in sources])
 
 
 def final_kernel(first, early, owners, place_ref, *refs):
     earlier, parts = refs[:early], refs[early:-4]
     new_ref, level_ref, out_ref, rows_ref = refs[-4:]
     group = lax.div(place_ref[0], owners)
-    for number, part in enumerate(parts):
+    count = len(parts) // 2
+    for number in range(count):
         d = first + number
-        shares, _ = blend([unpack_stats(part[BODY:LONE, :]), level_ref[d]])
-        for index, tile in enumerate(mix(shares, (part, new_ref.at[d]), 0, 0)):
+        both = (parts[2 * number], parts[2 * number + 1])
+        shares, _ = blend([unpack_stats(part[BODY:LONE, :]) for part in both] + [level_ref[d]])
+        for index, tile in enumerate(mix(shares, both + (new_ref.at[d],), 0, 0)):
             row = tile_start(index)
             rows_ref[number, row : row + HALF, :] = tile
-    for number in range(len(parts)):
+    for number in range(count):
         row = group ^ (first + number) if early else number
         for head in range(KVH * GQ):
             tile = rows_ref[number, head * STEPS : (head + 1) * STEPS, :]
             out_ref[row, :, head * HD : (head + 1) * HD] = tile.astype(BF16)
     for ref in earlier:
         for number in range(ref.shape[0]):
-            out_ref[group ^ (len(parts) + number)] = ref[number]
+            out_ref[group ^ (count + number)] = ref[number]
 
 
 def final(place, owners, parts, first, new_out, new_level, earlier=()):
-    requests = len(parts) + sum(e.shape[0] for e in earlier)
+    count = len(parts) // 2
+    requests = count + sum(e.shape[0] for e in earlier)
     return pl.pallas_call(
         functools.partial(final_kernel, first, len(earlier), owners),
         out_shape=jax.ShapeDtypeStruct((requests, STEPS, KVH * GQ * HD), BF16),
         in_specs=[IN_SMEM] + [IN_VMEM] * (len(earlier) + len(parts) + 2),
         out_specs=IN_VMEM,
-        scratch_shapes=[pltpu.VMEM((len(parts), BODY, HD), F32)],
-        compiler_params=params(),
-        cost_estimate=cost(0, len(parts) * BODY * HD * 8),
+        scratch_shapes=[pltpu.VMEM((count, BODY, HD), F32)],
+        compiler_params=params(),
+        cost_estimate=cost(0, count * BODY * HD * 10),
     )(place, *earlier, *parts, new_out, new_level)
 
 
@@ -437,24 +438,27 @@
             done[half] = [both]
     far = owned([up(below[0])], slots[:1]), owned([down(above[1])], slots[1:])
 
-    arrived = []
+    def straight(array, ring, d):
+        pairs = [(g * owners + a, (g ^ d) * owners + b) for g in range(groups) for a, b in ring]
+        return lax.ppermute(array, ("grp", "cache"), pairs)
+
+    home = [None] * requests
     for half in range(2):
-        for move, sign in ((up, 1), (down, -1)):
-            if half == (0 if sign == 1 else 1):
-                chain, steps = far[half], range(reach - 1, -1, -1)
-            else:
-                own, first = parts[half, sign * (reach - 1)]
-                chain, steps = own[first : first + size], range(reach - 2, -1, -1)
-            for step in steps:
-                chain = move(chain)
-                if step > 0:
-                    chain = merge(chain, parts[half, sign * step])
-            arrived.append(chain)
-    back = gather(arrived[2], arrived[3], parts[1, 0])
-    front = gather(arrived[0], arrived[1], (after(parts[0, 0][0], *back), 0))
-    home = [swap(part, d) for d, part in enumerate(front + back)]
-    early = final(place, owners, home[cut:], cut, new_out, new_level)
-    return final(place, owners, home[:cut], 0, new_out, new_level, [early])
+        move, ring, sign = ((up, forward, 1), (down, backward, -1))[half]
+        chain = far[half]
+        for step in range(reach - 1, 1, -1):
+            chain = merge(move(chain), parts[half, sign * step])
+        long = split([(move(chain), 0), parts[half, sign]], cut)
+        move, sign = ((down, -1), (up, 1))[half]
+        own, first = parts[half, sign * (reach - 1)]
+        chain = move(own[first : first + size])
+        for step in range(reach - 2, 0, -1):
+            chain = move(merge(chain, parts[half, sign * step]))
+        short = split([parts[half, 0], (chain, 0)], cut)
+        for number, d in enumerate(slots[half]):
+            home[d] = [swap(short[number], d), straight(long[number], ring, d)]
+    early = final(place, owners, sum(home[cut:], []), cut, new_out, new_level)
+    return final(place, owners, sum(home[:cut], []), 0, new_out, new_level, [early])
 
 
 def solution(mesh):

time: 67.6 us -> 67.8 us (level)
  waiting for transfers between devices: 9.94 us -> 12.5 us
  Pallas kernels: 11.9 us -> 10.8 us
  other arithmetic: 1.52 us -> 0.79 us
    ppermute x14 -> x13, starting transfers between devices: 18.1 us -> 5.45 us  [up(): return lax.ppermute(array, 'cache', forward)]
    ppermute x14 -> x13, starting transfers between devices: 15.9 us -> 23.9 us  [down(): return lax.ppermute(array, 'cache', backward)]
    ppermute x0 -> x4, starting transfers between devices: none -> 4.48 us  [straight(): return lax.ppermute(array, ('grp', 'cache'), pairs)]
    ppermute x0 -> x4, waiting for transfers between devices: none -> 4.23 us  [straight(): return lax.ppermute(array, ('grp', 'cache'), pairs)]
    ppermute x14 -> x13, waiting for transfers between devices: 3.79 us -> 6.14 us  [up(): return lax.ppermute(array, 'cache', forward)]
    ppermute x6, waiting for transfers between devices: 2.22 us -> 0.02 us  [swap(): lax.ppermute(array, 'grp', [(g, g ^ d) for g in range(groups)])]
    ppermute x14 -> x13, waiting for transfers between devices: 3.93 us -> 2.1 us  [down(): return lax.ppermute(array, 'cache', backward)]
    pallas_call x9, Pallas kernels: 5.97 us -> 4.65 us  [items(): pl.pallas_call(functools.partial(item_kernel, slots, visitors, owners), o...]
  transfers between devices with their start and end apart: 34 -> 36, of which waited for: 12 -> 12; matrix products, arithmetic and copies ran while one was open for 2% -> 1% of each run, Pallas kernels for 16% -> 14%
where the time goes in v12:
time: 67.8 us; the launch traced here: 67.9 us
  starting transfers between devices  39.2 us (58%)
  waiting for transfers between devices  12.5 us (18%)
  Pallas kernels  10.8 us (16%)
  local copies, waits for them, and re-layouts  4.36 us (6%)
  other arithmetic  0.79 us (1%)
    ppermute x13, starting transfers between devices, down(): return lax.ppermute(array, 'cache', backward)  23.9 us
    ppermute x13, waiting for transfers between devices, up(): return lax.ppermute(array, 'cache', forward)  6.14 us
    ppermute x13, starting transfers between devices, up(): return lax.ppermute(array, 'cache', forward)  5.45 us
    ppermute x6, starting transfers between devices, swap(): lax.ppermute(array, 'grp', [(g, g ^ d) for g in range(groups)])  5.41 us
    pallas_call x9, Pallas kernels, items(): pl.pallas_call(functools.partial(item_kernel, slots, visitors, owners), o...  4.65 us
    ppermute x4, starting transfers between devices, straight(): return lax.ppermute(array, ('grp', 'cache'), pairs)  4.48 us
    unnamed x8, local copies, waits for them, and re-layouts  4.33 us
    ppermute x4, waiting for transfers between devices, straight(): return lax.ppermute(array, ('grp', 'cache'), pairs)  4.23 us
  transfers between devices with their start and end apart: 36, of which 12 were waited for; matrix products, arithmetic and copies ran while one was open for 1% of the time, Pallas kernels for 14%

profile of v12, /device:TPU:0, one launch (start us, length us, event | category | flops | bytes accessed | tf_op | source)
XLA Modules:
  0.0 67.9 jit_solution(10316680500996527256)
XLA Ops:
  1.5 2.6 %collective-permute-start.1 = (bf16[256,128]{1,0:T(8,128)(2,1)S(1)}, bf16[256,128]{1,0:T(8,128)(2,1)S(1)}, u32[]{:S(2)}, u32[]{:S(2)}) collective-permute-start(bf16[256,128]{1,0:T(8,128)(2,1)S(1)} %get-tuple-element.34.refs_2_), channel_id=1, source_target_pairs={{0,16},{8,24},{16,0},{24,8},{1,17},{9,25},{17,1},{25,9},{2,18},{10... | collective-permute-start | bytes 196616 | tf_op jit(solution)/shard_map/ppermute | solution.py:402
  5.0 3.4 %copy-done = bf16[16,128,2048]{2,1,0:T(8,128)(2,1)S(1)} copy-done((bf16[16,128,2048]{2,1,0:T(8,128)(2,1)S(1)}, bf16[16,128,2048]{2,1,0:T(8,128)(2,1)}, u32[]{:S(2)}) %copy-start) | copy-done | bytes 8388632
  8.4 1.8 %collective-permute-start.5 = (bf16[528,128]{1,0:T(8,128)(2,1)S(1)}, bf16[528,128]{1,0:T(8,128)(2,1)S(1)}, u32[]{:S(2)}, u32[]{:S(2)}) collective-permute-start(bf16[528,128]{1,0:T(8,128)(2,1)S(1)} %shard_map.67.refs_1_), channel_id=1, source_target_pairs={{2,0},{4,2},{6,4},{7,6},{5,7},{3,5},{1,3},{0,1},{10,8},{12,10},{14... | collective-permute-start | bytes 405512 | tf_op jit(solution)/shard_map/ppermute | solution.py:418
  10.5 1.8 %collective-permute-start.3 = (bf16[528,128]{1,0:T(8,128)(2,1)S(1)}, bf16[528,128]{1,0:T(8,128)(2,1)S(1)}, u32[]{:S(2)}, u32[]{:S(2)}) collective-permute-start(bf16[528,128]{1,0:T(8,128)(2,1)S(1)} %shard_map.67.refs_1_), channel_id=1, source_target_pairs={{0,2},{2,4},{4,6},{6,7},{7,5},{5,3},{3,1},{1,0},{8,10},{10,12},{12... | collective-permute-start | bytes 405512 | tf_op jit(solution)/shard_map/ppermute | solution.py:415
  14.4 2.2 %collective-permute-start.7 = (bf16[528,128]{1,0:T(8,128)(2,1)S(1)}, bf16[528,128]{1,0:T(8,128)(2,1)S(1)}, u32[]{:S(2)}, u32[]{:S(2)}) collective-permute-start(bf16[528,128]{1,0:T(8,128)(2,1)S(1)} %collective-permute-done.5.refs_1_), channel_id=1, source_target_pairs={{2,0},{4,2},{6,4},{7,6},{5,7},{3,5},{1,3},{0,1},{10,8},{12,10},{14... | collective-permute-start | bytes 405512 | tf_op jit(solution)/shard_map/ppermute | solution.py:418
  16.9 2.0 %collective-permute-done.3.refs_0_ = bf16[528,128]{1,0:T(8,128)(2,1)S(1)} collective-permute-done((bf16[528,128]{1,0:T(8,128)(2,1)S(1)}, bf16[528,128]{1,0:T(8,128)(2,1)S(1)}, u32[]{:S(2)}, u32[]{:S(2)}) %collective-permute-start.3) | collective-permute-done | bytes 135200 | tf_op jit(solution)/shard_map/ppermute | solution.py:415
  19.4 1.6 %collective-permute-start.24 = (bf16[528,128]{1,0:T(8,128)(2,1)S(1)}, bf16[528,128]{1,0:T(8,128)(2,1)S(1)}, u32[]{:S(2)}, u32[]{:S(2)}) collective-permute-start(bf16[528,128]{1,0:T(8,128)(2,1)S(1)} %collective-permute-done.22.refs_1_), channel_id=1, source_target_pairs={{2,0},{4,2},{6,4},{7,6},{5,7},{3,5},{1,3},{0,1},{10,8},{12,10},{14... | collective-permute-start | bytes 405512 | tf_op jit(solution)/shard_map/ppermute | solution.py:418
  21.2 1.6 %collective-permute-start.8 = (bf16[528,128]{1,0:T(8,128)(2,1)S(1)}, bf16[528,128]{1,0:T(8,128)(2,1)S(1)}, u32[]{:S(2)}, u32[]{:S(2)}) collective-permute-start(bf16[528,128]{1,0:T(8,128)(2,1)S(1)} %collective-permute-done.7.refs_1_), channel_id=1, source_target_pairs={{2,0},{4,2},{6,4},{7,6},{5,7},{3,5},{1,3},{0,1},{10,8},{12,10},{14... | collective-permute-start | bytes 405512 | tf_op jit(solution)/shard_map/ppermute | solution.py:418
  25.7 1.3 %collective-permute-start.25 = (bf16[528,128]{1,0:T(8,128)(2,1)S(1)}, bf16[528,128]{1,0:T(8,128)(2,1)S(1)}, u32[]{:S(2)}, u32[]{:S(2)}) collective-permute-start(bf16[528,128]{1,0:T(8,128)(2,1)S(1)} %collective-permute-done.24.refs_1_), channel_id=1, source_target_pairs={{2,0},{4,2},{6,4},{7,6},{5,7},{3,5},{1,3},{0,1},{10,8},{12,10},{14... | collective-permute-start | bytes 405512 | tf_op jit(solution)/shard_map/ppermute | solution.py:418
  28.0 1.9 %collective-permute-start.13 = (bf16[528,128]{1,0:T(8,128)(2,1)S(1)}, bf16[528,128]{1,0:T(8,128)(2,1)S(1)}, u32[]{:S(2)}, u32[]{:S(2)}) collective-permute-start(bf16[528,128]{1,0:T(8,128)(2,1)S(1)} %collective-permute-done.8.refs_1_), channel_id=1, source_target_pairs={{2,0},{4,2},{6,4},{7,6},{5,7},{3,5},{1,3},{0,1},{10,8},{12,10},{14... | collective-permute-start | bytes 405512 | tf_op jit(solution)/shard_map/ppermute | solution.py:418
  30.3 1.6 %collective-permute-done.6.refs_0_ = bf16[528,128]{1,0:T(8,128)(2,1)S(1)} collective-permute-done((bf16[528,128]{1,0:T(8,128)(2,1)S(1)}, bf16[528,128]{1,0:T(8,128)(2,1)S(1)}, u32[]{:S(2)}, u32[]{:S(2)}) %collective-permute-start.6) | collective-permute-done | bytes 135200 | tf_op jit(solution)/shard_map/ppermute | solution.py:415
  33.8 3.3 %collective-permute-start.26 = (bf16[528,128]{1,0:T(8,128)(2,1)S(1)}, bf16[528,128]{1,0:T(8,128)(2,1)S(1)}, u32[]{:S(2)}, u32[]{:S(2)}) collective-permute-start(bf16[528,128]{1,0:T(8,128)(2,1)S(1)} %slice.9), channel_id=1, source_target_pairs={{2,0},{4,2},{6,4},{7,6},{5,7},{3,5},{1,3},{0,1},{10,8},{12,10},{14... | collective-permute-start | bytes 405512 | tf_op jit(solution)/shard_map/ppermute | solution.py:418
  37.3 2.0 %collective-permute-start.14 = (bf16[528,128]{1,0:T(8,128)(2,1)S(1)}, bf16[528,128]{1,0:T(8,128)(2,1)S(1)}, u32[]{:S(2)}, u32[]{:S(2)}) collective-permute-start(bf16[528,128]{1,0:T(8,128)(2,1)S(1)} %shard_map.76), channel_id=1, source_target_pairs={{2,0},{4,2},{6,4},{7,6},{5,7},{3,5},{1,3},{0,1},{10,8},{12,10},{14... | collective-permute-start | bytes 405512 | tf_op jit(solution)/shard_map/ppermute | solution.py:418
  41.3 2.5 %collective-permute-start.27 = (bf16[528,128]{1,0:T(8,128)(2,1)S(1)}, bf16[528,128]{1,0:T(8,128)(2,1)S(1)}, u32[]{:S(2)}, u32[]{:S(2)}) collective-permute-start(bf16[528,128]{1,0:T(8,128)(2,1)S(1)} %shard_map.84), channel_id=1, source_target_pairs={{2,0},{4,2},{6,4},{7,6},{5,7},{3,5},{1,3},{0,1},{10,8},{12,10},{14... | collective-permute-start | bytes 405512 | tf_op jit(solution)/shard_map/ppermute | solution.py:418
  44.1 2.2 %collective-permute-start.15 = (bf16[528,128]{1,0:T(8,128)(2,1)S(1)}, bf16[528,128]{1,0:T(8,128)(2,1)S(1)}, u32[]{:S(2)}, u32[]{:S(2)}) collective-permute-start(bf16[528,128]{1,0:T(8,128)(2,1)S(1)} %shard_map.77), channel_id=1, source_target_pairs={{2,0},{4,2},{6,4},{7,6},{5,7},{3,5},{1,3},{0,1},{10,8},{12,10},{14... | collective-permute-start | bytes 405512 | tf_op jit(solution)/shard_map/ppermute | solution.py:418
  46.6 2.1 %collective-permute-done.10.arrived_ref = bf16[528,128]{1,0:T(8,128)(2,1)S(1)} collective-permute-done((bf16[528,128]{1,0:T(8,128)(2,1)S(1)}, bf16[528,128]{1,0:T(8,128)(2,1)S(1)}, u32[]{:S(2)}, u32[]{:S(2)}) %collective-permute-start.10) | collective-permute-done | bytes 135200 | tf_op jit(solution)/shard_map/ppermute | solution.py:415
  49.3 2.0 %collective-permute-start.28 = (bf16[528,128]{1,0:T(8,128)(2,1)S(1)}, bf16[528,128]{1,0:T(8,128)(2,1)S(1)}, u32[]{:S(2)}, u32[]{:S(2)}) collective-permute-start(bf16[528,128]{1,0:T(8,128)(2,1)S(1)} %shard_map.85), channel_id=1, source_target_pairs={{2,0},{4,2},{6,4},{7,6},{5,7},{3,5},{1,3},{0,1},{10,8},{12,10},{14... | collective-permute-start | bytes 405512 | tf_op jit(solution)/shard_map/ppermute | solution.py:418
  51.6 1.2 %collective-permute-start.16 = (bf16[528,128]{1,0:T(8,128)(2,1)S(1)}, bf16[528,128]{1,0:T(8,128)(2,1)S(1)}, u32[]{:S(2)}, u32[]{:S(2)}) collective-permute-start(bf16[528,128]{1,0:T(8,128)(2,1)S(1)} %shard_map.78), channel_id=1, source_target_pairs={{2,0},{4,2},{6,4},{7,6},{5,7},{3,5},{1,3},{0,1},{10,8},{12,10},{14... | collective-permute-start | bytes 405512 | tf_op jit(solution)/shard_map/ppermute | solution.py:418
  54.8 2.1 %collective-permute-start.34 = (bf16[272,128]{1,0:T(8,128)(2,1)S(1)}, bf16[272,128]{1,0:T(8,128)(2,1)S(1)}, u32[]{:S(2)}, u32[]{:S(2)}) collective-permute-start(bf16[272,128]{1,0:T(8,128)(2,1)S(1)} %get-tuple-element.57), channel_id=1, source_target_pairs={{0,8},{8,0},{16,24},{24,16},{1,9},{9,1},{17,25},{25,17},{2,10},{10... | collective-permute-start | bytes 208904 | tf_op jit(solution)/shard_map/ppermute | solution.py:402
  57.2 1.3 %collective-permute-start.17 = (bf16[272,128]{1,0:T(8,128)(2,1)S(1)}, bf16[272,128]{1,0:T(8,128)(2,1)S(1)}, u32[]{:S(2)}, u32[]{:S(2)}) collective-permute-start(bf16[272,128]{1,0:T(8,128)(2,1)S(1)} %get-tuple-element.45), channel_id=1, source_target_pairs={{2,16},{4,18},{6,20},{7,22},{5,23},{3,21},{1,19},{0,17},{10,24},{1... | collective-permute-start | bytes 208904 | tf_op jit(solution)/shard_map/ppermute | solution.py:443
  58.4 1.8 %collective-permute-start.19 = (bf16[272,128]{1,0:T(8,128)(2,1)S(1)}, bf16[272,128]{1,0:T(8,128)(2,1)S(1)}, u32[]{:S(2)}, u32[]{:S(2)}) collective-permute-start(bf16[272,128]{1,0:T(8,128)(2,1)S(1)} %get-tuple-element.47), channel_id=1, source_target_pairs={{2,24},{4,26},{6,28},{7,30},{5,31},{3,29},{1,27},{0,25},{10,16},{1... | collective-permute-start | bytes 208904 | tf_op jit(solution)/shard_map/ppermute | solution.py:443
  62.5 1.2 %collective-permute-done.19.refs_3_ = bf16[272,128]{1,0:T(8,128)(2,1)S(1)} collective-permute-done((bf16[272,128]{1,0:T(8,128)(2,1)S(1)}, bf16[272,128]{1,0:T(8,128)(2,1)S(1)}, u32[]{:S(2)}, u32[]{:S(2)}) %collective-permute-start.19) | collective-permute-done | bytes 69664 | tf_op jit(solution)/shard_map/ppermute | solution.py:443
  64.3 1.3 %collective-permute-done.33.refs_2_ = bf16[272,128]{1,0:T(8,128)(2,1)S(1)} collective-permute-done((bf16[272,128]{1,0:T(8,128)(2,1)S(1)}, bf16[272,128]{1,0:T(8,128)(2,1)S(1)}, u32[]{:S(2)}, u32[]{:S(2)}) %collective-permute-start.33) | collective-permute-done | bytes 69664 | tf_op jit(solution)/shard_map/ppermute | solution.py:443
  66.7 1.2 %shard_map.91 = bf16[4,4,8192]{2,1,0:T(4,128)(2,1)} custom-call(s32[1]{0:T(128)} %bitcast.place_ref, bf16[2,4,8192]{2,1,0:T(4,128)(2,1)S(1)} %shard_map.80.refs_0_, bf16[272,128]{1,0:T(8,128)(2,1)S(1)} %get-tuple-element.55.refs_1_, bf16[272,128]{1,0:T(8,128)(2,1)S(1)} %collective-permute-done.33.refs_2_, ...), custom_call_target="tpu_custom_call" | custom-call | bytes 655360 | tf_op jit(solution)/shard_map/pallas_call | solution.py:375
  (88 shorter events, 21.7 us)
Async XLA Ops:
  1.5 6.9 %collective-permute-start.1 = (bf16[256,128]{1,0:T(8,128)(2,1)S(1)}, bf16[256,128]{1,0:T(8,128)(2,1)S(1)}, u32[]{:S(2)}, u32[]{:S(2)}) collective-permute-start(bf16[256,128]{1,0:T(8,128)(2,1)S(1)} %get-tuple-element.34.refs_2_), channel_id=1, source_target_pairs={{0,16},{8,24},{16,0},{24,8},{1,17},{9,25},{17,1},{25,9},{2,18},{10... | collective-permute-start | bytes 196616 | tf_op jit(solution)/shard_map/ppermute | solution.py:402
  10.2 6.4 %collective-permute-start.20 = (bf16[528,128]{1,0:T(8,128)(2,1)S(1)}, bf16[528,128]{1,0:T(8,128)(2,1)S(1)}, u32[]{:S(2)}, u32[]{:S(2)}) collective-permute-start(bf16[528,128]{1,0:T(8,128)(2,1)S(1)} %shard_map.65.after_ref.refs_0_), channel_id=1, source_target_pairs={{0,2},{2,4},{4,6},{6,7},{7,5},{5,3},{3,1},{1,0},{8,10},{10,12},{12... | collective-permute-start | bytes 405512 | tf_op jit(solution)/shard_map/ppermute | solution.py:415
  10.5 8.5 %collective-permute-start.3 = (bf16[528,128]{1,0:T(8,128)(2,1)S(1)}, bf16[528,128]{1,0:T(8,128)(2,1)S(1)}, u32[]{:S(2)}, u32[]{:S(2)}) collective-permute-start(bf16[528,128]{1,0:T(8,128)(2,1)S(1)} %shard_map.67.refs_1_), channel_id=1, source_target_pairs={{0,2},{2,4},{4,6},{6,7},{7,5},{5,3},{3,1},{1,0},{8,10},{10,12},{12... | collective-permute-start | bytes 405512 | tf_op jit(solution)/shard_map/ppermute | solution.py:415
  12.3 7.1 %collective-permute-start.22 = (bf16[528,128]{1,0:T(8,128)(2,1)S(1)}, bf16[528,128]{1,0:T(8,128)(2,1)S(1)}, u32[]{:S(2)}, u32[]{:S(2)}) collective-permute-start(bf16[528,128]{1,0:T(8,128)(2,1)S(1)} %shard_map.65.after_ref.refs_0_), channel_id=1, source_target_pairs={{2,0},{4,2},{6,4},{7,6},{5,7},{3,5},{1,3},{0,1},{10,8},{12,10},{14... | collective-permute-start | bytes 405512 | tf_op jit(solution)/shard_map/ppermute | solution.py:418
  14.4 6.9 %collective-permute-start.7 = (bf16[528,128]{1,0:T(8,128)(2,1)S(1)}, bf16[528,128]{1,0:T(8,128)(2,1)S(1)}, u32[]{:S(2)}, u32[]{:S(2)}) collective-permute-start(bf16[528,128]{1,0:T(8,128)(2,1)S(1)} %collective-permute-done.5.refs_1_), channel_id=1, source_target_pairs={{2,0},{4,2},{6,4},{7,6},{5,7},{3,5},{1,3},{0,1},{10,8},{12,10},{14... | collective-permute-start | bytes 405512 | tf_op jit(solution)/shard_map/ppermute | solution.py:418
  16.6 7.1 %collective-permute-start.21 = (bf16[528,128]{1,0:T(8,128)(2,1)S(1)}, bf16[528,128]{1,0:T(8,128)(2,1)S(1)}, u32[]{:S(2)}, u32[]{:S(2)}) collective-permute-start(bf16[528,128]{1,0:T(8,128)(2,1)S(1)} %collective-permute-done.20.refs_0_), channel_id=1, source_target_pairs={{0,2},{2,4},{4,6},{6,7},{7,5},{5,3},{3,1},{1,0},{8,10},{10,12},{12... | collective-permute-start | bytes 405512 | tf_op jit(solution)/shard_map/ppermute | solution.py:415
  19.4 6.3 %collective-permute-start.24 = (bf16[528,128]{1,0:T(8,128)(2,1)S(1)}, bf16[528,128]{1,0:T(8,128)(2,1)S(1)}, u32[]{:S(2)}, u32[]{:S(2)}) collective-permute-start(bf16[528,128]{1,0:T(8,128)(2,1)S(1)} %collective-permute-done.22.refs_1_), channel_id=1, source_target_pairs={{2,0},{4,2},{6,4},{7,6},{5,7},{3,5},{1,3},{0,1},{10,8},{12,10},{14... | collective-permute-start | bytes 405512 | tf_op jit(solution)/shard_map/ppermute | solution.py:418
  21.2 6.8 %collective-permute-start.8 = (bf16[528,128]{1,0:T(8,128)(2,1)S(1)}, bf16[528,128]{1,0:T(8,128)(2,1)S(1)}, u32[]{:S(2)}, u32[]{:S(2)}) collective-permute-start(bf16[528,128]{1,0:T(8,128)(2,1)S(1)} %collective-permute-done.7.refs_1_), channel_id=1, source_target_pairs={{2,0},{4,2},{6,4},{7,6},{5,7},{3,5},{1,3},{0,1},{10,8},{12,10},{14... | collective-permute-start | bytes 405512 | tf_op jit(solution)/shard_map/ppermute | solution.py:418
  23.7 6.5 %collective-permute-start.23 = (bf16[528,128]{1,0:T(8,128)(2,1)S(1)}, bf16[528,128]{1,0:T(8,128)(2,1)S(1)}, u32[]{:S(2)}, u32[]{:S(2)}) collective-permute-start(bf16[528,128]{1,0:T(8,128)(2,1)S(1)} %collective-permute-done.21.refs_0_), channel_id=1, source_target_pairs={{0,2},{2,4},{4,6},{6,7},{7,5},{5,3},{3,1},{1,0},{8,10},{10,12},{12... | collective-permute-start | bytes 405512 | tf_op jit(solution)/shard_map/ppermute | solution.py:415
  24.5 7.4 %collective-permute-start.6 = (bf16[528,128]{1,0:T(8,128)(2,1)S(1)}, bf16[528,128]{1,0:T(8,128)(2,1)S(1)}, u32[]{:S(2)}, u32[]{:S(2)}) collective-permute-start(bf16[528,128]{1,0:T(8,128)(2,1)S(1)} %collective-permute-done.4.refs_0_), channel_id=1, source_target_pairs={{0,2},{2,4},{4,6},{6,7},{7,5},{5,3},{3,1},{1,0},{8,10},{10,12},{12... | collective-permute-start | bytes 405512 | tf_op jit(solution)/shard_map/ppermute | solution.py:415
  25.7 7.2 %collective-permute-start.25 = (bf16[528,128]{1,0:T(8,128)(2,1)S(1)}, bf16[528,128]{1,0:T(8,128)(2,1)S(1)}, u32[]{:S(2)}, u32[]{:S(2)}) collective-permute-start(bf16[528,128]{1,0:T(8,128)(2,1)S(1)} %collective-permute-done.24.refs_1_), channel_id=1, source_target_pairs={{2,0},{4,2},{6,4},{7,6},{5,7},{3,5},{1,3},{0,1},{10,8},{12,10},{14... | collective-permute-start | bytes 405512 | tf_op jit(solution)/shard_map/ppermute | solution.py:418
  28.0 9.1 %collective-permute-start.13 = (bf16[528,128]{1,0:T(8,128)(2,1)S(1)}, bf16[528,128]{1,0:T(8,128)(2,1)S(1)}, u32[]{:S(2)}, u32[]{:S(2)}) collective-permute-start(bf16[528,128]{1,0:T(8,128)(2,1)S(1)} %collective-permute-done.8.refs_1_), channel_id=1, source_target_pairs={{2,0},{4,2},{6,4},{7,6},{5,7},{3,5},{1,3},{0,1},{10,8},{12,10},{14... | collective-permute-start | bytes 405512 | tf_op jit(solution)/shard_map/ppermute | solution.py:418
  30.2 9.1 %collective-permute-start.29 = (bf16[528,128]{1,0:T(8,128)(2,1)S(1)}, bf16[528,128]{1,0:T(8,128)(2,1)S(1)}, u32[]{:S(2)}, u32[]{:S(2)}) collective-permute-start(bf16[528,128]{1,0:T(8,128)(2,1)S(1)} %collective-permute-done.23.refs_0_), channel_id=1, source_target_pairs={{0,2},{2,4},{4,6},{6,7},{7,5},{5,3},{3,1},{1,0},{8,10},{10,12},{12... | collective-permute-start | bytes 405512 | tf_op jit(solution)/shard_map/ppermute | solution.py:415
  32.9 6.7 %collective-permute-start.9 = (bf16[528,128]{1,0:T(8,128)(2,1)S(1)}, bf16[528,128]{1,0:T(8,128)(2,1)S(1)}, u32[]{:S(2)}, u32[]{:S(2)}) collective-permute-start(bf16[528,128]{1,0:T(8,128)(2,1)S(1)} %slice.8), channel_id=1, source_target_pairs={{0,2},{2,4},{4,6},{6,7},{7,5},{5,3},{3,1},{1,0},{8,10},{10,12},{12... | collective-permute-start | bytes 405512 | tf_op jit(solution)/shard_map/ppermute | solution.py:415
  33.8 7.2 %collective-permute-start.26 = (bf16[528,128]{1,0:T(8,128)(2,1)S(1)}, bf16[528,128]{1,0:T(8,128)(2,1)S(1)}, u32[]{:S(2)}, u32[]{:S(2)}) collective-permute-start(bf16[528,128]{1,0:T(8,128)(2,1)S(1)} %slice.9), channel_id=1, source_target_pairs={{2,0},{4,2},{6,4},{7,6},{5,7},{3,5},{1,3},{0,1},{10,8},{12,10},{14... | collective-permute-start | bytes 405512 | tf_op jit(solution)/shard_map/ppermute | solution.py:418
  37.3 6.5 %collective-permute-start.14 = (bf16[528,128]{1,0:T(8,128)(2,1)S(1)}, bf16[528,128]{1,0:T(8,128)(2,1)S(1)}, u32[]{:S(2)}, u32[]{:S(2)}) collective-permute-start(bf16[528,128]{1,0:T(8,128)(2,1)S(1)} %shard_map.76), channel_id=1, source_target_pairs={{2,0},{4,2},{6,4},{7,6},{5,7},{3,5},{1,3},{0,1},{10,8},{12,10},{14... | collective-permute-start | bytes 405512 | tf_op jit(solution)/shard_map/ppermute | solution.py:418
  39.6 6.7 %collective-permute-start.30 = (bf16[528,128]{1,0:T(8,128)(2,1)S(1)}, bf16[528,128]{1,0:T(8,128)(2,1)S(1)}, u32[]{:S(2)}, u32[]{:S(2)}) collective-permute-start(bf16[528,128]{1,0:T(8,128)(2,1)S(1)} %shard_map.87), channel_id=1, source_target_pairs={{0,2},{2,4},{4,6},{6,7},{7,5},{5,3},{3,1},{1,0},{8,10},{10,12},{12... | collective-permute-start | bytes 405512 | tf_op jit(solution)/shard_map/ppermute | solution.py:415
  39.8 8.8 %collective-permute-start.10 = (bf16[528,128]{1,0:T(8,128)(2,1)S(1)}, bf16[528,128]{1,0:T(8,128)(2,1)S(1)}, u32[]{:S(2)}, u32[]{:S(2)}) collective-permute-start(bf16[528,128]{1,0:T(8,128)(2,1)S(1)} %shard_map.73), channel_id=1, source_target_pairs={{0,2},{2,4},{4,6},{6,7},{7,5},{5,3},{3,1},{1,0},{8,10},{10,12},{12... | collective-permute-start | bytes 405512 | tf_op jit(solution)/shard_map/ppermute | solution.py:415
  41.3 7.8 %collective-permute-start.27 = (bf16[528,128]{1,0:T(8,128)(2,1)S(1)}, bf16[528,128]{1,0:T(8,128)(2,1)S(1)}, u32[]{:S(2)}, u32[]{:S(2)}) collective-permute-start(bf16[528,128]{1,0:T(8,128)(2,1)S(1)} %shard_map.84), channel_id=1, source_target_pairs={{2,0},{4,2},{6,4},{7,6},{5,7},{3,5},{1,3},{0,1},{10,8},{12,10},{14... | collective-permute-start | bytes 405512 | tf_op jit(solution)/shard_map/ppermute | solution.py:418
  44.1 7.3 %collective-permute-start.15 = (bf16[528,128]{1,0:T(8,128)(2,1)S(1)}, bf16[528,128]{1,0:T(8,128)(2,1)S(1)}, u32[]{:S(2)}, u32[]{:S(2)}) collective-permute-start(bf16[528,128]{1,0:T(8,128)(2,1)S(1)} %shard_map.77), channel_id=1, source_target_pairs={{2,0},{4,2},{6,4},{7,6},{5,7},{3,5},{1,3},{0,1},{10,8},{12,10},{14... | collective-permute-start | bytes 405512 | tf_op jit(solution)/shard_map/ppermute | solution.py:418
  46.5 6.3 %collective-permute-start.31 = (bf16[528,128]{1,0:T(8,128)(2,1)S(1)}, bf16[528,128]{1,0:T(8,128)(2,1)S(1)}, u32[]{:S(2)}, u32[]{:S(2)}) collective-permute-start(bf16[528,128]{1,0:T(8,128)(2,1)S(1)} %shard_map.88), channel_id=1, source_target_pairs={{0,2},{2,4},{4,6},{6,7},{7,5},{5,3},{3,1},{1,0},{8,10},{10,12},{12... | collective-permute-start | bytes 405512 | tf_op jit(solution)/shard_map/ppermute | solution.py:415
  54.3 6.2 %collective-permute-start.12 = (bf16[272,128]{1,0:T(8,128)(2,1)S(1)}, bf16[272,128]{1,0:T(8,128)(2,1)S(1)}, u32[]{:S(2)}, u32[]{:S(2)}) collective-permute-start(bf16[272,128]{1,0:T(8,128)(2,1)S(1)} %get-tuple-element.44), channel_id=1, source_target_pairs={{0,16},{8,24},{16,0},{24,8},{1,17},{9,25},{17,1},{25,9},{2,18},{10... | collective-permute-start | bytes 208904 | tf_op jit(solution)/shard_map/ppermute | solution.py:402
  54.4 6.5 %collective-permute-start.18 = (bf16[272,128]{1,0:T(8,128)(2,1)S(1)}, bf16[272,128]{1,0:T(8,128)(2,1)S(1)}, u32[]{:S(2)}, u32[]{:S(2)}) collective-permute-start(bf16[272,128]{1,0:T(8,128)(2,1)S(1)} %get-tuple-element.46), channel_id=1, source_target_pairs={{0,24},{8,16},{16,8},{24,0},{1,25},{9,17},{17,9},{25,1},{2,26},{10... | collective-permute-start | bytes 208904 | tf_op jit(solution)/shard_map/ppermute | solution.py:402
  54.8 9.5 %collective-permute-start.34 = (bf16[272,128]{1,0:T(8,128)(2,1)S(1)}, bf16[272,128]{1,0:T(8,128)(2,1)S(1)}, u32[]{:S(2)}, u32[]{:S(2)}) collective-permute-start(bf16[272,128]{1,0:T(8,128)(2,1)S(1)} %get-tuple-element.57), channel_id=1, source_target_pairs={{0,8},{8,0},{16,24},{24,16},{1,9},{9,1},{17,25},{25,17},{2,10},{10... | collective-permute-start | bytes 208904 | tf_op jit(solution)/shard_map/ppermute | solution.py:402
  (16 other events, 75.0 us)

commit v13 on v12

--- a/solution.py
+++ b/solution.py
@@ -19,6 +19,7 @@
 ROWS = GQ * STEPS
 HALF = 16
 BODY = KVH * ROWS
+BATCH = 4
 COLS = BODY // HALF
 SECOND = 3 * COLS
 PAIR = 2 * BODY + HALF
@@ -82,22 +83,24 @@
 def attend(requests):
     across = (((1,), (1,)), ((), ()))
     along = (((1,), (0,)), ((), ()))
-    heads = [(q, k, v, r[3]) for r in requests for q, k, v in zip(*r[:3])]
-    scores = [lax.dot_general(q, k, across, preferred_element_type=F32) for q, k, _, _ in heads]
-    scores = [jnp.where(head[3], s * SCALE, EMPTY) for s, head in zip(scores, heads)]
-    tops = [jnp.max(s, axis=1, keepdims=True) for s in scores]
-    weights = [jnp.exp2(s - t).astype(BF16) for s, t in zip(scores, tops)]
-    mixed = [lax.dot_general(w, head[2], along, preferred_element_type=F32) for w, head in zip(weights, heads)]
-    ones = jnp.ones((weights[0].shape[1], LANES), BF16)
-    total = lax.dot_general(jnp.concatenate(weights, axis=0), ones, along, preferred_element_type=F32)
-    totals = [total[number * ROWS : (number + 1) * ROWS, :] for number in range(len(heads))]
-    results = []
-    for number, request in enumerate(requests):
-        mine = slice(number * KVH, (number + 1) * KVH)
-        first = request[4]
-        level = by_lane(tops[mine], first) + jnp.log2(jnp.maximum(by_lane(totals[mine], first), 1.0))
-        results.append(([m / t for m, t in zip(mixed[mine], totals[mine])], level))
-    return results
+    ones = jnp.ones((requests[0][2][0].shape[0], LANES), BF16)
+    tops, mixed, totals = [[[] for _ in requests] for _ in range(3)]
+    for batch in range(0, KVH, BATCH):
+        heads = [(n, r[0][h], r[1][h], r[2][h], r[3]) for n, r in enumerate(requests) for h in range(batch, batch + BATCH)]
+        scores = [lax.dot_general(q, k, across, preferred_element_type=F32) for _, q, k, _, _ in heads]
+        scores = [jnp.where(head[4], s * SCALE, EMPTY) for s, head in zip(scores, heads)]
+        top = [jnp.max(s, axis=1, keepdims=True) for s in scores]
+        weights = [jnp.exp2(s - t).astype(BF16) for s, t in zip(scores, top)]
+        total = lax.dot_general(jnp.concatenate(weights, axis=0), ones, along, preferred_element_type=F32)
+        for place, (number, _, _, value, _) in enumerate(heads):
+            tops[number].append(top[place])
+            totals[number].append(total[place * ROWS : (place + 1) * ROWS, :])
+            out = lax.dot_general(weights[place], value, along, preferred_element_type=F32)
+            mixed[number].append(out / totals[number][-1])
+    return [
+        (m, by_lane(t, r[4]) + jnp.log2(jnp.maximum(by_lane(s, r[4]), 1.0)))
+        for m, t, s, r in zip(mixed, tops, totals, requests)
+    ]
 
 
 def relayout_kernel(owners, place_ref, queries_ref, *outs):

time: 67.8 us -> 69.5 us (1.025); the launches traced: 67.9 us -> 68.3 us
  Pallas kernels: 10.8 us -> 18.1 us
  waiting for transfers between devices: 12.5 us -> 8.95 us
  starting transfers between devices: 39.2 us -> 35.9 us
    ppermute x13, starting transfers between devices: 23.9 us -> 10.5 us  [down(): return lax.ppermute(array, 'cache', backward)]
    ppermute x13, starting transfers between devices: 5.45 us -> 15.9 us  [up(): return lax.ppermute(array, 'cache', forward)]
    pallas_call x9, Pallas kernels: 4.65 us -> 11.1 us  [items(): pl.pallas_call(functools.partial(item_kernel, slots, visitors, owners), o...]
    ppermute x13, waiting for transfers between devices: 6.14 us -> 1.96 us  [up(): return lax.ppermute(array, 'cache', forward)]
    ppermute x13, waiting for transfers between devices: 2.1 us -> 3.47 us  [down(): return lax.ppermute(array, 'cache', backward)]
    pallas_call x1, Pallas kernels: 1.13 us -> 1.97 us  [new_tokens(): pl.pallas_call(functools.partial(new_kernel, owners), out_shape=[jax.Shap...]
    ppermute x4, waiting for transfers between devices: 4.23 us -> 3.5 us  [straight(): return lax.ppermute(array, ('grp', 'cache'), pairs)]
  transfers between devices with their start and end apart: 36 -> 36, of which waited for: 12 -> 10; matrix products, arithmetic and copies ran while one was open for 1% -> 1% of each run, Pallas kernels for 14% -> 25%
where the time goes in v13:
time: 69.5 us; the launch traced here: 68.3 us
  starting transfers between devices  35.9 us (52%)
  Pallas kernels  18.1 us (26%)
  waiting for transfers between devices  8.95 us (13%)
  local copies, waits for them, and re-layouts  4.36 us (6%)
  other arithmetic  0.79 us (1%)
    ppermute x13, starting transfers between devices, up(): return lax.ppermute(array, 'cache', forward)  15.9 us
    pallas_call x9, Pallas kernels, items(): pl.pallas_call(functools.partial(item_kernel, slots, visitors, owners), o...  11.1 us
    ppermute x13, starting transfers between devices, down(): return lax.ppermute(array, 'cache', backward)  10.5 us
    ppermute x6, starting transfers between devices, swap(): lax.ppermute(array, 'grp', [(g, g ^ d) for g in range(groups)])  5.01 us
    ppermute x4, starting transfers between devices, straight(): return lax.ppermute(array, ('grp', 'cache'), pairs)  4.48 us
    unnamed x8, local copies, waits for them, and re-layouts  4.33 us
    ppermute x4, waiting for transfers between devices, straight(): return lax.ppermute(array, ('grp', 'cache'), pairs)  3.5 us
    ppermute x13, waiting for transfers between devices, down(): return lax.ppermute(array, 'cache', backward)  3.47 us
  transfers between devices with their start and end apart: 36, of which 10 were waited for; matrix products, arithmetic and copies ran while one was open for 1% of the time, Pallas kernels for 25%

profile of v13, /device:TPU:0, one launch (start us, length us, event | category | flops | bytes accessed | tf_op | source)
XLA Modules:
  0.0 68.3 jit_solution(16052118110999933335)
XLA Ops:
  1.5 2.6 %collective-permute-start.1 = (bf16[256,128]{1,0:T(8,128)(2,1)S(1)}, bf16[256,128]{1,0:T(8,128)(2,1)S(1)}, u32[]{:S(2)}, u32[]{:S(2)}) collective-permute-start(bf16[256,128]{1,0:T(8,128)(2,1)S(1)} %get-tuple-element.34.refs_2_), channel_id=1, source_target_pairs={{0,16},{8,24},{16,0},{24,8},{1,17},{9,25},{17,1},{25,9},{2,18},{10... | collective-permute-start | bytes 196616 | tf_op jit(solution)/shard_map/ppermute | solution.py:405
  5.0 3.4 %copy-done = bf16[16,128,2048]{2,1,0:T(8,128)(2,1)S(1)} copy-done((bf16[16,128,2048]{2,1,0:T(8,128)(2,1)S(1)}, bf16[16,128,2048]{2,1,0:T(8,128)(2,1)}, u32[]{:S(2)}) %copy-start) | copy-done | bytes 8388632
  8.4 1.8 %collective-permute-start.5 = (bf16[528,128]{1,0:T(8,128)(2,1)S(1)}, bf16[528,128]{1,0:T(8,128)(2,1)S(1)}, u32[]{:S(2)}, u32[]{:S(2)}) collective-permute-start(bf16[528,128]{1,0:T(8,128)(2,1)S(1)} %shard_map.67.refs_1_), channel_id=1, source_target_pairs={{2,0},{4,2},{6,4},{7,6},{5,7},{3,5},{1,3},{0,1},{10,8},{12,10},{14... | collective-permute-start | bytes 405512 | tf_op jit(solution)/shard_map/ppermute | solution.py:421
  10.5 1.8 %collective-permute-start.3 = (bf16[528,128]{1,0:T(8,128)(2,1)S(1)}, bf16[528,128]{1,0:T(8,128)(2,1)S(1)}, u32[]{:S(2)}, u32[]{:S(2)}) collective-permute-start(bf16[528,128]{1,0:T(8,128)(2,1)S(1)} %shard_map.67.refs_1_), channel_id=1, source_target_pairs={{0,2},{2,4},{4,6},{6,7},{7,5},{5,3},{3,1},{1,0},{8,10},{10,12},{12... | collective-permute-start | bytes 405512 | tf_op jit(solution)/shard_map/ppermute | solution.py:418
  12.5 1.1 %shard_map.68.refs_0_ = bf16[1056,128]{1,0:T(8,128)(2,1)S(1)} custom-call(s32[1]{0:T(128)} %bitcast.place_ref, bf16[16,128,2048]{2,1,0:T(8,128)(2,1)S(1)} %copy-done.1, bf16[528,128]{1,0:T(8,128)(2,1)S(1)} %shard_map.65.after_ref.refs_0_, bf16[528,128]{1,0:T(8,128)(2,1)S(1)} %shard_map.67.refs_1_), custom_call_target="tpu_custom_call" | custom-call | flops 67108864 | bytes 2097152 | tf_op jit(solution)/shard_map/pallas_call | solution.py:266
  13.7 2.0 %shard_map.69 = (f32[4,256,128]{2,1,0:T(8,128)S(1)}, f32[4,16,128]{2,1,0:T(8,128)S(1)}) custom-call(s32[1]{0:T(128)} %bitcast.place_ref, bf16[256,128]{1,0:T(8,128)(2,1)S(1)} %get-tuple-element.36.refs_0_, bf16[256,128]{1,0:T(8,128)(2,1)S(1)} %get-tuple-element.33.refs_1_, bf16[256,128]{1,0:T(8,128)(2,1)S(1)} %get-tuple-element.34.refs_2_, ...), custom_call_target="tpu_custom_call" | custom-call | flops 67108864 | bytes 786432 | tf_op jit(solution)/shard_map/pallas_call | solution.py:145
  18.6 1.4 %collective-permute-start.4 = (bf16[528,128]{1,0:T(8,128)(2,1)S(1)}, bf16[528,128]{1,0:T(8,128)(2,1)S(1)}, u32[]{:S(2)}, u32[]{:S(2)}) collective-permute-start(bf16[528,128]{1,0:T(8,128)(2,1)S(1)} %collective-permute-done.3.refs_0_), channel_id=1, source_target_pairs={{0,2},{2,4},{4,6},{6,7},{7,5},{5,3},{3,1},{1,0},{8,10},{10,12},{12... | collective-permute-start | bytes 405512 | tf_op jit(solution)/shard_map/ppermute | solution.py:418
  21.8 1.6 %collective-permute-start.8 = (bf16[528,128]{1,0:T(8,128)(2,1)S(1)}, bf16[528,128]{1,0:T(8,128)(2,1)S(1)}, u32[]{:S(2)}, u32[]{:S(2)}) collective-permute-start(bf16[528,128]{1,0:T(8,128)(2,1)S(1)} %collective-permute-done.7.refs_1_), channel_id=1, source_target_pairs={{2,0},{4,2},{6,4},{7,6},{5,7},{3,5},{1,3},{0,1},{10,8},{12,10},{14... | collective-permute-start | bytes 405512 | tf_op jit(solution)/shard_map/ppermute | solution.py:421
  23.4 2.0 %shard_map.81.own_ref.refs_1_ = bf16[1056,128]{1,0:T(8,128)(2,1)S(1)} custom-call(s32[1]{0:T(128)} %bitcast.place_ref, bf16[16,128,2048]{2,1,0:T(8,128)(2,1)S(1)} %copy-done.1, bf16[528,128]{1,0:T(8,128)(2,1)S(1)} %collective-permute-done.20.refs_0_, bf16[528,128]{1,0:T(8,128)(2,1)S(1)} %collective-permute-done.22.refs_1_), custom_call_target="tpu_custom_call" | custom-call | flops 67108864 | bytes 2097152 | tf_op jit(solution)/shard_map/pallas_call | solution.py:266
  25.5 1.9 %collective-permute-start.6 = (bf16[528,128]{1,0:T(8,128)(2,1)S(1)}, bf16[528,128]{1,0:T(8,128)(2,1)S(1)}, u32[]{:S(2)}, u32[]{:S(2)}) collective-permute-start(bf16[528,128]{1,0:T(8,128)(2,1)S(1)} %collective-permute-done.4.refs_0_), channel_id=1, source_target_pairs={{0,2},{2,4},{4,6},{6,7},{7,5},{5,3},{3,1},{1,0},{8,10},{10,12},{12... | collective-permute-start | bytes 405512 | tf_op jit(solution)/shard_map/ppermute | solution.py:418
  28.7 2.0 %collective-permute-start.13 = (bf16[528,128]{1,0:T(8,128)(2,1)S(1)}, bf16[528,128]{1,0:T(8,128)(2,1)S(1)}, u32[]{:S(2)}, u32[]{:S(2)}) collective-permute-start(bf16[528,128]{1,0:T(8,128)(2,1)S(1)} %collective-permute-done.8.refs_1_), channel_id=1, source_target_pairs={{2,0},{4,2},{6,4},{7,6},{5,7},{3,5},{1,3},{0,1},{10,8},{12,10},{14... | collective-permute-start | bytes 405512 | tf_op jit(solution)/shard_map/ppermute | solution.py:421
  32.6 1.1 %shard_map.72.own_ref = bf16[1056,128]{1,0:T(8,128)(2,1)S(1)} custom-call(s32[1]{0:T(128)} %bitcast.place_ref, bf16[16,128,2048]{2,1,0:T(8,128)(2,1)S(1)} %copy-done.1, bf16[528,128]{1,0:T(8,128)(2,1)S(1)} %collective-permute-done.6.refs_0_, bf16[528,128]{1,0:T(8,128)(2,1)S(1)} %collective-permute-done.8.refs_1_), custom_call_target="tpu_custom_call" | custom-call | flops 67108864 | bytes 2097152 | tf_op jit(solution)/shard_map/pallas_call | solution.py:266
  33.8 1.2 %collective-permute-start.9 = (bf16[528,128]{1,0:T(8,128)(2,1)S(1)}, bf16[528,128]{1,0:T(8,128)(2,1)S(1)}, u32[]{:S(2)}, u32[]{:S(2)}) collective-permute-start(bf16[528,128]{1,0:T(8,128)(2,1)S(1)} %slice.8), channel_id=1, source_target_pairs={{0,2},{2,4},{4,6},{6,7},{7,5},{5,3},{3,1},{1,0},{8,10},{10,12},{12... | collective-permute-start | bytes 405512 | tf_op jit(solution)/shard_map/ppermute | solution.py:418
  34.9 1.1 %shard_map.83.own_ref = bf16[1056,128]{1,0:T(8,128)(2,1)S(1)} custom-call(s32[1]{0:T(128)} %bitcast.place_ref, bf16[16,128,2048]{2,1,0:T(8,128)(2,1)S(1)} %copy-done.1, bf16[528,128]{1,0:T(8,128)(2,1)S(1)} %collective-permute-done.23.refs_0_, bf16[528,128]{1,0:T(8,128)(2,1)S(1)} %collective-permute-done.25.refs_1_), custom_call_target="tpu_custom_call" | custom-call | flops 67108864 | bytes 2097152 | tf_op jit(solution)/shard_map/pallas_call | solution.py:266
  37.3 2.2 %collective-permute-start.14 = (bf16[528,128]{1,0:T(8,128)(2,1)S(1)}, bf16[528,128]{1,0:T(8,128)(2,1)S(1)}, u32[]{:S(2)}, u32[]{:S(2)}) collective-permute-start(bf16[528,128]{1,0:T(8,128)(2,1)S(1)} %shard_map.76), channel_id=1, source_target_pairs={{2,0},{4,2},{6,4},{7,6},{5,7},{3,5},{1,3},{0,1},{10,8},{12,10},{14... | collective-permute-start | bytes 405512 | tf_op jit(solution)/shard_map/ppermute | solution.py:421
  41.5 2.1 %collective-permute-start.10 = (bf16[528,128]{1,0:T(8,128)(2,1)S(1)}, bf16[528,128]{1,0:T(8,128)(2,1)S(1)}, u32[]{:S(2)}, u32[]{:S(2)}) collective-permute-start(bf16[528,128]{1,0:T(8,128)(2,1)S(1)} %shard_map.73), channel_id=1, source_target_pairs={{0,2},{2,4},{4,6},{6,7},{7,5},{5,3},{3,1},{1,0},{8,10},{10,12},{12... | collective-permute-start | bytes 405512 | tf_op jit(solution)/shard_map/ppermute | solution.py:418
  43.9 2.0 %collective-permute-done.14.arrived_ref = bf16[528,128]{1,0:T(8,128)(2,1)S(1)} collective-permute-done((bf16[528,128]{1,0:T(8,128)(2,1)S(1)}, bf16[528,128]{1,0:T(8,128)(2,1)S(1)}, u32[]{:S(2)}, u32[]{:S(2)}) %collective-permute-start.14) | collective-permute-done | bytes 135200 | tf_op jit(solution)/shard_map/ppermute | solution.py:421
  47.3 1.3 %collective-permute-start.31 = (bf16[528,128]{1,0:T(8,128)(2,1)S(1)}, bf16[528,128]{1,0:T(8,128)(2,1)S(1)}, u32[]{:S(2)}, u32[]{:S(2)}) collective-permute-start(bf16[528,128]{1,0:T(8,128)(2,1)S(1)} %shard_map.88), channel_id=1, source_target_pairs={{0,2},{2,4},{4,6},{6,7},{7,5},{5,3},{3,1},{1,0},{8,10},{10,12},{12... | collective-permute-start | bytes 405512 | tf_op jit(solution)/shard_map/ppermute | solution.py:418
  49.1 1.6 %collective-permute-start.11 = (bf16[528,128]{1,0:T(8,128)(2,1)S(1)}, bf16[528,128]{1,0:T(8,128)(2,1)S(1)}, u32[]{:S(2)}, u32[]{:S(2)}) collective-permute-start(bf16[528,128]{1,0:T(8,128)(2,1)S(1)} %shard_map.74), channel_id=1, source_target_pairs={{0,2},{2,4},{4,6},{6,7},{7,5},{5,3},{3,1},{1,0},{8,10},{10,12},{12... | collective-permute-start | bytes 405512 | tf_op jit(solution)/shard_map/ppermute | solution.py:418
  53.4 1.8 %collective-permute-start.32 = (bf16[528,128]{1,0:T(8,128)(2,1)S(1)}, bf16[528,128]{1,0:T(8,128)(2,1)S(1)}, u32[]{:S(2)}, u32[]{:S(2)}) collective-permute-start(bf16[528,128]{1,0:T(8,128)(2,1)S(1)} %shard_map.89), channel_id=1, source_target_pairs={{0,2},{2,4},{4,6},{6,7},{7,5},{5,3},{3,1},{1,0},{8,10},{10,12},{12... | collective-permute-start | bytes 405512 | tf_op jit(solution)/shard_map/ppermute | solution.py:418
  56.3 1.7 %collective-permute-start.34 = (bf16[272,128]{1,0:T(8,128)(2,1)S(1)}, bf16[272,128]{1,0:T(8,128)(2,1)S(1)}, u32[]{:S(2)}, u32[]{:S(2)}) collective-permute-start(bf16[272,128]{1,0:T(8,128)(2,1)S(1)} %get-tuple-element.57), channel_id=1, source_target_pairs={{0,8},{8,0},{16,24},{24,16},{1,9},{9,1},{17,25},{25,17},{2,10},{10... | collective-permute-start | bytes 208904 | tf_op jit(solution)/shard_map/ppermute | solution.py:405
  59.4 1.3 %collective-permute-start.19 = (bf16[272,128]{1,0:T(8,128)(2,1)S(1)}, bf16[272,128]{1,0:T(8,128)(2,1)S(1)}, u32[]{:S(2)}, u32[]{:S(2)}) collective-permute-start(bf16[272,128]{1,0:T(8,128)(2,1)S(1)} %get-tuple-element.47), channel_id=1, source_target_pairs={{2,24},{4,26},{6,28},{7,30},{5,31},{3,29},{1,27},{0,25},{10,16},{1... | collective-permute-start | bytes 208904 | tf_op jit(solution)/shard_map/ppermute | solution.py:446
  61.9 1.2 %collective-permute-start.35 = (bf16[272,128]{1,0:T(8,128)(2,1)S(1)}, bf16[272,128]{1,0:T(8,128)(2,1)S(1)}, u32[]{:S(2)}, u32[]{:S(2)}) collective-permute-start(bf16[272,128]{1,0:T(8,128)(2,1)S(1)} %get-tuple-element.58), channel_id=1, source_target_pairs={{0,10},{2,12},{4,14},{6,15},{7,13},{5,11},{3,9},{1,8},{8,2},{10,4}... | collective-permute-start | bytes 208904 | tf_op jit(solution)/shard_map/ppermute | solution.py:446
  67.1 1.2 %shard_map.91 = bf16[4,4,8192]{2,1,0:T(4,128)(2,1)} custom-call(s32[1]{0:T(128)} %bitcast.place_ref, bf16[2,4,8192]{2,1,0:T(4,128)(2,1)S(1)} %shard_map.80.refs_0_, bf16[272,128]{1,0:T(8,128)(2,1)S(1)} %get-tuple-element.55.refs_1_, bf16[272,128]{1,0:T(8,128)(2,1)S(1)} %collective-permute-done.33.refs_2_, ...), custom_call_target="tpu_custom_call" | custom-call | bytes 655360 | tf_op jit(solution)/shard_map/pallas_call | solution.py:378
  (88 shorter events, 26.9 us)
Async XLA Ops:
  1.5 6.9 %collective-permute-start.1 = (bf16[256,128]{1,0:T(8,128)(2,1)S(1)}, bf16[256,128]{1,0:T(8,128)(2,1)S(1)}, u32[]{:S(2)}, u32[]{:S(2)}) collective-permute-start(bf16[256,128]{1,0:T(8,128)(2,1)S(1)} %get-tuple-element.34.refs_2_), channel_id=1, source_target_pairs={{0,16},{8,24},{16,0},{24,8},{1,17},{9,25},{17,1},{25,9},{2,18},{10... | collective-permute-start | bytes 196616 | tf_op jit(solution)/shard_map/ppermute | solution.py:405
  8.4 7.2 %collective-permute-start.5 = (bf16[528,128]{1,0:T(8,128)(2,1)S(1)}, bf16[528,128]{1,0:T(8,128)(2,1)S(1)}, u32[]{:S(2)}, u32[]{:S(2)}) collective-permute-start(bf16[528,128]{1,0:T(8,128)(2,1)S(1)} %shard_map.67.refs_1_), channel_id=1, source_target_pairs={{2,0},{4,2},{6,4},{7,6},{5,7},{3,5},{1,3},{0,1},{10,8},{12,10},{14... | collective-permute-start | bytes 405512 | tf_op jit(solution)/shard_map/ppermute | solution.py:421
  10.2 6.4 %collective-permute-start.20 = (bf16[528,128]{1,0:T(8,128)(2,1)S(1)}, bf16[528,128]{1,0:T(8,128)(2,1)S(1)}, u32[]{:S(2)}, u32[]{:S(2)}) collective-permute-start(bf16[528,128]{1,0:T(8,128)(2,1)S(1)} %shard_map.65.after_ref.refs_0_), channel_id=1, source_target_pairs={{0,2},{2,4},{4,6},{6,7},{7,5},{5,3},{3,1},{1,0},{8,10},{10,12},{12... | collective-permute-start | bytes 405512 | tf_op jit(solution)/shard_map/ppermute | solution.py:418
  10.5 8.1 %collective-permute-start.3 = (bf16[528,128]{1,0:T(8,128)(2,1)S(1)}, bf16[528,128]{1,0:T(8,128)(2,1)S(1)}, u32[]{:S(2)}, u32[]{:S(2)}) collective-permute-start(bf16[528,128]{1,0:T(8,128)(2,1)S(1)} %shard_map.67.refs_1_), channel_id=1, source_target_pairs={{0,2},{2,4},{4,6},{6,7},{7,5},{5,3},{3,1},{1,0},{8,10},{10,12},{12... | collective-permute-start | bytes 405512 | tf_op jit(solution)/shard_map/ppermute | solution.py:418
  12.3 7.8 %collective-permute-start.22 = (bf16[528,128]{1,0:T(8,128)(2,1)S(1)}, bf16[528,128]{1,0:T(8,128)(2,1)S(1)}, u32[]{:S(2)}, u32[]{:S(2)}) collective-permute-start(bf16[528,128]{1,0:T(8,128)(2,1)S(1)} %shard_map.65.after_ref.refs_0_), channel_id=1, source_target_pairs={{2,0},{4,2},{6,4},{7,6},{5,7},{3,5},{1,3},{0,1},{10,8},{12,10},{14... | collective-permute-start | bytes 405512 | tf_op jit(solution)/shard_map/ppermute | solution.py:421
  15.7 6.1 %collective-permute-start.7 = (bf16[528,128]{1,0:T(8,128)(2,1)S(1)}, bf16[528,128]{1,0:T(8,128)(2,1)S(1)}, u32[]{:S(2)}, u32[]{:S(2)}) collective-permute-start(bf16[528,128]{1,0:T(8,128)(2,1)S(1)} %collective-permute-done.5.refs_1_), channel_id=1, source_target_pairs={{2,0},{4,2},{6,4},{7,6},{5,7},{3,5},{1,3},{0,1},{10,8},{12,10},{14... | collective-permute-start | bytes 405512 | tf_op jit(solution)/shard_map/ppermute | solution.py:421
  16.6 8.8 %collective-permute-start.21 = (bf16[528,128]{1,0:T(8,128)(2,1)S(1)}, bf16[528,128]{1,0:T(8,128)(2,1)S(1)}, u32[]{:S(2)}, u32[]{:S(2)}) collective-permute-start(bf16[528,128]{1,0:T(8,128)(2,1)S(1)} %collective-permute-done.20.refs_0_), channel_id=1, source_target_pairs={{0,2},{2,4},{4,6},{6,7},{7,5},{5,3},{3,1},{1,0},{8,10},{10,12},{12... | collective-permute-start | bytes 405512 | tf_op jit(solution)/shard_map/ppermute | solution.py:418
  18.6 6.8 %collective-permute-start.4 = (bf16[528,128]{1,0:T(8,128)(2,1)S(1)}, bf16[528,128]{1,0:T(8,128)(2,1)S(1)}, u32[]{:S(2)}, u32[]{:S(2)}) collective-permute-start(bf16[528,128]{1,0:T(8,128)(2,1)S(1)} %collective-permute-done.3.refs_0_), channel_id=1, source_target_pairs={{0,2},{2,4},{4,6},{6,7},{7,5},{5,3},{3,1},{1,0},{8,10},{10,12},{12... | collective-permute-start | bytes 405512 | tf_op jit(solution)/shard_map/ppermute | solution.py:418
  20.1 7.3 %collective-permute-start.24 = (bf16[528,128]{1,0:T(8,128)(2,1)S(1)}, bf16[528,128]{1,0:T(8,128)(2,1)S(1)}, u32[]{:S(2)}, u32[]{:S(2)}) collective-permute-start(bf16[528,128]{1,0:T(8,128)(2,1)S(1)} %collective-permute-done.22.refs_1_), channel_id=1, source_target_pairs={{2,0},{4,2},{6,4},{7,6},{5,7},{3,5},{1,3},{0,1},{10,8},{12,10},{14... | collective-permute-start | bytes 405512 | tf_op jit(solution)/shard_map/ppermute | solution.py:421
  21.8 6.9 %collective-permute-start.8 = (bf16[528,128]{1,0:T(8,128)(2,1)S(1)}, bf16[528,128]{1,0:T(8,128)(2,1)S(1)}, u32[]{:S(2)}, u32[]{:S(2)}) collective-permute-start(bf16[528,128]{1,0:T(8,128)(2,1)S(1)} %collective-permute-done.7.refs_1_), channel_id=1, source_target_pairs={{2,0},{4,2},{6,4},{7,6},{5,7},{3,5},{1,3},{0,1},{10,8},{12,10},{14... | collective-permute-start | bytes 405512 | tf_op jit(solution)/shard_map/ppermute | solution.py:421
  25.4 6.4 %collective-permute-start.23 = (bf16[528,128]{1,0:T(8,128)(2,1)S(1)}, bf16[528,128]{1,0:T(8,128)(2,1)S(1)}, u32[]{:S(2)}, u32[]{:S(2)}) collective-permute-start(bf16[528,128]{1,0:T(8,128)(2,1)S(1)} %collective-permute-done.21.refs_0_), channel_id=1, source_target_pairs={{0,2},{2,4},{4,6},{6,7},{7,5},{5,3},{3,1},{1,0},{8,10},{10,12},{12... | collective-permute-start | bytes 405512 | tf_op jit(solution)/shard_map/ppermute | solution.py:418
  25.5 7.1 %collective-permute-start.6 = (bf16[528,128]{1,0:T(8,128)(2,1)S(1)}, bf16[528,128]{1,0:T(8,128)(2,1)S(1)}, u32[]{:S(2)}, u32[]{:S(2)}) collective-permute-start(bf16[528,128]{1,0:T(8,128)(2,1)S(1)} %collective-permute-done.4.refs_0_), channel_id=1, source_target_pairs={{0,2},{2,4},{4,6},{6,7},{7,5},{5,3},{3,1},{1,0},{8,10},{10,12},{12... | collective-permute-start | bytes 405512 | tf_op jit(solution)/shard_map/ppermute | solution.py:418
  27.3 7.6 %collective-permute-start.25 = (bf16[528,128]{1,0:T(8,128)(2,1)S(1)}, bf16[528,128]{1,0:T(8,128)(2,1)S(1)}, u32[]{:S(2)}, u32[]{:S(2)}) collective-permute-start(bf16[528,128]{1,0:T(8,128)(2,1)S(1)} %collective-permute-done.24.refs_1_), channel_id=1, source_target_pairs={{2,0},{4,2},{6,4},{7,6},{5,7},{3,5},{1,3},{0,1},{10,8},{12,10},{14... | collective-permute-start | bytes 405512 | tf_op jit(solution)/shard_map/ppermute | solution.py:421
  28.7 7.4 %collective-permute-start.13 = (bf16[528,128]{1,0:T(8,128)(2,1)S(1)}, bf16[528,128]{1,0:T(8,128)(2,1)S(1)}, u32[]{:S(2)}, u32[]{:S(2)}) collective-permute-start(bf16[528,128]{1,0:T(8,128)(2,1)S(1)} %collective-permute-done.8.refs_1_), channel_id=1, source_target_pairs={{2,0},{4,2},{6,4},{7,6},{5,7},{3,5},{1,3},{0,1},{10,8},{12,10},{14... | collective-permute-start | bytes 405512 | tf_op jit(solution)/shard_map/ppermute | solution.py:421
  31.8 7.6 %collective-permute-start.29 = (bf16[528,128]{1,0:T(8,128)(2,1)S(1)}, bf16[528,128]{1,0:T(8,128)(2,1)S(1)}, u32[]{:S(2)}, u32[]{:S(2)}) collective-permute-start(bf16[528,128]{1,0:T(8,128)(2,1)S(1)} %collective-permute-done.23.refs_0_), channel_id=1, source_target_pairs={{0,2},{2,4},{4,6},{6,7},{7,5},{5,3},{3,1},{1,0},{8,10},{10,12},{12... | collective-permute-start | bytes 405512 | tf_op jit(solution)/shard_map/ppermute | solution.py:418
  33.8 7.4 %collective-permute-start.9 = (bf16[528,128]{1,0:T(8,128)(2,1)S(1)}, bf16[528,128]{1,0:T(8,128)(2,1)S(1)}, u32[]{:S(2)}, u32[]{:S(2)}) collective-permute-start(bf16[528,128]{1,0:T(8,128)(2,1)S(1)} %slice.8), channel_id=1, source_target_pairs={{0,2},{2,4},{4,6},{6,7},{7,5},{5,3},{3,1},{1,0},{8,10},{10,12},{12... | collective-permute-start | bytes 405512 | tf_op jit(solution)/shard_map/ppermute | solution.py:418
  36.1 7.5 %collective-permute-start.26 = (bf16[528,128]{1,0:T(8,128)(2,1)S(1)}, bf16[528,128]{1,0:T(8,128)(2,1)S(1)}, u32[]{:S(2)}, u32[]{:S(2)}) collective-permute-start(bf16[528,128]{1,0:T(8,128)(2,1)S(1)} %slice.9), channel_id=1, source_target_pairs={{2,0},{4,2},{6,4},{7,6},{5,7},{3,5},{1,3},{0,1},{10,8},{12,10},{14... | collective-permute-start | bytes 405512 | tf_op jit(solution)/shard_map/ppermute | solution.py:421
  37.3 8.6 %collective-permute-start.14 = (bf16[528,128]{1,0:T(8,128)(2,1)S(1)}, bf16[528,128]{1,0:T(8,128)(2,1)S(1)}, u32[]{:S(2)}, u32[]{:S(2)}) collective-permute-start(bf16[528,128]{1,0:T(8,128)(2,1)S(1)} %shard_map.76), channel_id=1, source_target_pairs={{2,0},{4,2},{6,4},{7,6},{5,7},{3,5},{1,3},{0,1},{10,8},{12,10},{14... | collective-permute-start | bytes 405512 | tf_op jit(solution)/shard_map/ppermute | solution.py:421
  40.6 6.5 %collective-permute-start.30 = (bf16[528,128]{1,0:T(8,128)(2,1)S(1)}, bf16[528,128]{1,0:T(8,128)(2,1)S(1)}, u32[]{:S(2)}, u32[]{:S(2)}) collective-permute-start(bf16[528,128]{1,0:T(8,128)(2,1)S(1)} %shard_map.87), channel_id=1, source_target_pairs={{0,2},{2,4},{4,6},{6,7},{7,5},{5,3},{3,1},{1,0},{8,10},{10,12},{12... | collective-permute-start | bytes 405512 | tf_op jit(solution)/shard_map/ppermute | solution.py:418
  41.5 7.3 %collective-permute-start.10 = (bf16[528,128]{1,0:T(8,128)(2,1)S(1)}, bf16[528,128]{1,0:T(8,128)(2,1)S(1)}, u32[]{:S(2)}, u32[]{:S(2)}) collective-permute-start(bf16[528,128]{1,0:T(8,128)(2,1)S(1)} %shard_map.73), channel_id=1, source_target_pairs={{0,2},{2,4},{4,6},{6,7},{7,5},{5,3},{3,1},{1,0},{8,10},{10,12},{12... | collective-permute-start | bytes 405512 | tf_op jit(solution)/shard_map/ppermute | solution.py:418
  43.8 6.9 %collective-permute-start.27 = (bf16[528,128]{1,0:T(8,128)(2,1)S(1)}, bf16[528,128]{1,0:T(8,128)(2,1)S(1)}, u32[]{:S(2)}, u32[]{:S(2)}) collective-permute-start(bf16[528,128]{1,0:T(8,128)(2,1)S(1)} %shard_map.84), channel_id=1, source_target_pairs={{2,0},{4,2},{6,4},{7,6},{5,7},{3,5},{1,3},{0,1},{10,8},{12,10},{14... | collective-permute-start | bytes 405512 | tf_op jit(solution)/shard_map/ppermute | solution.py:421
  46.2 6.3 %collective-permute-start.15 = (bf16[528,128]{1,0:T(8,128)(2,1)S(1)}, bf16[528,128]{1,0:T(8,128)(2,1)S(1)}, u32[]{:S(2)}, u32[]{:S(2)}) collective-permute-start(bf16[528,128]{1,0:T(8,128)(2,1)S(1)} %shard_map.77), channel_id=1, source_target_pairs={{2,0},{4,2},{6,4},{7,6},{5,7},{3,5},{1,3},{0,1},{10,8},{12,10},{14... | collective-permute-start | bytes 405512 | tf_op jit(solution)/shard_map/ppermute | solution.py:421
  55.5 6.3 %collective-permute-start.18 = (bf16[272,128]{1,0:T(8,128)(2,1)S(1)}, bf16[272,128]{1,0:T(8,128)(2,1)S(1)}, u32[]{:S(2)}, u32[]{:S(2)}) collective-permute-start(bf16[272,128]{1,0:T(8,128)(2,1)S(1)} %get-tuple-element.46), channel_id=1, source_target_pairs={{0,24},{8,16},{16,8},{24,0},{1,25},{9,17},{17,9},{25,1},{2,26},{10... | collective-permute-start | bytes 208904 | tf_op jit(solution)/shard_map/ppermute | solution.py:405
  56.3 8.8 %collective-permute-start.34 = (bf16[272,128]{1,0:T(8,128)(2,1)S(1)}, bf16[272,128]{1,0:T(8,128)(2,1)S(1)}, u32[]{:S(2)}, u32[]{:S(2)}) collective-permute-start(bf16[272,128]{1,0:T(8,128)(2,1)S(1)} %get-tuple-element.57), channel_id=1, source_target_pairs={{0,8},{8,0},{16,24},{24,16},{1,9},{9,1},{17,25},{25,17},{2,10},{10... | collective-permute-start | bytes 208904 | tf_op jit(solution)/shard_map/ppermute | solution.py:405
  (16 other events, 76.9 us)

commit v14 on v12

--- a/solution.py
+++ b/solution.py
@@ -127,14 +127,17 @@
     queries, (new_ref, out_ref, level_ref) = refs[:-3], refs[-3:]
     step = lax.broadcasted_iota(jnp.int32, (ROWS, STEPS), 0) % STEPS
     usable = lax.broadcasted_iota(jnp.int32, (ROWS, STEPS), 1) <= step
-    for d, query in enumerate(queries):
-        new = new_ref[group ^ d]
-        heads = [new[:, head * HD : (head + 1) * HD] for head in range(2 * KVH)]
-        rows = [query[head * ROWS : (head + 1) * ROWS, :] for head in range(KVH)]
-        [(mixed, level)] = attend([(rows, heads[:KVH], heads[KVH:], usable, 0)])
-        for head, values in enumerate(mixed):
-            out_ref[d, head * ROWS : (head + 1) * ROWS, :] = values
-        level_ref[d] = level
+    for pair in range(0, len(queries), 2):
+        requests = []
+        for d in (pair, pair + 1):
+            new = new_ref[group ^ d]
+            heads = [new[:, head * HD : (head + 1) * HD] for head in range(2 * KVH)]
+            rows = [queries[d][head * ROWS : (head + 1) * ROWS, :] for head in range(KVH)]
+            requests.append((rows, heads[:KVH], heads[KVH:], usable, 0))
+        for d, (mixed, level) in zip((pair, pair + 1), attend(requests)):
+            for head, values in enumerate(mixed):
+                out_ref[d, head * ROWS : (head + 1) * ROWS, :] = values
+            level_ref[d] = level
 
 
 def new_tokens(place, owners, queries, new_kv):
@@ -232,14 +235,12 @@
         code_ref[entry] = code
         order_ref[found] = entry
         found = found + jnp.where((code & 255) > 0, 1, 0)
-    order_ref[found] = order_ref[jnp.maximum(found - 1, 0)]
     tokens = lax.broadcasted_iota(jnp.int32, (ROWS, PAGE), 1)
 
-    @pl.loop(0, (found + 1) >> 1)
-    def _(two):
+    def work(numbers):
         requests, places = [], []
-        for number in range(2):
-            entry = order_ref[2 * two + number]
+        for number in numbers:
+            entry = order_ref[number]
             code = code_ref[entry]
             page, odd = code >> 8, entry & 1
             start = entry * BODY
@@ -252,6 +253,14 @@
             for head, part in enumerate(mixed):
                 out_ref[pl.ds(pl.multiple_of(out + head * ROWS, HALF), ROWS), :] = part.astype(BF16)
             level_ref[entry] = level
+
+    @pl.loop(0, found >> 1)
+    def _(two):
+        work([2 * two, 2 * two + 1])
+
+    @pl.when((found & 1) == 1)
+    def _():
+        work([found - 1])
 
     for pair in range(entries // 2):
         start = pair * PAIR + 2 * BODY

time: 67.8 us -> 67.2 us (level)
  waiting for transfers between devices: 12.5 us -> 10.1 us
  starting transfers between devices: 39.2 us -> 41 us
    ppermute x13, starting transfers between devices: 5.45 us -> 12 us  [up(): return lax.ppermute(array, 'cache', forward)]
    ppermute x13, starting transfers between devices: 23.9 us -> 18.8 us  [down(): return lax.ppermute(array, 'cache', backward)]
    ppermute x13, waiting for transfers between devices: 6.14 us -> 3.52 us  [up(): return lax.ppermute(array, 'cache', forward)]
  transfers between devices with their start and end apart: 36 -> 36, of which waited for: 12 -> 10; matrix products, arithmetic and copies ran while one was open for 1% -> 1% of each run, Pallas kernels for 14% -> 14%
where the time goes in v14:
time: 67.2 us; the launch traced here: 67.1 us
  starting transfers between devices  41 us (61%)
  Pallas kernels  10.7 us (16%)
  waiting for transfers between devices  10.1 us (15%)
  local copies, waits for them, and re-layouts  4.35 us (6%)
  other arithmetic  0.79 us (1%)
    ppermute x13, starting transfers between devices, down(): return lax.ppermute(array, 'cache', backward)  18.8 us
    ppermute x13, starting transfers between devices, up(): return lax.ppermute(array, 'cache', forward)  12 us
    ppermute x6, starting transfers between devices, swap(): lax.ppermute(array, 'grp', [(g, g ^ d) for g in range(groups)])  5.42 us
    pallas_call x9, Pallas kernels, items(): pl.pallas_call(functools.partial(item_kernel, slots, visitors, owners), o...  4.91 us
    ppermute x4, starting transfers between devices, straight(): return lax.ppermute(array, ('grp', 'cache'), pairs)  4.8 us
    ppermute x4, waiting for transfers between devices, straight(): return lax.ppermute(array, ('grp', 'cache'), pairs)  4.69 us
    unnamed x8, local copies, waits for them, and re-layouts  4.33 us
    ppermute x13, waiting for transfers between devices, up(): return lax.ppermute(array, 'cache', forward)  3.52 us
  transfers between devices with their start and end apart: 36, of which 10 were waited for; matrix products, arithmetic and copies ran while one was open for 1% of the time, Pallas kernels for 14%

profile of v14, /device:TPU:0, one launch (start us, length us, event | category | flops | bytes accessed | tf_op | source)
XLA Modules:
  0.0 67.1 jit_solution(13887057318923286778)
XLA Ops:
  1.5 2.6 %collective-permute-start.1 = (bf16[256,128]{1,0:T(8,128)(2,1)S(1)}, bf16[256,128]{1,0:T(8,128)(2,1)S(1)}, u32[]{:S(2)}, u32[]{:S(2)}) collective-permute-start(bf16[256,128]{1,0:T(8,128)(2,1)S(1)} %get-tuple-element.34.refs_2_), channel_id=1, source_target_pairs={{0,16},{8,24},{16,0},{24,8},{1,17},{9,25},{17,1},{25,9},{2,18},{10... | collective-permute-start | bytes 196616 | tf_op jit(solution)/shard_map/ppermute | solution.py:411
  5.0 3.4 %copy-done = bf16[16,128,2048]{2,1,0:T(8,128)(2,1)S(1)} copy-done((bf16[16,128,2048]{2,1,0:T(8,128)(2,1)S(1)}, bf16[16,128,2048]{2,1,0:T(8,128)(2,1)}, u32[]{:S(2)}) %copy-start) | copy-done | bytes 8388632
  8.4 1.8 %collective-permute-start.5 = (bf16[528,128]{1,0:T(8,128)(2,1)S(1)}, bf16[528,128]{1,0:T(8,128)(2,1)S(1)}, u32[]{:S(2)}, u32[]{:S(2)}) collective-permute-start(bf16[528,128]{1,0:T(8,128)(2,1)S(1)} %shard_map.67.refs_1_), channel_id=1, source_target_pairs={{2,0},{4,2},{6,4},{7,6},{5,7},{3,5},{1,3},{0,1},{10,8},{12,10},{14... | collective-permute-start | bytes 405512 | tf_op jit(solution)/shard_map/ppermute | solution.py:427
  10.5 1.8 %collective-permute-start.3 = (bf16[528,128]{1,0:T(8,128)(2,1)S(1)}, bf16[528,128]{1,0:T(8,128)(2,1)S(1)}, u32[]{:S(2)}, u32[]{:S(2)}) collective-permute-start(bf16[528,128]{1,0:T(8,128)(2,1)S(1)} %shard_map.67.refs_1_), channel_id=1, source_target_pairs={{0,2},{2,4},{4,6},{6,7},{7,5},{5,3},{3,1},{1,0},{8,10},{10,12},{12... | collective-permute-start | bytes 405512 | tf_op jit(solution)/shard_map/ppermute | solution.py:424
  14.4 2.2 %collective-permute-start.7 = (bf16[528,128]{1,0:T(8,128)(2,1)S(1)}, bf16[528,128]{1,0:T(8,128)(2,1)S(1)}, u32[]{:S(2)}, u32[]{:S(2)}) collective-permute-start(bf16[528,128]{1,0:T(8,128)(2,1)S(1)} %collective-permute-done.5.refs_1_), channel_id=1, source_target_pairs={{2,0},{4,2},{6,4},{7,6},{5,7},{3,5},{1,3},{0,1},{10,8},{12,10},{14... | collective-permute-start | bytes 405512 | tf_op jit(solution)/shard_map/ppermute | solution.py:427
  16.9 2.4 %collective-permute-done.3.refs_0_ = bf16[528,128]{1,0:T(8,128)(2,1)S(1)} collective-permute-done((bf16[528,128]{1,0:T(8,128)(2,1)S(1)}, bf16[528,128]{1,0:T(8,128)(2,1)S(1)}, u32[]{:S(2)}, u32[]{:S(2)}) %collective-permute-start.3) | collective-permute-done | bytes 135200 | tf_op jit(solution)/shard_map/ppermute | solution.py:424
  19.8 1.6 %collective-permute-start.24 = (bf16[528,128]{1,0:T(8,128)(2,1)S(1)}, bf16[528,128]{1,0:T(8,128)(2,1)S(1)}, u32[]{:S(2)}, u32[]{:S(2)}) collective-permute-start(bf16[528,128]{1,0:T(8,128)(2,1)S(1)} %collective-permute-done.22.refs_1_), channel_id=1, source_target_pairs={{2,0},{4,2},{6,4},{7,6},{5,7},{3,5},{1,3},{0,1},{10,8},{12,10},{14... | collective-permute-start | bytes 405512 | tf_op jit(solution)/shard_map/ppermute | solution.py:427
  21.6 2.3 %collective-permute-start.8 = (bf16[528,128]{1,0:T(8,128)(2,1)S(1)}, bf16[528,128]{1,0:T(8,128)(2,1)S(1)}, u32[]{:S(2)}, u32[]{:S(2)}) collective-permute-start(bf16[528,128]{1,0:T(8,128)(2,1)S(1)} %collective-permute-done.7.refs_1_), channel_id=1, source_target_pairs={{2,0},{4,2},{6,4},{7,6},{5,7},{3,5},{1,3},{0,1},{10,8},{12,10},{14... | collective-permute-start | bytes 405512 | tf_op jit(solution)/shard_map/ppermute | solution.py:427
  25.7 1.6 %collective-permute-start.25 = (bf16[528,128]{1,0:T(8,128)(2,1)S(1)}, bf16[528,128]{1,0:T(8,128)(2,1)S(1)}, u32[]{:S(2)}, u32[]{:S(2)}) collective-permute-start(bf16[528,128]{1,0:T(8,128)(2,1)S(1)} %collective-permute-done.24.refs_1_), channel_id=1, source_target_pairs={{2,0},{4,2},{6,4},{7,6},{5,7},{3,5},{1,3},{0,1},{10,8},{12,10},{14... | collective-permute-start | bytes 405512 | tf_op jit(solution)/shard_map/ppermute | solution.py:427
  28.1 2.0 %collective-permute-start.13 = (bf16[528,128]{1,0:T(8,128)(2,1)S(1)}, bf16[528,128]{1,0:T(8,128)(2,1)S(1)}, u32[]{:S(2)}, u32[]{:S(2)}) collective-permute-start(bf16[528,128]{1,0:T(8,128)(2,1)S(1)} %collective-permute-done.8.refs_1_), channel_id=1, source_target_pairs={{2,0},{4,2},{6,4},{7,6},{5,7},{3,5},{1,3},{0,1},{10,8},{12,10},{14... | collective-permute-start | bytes 405512 | tf_op jit(solution)/shard_map/ppermute | solution.py:427
  33.7 1.2 %collective-permute-start.26 = (bf16[528,128]{1,0:T(8,128)(2,1)S(1)}, bf16[528,128]{1,0:T(8,128)(2,1)S(1)}, u32[]{:S(2)}, u32[]{:S(2)}) collective-permute-start(bf16[528,128]{1,0:T(8,128)(2,1)S(1)} %slice.9), channel_id=1, source_target_pairs={{2,0},{4,2},{6,4},{7,6},{5,7},{3,5},{1,3},{0,1},{10,8},{12,10},{14... | collective-permute-start | bytes 405512 | tf_op jit(solution)/shard_map/ppermute | solution.py:427
  35.6 1.2 %collective-permute-start.14 = (bf16[528,128]{1,0:T(8,128)(2,1)S(1)}, bf16[528,128]{1,0:T(8,128)(2,1)S(1)}, u32[]{:S(2)}, u32[]{:S(2)}) collective-permute-start(bf16[528,128]{1,0:T(8,128)(2,1)S(1)} %shard_map.76), channel_id=1, source_target_pairs={{2,0},{4,2},{6,4},{7,6},{5,7},{3,5},{1,3},{0,1},{10,8},{12,10},{14... | collective-permute-start | bytes 405512 | tf_op jit(solution)/shard_map/ppermute | solution.py:427
  37.0 1.3 %collective-permute-start.30 = (bf16[528,128]{1,0:T(8,128)(2,1)S(1)}, bf16[528,128]{1,0:T(8,128)(2,1)S(1)}, u32[]{:S(2)}, u32[]{:S(2)}) collective-permute-start(bf16[528,128]{1,0:T(8,128)(2,1)S(1)} %shard_map.87), channel_id=1, source_target_pairs={{0,2},{2,4},{4,6},{6,7},{7,5},{5,3},{3,1},{1,0},{8,10},{10,12},{12... | collective-permute-start | bytes 405512 | tf_op jit(solution)/shard_map/ppermute | solution.py:424
  39.6 1.4 %collective-permute-start.27 = (bf16[528,128]{1,0:T(8,128)(2,1)S(1)}, bf16[528,128]{1,0:T(8,128)(2,1)S(1)}, u32[]{:S(2)}, u32[]{:S(2)}) collective-permute-start(bf16[528,128]{1,0:T(8,128)(2,1)S(1)} %shard_map.84), channel_id=1, source_target_pairs={{2,0},{4,2},{6,4},{7,6},{5,7},{3,5},{1,3},{0,1},{10,8},{12,10},{14... | collective-permute-start | bytes 405512 | tf_op jit(solution)/shard_map/ppermute | solution.py:427
  42.4 1.3 %collective-permute-start.15 = (bf16[528,128]{1,0:T(8,128)(2,1)S(1)}, bf16[528,128]{1,0:T(8,128)(2,1)S(1)}, u32[]{:S(2)}, u32[]{:S(2)}) collective-permute-start(bf16[528,128]{1,0:T(8,128)(2,1)S(1)} %shard_map.77), channel_id=1, source_target_pairs={{2,0},{4,2},{6,4},{7,6},{5,7},{3,5},{1,3},{0,1},{10,8},{12,10},{14... | collective-permute-start | bytes 405512 | tf_op jit(solution)/shard_map/ppermute | solution.py:427
  44.0 1.9 %collective-permute-start.31 = (bf16[528,128]{1,0:T(8,128)(2,1)S(1)}, bf16[528,128]{1,0:T(8,128)(2,1)S(1)}, u32[]{:S(2)}, u32[]{:S(2)}) collective-permute-start(bf16[528,128]{1,0:T(8,128)(2,1)S(1)} %shard_map.88), channel_id=1, source_target_pairs={{0,2},{2,4},{4,6},{6,7},{7,5},{5,3},{3,1},{1,0},{8,10},{10,12},{12... | collective-permute-start | bytes 405512 | tf_op jit(solution)/shard_map/ppermute | solution.py:424
  46.5 1.9 %collective-permute-start.11 = (bf16[528,128]{1,0:T(8,128)(2,1)S(1)}, bf16[528,128]{1,0:T(8,128)(2,1)S(1)}, u32[]{:S(2)}, u32[]{:S(2)}) collective-permute-start(bf16[528,128]{1,0:T(8,128)(2,1)S(1)} %shard_map.74), channel_id=1, source_target_pairs={{0,2},{2,4},{4,6},{6,7},{7,5},{5,3},{3,1},{1,0},{8,10},{10,12},{12... | collective-permute-start | bytes 405512 | tf_op jit(solution)/shard_map/ppermute | solution.py:424
  50.1 1.4 %collective-permute-start.16 = (bf16[528,128]{1,0:T(8,128)(2,1)S(1)}, bf16[528,128]{1,0:T(8,128)(2,1)S(1)}, u32[]{:S(2)}, u32[]{:S(2)}) collective-permute-start(bf16[528,128]{1,0:T(8,128)(2,1)S(1)} %shard_map.78), channel_id=1, source_target_pairs={{2,0},{4,2},{6,4},{7,6},{5,7},{3,5},{1,3},{0,1},{10,8},{12,10},{14... | collective-permute-start | bytes 405512 | tf_op jit(solution)/shard_map/ppermute | solution.py:427
  52.8 2.0 %collective-permute-start.12 = (bf16[272,128]{1,0:T(8,128)(2,1)S(1)}, bf16[272,128]{1,0:T(8,128)(2,1)S(1)}, u32[]{:S(2)}, u32[]{:S(2)}) collective-permute-start(bf16[272,128]{1,0:T(8,128)(2,1)S(1)} %get-tuple-element.44), channel_id=1, source_target_pairs={{0,16},{8,24},{16,0},{24,8},{1,17},{9,25},{17,1},{25,9},{2,18},{10... | collective-permute-start | bytes 208904 | tf_op jit(solution)/shard_map/ppermute | solution.py:411
  55.6 2.7 %collective-permute-start.17 = (bf16[272,128]{1,0:T(8,128)(2,1)S(1)}, bf16[272,128]{1,0:T(8,128)(2,1)S(1)}, u32[]{:S(2)}, u32[]{:S(2)}) collective-permute-start(bf16[272,128]{1,0:T(8,128)(2,1)S(1)} %get-tuple-element.45), channel_id=1, source_target_pairs={{2,16},{4,18},{6,20},{7,22},{5,23},{3,21},{1,19},{0,17},{10,24},{1... | collective-permute-start | bytes 208904 | tf_op jit(solution)/shard_map/ppermute | solution.py:452
  58.3 1.1 %collective-permute-start.19 = (bf16[272,128]{1,0:T(8,128)(2,1)S(1)}, bf16[272,128]{1,0:T(8,128)(2,1)S(1)}, u32[]{:S(2)}, u32[]{:S(2)}) collective-permute-start(bf16[272,128]{1,0:T(8,128)(2,1)S(1)} %get-tuple-element.47), channel_id=1, source_target_pairs={{2,24},{4,26},{6,28},{7,30},{5,31},{3,29},{1,27},{0,25},{10,16},{1... | collective-permute-start | bytes 208904 | tf_op jit(solution)/shard_map/ppermute | solution.py:452
  61.2 2.4 %collective-permute-done.19.refs_3_ = bf16[272,128]{1,0:T(8,128)(2,1)S(1)} collective-permute-done((bf16[272,128]{1,0:T(8,128)(2,1)S(1)}, bf16[272,128]{1,0:T(8,128)(2,1)S(1)}, u32[]{:S(2)}, u32[]{:S(2)}) %collective-permute-start.19) | collective-permute-done | bytes 69664 | tf_op jit(solution)/shard_map/ppermute | solution.py:452
  64.8 1.1 %collective-permute-done.35.refs_4_ = bf16[272,128]{1,0:T(8,128)(2,1)S(1)} collective-permute-done((bf16[272,128]{1,0:T(8,128)(2,1)S(1)}, bf16[272,128]{1,0:T(8,128)(2,1)S(1)}, u32[]{:S(2)}, u32[]{:S(2)}) %collective-permute-start.35) | collective-permute-done | bytes 69664 | tf_op jit(solution)/shard_map/ppermute | solution.py:452
  65.9 1.2 %shard_map.91 = bf16[4,4,8192]{2,1,0:T(4,128)(2,1)} custom-call(s32[1]{0:T(128)} %bitcast.place_ref, bf16[2,4,8192]{2,1,0:T(4,128)(2,1)S(1)} %shard_map.80.refs_0_, bf16[272,128]{1,0:T(8,128)(2,1)S(1)} %get-tuple-element.55.refs_1_, bf16[272,128]{1,0:T(8,128)(2,1)S(1)} %collective-permute-done.33.refs_2_, ...), custom_call_target="tpu_custom_call" | custom-call | bytes 655360 | tf_op jit(solution)/shard_map/pallas_call | solution.py:384
  (88 shorter events, 23.1 us)
Async XLA Ops:
  1.5 6.9 %collective-permute-start.1 = (bf16[256,128]{1,0:T(8,128)(2,1)S(1)}, bf16[256,128]{1,0:T(8,128)(2,1)S(1)}, u32[]{:S(2)}, u32[]{:S(2)}) collective-permute-start(bf16[256,128]{1,0:T(8,128)(2,1)S(1)} %get-tuple-element.34.refs_2_), channel_id=1, source_target_pairs={{0,16},{8,24},{16,0},{24,8},{1,17},{9,25},{17,1},{25,9},{2,18},{10... | collective-permute-start | bytes 196616 | tf_op jit(solution)/shard_map/ppermute | solution.py:411
  8.4 5.9 %collective-permute-start.5 = (bf16[528,128]{1,0:T(8,128)(2,1)S(1)}, bf16[528,128]{1,0:T(8,128)(2,1)S(1)}, u32[]{:S(2)}, u32[]{:S(2)}) collective-permute-start(bf16[528,128]{1,0:T(8,128)(2,1)S(1)} %shard_map.67.refs_1_), channel_id=1, source_target_pairs={{2,0},{4,2},{6,4},{7,6},{5,7},{3,5},{1,3},{0,1},{10,8},{12,10},{14... | collective-permute-start | bytes 405512 | tf_op jit(solution)/shard_map/ppermute | solution.py:427
  10.2 6.4 %collective-permute-start.20 = (bf16[528,128]{1,0:T(8,128)(2,1)S(1)}, bf16[528,128]{1,0:T(8,128)(2,1)S(1)}, u32[]{:S(2)}, u32[]{:S(2)}) collective-permute-start(bf16[528,128]{1,0:T(8,128)(2,1)S(1)} %shard_map.65.after_ref.refs_0_), channel_id=1, source_target_pairs={{0,2},{2,4},{4,6},{6,7},{7,5},{5,3},{3,1},{1,0},{8,10},{10,12},{12... | collective-permute-start | bytes 405512 | tf_op jit(solution)/shard_map/ppermute | solution.py:424
  10.5 8.8 %collective-permute-start.3 = (bf16[528,128]{1,0:T(8,128)(2,1)S(1)}, bf16[528,128]{1,0:T(8,128)(2,1)S(1)}, u32[]{:S(2)}, u32[]{:S(2)}) collective-permute-start(bf16[528,128]{1,0:T(8,128)(2,1)S(1)} %shard_map.67.refs_1_), channel_id=1, source_target_pairs={{0,2},{2,4},{4,6},{6,7},{7,5},{5,3},{3,1},{1,0},{8,10},{10,12},{12... | collective-permute-start | bytes 405512 | tf_op jit(solution)/shard_map/ppermute | solution.py:424
  12.3 7.5 %collective-permute-start.22 = (bf16[528,128]{1,0:T(8,128)(2,1)S(1)}, bf16[528,128]{1,0:T(8,128)(2,1)S(1)}, u32[]{:S(2)}, u32[]{:S(2)}) collective-permute-start(bf16[528,128]{1,0:T(8,128)(2,1)S(1)} %shard_map.65.after_ref.refs_0_), channel_id=1, source_target_pairs={{2,0},{4,2},{6,4},{7,6},{5,7},{3,5},{1,3},{0,1},{10,8},{12,10},{14... | collective-permute-start | bytes 405512 | tf_op jit(solution)/shard_map/ppermute | solution.py:427
  14.4 7.2 %collective-permute-start.7 = (bf16[528,128]{1,0:T(8,128)(2,1)S(1)}, bf16[528,128]{1,0:T(8,128)(2,1)S(1)}, u32[]{:S(2)}, u32[]{:S(2)}) collective-permute-start(bf16[528,128]{1,0:T(8,128)(2,1)S(1)} %collective-permute-done.5.refs_1_), channel_id=1, source_target_pairs={{2,0},{4,2},{6,4},{7,6},{5,7},{3,5},{1,3},{0,1},{10,8},{12,10},{14... | collective-permute-start | bytes 405512 | tf_op jit(solution)/shard_map/ppermute | solution.py:427
  16.6 8.0 %collective-permute-start.21 = (bf16[528,128]{1,0:T(8,128)(2,1)S(1)}, bf16[528,128]{1,0:T(8,128)(2,1)S(1)}, u32[]{:S(2)}, u32[]{:S(2)}) collective-permute-start(bf16[528,128]{1,0:T(8,128)(2,1)S(1)} %collective-permute-done.20.refs_0_), channel_id=1, source_target_pairs={{0,2},{2,4},{4,6},{6,7},{7,5},{5,3},{3,1},{1,0},{8,10},{10,12},{12... | collective-permute-start | bytes 405512 | tf_op jit(solution)/shard_map/ppermute | solution.py:424
  21.6 6.5 %collective-permute-start.8 = (bf16[528,128]{1,0:T(8,128)(2,1)S(1)}, bf16[528,128]{1,0:T(8,128)(2,1)S(1)}, u32[]{:S(2)}, u32[]{:S(2)}) collective-permute-start(bf16[528,128]{1,0:T(8,128)(2,1)S(1)} %collective-permute-done.7.refs_1_), channel_id=1, source_target_pairs={{2,0},{4,2},{6,4},{7,6},{5,7},{3,5},{1,3},{0,1},{10,8},{12,10},{14... | collective-permute-start | bytes 405512 | tf_op jit(solution)/shard_map/ppermute | solution.py:427
  24.6 6.9 %collective-permute-start.6 = (bf16[528,128]{1,0:T(8,128)(2,1)S(1)}, bf16[528,128]{1,0:T(8,128)(2,1)S(1)}, u32[]{:S(2)}, u32[]{:S(2)}) collective-permute-start(bf16[528,128]{1,0:T(8,128)(2,1)S(1)} %collective-permute-done.4.refs_0_), channel_id=1, source_target_pairs={{0,2},{2,4},{4,6},{6,7},{7,5},{5,3},{3,1},{1,0},{8,10},{10,12},{12... | collective-permute-start | bytes 405512 | tf_op jit(solution)/shard_map/ppermute | solution.py:424
  25.7 7.1 %collective-permute-start.25 = (bf16[528,128]{1,0:T(8,128)(2,1)S(1)}, bf16[528,128]{1,0:T(8,128)(2,1)S(1)}, u32[]{:S(2)}, u32[]{:S(2)}) collective-permute-start(bf16[528,128]{1,0:T(8,128)(2,1)S(1)} %collective-permute-done.24.refs_1_), channel_id=1, source_target_pairs={{2,0},{4,2},{6,4},{7,6},{5,7},{3,5},{1,3},{0,1},{10,8},{12,10},{14... | collective-permute-start | bytes 405512 | tf_op jit(solution)/shard_map/ppermute | solution.py:427
  28.1 6.8 %collective-permute-start.13 = (bf16[528,128]{1,0:T(8,128)(2,1)S(1)}, bf16[528,128]{1,0:T(8,128)(2,1)S(1)}, u32[]{:S(2)}, u32[]{:S(2)}) collective-permute-start(bf16[528,128]{1,0:T(8,128)(2,1)S(1)} %collective-permute-done.8.refs_1_), channel_id=1, source_target_pairs={{2,0},{4,2},{6,4},{7,6},{5,7},{3,5},{1,3},{0,1},{10,8},{12,10},{14... | collective-permute-start | bytes 405512 | tf_op jit(solution)/shard_map/ppermute | solution.py:427
  30.3 6.6 %collective-permute-start.29 = (bf16[528,128]{1,0:T(8,128)(2,1)S(1)}, bf16[528,128]{1,0:T(8,128)(2,1)S(1)}, u32[]{:S(2)}, u32[]{:S(2)}) collective-permute-start(bf16[528,128]{1,0:T(8,128)(2,1)S(1)} %collective-permute-done.23.refs_0_), channel_id=1, source_target_pairs={{0,2},{2,4},{4,6},{6,7},{7,5},{5,3},{3,1},{1,0},{8,10},{10,12},{12... | collective-permute-start | bytes 405512 | tf_op jit(solution)/shard_map/ppermute | solution.py:424
  31.8 6.6 %collective-permute-start.9 = (bf16[528,128]{1,0:T(8,128)(2,1)S(1)}, bf16[528,128]{1,0:T(8,128)(2,1)S(1)}, u32[]{:S(2)}, u32[]{:S(2)}) collective-permute-start(bf16[528,128]{1,0:T(8,128)(2,1)S(1)} %slice.8), channel_id=1, source_target_pairs={{0,2},{2,4},{4,6},{6,7},{7,5},{5,3},{3,1},{1,0},{8,10},{10,12},{12... | collective-permute-start | bytes 405512 | tf_op jit(solution)/shard_map/ppermute | solution.py:424
  35.6 6.5 %collective-permute-start.14 = (bf16[528,128]{1,0:T(8,128)(2,1)S(1)}, bf16[528,128]{1,0:T(8,128)(2,1)S(1)}, u32[]{:S(2)}, u32[]{:S(2)}) collective-permute-start(bf16[528,128]{1,0:T(8,128)(2,1)S(1)} %shard_map.76), channel_id=1, source_target_pairs={{2,0},{4,2},{6,4},{7,6},{5,7},{3,5},{1,3},{0,1},{10,8},{12,10},{14... | collective-permute-start | bytes 405512 | tf_op jit(solution)/shard_map/ppermute | solution.py:427
  37.0 6.7 %collective-permute-start.30 = (bf16[528,128]{1,0:T(8,128)(2,1)S(1)}, bf16[528,128]{1,0:T(8,128)(2,1)S(1)}, u32[]{:S(2)}, u32[]{:S(2)}) collective-permute-start(bf16[528,128]{1,0:T(8,128)(2,1)S(1)} %shard_map.87), channel_id=1, source_target_pairs={{0,2},{2,4},{4,6},{6,7},{7,5},{5,3},{3,1},{1,0},{8,10},{10,12},{12... | collective-permute-start | bytes 405512 | tf_op jit(solution)/shard_map/ppermute | solution.py:424
  38.6 7.6 %collective-permute-start.10 = (bf16[528,128]{1,0:T(8,128)(2,1)S(1)}, bf16[528,128]{1,0:T(8,128)(2,1)S(1)}, u32[]{:S(2)}, u32[]{:S(2)}) collective-permute-start(bf16[528,128]{1,0:T(8,128)(2,1)S(1)} %shard_map.73), channel_id=1, source_target_pairs={{0,2},{2,4},{4,6},{6,7},{7,5},{5,3},{3,1},{1,0},{8,10},{10,12},{12... | collective-permute-start | bytes 405512 | tf_op jit(solution)/shard_map/ppermute | solution.py:424
  39.6 8.8 %collective-permute-start.27 = (bf16[528,128]{1,0:T(8,128)(2,1)S(1)}, bf16[528,128]{1,0:T(8,128)(2,1)S(1)}, u32[]{:S(2)}, u32[]{:S(2)}) collective-permute-start(bf16[528,128]{1,0:T(8,128)(2,1)S(1)} %shard_map.84), channel_id=1, source_target_pairs={{2,0},{4,2},{6,4},{7,6},{5,7},{3,5},{1,3},{0,1},{10,8},{12,10},{14... | collective-permute-start | bytes 405512 | tf_op jit(solution)/shard_map/ppermute | solution.py:427
  42.4 7.4 %collective-permute-start.15 = (bf16[528,128]{1,0:T(8,128)(2,1)S(1)}, bf16[528,128]{1,0:T(8,128)(2,1)S(1)}, u32[]{:S(2)}, u32[]{:S(2)}) collective-permute-start(bf16[528,128]{1,0:T(8,128)(2,1)S(1)} %shard_map.77), channel_id=1, source_target_pairs={{2,0},{4,2},{6,4},{7,6},{5,7},{3,5},{1,3},{0,1},{10,8},{12,10},{14... | collective-permute-start | bytes 405512 | tf_op jit(solution)/shard_map/ppermute | solution.py:427
  44.0 7.5 %collective-permute-start.31 = (bf16[528,128]{1,0:T(8,128)(2,1)S(1)}, bf16[528,128]{1,0:T(8,128)(2,1)S(1)}, u32[]{:S(2)}, u32[]{:S(2)}) collective-permute-start(bf16[528,128]{1,0:T(8,128)(2,1)S(1)} %shard_map.88), channel_id=1, source_target_pairs={{0,2},{2,4},{4,6},{6,7},{7,5},{5,3},{3,1},{1,0},{8,10},{10,12},{12... | collective-permute-start | bytes 405512 | tf_op jit(solution)/shard_map/ppermute | solution.py:424
  46.5 5.9 %collective-permute-start.11 = (bf16[528,128]{1,0:T(8,128)(2,1)S(1)}, bf16[528,128]{1,0:T(8,128)(2,1)S(1)}, u32[]{:S(2)}, u32[]{:S(2)}) collective-permute-start(bf16[528,128]{1,0:T(8,128)(2,1)S(1)} %shard_map.74), channel_id=1, source_target_pairs={{0,2},{2,4},{4,6},{6,7},{7,5},{5,3},{3,1},{1,0},{8,10},{10,12},{12... | collective-permute-start | bytes 405512 | tf_op jit(solution)/shard_map/ppermute | solution.py:424
  48.7 6.0 %collective-permute-start.28 = (bf16[528,128]{1,0:T(8,128)(2,1)S(1)}, bf16[528,128]{1,0:T(8,128)(2,1)S(1)}, u32[]{:S(2)}, u32[]{:S(2)}) collective-permute-start(bf16[528,128]{1,0:T(8,128)(2,1)S(1)} %shard_map.85), channel_id=1, source_target_pairs={{2,0},{4,2},{6,4},{7,6},{5,7},{3,5},{1,3},{0,1},{10,8},{12,10},{14... | collective-permute-start | bytes 405512 | tf_op jit(solution)/shard_map/ppermute | solution.py:427
  51.8 6.5 %collective-permute-start.32 = (bf16[528,128]{1,0:T(8,128)(2,1)S(1)}, bf16[528,128]{1,0:T(8,128)(2,1)S(1)}, u32[]{:S(2)}, u32[]{:S(2)}) collective-permute-start(bf16[528,128]{1,0:T(8,128)(2,1)S(1)} %shard_map.89), channel_id=1, source_target_pairs={{0,2},{2,4},{4,6},{6,7},{7,5},{5,3},{3,1},{1,0},{8,10},{10,12},{12... | collective-permute-start | bytes 405512 | tf_op jit(solution)/shard_map/ppermute | solution.py:424
  52.8 6.9 %collective-permute-start.12 = (bf16[272,128]{1,0:T(8,128)(2,1)S(1)}, bf16[272,128]{1,0:T(8,128)(2,1)S(1)}, u32[]{:S(2)}, u32[]{:S(2)}) collective-permute-start(bf16[272,128]{1,0:T(8,128)(2,1)S(1)} %get-tuple-element.44), channel_id=1, source_target_pairs={{0,16},{8,24},{16,0},{24,8},{1,17},{9,25},{17,1},{25,9},{2,18},{10... | collective-permute-start | bytes 208904 | tf_op jit(solution)/shard_map/ppermute | solution.py:411
  55.1 9.1 %collective-permute-start.34 = (bf16[272,128]{1,0:T(8,128)(2,1)S(1)}, bf16[272,128]{1,0:T(8,128)(2,1)S(1)}, u32[]{:S(2)}, u32[]{:S(2)}) collective-permute-start(bf16[272,128]{1,0:T(8,128)(2,1)S(1)} %get-tuple-element.57), channel_id=1, source_target_pairs={{0,8},{8,0},{16,24},{24,16},{1,9},{9,1},{17,25},{25,17},{2,10},{10... | collective-permute-start | bytes 208904 | tf_op jit(solution)/shard_map/ppermute | solution.py:411
  (16 other events, 76.7 us)

commit v15 on v14

--- a/solution.py
+++ b/solution.py
@@ -254,11 +254,17 @@
                 out_ref[pl.ds(pl.multiple_of(out + head * ROWS, HALF), ROWS), :] = part.astype(BF16)
             level_ref[entry] = level
 
-    @pl.loop(0, found >> 1)
+    three = ((found & 1) == 1) & (found > 1)
+
+    @pl.loop(0, (found - jnp.where(three, 3, 0)) >> 1)
     def _(two):
         work([2 * two, 2 * two + 1])
 
-    @pl.when((found & 1) == 1)
+    @pl.when(three)
+    def _():
+        work([found - 3, found - 2, found - 1])
+
+    @pl.when(found == 1)
     def _():
         work([found - 1])
 

time: 67.2 us -> 67.6 us (level)
  starting transfers between devices: 41 us -> 40 us
  waiting for transfers between devices: 10.1 us -> 10.8 us
    ppermute x13, starting transfers between devices: 12 us -> 9.17 us  [up(): return lax.ppermute(array, 'cache', forward)]
    ppermute x13, starting transfers between devices: 18.8 us -> 20.9 us  [down(): return lax.ppermute(array, 'cache', backward)]
    ppermute x13, waiting for transfers between devices: 3.52 us -> 5 us  [up(): return lax.ppermute(array, 'cache', forward)]
    ppermute x13, waiting for transfers between devices: 1.86 us -> 0.69 us  [down(): return lax.ppermute(array, 'cache', backward)]
  transfers between devices with their start and end apart: 36 -> 36, of which waited for: 10 -> 10; matrix products, arithmetic and copies ran while one was open for 1% -> 1% of each run, Pallas kernels for 14% -> 15%
where the time goes in v15:
time: 67.6 us; the launch traced here: 67.4 us
  starting transfers between devices  40 us (59%)
  Pallas kernels  11.3 us (17%)
  waiting for transfers between devices  10.8 us (16%)
  local copies, waits for them, and re-layouts  4.36 us (6%)
  other arithmetic  0.79 us (1%)
    ppermute x13, starting transfers between devices, down(): return lax.ppermute(array, 'cache', backward)  20.9 us
    ppermute x13, starting transfers between devices, up(): return lax.ppermute(array, 'cache', forward)  9.17 us
    pallas_call x9, Pallas kernels, items(): pl.pallas_call(functools.partial(item_kernel, slots, visitors, owners), o...  5.52 us
    ppermute x6, starting transfers between devices, swap(): lax.ppermute(array, 'grp', [(g, g ^ d) for g in range(groups)])  5.42 us
    ppermute x4, waiting for transfers between devices, straight(): return lax.ppermute(array, ('grp', 'cache'), pairs)  5.07 us
    ppermute x13, waiting for transfers between devices, up(): return lax.ppermute(array, 'cache', forward)  5 us
    ppermute x4, starting transfers between devices, straight(): return lax.ppermute(array, ('grp', 'cache'), pairs)  4.48 us
    unnamed x8, local copies, waits for them, and re-layouts  4.33 us
  transfers between devices with their start and end apart: 36, of which 10 were waited for; matrix products, arithmetic and copies ran while one was open for 1% of the time, Pallas kernels for 15%

profile of v15, /device:TPU:0, one launch (start us, length us, event | category | flops | bytes accessed | tf_op | source)
XLA Modules:
  0.0 67.4 jit_solution(16863238414699912501)
XLA Ops:
  1.5 2.6 %collective-permute-start.1 = (bf16[256,128]{1,0:T(8,128)(2,1)S(1)}, bf16[256,128]{1,0:T(8,128)(2,1)S(1)}, u32[]{:S(2)}, u32[]{:S(2)}) collective-permute-start(bf16[256,128]{1,0:T(8,128)(2,1)S(1)} %get-tuple-element.34.refs_2_), channel_id=1, source_target_pairs={{0,16},{8,24},{16,0},{24,8},{1,17},{9,25},{17,1},{25,9},{2,18},{10... | collective-permute-start | bytes 196616 | tf_op jit(solution)/shard_map/ppermute | solution.py:417
  5.0 3.4 %copy-done = bf16[16,128,2048]{2,1,0:T(8,128)(2,1)S(1)} copy-done((bf16[16,128,2048]{2,1,0:T(8,128)(2,1)S(1)}, bf16[16,128,2048]{2,1,0:T(8,128)(2,1)}, u32[]{:S(2)}) %copy-start) | copy-done | bytes 8388632
  8.4 1.8 %collective-permute-start.5 = (bf16[528,128]{1,0:T(8,128)(2,1)S(1)}, bf16[528,128]{1,0:T(8,128)(2,1)S(1)}, u32[]{:S(2)}, u32[]{:S(2)}) collective-permute-start(bf16[528,128]{1,0:T(8,128)(2,1)S(1)} %shard_map.67.refs_1_), channel_id=1, source_target_pairs={{2,0},{4,2},{6,4},{7,6},{5,7},{3,5},{1,3},{0,1},{10,8},{12,10},{14... | collective-permute-start | bytes 405512 | tf_op jit(solution)/shard_map/ppermute | solution.py:433
  10.5 1.8 %collective-permute-start.3 = (bf16[528,128]{1,0:T(8,128)(2,1)S(1)}, bf16[528,128]{1,0:T(8,128)(2,1)S(1)}, u32[]{:S(2)}, u32[]{:S(2)}) collective-permute-start(bf16[528,128]{1,0:T(8,128)(2,1)S(1)} %shard_map.67.refs_1_), channel_id=1, source_target_pairs={{0,2},{2,4},{4,6},{6,7},{7,5},{5,3},{3,1},{1,0},{8,10},{10,12},{12... | collective-permute-start | bytes 405512 | tf_op jit(solution)/shard_map/ppermute | solution.py:430
  14.4 2.2 %collective-permute-start.7 = (bf16[528,128]{1,0:T(8,128)(2,1)S(1)}, bf16[528,128]{1,0:T(8,128)(2,1)S(1)}, u32[]{:S(2)}, u32[]{:S(2)}) collective-permute-start(bf16[528,128]{1,0:T(8,128)(2,1)S(1)} %collective-permute-done.5.refs_1_), channel_id=1, source_target_pairs={{2,0},{4,2},{6,4},{7,6},{5,7},{3,5},{1,3},{0,1},{10,8},{12,10},{14... | collective-permute-start | bytes 405512 | tf_op jit(solution)/shard_map/ppermute | solution.py:433
  16.9 2.4 %collective-permute-done.3.refs_0_ = bf16[528,128]{1,0:T(8,128)(2,1)S(1)} collective-permute-done((bf16[528,128]{1,0:T(8,128)(2,1)S(1)}, bf16[528,128]{1,0:T(8,128)(2,1)S(1)}, u32[]{:S(2)}, u32[]{:S(2)}) %collective-permute-start.3) | collective-permute-done | bytes 135200 | tf_op jit(solution)/shard_map/ppermute | solution.py:430
  19.8 1.6 %collective-permute-start.24 = (bf16[528,128]{1,0:T(8,128)(2,1)S(1)}, bf16[528,128]{1,0:T(8,128)(2,1)S(1)}, u32[]{:S(2)}, u32[]{:S(2)}) collective-permute-start(bf16[528,128]{1,0:T(8,128)(2,1)S(1)} %collective-permute-done.22.refs_1_), channel_id=1, source_target_pairs={{2,0},{4,2},{6,4},{7,6},{5,7},{3,5},{1,3},{0,1},{10,8},{12,10},{14... | collective-permute-start | bytes 405512 | tf_op jit(solution)/shard_map/ppermute | solution.py:433
  22.1 1.1 %collective-permute-start.8 = (bf16[528,128]{1,0:T(8,128)(2,1)S(1)}, bf16[528,128]{1,0:T(8,128)(2,1)S(1)}, u32[]{:S(2)}, u32[]{:S(2)}) collective-permute-start(bf16[528,128]{1,0:T(8,128)(2,1)S(1)} %collective-permute-done.7.refs_1_), channel_id=1, source_target_pairs={{2,0},{4,2},{6,4},{7,6},{5,7},{3,5},{1,3},{0,1},{10,8},{12,10},{14... | collective-permute-start | bytes 405512 | tf_op jit(solution)/shard_map/ppermute | solution.py:433
  25.7 1.5 %collective-permute-start.25 = (bf16[528,128]{1,0:T(8,128)(2,1)S(1)}, bf16[528,128]{1,0:T(8,128)(2,1)S(1)}, u32[]{:S(2)}, u32[]{:S(2)}) collective-permute-start(bf16[528,128]{1,0:T(8,128)(2,1)S(1)} %collective-permute-done.24.refs_1_), channel_id=1, source_target_pairs={{2,0},{4,2},{6,4},{7,6},{5,7},{3,5},{1,3},{0,1},{10,8},{12,10},{14... | collective-permute-start | bytes 405512 | tf_op jit(solution)/shard_map/ppermute | solution.py:433
  28.3 1.2 %collective-permute-start.13 = (bf16[528,128]{1,0:T(8,128)(2,1)S(1)}, bf16[528,128]{1,0:T(8,128)(2,1)S(1)}, u32[]{:S(2)}, u32[]{:S(2)}) collective-permute-start(bf16[528,128]{1,0:T(8,128)(2,1)S(1)} %collective-permute-done.8.refs_1_), channel_id=1, source_target_pairs={{2,0},{4,2},{6,4},{7,6},{5,7},{3,5},{1,3},{0,1},{10,8},{12,10},{14... | collective-permute-start | bytes 405512 | tf_op jit(solution)/shard_map/ppermute | solution.py:433
  29.7 1.5 %collective-permute-start.29 = (bf16[528,128]{1,0:T(8,128)(2,1)S(1)}, bf16[528,128]{1,0:T(8,128)(2,1)S(1)}, u32[]{:S(2)}, u32[]{:S(2)}) collective-permute-start(bf16[528,128]{1,0:T(8,128)(2,1)S(1)} %collective-permute-done.23.refs_0_), channel_id=1, source_target_pairs={{0,2},{2,4},{4,6},{6,7},{7,5},{5,3},{3,1},{1,0},{8,10},{10,12},{12... | collective-permute-start | bytes 405512 | tf_op jit(solution)/shard_map/ppermute | solution.py:430
  33.4 1.7 %collective-permute-start.26 = (bf16[528,128]{1,0:T(8,128)(2,1)S(1)}, bf16[528,128]{1,0:T(8,128)(2,1)S(1)}, u32[]{:S(2)}, u32[]{:S(2)}) collective-permute-start(bf16[528,128]{1,0:T(8,128)(2,1)S(1)} %slice.9), channel_id=1, source_target_pairs={{2,0},{4,2},{6,4},{7,6},{5,7},{3,5},{1,3},{0,1},{10,8},{12,10},{14... | collective-permute-start | bytes 405512 | tf_op jit(solution)/shard_map/ppermute | solution.py:433
  35.3 2.1 %collective-permute-start.14 = (bf16[528,128]{1,0:T(8,128)(2,1)S(1)}, bf16[528,128]{1,0:T(8,128)(2,1)S(1)}, u32[]{:S(2)}, u32[]{:S(2)}) collective-permute-start(bf16[528,128]{1,0:T(8,128)(2,1)S(1)} %shard_map.76), channel_id=1, source_target_pairs={{2,0},{4,2},{6,4},{7,6},{5,7},{3,5},{1,3},{0,1},{10,8},{12,10},{14... | collective-permute-start | bytes 405512 | tf_op jit(solution)/shard_map/ppermute | solution.py:433
  38.5 1.3 %collective-permute-start.10 = (bf16[528,128]{1,0:T(8,128)(2,1)S(1)}, bf16[528,128]{1,0:T(8,128)(2,1)S(1)}, u32[]{:S(2)}, u32[]{:S(2)}) collective-permute-start(bf16[528,128]{1,0:T(8,128)(2,1)S(1)} %shard_map.73), channel_id=1, source_target_pairs={{0,2},{2,4},{4,6},{6,7},{7,5},{5,3},{3,1},{1,0},{8,10},{10,12},{12... | collective-permute-start | bytes 405512 | tf_op jit(solution)/shard_map/ppermute | solution.py:430
  40.1 1.5 %collective-permute-start.27 = (bf16[528,128]{1,0:T(8,128)(2,1)S(1)}, bf16[528,128]{1,0:T(8,128)(2,1)S(1)}, u32[]{:S(2)}, u32[]{:S(2)}) collective-permute-start(bf16[528,128]{1,0:T(8,128)(2,1)S(1)} %shard_map.84), channel_id=1, source_target_pairs={{2,0},{4,2},{6,4},{7,6},{5,7},{3,5},{1,3},{0,1},{10,8},{12,10},{14... | collective-permute-start | bytes 405512 | tf_op jit(solution)/shard_map/ppermute | solution.py:433
  42.0 2.5 %collective-permute-start.15 = (bf16[528,128]{1,0:T(8,128)(2,1)S(1)}, bf16[528,128]{1,0:T(8,128)(2,1)S(1)}, u32[]{:S(2)}, u32[]{:S(2)}) collective-permute-start(bf16[528,128]{1,0:T(8,128)(2,1)S(1)} %shard_map.77), channel_id=1, source_target_pairs={{2,0},{4,2},{6,4},{7,6},{5,7},{3,5},{1,3},{0,1},{10,8},{12,10},{14... | collective-permute-start | bytes 405512 | tf_op jit(solution)/shard_map/ppermute | solution.py:433
  45.0 2.4 %collective-permute-done.10.arrived_ref = bf16[528,128]{1,0:T(8,128)(2,1)S(1)} collective-permute-done((bf16[528,128]{1,0:T(8,128)(2,1)S(1)}, bf16[528,128]{1,0:T(8,128)(2,1)S(1)}, u32[]{:S(2)}, u32[]{:S(2)}) %collective-permute-start.10) | collective-permute-done | bytes 135200 | tf_op jit(solution)/shard_map/ppermute | solution.py:430
  48.1 2.0 %collective-permute-start.28 = (bf16[528,128]{1,0:T(8,128)(2,1)S(1)}, bf16[528,128]{1,0:T(8,128)(2,1)S(1)}, u32[]{:S(2)}, u32[]{:S(2)}) collective-permute-start(bf16[528,128]{1,0:T(8,128)(2,1)S(1)} %shard_map.85), channel_id=1, source_target_pairs={{2,0},{4,2},{6,4},{7,6},{5,7},{3,5},{1,3},{0,1},{10,8},{12,10},{14... | collective-permute-start | bytes 405512 | tf_op jit(solution)/shard_map/ppermute | solution.py:433
  50.3 1.6 %collective-permute-start.16 = (bf16[528,128]{1,0:T(8,128)(2,1)S(1)}, bf16[528,128]{1,0:T(8,128)(2,1)S(1)}, u32[]{:S(2)}, u32[]{:S(2)}) collective-permute-start(bf16[528,128]{1,0:T(8,128)(2,1)S(1)} %shard_map.78), channel_id=1, source_target_pairs={{2,0},{4,2},{6,4},{7,6},{5,7},{3,5},{1,3},{0,1},{10,8},{12,10},{14... | collective-permute-start | bytes 405512 | tf_op jit(solution)/shard_map/ppermute | solution.py:433
  53.0 1.5 %collective-permute-start.12 = (bf16[272,128]{1,0:T(8,128)(2,1)S(1)}, bf16[272,128]{1,0:T(8,128)(2,1)S(1)}, u32[]{:S(2)}, u32[]{:S(2)}) collective-permute-start(bf16[272,128]{1,0:T(8,128)(2,1)S(1)} %get-tuple-element.44), channel_id=1, source_target_pairs={{0,16},{8,24},{16,0},{24,8},{1,17},{9,25},{17,1},{25,9},{2,18},{10... | collective-permute-start | bytes 208904 | tf_op jit(solution)/shard_map/ppermute | solution.py:417
  55.9 2.7 %collective-permute-start.17 = (bf16[272,128]{1,0:T(8,128)(2,1)S(1)}, bf16[272,128]{1,0:T(8,128)(2,1)S(1)}, u32[]{:S(2)}, u32[]{:S(2)}) collective-permute-start(bf16[272,128]{1,0:T(8,128)(2,1)S(1)} %get-tuple-element.45), channel_id=1, source_target_pairs={{2,16},{4,18},{6,20},{7,22},{5,23},{3,21},{1,19},{0,17},{10,24},{1... | collective-permute-start | bytes 208904 | tf_op jit(solution)/shard_map/ppermute | solution.py:458
  58.6 1.2 %collective-permute-start.19 = (bf16[272,128]{1,0:T(8,128)(2,1)S(1)}, bf16[272,128]{1,0:T(8,128)(2,1)S(1)}, u32[]{:S(2)}, u32[]{:S(2)}) collective-permute-start(bf16[272,128]{1,0:T(8,128)(2,1)S(1)} %get-tuple-element.47), channel_id=1, source_target_pairs={{2,24},{4,26},{6,28},{7,30},{5,31},{3,29},{1,27},{0,25},{10,16},{1... | collective-permute-start | bytes 208904 | tf_op jit(solution)/shard_map/ppermute | solution.py:458
  61.1 2.8 %collective-permute-done.19.refs_3_ = bf16[272,128]{1,0:T(8,128)(2,1)S(1)} collective-permute-done((bf16[272,128]{1,0:T(8,128)(2,1)S(1)}, bf16[272,128]{1,0:T(8,128)(2,1)S(1)}, u32[]{:S(2)}, u32[]{:S(2)}) %collective-permute-start.19) | collective-permute-done | bytes 69664 | tf_op jit(solution)/shard_map/ppermute | solution.py:458
  66.2 1.2 %shard_map.91 = bf16[4,4,8192]{2,1,0:T(4,128)(2,1)} custom-call(s32[1]{0:T(128)} %bitcast.place_ref, bf16[2,4,8192]{2,1,0:T(4,128)(2,1)S(1)} %shard_map.80.refs_0_, bf16[272,128]{1,0:T(8,128)(2,1)S(1)} %get-tuple-element.55.refs_1_, bf16[272,128]{1,0:T(8,128)(2,1)S(1)} %collective-permute-done.33.refs_2_, ...), custom_call_target="tpu_custom_call" | custom-call | bytes 655360 | tf_op jit(solution)/shard_map/pallas_call | solution.py:390
  (88 shorter events, 21.9 us)
Async XLA Ops:
  1.5 6.9 %collective-permute-start.1 = (bf16[256,128]{1,0:T(8,128)(2,1)S(1)}, bf16[256,128]{1,0:T(8,128)(2,1)S(1)}, u32[]{:S(2)}, u32[]{:S(2)}) collective-permute-start(bf16[256,128]{1,0:T(8,128)(2,1)S(1)} %get-tuple-element.34.refs_2_), channel_id=1, source_target_pairs={{0,16},{8,24},{16,0},{24,8},{1,17},{9,25},{17,1},{25,9},{2,18},{10... | collective-permute-start | bytes 196616 | tf_op jit(solution)/shard_map/ppermute | solution.py:417
  10.2 6.4 %collective-permute-start.20 = (bf16[528,128]{1,0:T(8,128)(2,1)S(1)}, bf16[528,128]{1,0:T(8,128)(2,1)S(1)}, u32[]{:S(2)}, u32[]{:S(2)}) collective-permute-start(bf16[528,128]{1,0:T(8,128)(2,1)S(1)} %shard_map.65.after_ref.refs_0_), channel_id=1, source_target_pairs={{0,2},{2,4},{4,6},{6,7},{7,5},{5,3},{3,1},{1,0},{8,10},{10,12},{12... | collective-permute-start | bytes 405512 | tf_op jit(solution)/shard_map/ppermute | solution.py:430
  10.5 8.8 %collective-permute-start.3 = (bf16[528,128]{1,0:T(8,128)(2,1)S(1)}, bf16[528,128]{1,0:T(8,128)(2,1)S(1)}, u32[]{:S(2)}, u32[]{:S(2)}) collective-permute-start(bf16[528,128]{1,0:T(8,128)(2,1)S(1)} %shard_map.67.refs_1_), channel_id=1, source_target_pairs={{0,2},{2,4},{4,6},{6,7},{7,5},{5,3},{3,1},{1,0},{8,10},{10,12},{12... | collective-permute-start | bytes 405512 | tf_op jit(solution)/shard_map/ppermute | solution.py:430
  12.3 7.5 %collective-permute-start.22 = (bf16[528,128]{1,0:T(8,128)(2,1)S(1)}, bf16[528,128]{1,0:T(8,128)(2,1)S(1)}, u32[]{:S(2)}, u32[]{:S(2)}) collective-permute-start(bf16[528,128]{1,0:T(8,128)(2,1)S(1)} %shard_map.65.after_ref.refs_0_), channel_id=1, source_target_pairs={{2,0},{4,2},{6,4},{7,6},{5,7},{3,5},{1,3},{0,1},{10,8},{12,10},{14... | collective-permute-start | bytes 405512 | tf_op jit(solution)/shard_map/ppermute | solution.py:433
  14.4 7.7 %collective-permute-start.7 = (bf16[528,128]{1,0:T(8,128)(2,1)S(1)}, bf16[528,128]{1,0:T(8,128)(2,1)S(1)}, u32[]{:S(2)}, u32[]{:S(2)}) collective-permute-start(bf16[528,128]{1,0:T(8,128)(2,1)S(1)} %collective-permute-done.5.refs_1_), channel_id=1, source_target_pairs={{2,0},{4,2},{6,4},{7,6},{5,7},{3,5},{1,3},{0,1},{10,8},{12,10},{14... | collective-permute-start | bytes 405512 | tf_op jit(solution)/shard_map/ppermute | solution.py:433
  16.6 7.3 %collective-permute-start.21 = (bf16[528,128]{1,0:T(8,128)(2,1)S(1)}, bf16[528,128]{1,0:T(8,128)(2,1)S(1)}, u32[]{:S(2)}, u32[]{:S(2)}) collective-permute-start(bf16[528,128]{1,0:T(8,128)(2,1)S(1)} %collective-permute-done.20.refs_0_), channel_id=1, source_target_pairs={{0,2},{2,4},{4,6},{6,7},{7,5},{5,3},{3,1},{1,0},{8,10},{10,12},{12... | collective-permute-start | bytes 405512 | tf_op jit(solution)/shard_map/ppermute | solution.py:430
  22.1 6.2 %collective-permute-start.8 = (bf16[528,128]{1,0:T(8,128)(2,1)S(1)}, bf16[528,128]{1,0:T(8,128)(2,1)S(1)}, u32[]{:S(2)}, u32[]{:S(2)}) collective-permute-start(bf16[528,128]{1,0:T(8,128)(2,1)S(1)} %collective-permute-done.7.refs_1_), channel_id=1, source_target_pairs={{2,0},{4,2},{6,4},{7,6},{5,7},{3,5},{1,3},{0,1},{10,8},{12,10},{14... | collective-permute-start | bytes 405512 | tf_op jit(solution)/shard_map/ppermute | solution.py:433
  24.9 6.3 %collective-permute-start.6 = (bf16[528,128]{1,0:T(8,128)(2,1)S(1)}, bf16[528,128]{1,0:T(8,128)(2,1)S(1)}, u32[]{:S(2)}, u32[]{:S(2)}) collective-permute-start(bf16[528,128]{1,0:T(8,128)(2,1)S(1)} %collective-permute-done.4.refs_0_), channel_id=1, source_target_pairs={{0,2},{2,4},{4,6},{6,7},{7,5},{5,3},{3,1},{1,0},{8,10},{10,12},{12... | collective-permute-start | bytes 405512 | tf_op jit(solution)/shard_map/ppermute | solution.py:430
  25.7 7.3 %collective-permute-start.25 = (bf16[528,128]{1,0:T(8,128)(2,1)S(1)}, bf16[528,128]{1,0:T(8,128)(2,1)S(1)}, u32[]{:S(2)}, u32[]{:S(2)}) collective-permute-start(bf16[528,128]{1,0:T(8,128)(2,1)S(1)} %collective-permute-done.24.refs_1_), channel_id=1, source_target_pairs={{2,0},{4,2},{6,4},{7,6},{5,7},{3,5},{1,3},{0,1},{10,8},{12,10},{14... | collective-permute-start | bytes 405512 | tf_op jit(solution)/shard_map/ppermute | solution.py:433
  28.3 6.8 %collective-permute-start.13 = (bf16[528,128]{1,0:T(8,128)(2,1)S(1)}, bf16[528,128]{1,0:T(8,128)(2,1)S(1)}, u32[]{:S(2)}, u32[]{:S(2)}) collective-permute-start(bf16[528,128]{1,0:T(8,128)(2,1)S(1)} %collective-permute-done.8.refs_1_), channel_id=1, source_target_pairs={{2,0},{4,2},{6,4},{7,6},{5,7},{3,5},{1,3},{0,1},{10,8},{12,10},{14... | collective-permute-start | bytes 405512 | tf_op jit(solution)/shard_map/ppermute | solution.py:433
  29.7 7.7 %collective-permute-start.29 = (bf16[528,128]{1,0:T(8,128)(2,1)S(1)}, bf16[528,128]{1,0:T(8,128)(2,1)S(1)}, u32[]{:S(2)}, u32[]{:S(2)}) collective-permute-start(bf16[528,128]{1,0:T(8,128)(2,1)S(1)} %collective-permute-done.23.refs_0_), channel_id=1, source_target_pairs={{0,2},{2,4},{4,6},{6,7},{7,5},{5,3},{3,1},{1,0},{8,10},{10,12},{12... | collective-permute-start | bytes 405512 | tf_op jit(solution)/shard_map/ppermute | solution.py:430
  32.0 6.2 %collective-permute-start.9 = (bf16[528,128]{1,0:T(8,128)(2,1)S(1)}, bf16[528,128]{1,0:T(8,128)(2,1)S(1)}, u32[]{:S(2)}, u32[]{:S(2)}) collective-permute-start(bf16[528,128]{1,0:T(8,128)(2,1)S(1)} %slice.8), channel_id=1, source_target_pairs={{0,2},{2,4},{4,6},{6,7},{7,5},{5,3},{3,1},{1,0},{8,10},{10,12},{12... | collective-permute-start | bytes 405512 | tf_op jit(solution)/shard_map/ppermute | solution.py:430
  33.4 6.3 %collective-permute-start.26 = (bf16[528,128]{1,0:T(8,128)(2,1)S(1)}, bf16[528,128]{1,0:T(8,128)(2,1)S(1)}, u32[]{:S(2)}, u32[]{:S(2)}) collective-permute-start(bf16[528,128]{1,0:T(8,128)(2,1)S(1)} %slice.9), channel_id=1, source_target_pairs={{2,0},{4,2},{6,4},{7,6},{5,7},{3,5},{1,3},{0,1},{10,8},{12,10},{14... | collective-permute-start | bytes 405512 | tf_op jit(solution)/shard_map/ppermute | solution.py:433
  35.3 6.4 %collective-permute-start.14 = (bf16[528,128]{1,0:T(8,128)(2,1)S(1)}, bf16[528,128]{1,0:T(8,128)(2,1)S(1)}, u32[]{:S(2)}, u32[]{:S(2)}) collective-permute-start(bf16[528,128]{1,0:T(8,128)(2,1)S(1)} %shard_map.76), channel_id=1, source_target_pairs={{2,0},{4,2},{6,4},{7,6},{5,7},{3,5},{1,3},{0,1},{10,8},{12,10},{14... | collective-permute-start | bytes 405512 | tf_op jit(solution)/shard_map/ppermute | solution.py:433
  38.2 6.5 %collective-permute-start.30 = (bf16[528,128]{1,0:T(8,128)(2,1)S(1)}, bf16[528,128]{1,0:T(8,128)(2,1)S(1)}, u32[]{:S(2)}, u32[]{:S(2)}) collective-permute-start(bf16[528,128]{1,0:T(8,128)(2,1)S(1)} %shard_map.87), channel_id=1, source_target_pairs={{0,2},{2,4},{4,6},{6,7},{7,5},{5,3},{3,1},{1,0},{8,10},{10,12},{12... | collective-permute-start | bytes 405512 | tf_op jit(solution)/shard_map/ppermute | solution.py:430
  38.5 8.9 %collective-permute-start.10 = (bf16[528,128]{1,0:T(8,128)(2,1)S(1)}, bf16[528,128]{1,0:T(8,128)(2,1)S(1)}, u32[]{:S(2)}, u32[]{:S(2)}) collective-permute-start(bf16[528,128]{1,0:T(8,128)(2,1)S(1)} %shard_map.73), channel_id=1, source_target_pairs={{0,2},{2,4},{4,6},{6,7},{7,5},{5,3},{3,1},{1,0},{8,10},{10,12},{12... | collective-permute-start | bytes 405512 | tf_op jit(solution)/shard_map/ppermute | solution.py:430
  40.1 7.7 %collective-permute-start.27 = (bf16[528,128]{1,0:T(8,128)(2,1)S(1)}, bf16[528,128]{1,0:T(8,128)(2,1)S(1)}, u32[]{:S(2)}, u32[]{:S(2)}) collective-permute-start(bf16[528,128]{1,0:T(8,128)(2,1)S(1)} %shard_map.84), channel_id=1, source_target_pairs={{2,0},{4,2},{6,4},{7,6},{5,7},{3,5},{1,3},{0,1},{10,8},{12,10},{14... | collective-permute-start | bytes 405512 | tf_op jit(solution)/shard_map/ppermute | solution.py:433
  42.0 8.1 %collective-permute-start.15 = (bf16[528,128]{1,0:T(8,128)(2,1)S(1)}, bf16[528,128]{1,0:T(8,128)(2,1)S(1)}, u32[]{:S(2)}, u32[]{:S(2)}) collective-permute-start(bf16[528,128]{1,0:T(8,128)(2,1)S(1)} %shard_map.77), channel_id=1, source_target_pairs={{2,0},{4,2},{6,4},{7,6},{5,7},{3,5},{1,3},{0,1},{10,8},{12,10},{14... | collective-permute-start | bytes 405512 | tf_op jit(solution)/shard_map/ppermute | solution.py:433
  44.9 7.0 %collective-permute-start.31 = (bf16[528,128]{1,0:T(8,128)(2,1)S(1)}, bf16[528,128]{1,0:T(8,128)(2,1)S(1)}, u32[]{:S(2)}, u32[]{:S(2)}) collective-permute-start(bf16[528,128]{1,0:T(8,128)(2,1)S(1)} %shard_map.88), channel_id=1, source_target_pairs={{0,2},{2,4},{4,6},{6,7},{7,5},{5,3},{3,1},{1,0},{8,10},{10,12},{12... | collective-permute-start | bytes 405512 | tf_op jit(solution)/shard_map/ppermute | solution.py:430
  48.1 6.5 %collective-permute-start.28 = (bf16[528,128]{1,0:T(8,128)(2,1)S(1)}, bf16[528,128]{1,0:T(8,128)(2,1)S(1)}, u32[]{:S(2)}, u32[]{:S(2)}) collective-permute-start(bf16[528,128]{1,0:T(8,128)(2,1)S(1)} %shard_map.85), channel_id=1, source_target_pairs={{2,0},{4,2},{6,4},{7,6},{5,7},{3,5},{1,3},{0,1},{10,8},{12,10},{14... | collective-permute-start | bytes 405512 | tf_op jit(solution)/shard_map/ppermute | solution.py:433
  52.2 6.4 %collective-permute-start.32 = (bf16[528,128]{1,0:T(8,128)(2,1)S(1)}, bf16[528,128]{1,0:T(8,128)(2,1)S(1)}, u32[]{:S(2)}, u32[]{:S(2)}) collective-permute-start(bf16[528,128]{1,0:T(8,128)(2,1)S(1)} %shard_map.89), channel_id=1, source_target_pairs={{0,2},{2,4},{4,6},{6,7},{7,5},{5,3},{3,1},{1,0},{8,10},{10,12},{12... | collective-permute-start | bytes 405512 | tf_op jit(solution)/shard_map/ppermute | solution.py:430
  53.0 7.0 %collective-permute-start.12 = (bf16[272,128]{1,0:T(8,128)(2,1)S(1)}, bf16[272,128]{1,0:T(8,128)(2,1)S(1)}, u32[]{:S(2)}, u32[]{:S(2)}) collective-permute-start(bf16[272,128]{1,0:T(8,128)(2,1)S(1)} %get-tuple-element.44), channel_id=1, source_target_pairs={{0,16},{8,24},{16,0},{24,8},{1,17},{9,25},{17,1},{25,9},{2,18},{10... | collective-permute-start | bytes 208904 | tf_op jit(solution)/shard_map/ppermute | solution.py:417
  54.9 9.5 %collective-permute-start.34 = (bf16[272,128]{1,0:T(8,128)(2,1)S(1)}, bf16[272,128]{1,0:T(8,128)(2,1)S(1)}, u32[]{:S(2)}, u32[]{:S(2)}) collective-permute-start(bf16[272,128]{1,0:T(8,128)(2,1)S(1)} %get-tuple-element.57), channel_id=1, source_target_pairs={{0,8},{8,0},{16,24},{24,16},{1,9},{9,1},{17,25},{25,17},{2,10},{10... | collective-permute-start | bytes 208904 | tf_op jit(solution)/shard_map/ppermute | solution.py:417
  60.1 6.1 %collective-permute-start.35 = (bf16[272,128]{1,0:T(8,128)(2,1)S(1)}, bf16[272,128]{1,0:T(8,128)(2,1)S(1)}, u32[]{:S(2)}, u32[]{:S(2)}) collective-permute-start(bf16[272,128]{1,0:T(8,128)(2,1)S(1)} %get-tuple-element.58), channel_id=1, source_target_pairs={{0,10},{2,12},{4,14},{6,15},{7,13},{5,11},{3,9},{1,8},{8,2},{10,4}... | collective-permute-start | bytes 208904 | tf_op jit(solution)/shard_map/ppermute | solution.py:458
  (16 other events, 76.5 us)

commit v16 on v14

--- a/solution.py
+++ b/solution.py
@@ -127,14 +127,14 @@
     queries, (new_ref, out_ref, level_ref) = refs[:-3], refs[-3:]
     step = lax.broadcasted_iota(jnp.int32, (ROWS, STEPS), 0) % STEPS
     usable = lax.broadcasted_iota(jnp.int32, (ROWS, STEPS), 1) <= step
-    for pair in range(0, len(queries), 2):
+    for four in range(0, len(queries), 4):
         requests = []
-        for d in (pair, pair + 1):
+        for d in range(four, four + 4):
             new = new_ref[group ^ d]
             heads = [new[:, head * HD : (head + 1) * HD] for head in range(2 * KVH)]
             rows = [queries[d][head * ROWS : (head + 1) * ROWS, :] for head in range(KVH)]
             requests.append((rows, heads[:KVH], heads[KVH:], usable, 0))
-        for d, (mixed, level) in zip((pair, pair + 1), attend(requests)):
+        for d, (mixed, level) in zip(range(four, four + 4), attend(requests)):
             for head, values in enumerate(mixed):
                 out_ref[d, head * ROWS : (head + 1) * ROWS, :] = values
             level_ref[d] = level

time: 67.2 us -> 66.8 us (level)
  starting transfers between devices: 41 us -> 38.3 us
  Pallas kernels: 10.7 us -> 12.3 us
    ppermute x13, starting transfers between devices: 18.8 us -> 15 us  [down(): return lax.ppermute(array, 'cache', backward)]
    pallas_call x9, Pallas kernels: 4.91 us -> 6.73 us  [items(): pl.pallas_call(functools.partial(item_kernel, slots, visitors, owners), o...]
    ppermute x13, waiting for transfers between devices: 1.86 us -> 3.41 us  [down(): return lax.ppermute(array, 'cache', backward)]
  transfers between devices with their start and end apart: 36 -> 36, of which waited for: 10 -> 11; matrix products, arithmetic and copies ran while one was open for 1% -> 1% of each run, Pallas kernels for 14% -> 17%
where the time goes in v16:
time: 66.8 us; the launch traced here: 66.4 us
  starting transfers between devices  38.3 us (57%)
  Pallas kernels  12.3 us (18%)
  waiting for transfers between devices  10.4 us (16%)
  local copies, waits for them, and re-layouts  4.35 us (7%)
  other arithmetic  0.79 us (1%)
    ppermute x13, starting transfers between devices, down(): return lax.ppermute(array, 'cache', backward)  15 us
    ppermute x13, starting transfers between devices, up(): return lax.ppermute(array, 'cache', forward)  12.6 us
    pallas_call x9, Pallas kernels, items(): pl.pallas_call(functools.partial(item_kernel, slots, visitors, owners), o...  6.73 us
    ppermute x6, starting transfers between devices, swap(): lax.ppermute(array, 'grp', [(g, g ^ d) for g in range(groups)])  6 us
    ppermute x4, starting transfers between devices, straight(): return lax.ppermute(array, ('grp', 'cache'), pairs)  4.77 us
    unnamed x8, local copies, waits for them, and re-layouts  4.33 us
    ppermute x4, waiting for transfers between devices, straight(): return lax.ppermute(array, ('grp', 'cache'), pairs)  4.02 us
    ppermute x13, waiting for transfers between devices, down(): return lax.ppermute(array, 'cache', backward)  3.41 us
  transfers between devices with their start and end apart: 36, of which 11 were waited for; matrix products, arithmetic and copies ran while one was open for 1% of the time, Pallas kernels for 17%

profile of v16, /device:TPU:0, one launch (start us, length us, event | category | flops | bytes accessed | tf_op | source)
XLA Modules:
  0.0 66.4 jit_solution(15342993835026941138)
XLA Ops:
  1.5 2.6 %collective-permute-start.1 = (bf16[256,128]{1,0:T(8,128)(2,1)S(1)}, bf16[256,128]{1,0:T(8,128)(2,1)S(1)}, u32[]{:S(2)}, u32[]{:S(2)}) collective-permute-start(bf16[256,128]{1,0:T(8,128)(2,1)S(1)} %get-tuple-element.34.refs_2_), channel_id=1, source_target_pairs={{0,16},{8,24},{16,0},{24,8},{1,17},{9,25},{17,1},{25,9},{2,18},{10... | collective-permute-start | bytes 196616 | tf_op jit(solution)/shard_map/ppermute | solution.py:411
  5.0 3.4 %copy-done = bf16[16,128,2048]{2,1,0:T(8,128)(2,1)S(1)} copy-done((bf16[16,128,2048]{2,1,0:T(8,128)(2,1)S(1)}, bf16[16,128,2048]{2,1,0:T(8,128)(2,1)}, u32[]{:S(2)}) %copy-start) | copy-done | bytes 8388632
  8.4 1.8 %collective-permute-start.5 = (bf16[528,128]{1,0:T(8,128)(2,1)S(1)}, bf16[528,128]{1,0:T(8,128)(2,1)S(1)}, u32[]{:S(2)}, u32[]{:S(2)}) collective-permute-start(bf16[528,128]{1,0:T(8,128)(2,1)S(1)} %shard_map.67.refs_1_), channel_id=1, source_target_pairs={{2,0},{4,2},{6,4},{7,6},{5,7},{3,5},{1,3},{0,1},{10,8},{12,10},{14... | collective-permute-start | bytes 405512 | tf_op jit(solution)/shard_map/ppermute | solution.py:427
  10.5 1.8 %collective-permute-start.3 = (bf16[528,128]{1,0:T(8,128)(2,1)S(1)}, bf16[528,128]{1,0:T(8,128)(2,1)S(1)}, u32[]{:S(2)}, u32[]{:S(2)}) collective-permute-start(bf16[528,128]{1,0:T(8,128)(2,1)S(1)} %shard_map.67.refs_1_), channel_id=1, source_target_pairs={{0,2},{2,4},{4,6},{6,7},{7,5},{5,3},{3,1},{1,0},{8,10},{10,12},{12... | collective-permute-start | bytes 405512 | tf_op jit(solution)/shard_map/ppermute | solution.py:424
  14.4 2.2 %collective-permute-start.7 = (bf16[528,128]{1,0:T(8,128)(2,1)S(1)}, bf16[528,128]{1,0:T(8,128)(2,1)S(1)}, u32[]{:S(2)}, u32[]{:S(2)}) collective-permute-start(bf16[528,128]{1,0:T(8,128)(2,1)S(1)} %collective-permute-done.5.refs_1_), channel_id=1, source_target_pairs={{2,0},{4,2},{6,4},{7,6},{5,7},{3,5},{1,3},{0,1},{10,8},{12,10},{14... | collective-permute-start | bytes 405512 | tf_op jit(solution)/shard_map/ppermute | solution.py:427
  16.9 2.4 %collective-permute-done.3.refs_0_ = bf16[528,128]{1,0:T(8,128)(2,1)S(1)} collective-permute-done((bf16[528,128]{1,0:T(8,128)(2,1)S(1)}, bf16[528,128]{1,0:T(8,128)(2,1)S(1)}, u32[]{:S(2)}, u32[]{:S(2)}) %collective-permute-start.3) | collective-permute-done | bytes 135200 | tf_op jit(solution)/shard_map/ppermute | solution.py:424
  19.8 1.6 %collective-permute-start.24 = (bf16[528,128]{1,0:T(8,128)(2,1)S(1)}, bf16[528,128]{1,0:T(8,128)(2,1)S(1)}, u32[]{:S(2)}, u32[]{:S(2)}) collective-permute-start(bf16[528,128]{1,0:T(8,128)(2,1)S(1)} %collective-permute-done.22.refs_1_), channel_id=1, source_target_pairs={{2,0},{4,2},{6,4},{7,6},{5,7},{3,5},{1,3},{0,1},{10,8},{12,10},{14... | collective-permute-start | bytes 405512 | tf_op jit(solution)/shard_map/ppermute | solution.py:427
  22.1 1.1 %collective-permute-start.8 = (bf16[528,128]{1,0:T(8,128)(2,1)S(1)}, bf16[528,128]{1,0:T(8,128)(2,1)S(1)}, u32[]{:S(2)}, u32[]{:S(2)}) collective-permute-start(bf16[528,128]{1,0:T(8,128)(2,1)S(1)} %collective-permute-done.7.refs_1_), channel_id=1, source_target_pairs={{2,0},{4,2},{6,4},{7,6},{5,7},{3,5},{1,3},{0,1},{10,8},{12,10},{14... | collective-permute-start | bytes 405512 | tf_op jit(solution)/shard_map/ppermute | solution.py:427
  25.7 1.4 %collective-permute-start.25 = (bf16[528,128]{1,0:T(8,128)(2,1)S(1)}, bf16[528,128]{1,0:T(8,128)(2,1)S(1)}, u32[]{:S(2)}, u32[]{:S(2)}) collective-permute-start(bf16[528,128]{1,0:T(8,128)(2,1)S(1)} %collective-permute-done.24.refs_1_), channel_id=1, source_target_pairs={{2,0},{4,2},{6,4},{7,6},{5,7},{3,5},{1,3},{0,1},{10,8},{12,10},{14... | collective-permute-start | bytes 405512 | tf_op jit(solution)/shard_map/ppermute | solution.py:427
  28.0 1.6 %collective-permute-start.13 = (bf16[528,128]{1,0:T(8,128)(2,1)S(1)}, bf16[528,128]{1,0:T(8,128)(2,1)S(1)}, u32[]{:S(2)}, u32[]{:S(2)}) collective-permute-start(bf16[528,128]{1,0:T(8,128)(2,1)S(1)} %collective-permute-done.8.refs_1_), channel_id=1, source_target_pairs={{2,0},{4,2},{6,4},{7,6},{5,7},{3,5},{1,3},{0,1},{10,8},{12,10},{14... | collective-permute-start | bytes 405512 | tf_op jit(solution)/shard_map/ppermute | solution.py:427
  31.9 1.1 %collective-permute-start.9 = (bf16[528,128]{1,0:T(8,128)(2,1)S(1)}, bf16[528,128]{1,0:T(8,128)(2,1)S(1)}, u32[]{:S(2)}, u32[]{:S(2)}) collective-permute-start(bf16[528,128]{1,0:T(8,128)(2,1)S(1)} %slice.8), channel_id=1, source_target_pairs={{0,2},{2,4},{4,6},{6,7},{7,5},{5,3},{3,1},{1,0},{8,10},{10,12},{12... | collective-permute-start | bytes 405512 | tf_op jit(solution)/shard_map/ppermute | solution.py:424
  35.0 1.1 %collective-permute-start.14 = (bf16[528,128]{1,0:T(8,128)(2,1)S(1)}, bf16[528,128]{1,0:T(8,128)(2,1)S(1)}, u32[]{:S(2)}, u32[]{:S(2)}) collective-permute-start(bf16[528,128]{1,0:T(8,128)(2,1)S(1)} %shard_map.76), channel_id=1, source_target_pairs={{2,0},{4,2},{6,4},{7,6},{5,7},{3,5},{1,3},{0,1},{10,8},{12,10},{14... | collective-permute-start | bytes 405512 | tf_op jit(solution)/shard_map/ppermute | solution.py:427
  38.0 1.8 %collective-permute-start.10 = (bf16[528,128]{1,0:T(8,128)(2,1)S(1)}, bf16[528,128]{1,0:T(8,128)(2,1)S(1)}, u32[]{:S(2)}, u32[]{:S(2)}) collective-permute-start(bf16[528,128]{1,0:T(8,128)(2,1)S(1)} %shard_map.73), channel_id=1, source_target_pairs={{0,2},{2,4},{4,6},{6,7},{7,5},{5,3},{3,1},{1,0},{8,10},{10,12},{12... | collective-permute-start | bytes 405512 | tf_op jit(solution)/shard_map/ppermute | solution.py:424
  40.8 1.4 %collective-permute-done.14.arrived_ref = bf16[528,128]{1,0:T(8,128)(2,1)S(1)} collective-permute-done((bf16[528,128]{1,0:T(8,128)(2,1)S(1)}, bf16[528,128]{1,0:T(8,128)(2,1)S(1)}, u32[]{:S(2)}, u32[]{:S(2)}) %collective-permute-start.14) | collective-permute-done | bytes 135200 | tf_op jit(solution)/shard_map/ppermute | solution.py:427
  42.4 1.2 %collective-permute-start.15 = (bf16[528,128]{1,0:T(8,128)(2,1)S(1)}, bf16[528,128]{1,0:T(8,128)(2,1)S(1)}, u32[]{:S(2)}, u32[]{:S(2)}) collective-permute-start(bf16[528,128]{1,0:T(8,128)(2,1)S(1)} %shard_map.77), channel_id=1, source_target_pairs={{2,0},{4,2},{6,4},{7,6},{5,7},{3,5},{1,3},{0,1},{10,8},{12,10},{14... | collective-permute-start | bytes 405512 | tf_op jit(solution)/shard_map/ppermute | solution.py:427
  43.9 1.3 %collective-permute-start.31 = (bf16[528,128]{1,0:T(8,128)(2,1)S(1)}, bf16[528,128]{1,0:T(8,128)(2,1)S(1)}, u32[]{:S(2)}, u32[]{:S(2)}) collective-permute-start(bf16[528,128]{1,0:T(8,128)(2,1)S(1)} %shard_map.88), channel_id=1, source_target_pairs={{0,2},{2,4},{4,6},{6,7},{7,5},{5,3},{3,1},{1,0},{8,10},{10,12},{12... | collective-permute-start | bytes 405512 | tf_op jit(solution)/shard_map/ppermute | solution.py:424
  45.5 2.1 %collective-permute-start.11 = (bf16[528,128]{1,0:T(8,128)(2,1)S(1)}, bf16[528,128]{1,0:T(8,128)(2,1)S(1)}, u32[]{:S(2)}, u32[]{:S(2)}) collective-permute-start(bf16[528,128]{1,0:T(8,128)(2,1)S(1)} %shard_map.74), channel_id=1, source_target_pairs={{0,2},{2,4},{4,6},{6,7},{7,5},{5,3},{3,1},{1,0},{8,10},{10,12},{12... | collective-permute-start | bytes 405512 | tf_op jit(solution)/shard_map/ppermute | solution.py:424
  47.9 1.3 %collective-permute-done.15.arrived_ref = bf16[528,128]{1,0:T(8,128)(2,1)S(1)} collective-permute-done((bf16[528,128]{1,0:T(8,128)(2,1)S(1)}, bf16[528,128]{1,0:T(8,128)(2,1)S(1)}, u32[]{:S(2)}, u32[]{:S(2)}) %collective-permute-start.15) | collective-permute-done | bytes 135200 | tf_op jit(solution)/shard_map/ppermute | solution.py:427
  50.7 1.2 %collective-permute-start.32 = (bf16[528,128]{1,0:T(8,128)(2,1)S(1)}, bf16[528,128]{1,0:T(8,128)(2,1)S(1)}, u32[]{:S(2)}, u32[]{:S(2)}) collective-permute-start(bf16[528,128]{1,0:T(8,128)(2,1)S(1)} %shard_map.89), channel_id=1, source_target_pairs={{0,2},{2,4},{4,6},{6,7},{7,5},{5,3},{3,1},{1,0},{8,10},{10,12},{12... | collective-permute-start | bytes 405512 | tf_op jit(solution)/shard_map/ppermute | solution.py:424
  52.2 2.6 %collective-permute-start.12 = (bf16[272,128]{1,0:T(8,128)(2,1)S(1)}, bf16[272,128]{1,0:T(8,128)(2,1)S(1)}, u32[]{:S(2)}, u32[]{:S(2)}) collective-permute-start(bf16[272,128]{1,0:T(8,128)(2,1)S(1)} %get-tuple-element.44), channel_id=1, source_target_pairs={{0,16},{8,24},{16,0},{24,8},{1,17},{9,25},{17,1},{25,9},{2,18},{10... | collective-permute-start | bytes 208904 | tf_op jit(solution)/shard_map/ppermute | solution.py:411
  55.6 2.4 %collective-permute-start.17 = (bf16[272,128]{1,0:T(8,128)(2,1)S(1)}, bf16[272,128]{1,0:T(8,128)(2,1)S(1)}, u32[]{:S(2)}, u32[]{:S(2)}) collective-permute-start(bf16[272,128]{1,0:T(8,128)(2,1)S(1)} %get-tuple-element.45), channel_id=1, source_target_pairs={{2,16},{4,18},{6,20},{7,22},{5,23},{3,21},{1,19},{0,17},{10,24},{1... | collective-permute-start | bytes 208904 | tf_op jit(solution)/shard_map/ppermute | solution.py:452
  59.5 1.2 %collective-permute-start.35 = (bf16[272,128]{1,0:T(8,128)(2,1)S(1)}, bf16[272,128]{1,0:T(8,128)(2,1)S(1)}, u32[]{:S(2)}, u32[]{:S(2)}) collective-permute-start(bf16[272,128]{1,0:T(8,128)(2,1)S(1)} %get-tuple-element.58), channel_id=1, source_target_pairs={{0,10},{2,12},{4,14},{6,15},{7,13},{5,11},{3,9},{1,8},{8,2},{10,4}... | collective-permute-start | bytes 208904 | tf_op jit(solution)/shard_map/ppermute | solution.py:452
  60.9 2.3 %collective-permute-done.19.refs_3_ = bf16[272,128]{1,0:T(8,128)(2,1)S(1)} collective-permute-done((bf16[272,128]{1,0:T(8,128)(2,1)S(1)}, bf16[272,128]{1,0:T(8,128)(2,1)S(1)}, u32[]{:S(2)}, u32[]{:S(2)}) %collective-permute-start.19) | collective-permute-done | bytes 69664 | tf_op jit(solution)/shard_map/ppermute | solution.py:452
  65.2 1.2 %shard_map.91 = bf16[4,4,8192]{2,1,0:T(4,128)(2,1)} custom-call(s32[1]{0:T(128)} %bitcast.place_ref, bf16[2,4,8192]{2,1,0:T(4,128)(2,1)S(1)} %shard_map.80.refs_0_, bf16[272,128]{1,0:T(8,128)(2,1)S(1)} %get-tuple-element.55.refs_1_, bf16[272,128]{1,0:T(8,128)(2,1)S(1)} %collective-permute-done.33.refs_2_, ...), custom_call_target="tpu_custom_call" | custom-call | bytes 655360 | tf_op jit(solution)/shard_map/pallas_call | solution.py:384
  (88 shorter events, 24.4 us)
Async XLA Ops:
  1.5 6.9 %collective-permute-start.1 = (bf16[256,128]{1,0:T(8,128)(2,1)S(1)}, bf16[256,128]{1,0:T(8,128)(2,1)S(1)}, u32[]{:S(2)}, u32[]{:S(2)}) collective-permute-start(bf16[256,128]{1,0:T(8,128)(2,1)S(1)} %get-tuple-element.34.refs_2_), channel_id=1, source_target_pairs={{0,16},{8,24},{16,0},{24,8},{1,17},{9,25},{17,1},{25,9},{2,18},{10... | collective-permute-start | bytes 196616 | tf_op jit(solution)/shard_map/ppermute | solution.py:411
  8.4 5.9 %collective-permute-start.5 = (bf16[528,128]{1,0:T(8,128)(2,1)S(1)}, bf16[528,128]{1,0:T(8,128)(2,1)S(1)}, u32[]{:S(2)}, u32[]{:S(2)}) collective-permute-start(bf16[528,128]{1,0:T(8,128)(2,1)S(1)} %shard_map.67.refs_1_), channel_id=1, source_target_pairs={{2,0},{4,2},{6,4},{7,6},{5,7},{3,5},{1,3},{0,1},{10,8},{12,10},{14... | collective-permute-start | bytes 405512 | tf_op jit(solution)/shard_map/ppermute | solution.py:427
  10.2 6.4 %collective-permute-start.20 = (bf16[528,128]{1,0:T(8,128)(2,1)S(1)}, bf16[528,128]{1,0:T(8,128)(2,1)S(1)}, u32[]{:S(2)}, u32[]{:S(2)}) collective-permute-start(bf16[528,128]{1,0:T(8,128)(2,1)S(1)} %shard_map.65.after_ref.refs_0_), channel_id=1, source_target_pairs={{0,2},{2,4},{4,6},{6,7},{7,5},{5,3},{3,1},{1,0},{8,10},{10,12},{12... | collective-permute-start | bytes 405512 | tf_op jit(solution)/shard_map/ppermute | solution.py:424
  10.5 8.8 %collective-permute-start.3 = (bf16[528,128]{1,0:T(8,128)(2,1)S(1)}, bf16[528,128]{1,0:T(8,128)(2,1)S(1)}, u32[]{:S(2)}, u32[]{:S(2)}) collective-permute-start(bf16[528,128]{1,0:T(8,128)(2,1)S(1)} %shard_map.67.refs_1_), channel_id=1, source_target_pairs={{0,2},{2,4},{4,6},{6,7},{7,5},{5,3},{3,1},{1,0},{8,10},{10,12},{12... | collective-permute-start | bytes 405512 | tf_op jit(solution)/shard_map/ppermute | solution.py:424
  12.3 7.5 %collective-permute-start.22 = (bf16[528,128]{1,0:T(8,128)(2,1)S(1)}, bf16[528,128]{1,0:T(8,128)(2,1)S(1)}, u32[]{:S(2)}, u32[]{:S(2)}) collective-permute-start(bf16[528,128]{1,0:T(8,128)(2,1)S(1)} %shard_map.65.after_ref.refs_0_), channel_id=1, source_target_pairs={{2,0},{4,2},{6,4},{7,6},{5,7},{3,5},{1,3},{0,1},{10,8},{12,10},{14... | collective-permute-start | bytes 405512 | tf_op jit(solution)/shard_map/ppermute | solution.py:427
  14.4 7.7 %collective-permute-start.7 = (bf16[528,128]{1,0:T(8,128)(2,1)S(1)}, bf16[528,128]{1,0:T(8,128)(2,1)S(1)}, u32[]{:S(2)}, u32[]{:S(2)}) collective-permute-start(bf16[528,128]{1,0:T(8,128)(2,1)S(1)} %collective-permute-done.5.refs_1_), channel_id=1, source_target_pairs={{2,0},{4,2},{6,4},{7,6},{5,7},{3,5},{1,3},{0,1},{10,8},{12,10},{14... | collective-permute-start | bytes 405512 | tf_op jit(solution)/shard_map/ppermute | solution.py:427
  16.6 7.4 %collective-permute-start.21 = (bf16[528,128]{1,0:T(8,128)(2,1)S(1)}, bf16[528,128]{1,0:T(8,128)(2,1)S(1)}, u32[]{:S(2)}, u32[]{:S(2)}) collective-permute-start(bf16[528,128]{1,0:T(8,128)(2,1)S(1)} %collective-permute-done.20.refs_0_), channel_id=1, source_target_pairs={{0,2},{2,4},{4,6},{6,7},{7,5},{5,3},{3,1},{1,0},{8,10},{10,12},{12... | collective-permute-start | bytes 405512 | tf_op jit(solution)/shard_map/ppermute | solution.py:424
  19.8 6.0 %collective-permute-start.24 = (bf16[528,128]{1,0:T(8,128)(2,1)S(1)}, bf16[528,128]{1,0:T(8,128)(2,1)S(1)}, u32[]{:S(2)}, u32[]{:S(2)}) collective-permute-start(bf16[528,128]{1,0:T(8,128)(2,1)S(1)} %collective-permute-done.22.refs_1_), channel_id=1, source_target_pairs={{2,0},{4,2},{6,4},{7,6},{5,7},{3,5},{1,3},{0,1},{10,8},{12,10},{14... | collective-permute-start | bytes 405512 | tf_op jit(solution)/shard_map/ppermute | solution.py:427
  22.1 5.9 %collective-permute-start.8 = (bf16[528,128]{1,0:T(8,128)(2,1)S(1)}, bf16[528,128]{1,0:T(8,128)(2,1)S(1)}, u32[]{:S(2)}, u32[]{:S(2)}) collective-permute-start(bf16[528,128]{1,0:T(8,128)(2,1)S(1)} %collective-permute-done.7.refs_1_), channel_id=1, source_target_pairs={{2,0},{4,2},{6,4},{7,6},{5,7},{3,5},{1,3},{0,1},{10,8},{12,10},{14... | collective-permute-start | bytes 405512 | tf_op jit(solution)/shard_map/ppermute | solution.py:427
  24.1 6.3 %collective-permute-start.23 = (bf16[528,128]{1,0:T(8,128)(2,1)S(1)}, bf16[528,128]{1,0:T(8,128)(2,1)S(1)}, u32[]{:S(2)}, u32[]{:S(2)}) collective-permute-start(bf16[528,128]{1,0:T(8,128)(2,1)S(1)} %collective-permute-done.21.refs_0_), channel_id=1, source_target_pairs={{0,2},{2,4},{4,6},{6,7},{7,5},{5,3},{3,1},{1,0},{8,10},{10,12},{12... | collective-permute-start | bytes 405512 | tf_op jit(solution)/shard_map/ppermute | solution.py:424
  25.1 5.9 %collective-permute-start.6 = (bf16[528,128]{1,0:T(8,128)(2,1)S(1)}, bf16[528,128]{1,0:T(8,128)(2,1)S(1)}, u32[]{:S(2)}, u32[]{:S(2)}) collective-permute-start(bf16[528,128]{1,0:T(8,128)(2,1)S(1)} %collective-permute-done.4.refs_0_), channel_id=1, source_target_pairs={{0,2},{2,4},{4,6},{6,7},{7,5},{5,3},{3,1},{1,0},{8,10},{10,12},{12... | collective-permute-start | bytes 405512 | tf_op jit(solution)/shard_map/ppermute | solution.py:424
  25.7 7.2 %collective-permute-start.25 = (bf16[528,128]{1,0:T(8,128)(2,1)S(1)}, bf16[528,128]{1,0:T(8,128)(2,1)S(1)}, u32[]{:S(2)}, u32[]{:S(2)}) collective-permute-start(bf16[528,128]{1,0:T(8,128)(2,1)S(1)} %collective-permute-done.24.refs_1_), channel_id=1, source_target_pairs={{2,0},{4,2},{6,4},{7,6},{5,7},{3,5},{1,3},{0,1},{10,8},{12,10},{14... | collective-permute-start | bytes 405512 | tf_op jit(solution)/shard_map/ppermute | solution.py:427
  28.0 6.7 %collective-permute-start.13 = (bf16[528,128]{1,0:T(8,128)(2,1)S(1)}, bf16[528,128]{1,0:T(8,128)(2,1)S(1)}, u32[]{:S(2)}, u32[]{:S(2)}) collective-permute-start(bf16[528,128]{1,0:T(8,128)(2,1)S(1)} %collective-permute-done.8.refs_1_), channel_id=1, source_target_pairs={{2,0},{4,2},{6,4},{7,6},{5,7},{3,5},{1,3},{0,1},{10,8},{12,10},{14... | collective-permute-start | bytes 405512 | tf_op jit(solution)/shard_map/ppermute | solution.py:427
  35.0 7.2 %collective-permute-start.14 = (bf16[528,128]{1,0:T(8,128)(2,1)S(1)}, bf16[528,128]{1,0:T(8,128)(2,1)S(1)}, u32[]{:S(2)}, u32[]{:S(2)}) collective-permute-start(bf16[528,128]{1,0:T(8,128)(2,1)S(1)} %shard_map.76), channel_id=1, source_target_pairs={{2,0},{4,2},{6,4},{7,6},{5,7},{3,5},{1,3},{0,1},{10,8},{12,10},{14... | collective-permute-start | bytes 405512 | tf_op jit(solution)/shard_map/ppermute | solution.py:427
  36.9 6.8 %collective-permute-start.30 = (bf16[528,128]{1,0:T(8,128)(2,1)S(1)}, bf16[528,128]{1,0:T(8,128)(2,1)S(1)}, u32[]{:S(2)}, u32[]{:S(2)}) collective-permute-start(bf16[528,128]{1,0:T(8,128)(2,1)S(1)} %shard_map.87), channel_id=1, source_target_pairs={{0,2},{2,4},{4,6},{6,7},{7,5},{5,3},{3,1},{1,0},{8,10},{10,12},{12... | collective-permute-start | bytes 405512 | tf_op jit(solution)/shard_map/ppermute | solution.py:424
  38.0 7.2 %collective-permute-start.10 = (bf16[528,128]{1,0:T(8,128)(2,1)S(1)}, bf16[528,128]{1,0:T(8,128)(2,1)S(1)}, u32[]{:S(2)}, u32[]{:S(2)}) collective-permute-start(bf16[528,128]{1,0:T(8,128)(2,1)S(1)} %shard_map.73), channel_id=1, source_target_pairs={{0,2},{2,4},{4,6},{6,7},{7,5},{5,3},{3,1},{1,0},{8,10},{10,12},{12... | collective-permute-start | bytes 405512 | tf_op jit(solution)/shard_map/ppermute | solution.py:424
  40.0 7.5 %collective-permute-start.27 = (bf16[528,128]{1,0:T(8,128)(2,1)S(1)}, bf16[528,128]{1,0:T(8,128)(2,1)S(1)}, u32[]{:S(2)}, u32[]{:S(2)}) collective-permute-start(bf16[528,128]{1,0:T(8,128)(2,1)S(1)} %shard_map.84), channel_id=1, source_target_pairs={{2,0},{4,2},{6,4},{7,6},{5,7},{3,5},{1,3},{0,1},{10,8},{12,10},{14... | collective-permute-start | bytes 405512 | tf_op jit(solution)/shard_map/ppermute | solution.py:427
  42.4 6.7 %collective-permute-start.15 = (bf16[528,128]{1,0:T(8,128)(2,1)S(1)}, bf16[528,128]{1,0:T(8,128)(2,1)S(1)}, u32[]{:S(2)}, u32[]{:S(2)}) collective-permute-start(bf16[528,128]{1,0:T(8,128)(2,1)S(1)} %shard_map.77), channel_id=1, source_target_pairs={{2,0},{4,2},{6,4},{7,6},{5,7},{3,5},{1,3},{0,1},{10,8},{12,10},{14... | collective-permute-start | bytes 405512 | tf_op jit(solution)/shard_map/ppermute | solution.py:427
  43.9 6.5 %collective-permute-start.31 = (bf16[528,128]{1,0:T(8,128)(2,1)S(1)}, bf16[528,128]{1,0:T(8,128)(2,1)S(1)}, u32[]{:S(2)}, u32[]{:S(2)}) collective-permute-start(bf16[528,128]{1,0:T(8,128)(2,1)S(1)} %shard_map.88), channel_id=1, source_target_pairs={{0,2},{2,4},{4,6},{6,7},{7,5},{5,3},{3,1},{1,0},{8,10},{10,12},{12... | collective-permute-start | bytes 405512 | tf_op jit(solution)/shard_map/ppermute | solution.py:424
  45.5 6.4 %collective-permute-start.11 = (bf16[528,128]{1,0:T(8,128)(2,1)S(1)}, bf16[528,128]{1,0:T(8,128)(2,1)S(1)}, u32[]{:S(2)}, u32[]{:S(2)}) collective-permute-start(bf16[528,128]{1,0:T(8,128)(2,1)S(1)} %shard_map.74), channel_id=1, source_target_pairs={{0,2},{2,4},{4,6},{6,7},{7,5},{5,3},{3,1},{1,0},{8,10},{10,12},{12... | collective-permute-start | bytes 405512 | tf_op jit(solution)/shard_map/ppermute | solution.py:424
  47.8 7.0 %collective-permute-start.28 = (bf16[528,128]{1,0:T(8,128)(2,1)S(1)}, bf16[528,128]{1,0:T(8,128)(2,1)S(1)}, u32[]{:S(2)}, u32[]{:S(2)}) collective-permute-start(bf16[528,128]{1,0:T(8,128)(2,1)S(1)} %shard_map.85), channel_id=1, source_target_pairs={{2,0},{4,2},{6,4},{7,6},{5,7},{3,5},{1,3},{0,1},{10,8},{12,10},{14... | collective-permute-start | bytes 405512 | tf_op jit(solution)/shard_map/ppermute | solution.py:427
  50.7 7.2 %collective-permute-start.32 = (bf16[528,128]{1,0:T(8,128)(2,1)S(1)}, bf16[528,128]{1,0:T(8,128)(2,1)S(1)}, u32[]{:S(2)}, u32[]{:S(2)}) collective-permute-start(bf16[528,128]{1,0:T(8,128)(2,1)S(1)} %shard_map.89), channel_id=1, source_target_pairs={{0,2},{2,4},{4,6},{6,7},{7,5},{5,3},{3,1},{1,0},{8,10},{10,12},{12... | collective-permute-start | bytes 405512 | tf_op jit(solution)/shard_map/ppermute | solution.py:424
  52.2 6.8 %collective-permute-start.12 = (bf16[272,128]{1,0:T(8,128)(2,1)S(1)}, bf16[272,128]{1,0:T(8,128)(2,1)S(1)}, u32[]{:S(2)}, u32[]{:S(2)}) collective-permute-start(bf16[272,128]{1,0:T(8,128)(2,1)S(1)} %get-tuple-element.44), channel_id=1, source_target_pairs={{0,16},{8,24},{16,0},{24,8},{1,17},{9,25},{17,1},{25,9},{2,18},{10... | collective-permute-start | bytes 208904 | tf_op jit(solution)/shard_map/ppermute | solution.py:411
  55.0 8.7 %collective-permute-start.34 = (bf16[272,128]{1,0:T(8,128)(2,1)S(1)}, bf16[272,128]{1,0:T(8,128)(2,1)S(1)}, u32[]{:S(2)}, u32[]{:S(2)}) collective-permute-start(bf16[272,128]{1,0:T(8,128)(2,1)S(1)} %get-tuple-element.57), channel_id=1, source_target_pairs={{0,8},{8,0},{16,24},{24,16},{1,9},{9,1},{17,25},{25,17},{2,10},{10... | collective-permute-start | bytes 208904 | tf_op jit(solution)/shard_map/ppermute | solution.py:411
  (16 other events, 77.0 us)
